TPU v7x, 32 devices: a whole 2x2x4 slice. The times are simulated.
32 devices in a mesh: atoms: 16 (over z, x, core), dirs: 2 (over y).
Axes of the slice: x: 2, y: 2, z: 4, core: 2. Of those that a mesh axis runs over, the one named last changes fastest.
Arguments:
- queries: bfloat16 [32768, 128], P('atoms'), may hold values from -6 to 6
- keys: bfloat16 [32768, 128], P('atoms'), may hold values from -6 to 6
- values: bfloat16 [32768, 128], P('atoms'), may hold values from -6 to 6
- cotangent: bfloat16 [32768, 128], P('atoms'), may hold values from -6 to 6
- positions: float32 [3, 32768], P(None, 'atoms'), may hold values from -32 to 32
- species: int32 [32768], P('atoms'), may hold values from 0 to 4
- domain: int32 [32768], P('atoms'), may hold values from 0 to 16, as said below
- species_gain: float32 [5, 128], replicated, may hold values from 0.1 to 1.9
- frequency: float32 [32], replicated, may hold values from 0.02 to 1
- directions: float32 [3, 88], P(None, 'dirs'), may hold values from -1 to 1, as said below
- dir_weight: float32 [88], P('dirs'), may hold values from 0.003 to 0.03
- dir_mask: int32 [88], P('dirs'), may hold values from 0 to 1, as said below
Outputs:
- attended: bfloat16 [32768, 128], P(('atoms', 'dirs'))
- grad_queries: bfloat16 [32768, 128], P(('atoms', 'dirs'))
- grad_keys: bfloat16 [32768, 128], P(('atoms', 'dirs'))
- grad_values: bfloat16 [32768, 128], P(('atoms', 'dirs'))
Inputs may be any that keep to these rules, and one draw needn't show every extreme that they name: The 2048 slots from b * 2048 on belong to domain b: they hold b for its atoms first, then 32768 // 2048 for empty slots; every domain has 1024 to 2048 atoms. `directions`: each column is a unit vector. `dir_mask`: exactly 86 entries are 1.
All inputs are finite; a program needn't handle non-finite values.
Results may differ from a plain program's by a relative error of at most 0.012.
Values may be sent and summed in bfloat16 or wider, within the bound.
No kernel may reach another device: no remote copies, remote signals or barrier semaphores. Data moves between devices by JAX's collectives and lax.ppermute only.
A program may use at most 128 MiB of HBM per device.

v0:
```python
import math

import jax
import jax.numpy as jnp
from jax import lax
from jax.sharding import PartitionSpec as P


def rotate(features, cosine, sine_val):
    half_width = features.shape[-1] // 2
    leading = features[..., :half_width]
    trailing = features[..., half_width:]
    return jnp.concatenate(
        [leading * cosine - trailing * sine_val, leading * sine_val + trailing * cosine], axis=-1
    )


def phases(dir_proj, pair_freq):
    phase_angle = dir_proj[..., None] * pair_freq
    return (jnp.cos(phase_angle), jnp.sin(phase_angle))


def sum_states(states):
    return lax.psum(states, "atoms").astype(jnp.bfloat16)


def sum_grads(state_grads):
    return lax.psum(state_grads, "atoms").astype(jnp.bfloat16)


def per_device(
    queries,
    keys,
    values,
    cotangent,
    positions,
    species,
    domain,
    species_gain,
    frequency,
    directions,
    dir_weight,
    dir_mask,
):
    atom_count = queries.shape[0]
    feat_width = queries.shape[1]
    local_dirs = dir_weight.shape[0]
    group_size = 4
    group_count = local_dirs // group_size
    alive_mask = (domain == lax.axis_index("atoms")).astype(jnp.float32)[:, None]
    species_ids = jnp.arange(species_gain.shape[0], dtype=jnp.int32)
    chosen = (species[:, None] == species_ids[None, :]).astype(jnp.float32)
    gain_rows = jnp.sum(chosen[:, :, None] * species_gain[None, :, :], axis=1)
    keys_gained = keys.astype(jnp.float32) * gain_rows * alive_mask
    queries_full = queries.astype(jnp.float32)
    alive_half = alive_mask.astype(jnp.bfloat16)
    values_live = values * alive_half
    grad_live = cotangent * alive_half
    pair_freq = jnp.tile(frequency, feat_width // 2 // frequency.shape[0])
    projected = (
        directions[0][:, None] * positions[0][None, :]
        + directions[1][:, None] * positions[1][None, :]
    )
    projected = projected + directions[2][:, None] * positions[2][None, :]
    projected = projected.reshape(group_count, group_size, atom_count)
    dir_coef = (
        dir_weight * dir_mask.astype(jnp.float32) / math.sqrt(feat_width * atom_count)
    ).reshape(group_count, group_size)

    def key_states(dir_proj):
        cosine, sine_val = phases(dir_proj, pair_freq)
        key_rot = rotate(keys_gained, cosine, sine_val).astype(jnp.bfloat16)
        return jnp.einsum("gna,nb->gab", key_rot, values_live, preferred_element_type=jnp.float32)

    states = lax.map(key_states, projected)
    states_b = sum_states(states)

    def query_step(totals, inputs_step):
        out_total, query_total = totals
        dir_proj, dir_scale, state_group = inputs_step
        cosine, sine_val = phases(dir_proj, pair_freq)
        query_rot = rotate(queries_full, cosine, sine_val).astype(jnp.bfloat16)
        mixed_rows = jnp.einsum(
            "gna,gab->gnb", query_rot, state_group, preferred_element_type=jnp.float32
        )
        out_total = out_total + jnp.sum(dir_scale[:, None, None] * mixed_rows, axis=0)
        back_proj = jnp.einsum(
            "nb,gab->gna", grad_live, state_group, preferred_element_type=jnp.float32
        )
        query_total = query_total + jnp.sum(
            rotate(dir_scale[:, None, None] * back_proj, cosine, -sine_val), axis=0
        )
        state_grad = dir_scale[:, None, None] * jnp.einsum(
            "gna,nb->gab", query_rot, grad_live, preferred_element_type=jnp.float32
        )
        return ((out_total, query_total), state_grad)

    zeros_full = jnp.zeros((atom_count, feat_width), jnp.float32)
    query_totals, late_grads = lax.scan(
        query_step, (zeros_full, zeros_full), (projected, dir_coef, states_b)
    )
    out_total, query_total = query_totals
    attended = lax.psum_scatter(
        (out_total * alive_mask).astype(jnp.bfloat16), "dirs", scatter_dimension=0, tiled=True
    )
    grads_b = sum_grads(late_grads)

    def key_step(totals, inputs_step):
        key_total, value_total = totals
        dir_proj, grad_group = inputs_step
        cosine, sine_val = phases(dir_proj, pair_freq)
        key_rot = rotate(keys_gained, cosine, sine_val).astype(jnp.bfloat16)
        back_proj = jnp.einsum(
            "nb,gab->gna", values_live, grad_group, preferred_element_type=jnp.float32
        )
        key_total = key_total + jnp.sum(rotate(back_proj, cosine, -sine_val), axis=0)
        value_total = value_total + jnp.einsum(
            "gna,gab->nb", key_rot, grad_group, preferred_element_type=jnp.float32
        )
        return ((key_total, value_total), None)

    key_totals, _ = lax.scan(key_step, (zeros_full, zeros_full), (projected, grads_b))
    key_total, value_total = key_totals
    key_terms = key_total * gain_rows * alive_mask
    grad_queries, grad_keys, grad_values = (
        lax.psum_scatter(
            query_total.astype(jnp.bfloat16), "dirs", scatter_dimension=0, tiled=True
        ).astype(jnp.float32),
        lax.psum_scatter(
            key_terms.astype(jnp.bfloat16), "dirs", scatter_dimension=0, tiled=True
        ).astype(jnp.float32),
        lax.psum_scatter(
            value_total.astype(jnp.bfloat16), "dirs", scatter_dimension=0, tiled=True
        ).astype(jnp.float32),
    )
    return (
        attended,
        grad_queries.astype(jnp.bfloat16),
        grad_keys.astype(jnp.bfloat16),
        grad_values.astype(jnp.bfloat16),
    )


def solution(mesh):
    return jax.shard_map(
        per_device,
        mesh=mesh,
        in_specs=(
            P("atoms", None),
            P("atoms", None),
            P("atoms", None),
            P("atoms", None),
            P(None, "atoms"),
            P("atoms"),
            P("atoms"),
            P(),
            P(),
            P(None, "dirs"),
            P("dirs"),
            P("dirs"),
        ),
        out_specs=(
            P(("atoms", "dirs"), None),
            P(("atoms", "dirs"), None),
            P(("atoms", "dirs"), None),
            P(("atoms", "dirs"), None),
        ),
        check_vma=False,
    )
```

profile of v0, /device:TPU:0, one launch (start us, length us, event | category | flops | bytes accessed | tf_op | source)
XLA Modules:
  0.0 1021.5 jit_solution(10191649756032339705)
XLA Ops:
  20.7 107.1 %while.39 = (s32[]{:T(128)}, f32[11,4,128,128]{3,2,1,0:T(8,128)}, f32[2048,128]{0,1:T(8,128)S(1)}, f32[11,4,2048]{2,1,0:T(4,128)S(1)}, bf16[2048,128]{1,0:T(8,128)(2,1)S(1)}, /*index=5*/f32[32]{0:T(128)S(1)}, s32[]{:T(128)}) while((s32[]{:T(128)}, f32[11,4,128,128]{3,2,1,0:T(8,128)}, f32[2048,128]{0,1:T(8,128)S(1)}, ...), condition=%wide.region_2.3_spmd.clone, body=%wide.region_1.2_spmd.clone.sunk | while | flops 277348352 | bytes 8226513 | solution.py:75
  127.8 79.0 %all-reduce.2 = bf16[11,4,128,128]{3,2,1,0:T(8,128)(2,1)} all-reduce(f32[11,4,128,128]{3,2,1,0:T(8,128)} %get-tuple-element.133), channel_id=1, replica_groups=mesh['atoms'=16,'dirs'=2] {'atoms'}, use_global_device_ids=true, to_apply=%region_3.4 | all-reduce | flops 720896 | bytes 4325376 | tf_op jit(solution)/shard_map/psum | solution.py:24
  209.6 421.8 %while.40 = (s32[]{:T(128)}, f32[2048,128]{1,0:T(8,128)}, f32[2048,128]{1,0:T(8,128)}, f32[11,4,128,128]{3,2,1,0:T(8,128)}, f32[11,4]{1,0:T(8,128)}, /*index=5*/...) while((s32[]{:T(128)}, f32[2048,128]{1,0:T(8,128)}, ...), condition=%wide.region_7.8_spmd.clone, body=%wide.region_4.7_spmd.clone.sunk | while | flops 827916288 | bytes 36278156 | solution.py:99
  216.8 19.9 %fusion.118 = (f32[4,2048,64]{2,1,0:T(8,128)S(1)}, f32[4,2048,64]{2,1,0:T(8,128)S(1)}, bf16[4,2048,64]{2,1,0:T(8,128)(2,1)S(1)}, bf16[4,2048,64]{2,1,0:T(8,128)(2,1)S(1)}) fusion(f32[4,2048,128]{2,1,0:T(8,128)} %multiply_bitcast_fusion.2, f32[64]{0:T(128)S(1)} %mul.663, f32[4,2048]{1,0:T(4,128)S(1)} %dynamic-slice_bitcast_fusion.7, ...), kind=kLoop, calls=%fused_computation.33.clone.1 | loop fusion | flops 8388608 | bytes 11567360 | tf_op jit(solution)/shard_map/while/body/eval_jaxpr/sub | solution.py:14
  254.6 19.9 %fusion.118 = (f32[4,2048,64]{2,1,0:T(8,128)S(1)}, f32[4,2048,64]{2,1,0:T(8,128)S(1)}, bf16[4,2048,64]{2,1,0:T(8,128)(2,1)S(1)}, bf16[4,2048,64]{2,1,0:T(8,128)(2,1)S(1)}) fusion(f32[4,2048,128]{2,1,0:T(8,128)} %multiply_bitcast_fusion.2, f32[64]{0:T(128)S(1)} %mul.663, f32[4,2048]{1,0:T(4,128)S(1)} %dynamic-slice_bitcast_fusion.7, ...), kind=kLoop, calls=%fused_computation.33.clone.1 | loop fusion | flops 8388608 | bytes 11567360 | tf_op jit(solution)/shard_map/while/body/eval_jaxpr/sub | solution.py:14
  293.0 19.9 %fusion.118 = (f32[4,2048,64]{2,1,0:T(8,128)S(1)}, f32[4,2048,64]{2,1,0:T(8,128)S(1)}, bf16[4,2048,64]{2,1,0:T(8,128)(2,1)S(1)}, bf16[4,2048,64]{2,1,0:T(8,128)(2,1)S(1)}) fusion(f32[4,2048,128]{2,1,0:T(8,128)} %multiply_bitcast_fusion.2, f32[64]{0:T(128)S(1)} %mul.663, f32[4,2048]{1,0:T(4,128)S(1)} %dynamic-slice_bitcast_fusion.7, ...), kind=kLoop, calls=%fused_computation.33.clone.1 | loop fusion | flops 8388608 | bytes 11567360 | tf_op jit(solution)/shard_map/while/body/eval_jaxpr/sub | solution.py:14
  331.4 19.9 %fusion.118 = (f32[4,2048,64]{2,1,0:T(8,128)S(1)}, f32[4,2048,64]{2,1,0:T(8,128)S(1)}, bf16[4,2048,64]{2,1,0:T(8,128)(2,1)S(1)}, bf16[4,2048,64]{2,1,0:T(8,128)(2,1)S(1)}) fusion(f32[4,2048,128]{2,1,0:T(8,128)} %multiply_bitcast_fusion.2, f32[64]{0:T(128)S(1)} %mul.663, f32[4,2048]{1,0:T(4,128)S(1)} %dynamic-slice_bitcast_fusion.7, ...), kind=kLoop, calls=%fused_computation.33.clone.1 | loop fusion | flops 8388608 | bytes 11567360 | tf_op jit(solution)/shard_map/while/body/eval_jaxpr/sub | solution.py:14
  369.8 19.9 %fusion.118 = (f32[4,2048,64]{2,1,0:T(8,128)S(1)}, f32[4,2048,64]{2,1,0:T(8,128)S(1)}, bf16[4,2048,64]{2,1,0:T(8,128)(2,1)S(1)}, bf16[4,2048,64]{2,1,0:T(8,128)(2,1)S(1)}) fusion(f32[4,2048,128]{2,1,0:T(8,128)} %multiply_bitcast_fusion.2, f32[64]{0:T(128)S(1)} %mul.663, f32[4,2048]{1,0:T(4,128)S(1)} %dynamic-slice_bitcast_fusion.7, ...), kind=kLoop, calls=%fused_computation.33.clone.1 | loop fusion | flops 8388608 | bytes 11567360 | tf_op jit(solution)/shard_map/while/body/eval_jaxpr/sub | solution.py:14
  408.2 19.9 %fusion.118 = (f32[4,2048,64]{2,1,0:T(8,128)S(1)}, f32[4,2048,64]{2,1,0:T(8,128)S(1)}, bf16[4,2048,64]{2,1,0:T(8,128)(2,1)S(1)}, bf16[4,2048,64]{2,1,0:T(8,128)(2,1)S(1)}) fusion(f32[4,2048,128]{2,1,0:T(8,128)} %multiply_bitcast_fusion.2, f32[64]{0:T(128)S(1)} %mul.663, f32[4,2048]{1,0:T(4,128)S(1)} %dynamic-slice_bitcast_fusion.7, ...), kind=kLoop, calls=%fused_computation.33.clone.1 | loop fusion | flops 8388608 | bytes 11567360 | tf_op jit(solution)/shard_map/while/body/eval_jaxpr/sub | solution.py:14
  446.6 19.9 %fusion.118 = (f32[4,2048,64]{2,1,0:T(8,128)S(1)}, f32[4,2048,64]{2,1,0:T(8,128)S(1)}, bf16[4,2048,64]{2,1,0:T(8,128)(2,1)S(1)}, bf16[4,2048,64]{2,1,0:T(8,128)(2,1)S(1)}) fusion(f32[4,2048,128]{2,1,0:T(8,128)} %multiply_bitcast_fusion.2, f32[64]{0:T(128)S(1)} %mul.663, f32[4,2048]{1,0:T(4,128)S(1)} %dynamic-slice_bitcast_fusion.7, ...), kind=kLoop, calls=%fused_computation.33.clone.1 | loop fusion | flops 8388608 | bytes 11567360 | tf_op jit(solution)/shard_map/while/body/eval_jaxpr/sub | solution.py:14
  485.0 19.9 %fusion.118 = (f32[4,2048,64]{2,1,0:T(8,128)S(1)}, f32[4,2048,64]{2,1,0:T(8,128)S(1)}, bf16[4,2048,64]{2,1,0:T(8,128)(2,1)S(1)}, bf16[4,2048,64]{2,1,0:T(8,128)(2,1)S(1)}) fusion(f32[4,2048,128]{2,1,0:T(8,128)} %multiply_bitcast_fusion.2, f32[64]{0:T(128)S(1)} %mul.663, f32[4,2048]{1,0:T(4,128)S(1)} %dynamic-slice_bitcast_fusion.7, ...), kind=kLoop, calls=%fused_computation.33.clone.1 | loop fusion | flops 8388608 | bytes 11567360 | tf_op jit(solution)/shard_map/while/body/eval_jaxpr/sub | solution.py:14
  523.4 19.9 %fusion.118 = (f32[4,2048,64]{2,1,0:T(8,128)S(1)}, f32[4,2048,64]{2,1,0:T(8,128)S(1)}, bf16[4,2048,64]{2,1,0:T(8,128)(2,1)S(1)}, bf16[4,2048,64]{2,1,0:T(8,128)(2,1)S(1)}) fusion(f32[4,2048,128]{2,1,0:T(8,128)} %multiply_bitcast_fusion.2, f32[64]{0:T(128)S(1)} %mul.663, f32[4,2048]{1,0:T(4,128)S(1)} %dynamic-slice_bitcast_fusion.7, ...), kind=kLoop, calls=%fused_computation.33.clone.1 | loop fusion | flops 8388608 | bytes 11567360 | tf_op jit(solution)/shard_map/while/body/eval_jaxpr/sub | solution.py:14
  561.8 19.9 %fusion.118 = (f32[4,2048,64]{2,1,0:T(8,128)S(1)}, f32[4,2048,64]{2,1,0:T(8,128)S(1)}, bf16[4,2048,64]{2,1,0:T(8,128)(2,1)S(1)}, bf16[4,2048,64]{2,1,0:T(8,128)(2,1)S(1)}) fusion(f32[4,2048,128]{2,1,0:T(8,128)} %multiply_bitcast_fusion.2, f32[64]{0:T(128)S(1)} %mul.663, f32[4,2048]{1,0:T(4,128)S(1)} %dynamic-slice_bitcast_fusion.7, ...), kind=kLoop, calls=%fused_computation.33.clone.1 | loop fusion | flops 8388608 | bytes 11567360 | tf_op jit(solution)/shard_map/while/body/eval_jaxpr/sub | solution.py:14
  600.2 19.9 %fusion.118 = (f32[4,2048,64]{2,1,0:T(8,128)S(1)}, f32[4,2048,64]{2,1,0:T(8,128)S(1)}, bf16[4,2048,64]{2,1,0:T(8,128)(2,1)S(1)}, bf16[4,2048,64]{2,1,0:T(8,128)(2,1)S(1)}) fusion(f32[4,2048,128]{2,1,0:T(8,128)} %multiply_bitcast_fusion.2, f32[64]{0:T(128)S(1)} %mul.663, f32[4,2048]{1,0:T(4,128)S(1)} %dynamic-slice_bitcast_fusion.7, ...), kind=kLoop, calls=%fused_computation.33.clone.1 | loop fusion | flops 8388608 | bytes 11567360 | tf_op jit(solution)/shard_map/while/body/eval_jaxpr/sub | solution.py:14
  631.4 73.9 %all-reduce.3 = bf16[11,4,128,128]{3,2,1,0:T(8,128)(2,1)S(1)} all-reduce(f32[11,4,128,128]{3,2,1,0:T(8,128)} %get-tuple-element.136), channel_id=1, replica_groups=mesh['atoms'=16,'dirs'=2] {'atoms'}, use_global_device_ids=true, to_apply=%region_10.11 | all-reduce | flops 720896 | bytes 4325376 | tf_op jit(solution)/shard_map/psum | solution.py:28
  705.4 241.8 %while.41 = (s32[]{:T(128)}, f32[2048,128]{0,1:T(8,128)}, f32[2048,128]{1,0:T(8,128)}, bf16[11,4,128,128]{3,2,1,0:T(8,128)(2,1)S(1)}, bf16[2048,128]{1,0:T(8,128...) while((s32[]{:T(128)}, f32[2048,128]{0,1:T(8,128)}, ...), condition=%wide.region_13.14_spmd.clone, body=%wide.region_11.13_spmd.clone.sunk | while | flops 552337408 | bytes 53315436 | solution.py:122
  709.3 11.5 %fusion.125 = (bf16[4,2048,64]{1,2,0:T(8,128)(2,1)}, bf16[4,2048,64]{1,2,0:T(8,128)(2,1)}, f32[4,2048,64]{1,2,0:T(8,128)S(1)}, f32[4,2048,64]{1,2,0:T(8,128)}) fusion(f32[2048,64]{0,1:T(8,128)} %get-tuple-element.535, f32[2048,64]{0,1:T(8,128)} %get-tuple-element.536, f32[64]{0:T(128)S(1)} %mul.671, f32[4,2048]{1,0:T(4,128)S(1)} %dynamic-slice_bitcast_fusion.8, ...), kind=kLoop, calls=%fused_computation.79.clone.1 | loop fusion | flops 8388608 | bytes 11567360 | tf_op jit(solution)/shard_map/convert.4
  774.6 11.5 %fusion.125 = (bf16[4,2048,64]{1,2,0:T(8,128)(2,1)}, bf16[4,2048,64]{1,2,0:T(8,128)(2,1)}, f32[4,2048,64]{1,2,0:T(8,128)S(1)}, f32[4,2048,64]{1,2,0:T(8,128)}) fusion(f32[2048,64]{0,1:T(8,128)} %get-tuple-element.535, f32[2048,64]{0,1:T(8,128)} %get-tuple-element.536, f32[64]{0:T(128)S(1)} %mul.671, f32[4,2048]{1,0:T(4,128)S(1)} %dynamic-slice_bitcast_fusion.8, ...), kind=kLoop, calls=%fused_computation.79.clone.1 | loop fusion | flops 8388608 | bytes 11567360 | tf_op jit(solution)/shard_map/convert.4
  796.6 11.5 %fusion.125 = (bf16[4,2048,64]{1,2,0:T(8,128)(2,1)}, bf16[4,2048,64]{1,2,0:T(8,128)(2,1)}, f32[4,2048,64]{1,2,0:T(8,128)S(1)}, f32[4,2048,64]{1,2,0:T(8,128)}) fusion(f32[2048,64]{0,1:T(8,128)} %get-tuple-element.535, f32[2048,64]{0,1:T(8,128)} %get-tuple-element.536, f32[64]{0:T(128)S(1)} %mul.671, f32[4,2048]{1,0:T(4,128)S(1)} %dynamic-slice_bitcast_fusion.8, ...), kind=kLoop, calls=%fused_computation.79.clone.1 | loop fusion | flops 8388608 | bytes 11567360 | tf_op jit(solution)/shard_map/convert.4
  862.8 11.5 %fusion.125 = (bf16[4,2048,64]{1,2,0:T(8,128)(2,1)}, bf16[4,2048,64]{1,2,0:T(8,128)(2,1)}, f32[4,2048,64]{1,2,0:T(8,128)S(1)}, f32[4,2048,64]{1,2,0:T(8,128)}) fusion(f32[2048,64]{0,1:T(8,128)} %get-tuple-element.535, f32[2048,64]{0,1:T(8,128)} %get-tuple-element.536, f32[64]{0:T(128)S(1)} %mul.671, f32[4,2048]{1,0:T(4,128)S(1)} %dynamic-slice_bitcast_fusion.8, ...), kind=kLoop, calls=%fused_computation.79.clone.1 | loop fusion | flops 8388608 | bytes 11567360 | tf_op jit(solution)/shard_map/convert.4
  884.9 11.5 %fusion.125 = (bf16[4,2048,64]{1,2,0:T(8,128)(2,1)}, bf16[4,2048,64]{1,2,0:T(8,128)(2,1)}, f32[4,2048,64]{1,2,0:T(8,128)S(1)}, f32[4,2048,64]{1,2,0:T(8,128)}) fusion(f32[2048,64]{0,1:T(8,128)} %get-tuple-element.535, f32[2048,64]{0,1:T(8,128)} %get-tuple-element.536, f32[64]{0:T(128)S(1)} %mul.671, f32[4,2048]{1,0:T(4,128)S(1)} %dynamic-slice_bitcast_fusion.8, ...), kind=kLoop, calls=%fused_computation.79.clone.1 | loop fusion | flops 8388608 | bytes 11567360 | tf_op jit(solution)/shard_map/convert.4
  962.7 17.5 %reduce-scatter.9.cloned.1.call-done = bf16[1024,128]{1,0:T(8,128)(2,1)} async-done(((bf16[2048,128]{1,0:T(8,128)(2,1)}), bf16[1024,128]{1,0:T(8,128)(2,1)}) %reduce-scatter.9.cloned.1.call-update) | async-done | bytes 262160 | tf_op jit(solution)/shard_map/reduce_scatter | solution.py:129
  980.2 17.4 %reduce-scatter.11.cloned.1.call-done = bf16[1024,128]{1,0:T(8,128)(2,1)} async-done(((bf16[2048,128]{1,0:T(8,128)(2,1)}), bf16[1024,128]{1,0:T(8,128)(2,1)}) %reduce-scatter.11.cloned.1.call-update) | async-done | bytes 262160 | tf_op jit(solution)/shard_map/reduce_scatter | solution.py:132
  997.6 17.3 %reduce-scatter.7.cloned.1.call-done = bf16[1024,128]{1,0:T(8,128)(2,1)} async-done(((bf16[2048,128]{1,0:T(8,128)(2,1)}), bf16[1024,128]{1,0:T(8,128)(2,1)}) %reduce-scatter.7.cloned.1.call-update) | async-done | bytes 262160 | tf_op jit(solution)/shard_map/reduce_scatter | solution.py:126
  (462 shorter events, 524.7 us)
Async XLA Ops:
  7.2 955.5 %reduce-scatter.5.cloned.1.call-start = ((), (), s32[]{:S(2)}) async-start(), calls=%async_computation.4 | async-start | bytes 786432 | tf_op jit(solution)/shard_map/reduce_scatter | solution.py:103
  127.8 79.0 %copy-start.3 = (bf16[2048,128]{1,0:T(8,128)(2,1)}, bf16[2048,128]{1,0:T(8,128)(2,1)S(1)}, u32[]{:S(2)}) copy-start(bf16[2048,128]{1,0:T(8,128)(2,1)S(1)} %get-tuple-element.633) | copy-start | bytes 1572868
  127.8 79.0 %copy-start.10 = (bf16[2048,128]{1,0:T(8,128)(2,1)S(1)}, bf16[2048,128]{1,0:T(8,128)(2,1)}, u32[]{:S(2)}) copy-start(bf16[2048,128]{1,0:T(8,128)(2,1)} %param.18) | copy-start | bytes 1572868
  127.8 79.1 %copy-start.13 = (f32[44]{0:T(128)S(1)}, f32[44]{0:T(128)}, u32[]{:S(2)}) copy-start(f32[44]{0:T(128)} %param.28) | copy-start | bytes 532
  127.8 79.1 %copy-start.14 = (s32[44]{0:T(128)S(1)}, s32[44]{0:T(128)}, u32[]{:S(2)}) copy-start(s32[44]{0:T(128)} %param.29) | copy-start | bytes 532
  209.6 5.9 copy-start.17
  247.4 5.9 copy-start.17
  285.8 5.9 copy-start.17
  324.2 5.9 copy-start.17
  362.6 5.9 copy-start.17
  401.0 5.9 copy-start.17
  439.3 5.9 copy-start.17
  477.7 5.9 copy-start.17
  516.2 5.9 copy-start.17
  554.6 5.9 copy-start.17
  593.0 5.9 copy-start.17
  631.4 73.9 %copy-start.4 = (bf16[2048,128]{1,0:T(8,128)(2,1)S(1)}, bf16[2048,128]{1,0:T(8,128)(2,1)}, u32[]{:S(2)}) copy-start(bf16[2048,128]{1,0:T(8,128)(2,1)} %copy-done.3) | copy-start | bytes 1572868
  786.0 3.8 copy-start
  830.1 3.8 copy-start
  874.3 3.8 copy-start
  918.4 3.8 copy-start
  950.4 29.8 %reduce-scatter.9.cloned.1.call-start = ((), (), s32[]{:S(2)}) async-start(), calls=%async_computation.6 | async-start | bytes 786432 | tf_op jit(solution)/shard_map/reduce_scatter | solution.py:129
  951.1 46.5 %reduce-scatter.11.cloned.1.call-start = ((), (), s32[]{:S(2)}) async-start(), calls=%async_computation.7 | async-start | bytes 786432 | tf_op jit(solution)/shard_map/reduce_scatter | solution.py:132
  953.2 61.7 %reduce-scatter.7.cloned.1.call-start = ((), (), s32[]{:S(2)}) async-start(), calls=%async_computation.5 | async-start | bytes 786432 | tf_op jit(solution)/shard_map/reduce_scatter | solution.py:126
  (59 other events, 163.5 us)
Sparse Core Ops, SparseCore 0:
  950.5 12.1 reduce-scatter.4
  965.6 14.5 reduce-scatter.8
  983.0 14.5 reduce-scatter.10
  1000.3 14.5 reduce-scatter.6
where the time goes:
time: 1030 us; the launch traced here: 1020 us
  other arithmetic  526 us (51%)
  matrix products  203 us (20%)
  blocking collectives  153 us (15%)
  local copies, waits for them, and re-layouts  62.8 us (6%)
  waiting for transfers between devices  61.5 us (6%)
  between operations  13.9 us (1%)
    sub x11, other arithmetic, rotate(): leading * cosine - trailing * sine_val  219 us
    another operation x22, other arithmetic  215 us
    psum x1, blocking collectives, sum_states(): return lax.psum(states, 'atoms').astype(jnp.bfloat16)  79 us
    psum x1, blocking collectives, sum_grads(): return lax.psum(state_grads, 'atoms').astype(jnp.bfloat16)  73.9 us
    dot_general x11, matrix products, query_step(): jnp.einsum('nb,gab->gna', grad_live, state_group, preferred_element_type=...  42.8 us
    dot_general x11, matrix products, key_step(): jnp.einsum('gna,gab->nb', key_rot, grad_group, preferred_element_type=jnp...  41.7 us
    dot_general x11, matrix products, query_step(): jnp.einsum('gna,gab->gnb', query_rot, state_group, preferred_element_type...  37.3 us
    add x11, other arithmetic, query_step(): query_total + jnp.sum(rotate(dir_scale[:, None, None] * back_proj, cosine...  37 us
  transfers between devices with their start and end apart: 4, of which 4 were waited for; matrix products, arithmetic and copies ran while one was open for 0% of the time, Pallas kernels for 0%

commit v1 on v0

v1 whole, which is shorter than its diff:
```python
import functools
import math

import jax
import jax.numpy as jnp
from jax import lax
from jax.experimental import pallas as pl
from jax.experimental.pallas import tpu as pltpu
from jax.sharding import PartitionSpec as P

BF16 = jnp.bfloat16
F32 = jnp.float32
GROUP = 4
LANES = 128
VMEM_LIMIT = 56 * 2**20

SIN_COEF = (4.4428679, -7.30744342, 3.59478808, -0.78437403)
COS_COEF = (1.41420408, -6.97764206, 5.71523839, -1.72834866)


def cos_sin_turns(turns):
    part = turns - jnp.round(turns)
    square = part * part
    sine = SIN_COEF[2] + square * SIN_COEF[3]
    sine = SIN_COEF[1] + square * sine
    sine = part * (SIN_COEF[0] + square * sine)
    cosine = COS_COEF[2] + square * COS_COEF[3]
    cosine = COS_COEF[1] + square * cosine
    cosine = COS_COEF[0] + square * cosine
    return 1.0 - sine * sine, sine * cosine


def states_kernel(
    chunk, dirs_ref, coef_ref, freq_ref, pos_ref, alive_ref, species_ref, gain_ref,
    q_ref, k_ref, v_ref, g_ref, state_ref, grad_ref, kt, qt, kr, qr,
):
    group = pl.program_id(0)
    atoms = pos_ref.shape[1]
    quarter = LANES // GROUP

    @pl.when(group == 0)
    def _():
        for start in range(0, atoms, chunk):
            cols = slice(start, start + chunk)
            alive = alive_ref[:, cols]
            species = species_ref[:, cols]
            gain = jnp.zeros((LANES, chunk), F32)
            for s in range(gain_ref.shape[1]):
                gain = jnp.where(species == s, gain_ref[:, s : s + 1], gain)
            kt[:, cols] = k_ref[cols, :].astype(F32).T * gain * alive
            qt[:, cols] = q_ref[cols, :].astype(F32).T * alive

    freq = freq_ref[...]
    for start in range(0, atoms, chunk):
        cols = slice(start, start + chunk)
        for i in range(GROUP):
            u = group * GROUP + i
            proj = (
                dirs_ref[0, u] * pos_ref[0:1, cols]
                + dirs_ref[1, u] * pos_ref[1:2, cols]
                + dirs_ref[2, u] * pos_ref[2:3, cols]
            )
            cosine, sine = cos_sin_turns(freq[:, :1] * proj)
            for src, dst in ((kt, kr), (qt, qr)):
                for m in range(2):
                    lead = src[quarter * m : quarter * (m + 1), cols]
                    trail = src[quarter * (m + 2) : quarter * (m + 3), cols]
                    row = (m - i) % GROUP * LANES + quarter * m
                    dst[row : row + quarter, cols] = (lead * cosine - trail * sine).astype(BF16)
                    row = (m + 2 - i) % GROUP * LANES + quarter * (m + 2)
                    dst[row : row + quarter, cols] = (lead * sine + trail * cosine).astype(BF16)

    for rot, other, out in ((kr, v_ref, state_ref), (qr, g_ref, grad_ref)):
        total = jnp.dot(rot[...], other[...], preferred_element_type=F32)
        for k in range(GROUP):
            for m in range(GROUP):
                rows = slice(k * LANES + m * quarter, k * LANES + (m + 1) * quarter)
                scale = coef_ref[group * GROUP + (m - k) % GROUP]
                out[rows, :] = (total[rows, :] * scale).astype(BF16)


def rolled_lanes(x, by):
    return x if by == 0 else pltpu.roll(x, by, axis=1)


def swapped(x):
    half = LANES // 2
    return jnp.concatenate([-x[:, half:], x[:, :half]], axis=1)


def rotate_kernel(wave_ref, pos_ref, q_ref, k_ref, qr_ref, kr_ref, cos_ref, sin_ref):
    position = pos_ref[...]
    wave = wave_ref[...]
    turns = (
        position[:, 0:1] * wave[0:1, :]
        + position[:, 1:2] * wave[1:2, :]
        + position[:, 2:3] * wave[2:3, :]
    )
    cosine, sine = cos_sin_turns(turns)
    cos_ref[...] = cosine.astype(BF16)
    sin_ref[...] = sine.astype(BF16)
    for src, dst in ((q_ref, qr_ref), (k_ref, kr_ref)):
        x = src[...]
        x_swapped = swapped(x)
        for k in range(GROUP):
            dst[:, k * LANES : (k + 1) * LANES] = (
                x * rolled_lanes(cosine, k * LANES // GROUP)
                + x_swapped * rolled_lanes(sine, k * LANES // GROUP)
            ).astype(BF16)


def mix_kernel(
    half_ref, state_ref, grad_ref, v_ref, g_ref, qr_ref, kr_ref, cos_ref, sin_ref,
    att_ref, gq_ref, gk_ref, gv_ref,
):
    del half_ref
    att_ref[...] = jnp.dot(qr_ref[...], state_ref[...], preferred_element_type=F32).astype(
        att_ref.dtype
    )
    gv_ref[...] = jnp.dot(kr_ref[...], grad_ref[...], preferred_element_type=F32).astype(
        gv_ref.dtype
    )
    rows = g_ref.shape[0]
    width = GROUP * LANES
    zero = jnp.zeros((rows, LANES), F32)
    sums = [zero, zero, zero, zero]
    for group in range(cos_ref.shape[1] // LANES):
        lanes = slice(group * LANES, (group + 1) * LANES)
        cosine = cos_ref[:, lanes].astype(F32)
        sine = sin_ref[:, lanes].astype(F32)
        cos_k = [rolled_lanes(cosine, k * LANES // GROUP) for k in range(GROUP)]
        sin_k = [rolled_lanes(sine, k * LANES // GROUP) for k in range(GROUP)]
        rows_g = slice(group * width, (group + 1) * width)
        for at, (left, right) in enumerate(((g_ref, state_ref), (v_ref, grad_ref))):
            back = lax.dot_general(
                left[...], right[rows_g, :], (((1,), (1,)), ((), ())), preferred_element_type=F32
            )
            for k in range(GROUP):
                part = back[:, k * LANES : (k + 1) * LANES]
                sums[2 * at] = sums[2 * at] + part * cos_k[k]
                sums[2 * at + 1] = sums[2 * at + 1] + part * sin_k[k]
    gq_ref[...] = (sums[0] - swapped(sums[1])).astype(gq_ref.dtype)
    gk_ref[...] = (sums[2] - swapped(sums[3])).astype(gk_ref.dtype)


def per_device(
    queries, keys, values, cotangent, positions, species, domain, species_gain, frequency,
    directions, dir_weight, dir_mask,
):
    atoms, feats = queries.shape
    dirs = dir_weight.shape[0]
    groups = dirs // GROUP
    rows = dirs * feats
    width = GROUP * feats
    alive = (domain == lax.axis_index("atoms")).astype(F32)
    turns_freq = frequency / (2.0 * math.pi)
    coef = dir_weight * dir_mask.astype(F32) / math.sqrt(feats * atoms)
    vmem = pl.BlockSpec(memory_space=pltpu.VMEM)
    smem = pl.BlockSpec(memory_space=pltpu.SMEM)
    params = functools.partial(pltpu.CompilerParams, vmem_limit_bytes=VMEM_LIMIT)

    states, grads = pl.pallas_call(
        functools.partial(states_kernel, 512),
        grid=(groups,),
        in_specs=[smem, smem] + [vmem] * 9,
        out_specs=[pl.BlockSpec((width, feats), lambda g: (g, 0))] * 2,
        out_shape=[jax.ShapeDtypeStruct((rows, feats), BF16)] * 2,
        scratch_shapes=[
            pltpu.VMEM((feats, atoms), F32),
            pltpu.VMEM((feats, atoms), F32),
            pltpu.VMEM((width, atoms), BF16),
            pltpu.VMEM((width, atoms), BF16),
        ],
        compiler_params=params(),
        cost_estimate=pl.CostEstimate(
            flops=4 * rows * atoms * feats, bytes_accessed=4 * rows * feats, transcendentals=0
        ),
        name="states",
    )(
        directions, coef, jnp.broadcast_to(turns_freq[:, None], (turns_freq.shape[0], LANES)),
        positions, alive[None, :], species[None, :], species_gain.T,
        queries, keys, values, cotangent,
    )

    both = jnp.concatenate([states, grads], axis=0)
    shard = lax.psum_scatter(both, "atoms", scatter_dimension=0, tiled=True)
    both = lax.all_gather(shard, "atoms", axis=0, tiled=True)

    species_ids = jnp.arange(species_gain.shape[0], dtype=jnp.int32)
    chosen = (species[:, None] == species_ids[None, :]).astype(F32)
    gain_rows = jnp.sum(chosen[:, :, None] * species_gain[None, :, :], axis=1) * alive[:, None]
    wave = (directions[:, :, None] * turns_freq[None, None, :]).reshape(3, groups * LANES)
    tile = 512
    by_group = pl.BlockSpec((tile, width), lambda n, g: (n, g))
    by_rows = pl.BlockSpec((tile, feats), lambda n, g: (n, 0))
    lanes_g = pl.BlockSpec((tile, LANES), lambda n, g: (n, g))
    q_rot, k_rot, cosines, sines = pl.pallas_call(
        rotate_kernel,
        grid=(atoms // tile, groups),
        in_specs=[
            pl.BlockSpec((3, LANES), lambda n, g: (0, g)),
            pl.BlockSpec((tile, 3), lambda n, g: (n, 0)),
            by_rows,
            by_rows,
        ],
        out_specs=[by_group, by_group, lanes_g, lanes_g],
        out_shape=[
            jax.ShapeDtypeStruct((atoms, rows), BF16),
            jax.ShapeDtypeStruct((atoms, rows), BF16),
            jax.ShapeDtypeStruct((atoms, groups * LANES), BF16),
            jax.ShapeDtypeStruct((atoms, groups * LANES), BF16),
        ],
        compiler_params=params(),
        cost_estimate=pl.CostEstimate(
            flops=atoms * rows * 10, bytes_accessed=5 * atoms * rows, transcendentals=0
        ),
        name="rotations",
    )(wave, positions.T, queries.astype(F32), keys.astype(F32) * gain_rows)

    states, grads = both[:rows], both[rows:]
    half_rows = atoms // 2
    block = 256
    steps = half_rows // block
    mine = lax.axis_index("dirs")

    def mix(half, dtype):
        def spec(lanes):
            return pl.BlockSpec((block, lanes), lambda n, half: (half[0] * steps + n, 0))

        out = pl.BlockSpec((block, feats), lambda n, half: (n, 0))
        whole = pl.BlockSpec((rows, feats), lambda n, half: (0, 0), pipeline_mode=pl.Buffered(1))
        return pl.pallas_call(
            mix_kernel,
            grid_spec=pltpu.PrefetchScalarGridSpec(
                num_scalar_prefetch=1,
                grid=(steps,),
                in_specs=[
                    whole, whole, spec(feats), spec(feats), spec(rows), spec(rows),
                    spec(groups * LANES), spec(groups * LANES),
                ],
                out_specs=[out] * 4,
            ),
            out_shape=[jax.ShapeDtypeStruct((half_rows, feats), dtype)] * 4,
            compiler_params=params(),
            cost_estimate=pl.CostEstimate(
                flops=8 * rows * half_rows * feats, bytes_accessed=5 * half_rows * rows,
                transcendentals=0,
            ),
            name="mix",
        )(
            half[None].astype(jnp.int32), states, grads, values, cotangent, q_rot, k_rot,
            cosines, sines,
        )

    away = jnp.concatenate(mix(1 - mine, BF16), axis=1)
    arrived = lax.ppermute(away, "dirs", [(0, 1), (1, 0)])
    kept = mix(mine, F32)
    alive_own = lax.dynamic_slice(alive, (mine * half_rows,), (half_rows,))[:, None]
    gain_own = lax.dynamic_slice(gain_rows, (mine * half_rows, 0), (half_rows, feats))
    results = []
    for at, scale in enumerate((alive_own, alive_own, gain_own, alive_own)):
        other = arrived[:, at * feats : (at + 1) * feats].astype(F32)
        results.append(((kept[at] + other) * scale).astype(BF16))
    return tuple(results)


def solution(mesh):
    return jax.shard_map(
        per_device,
        mesh=mesh,
        in_specs=(
            P("atoms", None),
            P("atoms", None),
            P("atoms", None),
            P("atoms", None),
            P(None, "atoms"),
            P("atoms"),
            P("atoms"),
            P(),
            P(),
            P(None, "dirs"),
            P("dirs"),
            P("dirs"),
        ),
        out_specs=(
            P(("atoms", "dirs"), None),
            P(("atoms", "dirs"), None),
            P(("atoms", "dirs"), None),
            P(("atoms", "dirs"), None),
        ),
        check_vma=False,
    )
```

time: 1030 us -> 241 us (0.23)
  other arithmetic: 526 us -> 16.4 us
  matrix products: 203 us -> 0 us
  blocking collectives: 153 us -> 0 us
  Pallas kernels: 0 us -> 133 us
  local copies, waits for them, and re-layouts: 62.8 us -> 7.35 us
    sub x11 -> x0, other arithmetic: 219 us -> none  [rotate(): leading * cosine - trailing * sine_val]
    another operation x22 -> x0, other arithmetic: 215 us -> none
    dot_general x66 -> x0, matrix products: 203 us -> none  [the longest x11 42.8 us: query_step(): jnp.einsum('nb,gab->gna', grad_live, state_group, preferred_element_type=...]
    psum x2 -> x0, blocking collectives: 153 us -> none  [the longest x1 79 us: sum_states(): return lax.psum(states, 'atoms').astype(jnp.bfloat16)]
    pallas_call x0 -> x4, Pallas kernels: none -> 133 us  [the longest x1 56.3 us: per_device(): pl.pallas_call(rotate_kernel, grid=(atoms // tile, groups), in_specs=[pl....]
    add x23 -> x0, other arithmetic: 63.2 us -> none  [the longest x11 37 us: query_step(): query_total + jnp.sum(rotate(dir_scale[:, None, None] * back_proj, cosine...]
    slice x35 -> x1, local copies, waits for them, and re-layouts: 29.6 us -> 3.59 us  [per_device(): states, grads = (both[:rows], both[rows:])]
    mul x80 -> x4, local copies, waits for them, and re-layouts: 18.1 us -> 0.26 us  [per_device(): directions[:, :, None] * turns_freq[None, None, :]]
  transfers between devices with their start and end apart: 4 -> 3, of which waited for: 4 -> 1; matrix products, arithmetic and copies ran while one was open for 0% -> 3% of each run, Pallas kernels for 0% -> 33%
where the time goes in v1:
time: 241 us; the launch traced here: 240 us
  Pallas kernels  133 us (55%)
  waiting for transfers between devices  67.9 us (28%)
  other arithmetic  16.4 us (7%)
  between operations  14.2 us (6%)
  local copies, waits for them, and re-layouts  7.35 us (3%)
    reduce_scatter x1, waiting for transfers between devices, per_device(): shard = lax.psum_scatter(both, 'atoms', scatter_dimension=0, tiled=True)  67.9 us
    pallas_call x1, Pallas kernels, per_device(): pl.pallas_call(rotate_kernel, grid=(atoms // tile, groups), in_specs=[pl....  56.3 us
    pallas_call x2, Pallas kernels, mix(): pl.pallas_call(mix_kernel, grid_spec=pltpu.PrefetchScalarGridSpec(num_sca...  48 us
    pallas_call x1, Pallas kernels, per_device(): pl.pallas_call(functools.partial(states_kernel, 512), grid=(groups,), in_...  28.6 us
  transfers between devices with their start and end apart: 3, of which 1 were waited for; matrix products, arithmetic and copies ran while one was open for 3% of the time, Pallas kernels for 33%

profile of v1, /device:TPU:0, one launch (start us, length us, event | category | flops | bytes accessed | tf_op | source)
XLA Modules:
  0.0 240.3 jit_solution(17895379530983994922)
XLA Ops:
  7.2 0.7 broadcast_multiply_fusion.2
  7.9 1.4 copy.20
  9.3 1.2 multiply_multiply_fusion.coef_ref
  10.5 1.3 compare_convert_fusion
  11.8 0.7 broadcast_in_dim.11.freq_ref
  12.5 28.6 %states.1 = (bf16[5632,128]{1,0:T(8,128)(2,1)}, bf16[5632,128]{1,0:T(8,128)(2,1)}) custom-call(f32[3,44]{1,0:T(4,128)} %dirs_ref.1, f32[44]{0:T(128)} %multiply_multiply_fusion.coef_ref, f32[32,128]{1,0:T(8,128)} %broadcast_in_dim.11.freq_ref, f32[3,2048]{1,0:T(4,128)} %pos_ref.1, f32[1,2048]{1,0:T(1,128)} %bitcast.8, s32[1,2048]{1,0:T(1,128)} %bitcast.9, ...), custom_call_target="tpu_custom_call" | custom-call | flops 5905580032 | bytes 2883584 | tf_op jit(solution)/shard_map/states/pallas_call | solution.py:162
  41.1 4.4 %pad_maximum_fusion = bf16[11264,128]{1,0:T(8,128)(2,1)} fusion(bf16[5632,128]{1,0:T(8,128)(2,1)} %get-tuple-element.19, bf16[5632,128]{1,0:T(8,128)(2,1)} %get-tuple-element.18), kind=kLoop, calls=%fused_computation.1 | loop fusion | flops 5767168 | bytes 5767168 | tf_op jit(solution)/shard_map/concatenate | solution.py:185
  45.5 0.0 all-gather.2.cloned.1.call-start
  45.6 67.9 %reduce-scatter.2.cloned.1.call-done = bf16[704,128]{1,0:T(8,128)(2,1)} async-done(((bf16[11264,128]{1,0:T(8,128)(2,1)}), bf16[704,128]{1,0:T(8,128)(2,1)}) %reduce-scatter.2.cloned.1.call-update) | async-done | bytes 180240 | tf_op jit(solution)/shard_map/reduce_scatter | solution.py:186
  113.5 1.0 convert_element_type.45.q_ref
  114.5 1.4 copy.21
  115.9 0.1 mul.78
  116.0 0.1 mul.75
  116.1 0.1 mul.76
  116.2 1.9 multiply_reduce_fusion
  118.1 0.6 broadcast_multiply_fusion.1.wave_ref
  118.7 1.3 convert_multiply_fusion
  120.0 56.3 %rotations.1 = (bf16[2048,5632]{1,0:T(8,128)(2,1)}, bf16[2048,5632]{1,0:T(8,128)(2,1)}, bf16[2048,1408]{1,0:T(8,128)(2,1)}, bf16[2048,1408]{1,0:T(8,128)(2,1)}) custom-call(f32[3,1408]{1,0:T(4,128)} %broadcast_multiply_fusion.1.wave_ref, f32[2048,3]{1,0:T(8,128)} %bitcast.6, f32[2048,128]{1,0:T(8,128)} %convert_element_type.45.q_ref, ...), custom_call_target="tpu_custom_call" | custom-call | flops 115343360 | bytes 57671680 | tf_op jit(solution)/shard_map/rotations/pallas_call | solution.py:197
  176.3 3.6 %fusion.1 = (bf16[5632,128]{1,0:T(8,128)(2,1)}, bf16[5632,128]{1,0:T(8,128)(2,1)}) fusion(bf16[11264,128]{1,0:T(8,128)(2,1)} %all-gather.2.cloned.1.call-done), kind=kLoop, calls=%fused_computation.15 | loop fusion | bytes 5767168 | tf_op jit(solution)/shard_map/slice | solution.py:220
  179.9 24.0 %mix.3 = (bf16[1024,128]{1,0:T(8,128)(2,1)}, bf16[1024,128]{1,0:T(8,128)(2,1)}, bf16[1024,128]{1,0:T(8,128)(2,1)}, bf16[1024,128]{1,0:T(8,128)(2,1)}) custom-call(s32[1]{0:T(128)} %bitcast.5.half_ref, bf16[5632,128]{1,0:T(8,128)(2,1)} %get-tuple-element.35.state_ref, bf16[5632,128]{1,0:T(8,128)(2,1)} %get-tuple-element.34.grad_ref, bf16[2048,128]{1,0:T(8,128)(2,1)} %v_ref.5, ...), custom_call_target="tpu_custom_call" | custom-call | flops 5905580032 | bytes 28835840 | tf_op jit(solution)/shard_map/mix/pallas_call | solution.py:232
  204.0 1.3 pad_maximum_fusion.1
  205.3 1.5 collective-permute-start
  206.8 23.9 %mix.2 = (f32[1024,128]{1,0:T(8,128)}, f32[1024,128]{1,0:T(8,128)}, f32[1024,128]{1,0:T(8,128)}, f32[1024,128]{1,0:T(8,128)}) custom-call(s32[1]{0:T(128)} %bitcast.half_ref, bf16[5632,128]{1,0:T(8,128)(2,1)} %get-tuple-element.35.state_ref, bf16[5632,128]{1,0:T(8,128)(2,1)} %get-tuple-element.34.grad_ref, bf16[2048,128]{1,0:T(8,128)(2,1)} %v_ref.5, ...), custom_call_target="tpu_custom_call" | custom-call | flops 5905580032 | bytes 28835840 | tf_op jit(solution)/shard_map/mix/pallas_call | solution.py:232
  230.7 2.7 %multiply_convert_fusion = (bf16[1024,128]{1,0:T(8,128)(2,1)}, bf16[1024,128]{1,0:T(8,128)(2,1)}, bf16[1024,128]{1,0:T(8,128)(2,1)}, bf16[1024,128]{1,0:T(8,128)(2,1)}) fusion(f32[1024,128]{1,0:T(8,128)} %get-tuple-element.31, bf16[1024,512]{1,0:T(8,128)(2,1)S(1)} %collective-permute-done, f32[1024]{0:T(1024)S(1)} %dynamic_slice.6, ...), kind=kLoop, calls=%fused_computation.4 | loop fusion | flops 2097152 | bytes 4722692 | tf_op jit(solution)/shard_map/convert_element_type | solution.py:263
  (22 shorter events, 0.1 us)
Async XLA Ops:
  7.2 106.3 %reduce-scatter.2.cloned.1.call-start = ((), (), s32[]{:S(2)}) async-start(), calls=%async_computation.1 | async-start | bytes 3063808 | tf_op jit(solution)/shard_map/reduce_scatter | solution.py:186
  45.4 68.1 %copy-start = (bf16[2048,128]{1,0:T(8,128)(2,1)S(1)}, bf16[2048,128]{1,0:T(8,128)(2,1)}, u32[]{:S(2)}) copy-start(bf16[2048,128]{1,0:T(8,128)(2,1)} %q_ref.1) | copy-start | bytes 1572868
  45.4 69.1 %copy-start.3 = (f32[3,2048]{1,0:T(4,128)S(1)}, f32[3,2048]{1,0:T(4,128)}, u32[]{:S(2)}) copy-start(f32[3,2048]{1,0:T(4,128)} %pos_ref.1) | copy-start | bytes 73732
  45.4 70.5 %copy-start.6 = (f32[3,44]{1,0:T(4,128)S(1)}, f32[3,44]{1,0:T(4,128)}, u32[]{:S(2)}) copy-start(f32[3,44]{1,0:T(4,128)} %dirs_ref.1) | copy-start | bytes 1588
  45.4 70.7 %copy-start.5 = (s32[2048]{0:T(1024)S(1)}, s32[2048]{0:T(1024)}, u32[]{:S(2)}) copy-start(s32[2048]{0:T(1024)} %param.17) | copy-start | bytes 24580
  45.4 70.7 %copy-start.4 = (f32[5,128]{1,0:T(8,128)S(1)}, f32[5,128]{1,0:T(8,128)}, u32[]{:S(2)}) copy-start(f32[5,128]{1,0:T(8,128)} %param.19) | copy-start | bytes 7684
  45.5 73.2 %copy-start.1 = (bf16[2048,128]{1,0:T(8,128)(2,1)S(1)}, bf16[2048,128]{1,0:T(8,128)(2,1)}, u32[]{:S(2)}) copy-start(bf16[2048,128]{1,0:T(8,128)(2,1)} %k_ref.1) | copy-start | bytes 1572868
  45.5 73.2 %copy-start.2 = (f32[2048]{0:T(1024)S(1)}, f32[2048]{0:T(1024)}, u32[]{:S(2)}) copy-start(f32[2048]{0:T(1024)} %compare_convert_fusion) | copy-start | bytes 24580
  45.5 130.8 %all-gather.2.cloned.1.call-start = ((), (), s32[]{:S(2)}) async-start(), calls=%async_computation.2 | async-start | bytes 3063808 | tf_op jit(solution)/shard_map/all_gather | solution.py:187
  205.3 25.5 %collective-permute-start = (bf16[1024,512]{1,0:T(8,128)(2,1)S(1)}, bf16[1024,512]{1,0:T(8,128)(2,1)S(1)}, u32[]{:S(2)}, u32[]{:S(2)}) collective-permute-start(bf16[1024,512]{1,0:T(8,128)(2,1)S(1)} %pad_maximum_fusion.1), channel_id=1, source_target_pairs={{0,1},{1,0},{2,3},{3,2},{4,5},{5,4},{6,7},{7,6},{8,9},{9,8},{10,11... | collective-permute-start | bytes 3145736 | tf_op jit(solution)/shard_map/ppermute | solution.py:256
Sparse Core Ops, SparseCore 0:
  45.6 67.7 reduce-scatter.1
  116.0 43.2 all-gather.1

commit v2 on v0

v2 whole, which is shorter than its diff:
```python
import functools
import math

import jax
import jax.numpy as jnp
from jax import lax
from jax.experimental import pallas as pl
from jax.experimental.pallas import tpu as pltpu
from jax.sharding import PartitionSpec as P

BF16 = jnp.bfloat16
F32 = jnp.float32
GROUP = 4
QUADS = 4
LANES = 128
QUARTER = LANES // QUADS
WIDTH = GROUP * LANES
VMEM_LIMIT = 56 * 2**20
CHUNKS = (3, 3, 3, 2)

SIN_COEF = (4.4428679, -7.30744342, 3.59478808, -0.78437403)
COS_COEF = (1.41420408, -6.97764206, 5.71523839, -1.72834866)


def cos_sin_turns(turns):
    part = turns - jnp.round(turns)
    square = part * part
    sine = SIN_COEF[2] + square * SIN_COEF[3]
    sine = SIN_COEF[1] + square * sine
    sine = part * (SIN_COEF[0] + square * sine)
    cosine = COS_COEF[2] + square * COS_COEF[3]
    cosine = COS_COEF[1] + square * cosine
    cosine = COS_COEF[0] + square * cosine
    return 1.0 - sine * sine, sine * cosine


def column(row):
    size = row.shape[1]
    at_row = lax.broadcasted_iota(jnp.int32, (size, size), 0)
    at_lane = lax.broadcasted_iota(jnp.int32, (size, size), 1)
    return jnp.sum(jnp.where(at_row == at_lane, row, 0.0), axis=1, keepdims=True)


def place_of(index):
    return index & 1, (index >> 1) & 1, (index >> 2) & 3


def prepare_kernel(
    index_ref, domain_ref, species_ref, gain_ref, q_ref, k_ref, v_ref, g_ref,
    qt_ref, kt_ref, vt_ref, gt_ref, gain_out,
):
    alive = (domain_ref[...] == index_ref[0]).astype(F32)
    species = species_ref[...]
    gain = jnp.zeros(gain_out.shape, F32)
    for s in range(gain_ref.shape[0]):
        gain = jnp.where(species == s, column(gain_ref[s : s + 1, :]), gain)
    gain_out[...] = gain
    kt_ref[...] = k_ref[...].astype(F32).T * gain * alive
    qt_ref[...] = q_ref[...].astype(F32).T * alive
    vt_ref[...] = (v_ref[...].astype(F32).T * alive).astype(BF16)
    gt_ref[...] = (g_ref[...].astype(F32).T * alive).astype(BF16)


def states_kernel(
    first, chunk, part, scale, index_ref, dirs_ref, weight_ref, mask_ref, freq_ref, pos_ref,
    qt_ref, kt_ref, v_ref, g_ref, kk_ref, ks_ref, sk_ref, ss_ref, kr_ref, qr_ref, cos_ref,
    sin_ref, k_total, q_total, slots,
):
    group = first + pl.program_id(0)
    atoms = pos_ref.shape[1]
    core, pair, quad = place_of(index_ref[0])
    freq = column(freq_ref[...]) * (1.0 / (2.0 * math.pi))
    for start in range(0, atoms, chunk):
        for at in range(start, start + chunk, part):
            cols = slice(at, at + part)
            for i in range(GROUP):
                u = group * GROUP + i
                proj = (
                    dirs_ref[0, u] * pos_ref[0:1, cols]
                    + dirs_ref[1, u] * pos_ref[1:2, cols]
                    + dirs_ref[2, u] * pos_ref[2:3, cols]
                )
                cosine, sine = cos_sin_turns(freq * proj)
                cos_ref[i * QUARTER : (i + 1) * QUARTER, cols] = cosine.astype(BF16)
                sin_ref[i * QUARTER : (i + 1) * QUARTER, cols] = sine.astype(BF16)
                for src, dst in ((kt_ref, kr_ref), (qt_ref, qr_ref)):
                    for m in range(2):
                        lead = src[QUARTER * m : QUARTER * (m + 1), cols]
                        trail = src[QUARTER * (m + 2) : QUARTER * (m + 3), cols]
                        row = i * LANES + QUARTER * m
                        dst[row : row + QUARTER, cols] = (lead * cosine - trail * sine).astype(BF16)
                        row = row + 2 * QUARTER
                        dst[row : row + QUARTER, cols] = (lead * sine + trail * cosine).astype(BF16)
        cols = slice(start, start + chunk)
        for rot, other, total in ((kr_ref, v_ref, k_total), (qr_ref, g_ref, q_total)):
            term = jnp.dot(rot[:, cols], other[cols, :], preferred_element_type=F32)
            total[...] = term if start == 0 else total[...] + term

    for kind, total in ((0, k_total), (1, q_total)):
        for i in range(GROUP):
            u = group * GROUP + i
            coef = weight_ref[u] * mask_ref[u].astype(F32) * scale
            rows = slice(i % 2 * QUARTER, (i % 2 + 1) * QUARTER)
            for m in range(QUADS):
                row = i * LANES + m * QUARTER
                slots[kind ^ core, (i // 2) ^ pair, (m - quad) & 3, rows, :] = (
                    total[row : row + QUARTER, :] * coef
                ).astype(BF16)
    for a, b, out in ((0, 0, kk_ref), (0, 1, ks_ref), (1, 0, sk_ref), (1, 1, ss_ref)):
        out[...] = slots[a, b]


def mix_kernel(
    has_totals, final, part, index_ref, half_ref, *refs,
):
    del half_ref
    refs = list(refs)
    sources, refs = refs[:4], refs[4:]
    vt_ref, gt_ref, kr_ref, qr_ref, cos_ref, sin_ref = refs[:6]
    refs = refs[6:]
    if final:
        gain_ref, refs = refs[0], refs[1:]
    if has_totals:
        before, refs = refs[:4], refs[4:]
    outs, refs = refs[:4], refs[4:]
    slots, states, states_t = refs[:3]
    totals = refs[3:7] if final else outs
    group = pl.program_id(1)
    groups = pl.num_programs(1)
    core, pair, quad = place_of(index_ref[0])

    @pl.when((group == 0) & (pl.program_id(0) == 0))
    def _():
        for at, source in enumerate(sources):
            slots[at // 2, at % 2] = source[...].reshape(slots.shape[2:])
        for g in range(slots.shape[3] // (2 * QUARTER)):
            for kind in range(2):
                for i in range(GROUP):
                    start = g * 2 * QUARTER + i % 2 * QUARTER
                    for m in range(QUADS):
                        states[kind, g, i * LANES + m * QUARTER : i * LANES + (m + 1) * QUARTER, :] = slots[
                            kind ^ core, (i // 2) ^ pair, (m - quad) & 3, start : start + QUARTER, :
                        ]
                    whole = states[kind, g, i * LANES : (i + 1) * LANES, :]
                    states_t[kind, g, :, i * LANES : (i + 1) * LANES] = (
                        whole.astype(F32).T.astype(BF16)
                    )

    @pl.when(group == 0)
    def _():
        for at, total in enumerate(totals):
            total[...] = before[at][...] if has_totals else jnp.zeros_like(total)

    for start in range(0, vt_ref.shape[1], part):
        cols = slice(start, start + part)
        for kind, rot, direct in ((0, qr_ref, totals[0]), (1, kr_ref, totals[3])):
            direct[:, cols] += jnp.dot(
                states_t[kind, group], rot[:, cols], preferred_element_type=F32
            )
        for kind, fixed, turned in ((0, gt_ref, totals[1]), (1, vt_ref, totals[2])):
            back = jnp.dot(states[kind, group], fixed[:, cols], preferred_element_type=F32)
            for m in range(2):
                lead_rows = slice(QUARTER * m, QUARTER * (m + 1))
                trail_rows = slice(QUARTER * (m + 2), QUARTER * (m + 3))
                lead_total = turned[lead_rows, cols]
                trail_total = turned[trail_rows, cols]
                for i in range(GROUP):
                    cosine = cos_ref[i * QUARTER : (i + 1) * QUARTER, cols].astype(F32)
                    sine = sin_ref[i * QUARTER : (i + 1) * QUARTER, cols].astype(F32)
                    row = i * LANES + QUARTER * m
                    lead = back[row : row + QUARTER, :]
                    trail = back[row + 2 * QUARTER : row + 3 * QUARTER, :]
                    lead_total = lead_total + (lead * cosine + trail * sine)
                    trail_total = trail_total + (trail * cosine - lead * sine)
                turned[lead_rows, cols] = lead_total
                turned[trail_rows, cols] = trail_total

    if final:
        @pl.when(group == groups - 1)
        def _():
            for at, (total, out) in enumerate(zip(totals, outs)):
                whole = total[...] * gain_ref[...] if at == 2 else total[...]
                out[...] = whole.T.astype(out.dtype)


def added(*terms):
    return sum(term.astype(F32) for term in terms).astype(BF16)


def per_device(
    atom_devices, queries, keys, values, cotangent, positions, species, domain, species_gain,
    frequency, directions, dir_weight, dir_mask,
):
    atoms, feats = queries.shape
    index = lax.axis_index("atoms")[None].astype(jnp.int32)
    mine = lax.axis_index("dirs").astype(jnp.int32)
    vmem = pl.BlockSpec(memory_space=pltpu.VMEM)
    smem = pl.BlockSpec(memory_space=pltpu.SMEM)
    params = pltpu.CompilerParams(vmem_limit_bytes=VMEM_LIMIT)
    shape = jax.ShapeDtypeStruct

    qt, kt, vt, gt, gain = pl.pallas_call(
        prepare_kernel,
        in_specs=[smem] + [vmem] * 7,
        out_specs=[vmem] * 5,
        out_shape=[
            shape((feats, atoms), F32), shape((feats, atoms), F32), shape((feats, atoms), BF16),
            shape((feats, atoms), BF16), shape((feats, atoms), F32),
        ],
        compiler_params=params,
        name="prepare",
    )(index, domain[None, :], species[None, :], species_gain, queries, keys, values, cotangent)

    chunk = min(512, atoms)
    part = min(256, chunk)

    def make_states(first, groups):
        sent = (QUADS, groups * 2 * QUARTER, feats)
        sent_spec = pl.BlockSpec((QUADS, 2 * QUARTER, feats), lambda g: (0, g, 0))
        results = pl.pallas_call(
            functools.partial(states_kernel, first, chunk, part, 1.0 / math.sqrt(feats * atoms)),
            grid=(groups,),
            in_specs=[smem] * 4 + [vmem] * 6,
            out_specs=[sent_spec] * 4
            + [pl.BlockSpec((WIDTH, atoms), lambda g: (g, 0))] * 2
            + [pl.BlockSpec((GROUP * QUARTER, atoms), lambda g: (g, 0))] * 2,
            out_shape=[shape(sent, BF16)] * 4
            + [shape((groups * WIDTH, atoms), BF16)] * 2
            + [shape((groups * GROUP * QUARTER, atoms), BF16)] * 2,
            scratch_shapes=[
                pltpu.VMEM((WIDTH, feats), F32),
                pltpu.VMEM((WIDTH, feats), F32),
                pltpu.VMEM((2, 2, QUADS, 2 * QUARTER, feats), BF16),
            ],
            compiler_params=params,
            cost_estimate=pl.CostEstimate(
                flops=8 * groups * WIDTH * atoms * feats,
                bytes_accessed=6 * groups * WIDTH * atoms, transcendentals=0,
            ),
            name="states",
        )(
            index, directions, dir_weight, dir_mask, frequency[None, :], positions, qt, kt,
            values, cotangent,
        )
        return results[:4], results[4:]

    def moved(x, target):
        return lax.ppermute(x, "atoms", [(i, target(i)) for i in range(atom_devices)])

    def by_core(x):
        return moved(x, lambda i: i ^ 1)

    def by_pair(x):
        return moved(x, lambda i: i ^ 2)

    def by_quad(x, step):
        return moved(x, lambda i: (i & ~12) | ((((i >> 2) + step) & 3) << 2))

    def summed(pieces):
        kept_kept, kept_sent, sent_kept, sent_sent = pieces
        arrived = by_core(sent_sent)
        arrived_kept = by_core(sent_kept)
        crossed = by_pair(added(kept_sent, arrived))
        half = added(kept_kept, arrived_kept, crossed)
        quarter = added(half[0], *(by_quad(half[step], step) for step in range(1, QUADS)))
        whole = quarter
        for step in range(16, atom_devices, 16):
            whole = added(whole, moved(quarter, lambda i: (i + step) % atom_devices))
        gathered = [whole] + [by_quad(whole, QUADS - step) for step in range(1, QUADS)]
        half = jnp.concatenate(gathered, axis=0)
        other = by_pair(half)
        return half, other, by_core(half), by_core(other)

    half_atoms = atoms // 2

    def mix(half, pieces, groups, kept, totals, final, dtype):
        blocks = 1 if final else 2
        mix_part = min(256, half_atoms)

        def at(n, half):
            return half[0] + n

        cols = lambda n, g, index, half: (0, at(n, half))
        rotated = lambda n, g, index, half: (g, at(n, half))
        rows_all = pl.BlockSpec((feats, half_atoms), cols)
        operands = [*pieces, vt, gt, *kept]
        specs = (
            [vmem] * 4
            + [rows_all] * 2
            + [pl.BlockSpec((WIDTH, half_atoms), rotated)] * 2
            + [pl.BlockSpec((GROUP * QUARTER, half_atoms), rotated)] * 2
        )
        if final:
            operands.append(gain)
            specs.append(rows_all)
        if totals is not None:
            operands += totals
            specs += [rows_all] * 4
        scratch = [
            pltpu.VMEM((2, 2, QUADS, groups * 2 * QUARTER, feats), BF16),
            pltpu.VMEM((2, groups, WIDTH, feats), BF16),
            pltpu.VMEM((2, groups, feats, WIDTH), BF16),
        ]
        if final:
            out_specs = [pl.BlockSpec((half_atoms, feats), lambda n, g, index, half: (0, 0))] * 4
            out_shape = [shape((half_atoms, feats), dtype)] * 4
            scratch += [pltpu.VMEM((feats, half_atoms), F32)] * 4
        else:
            out_specs = [rows_all] * 4
            out_shape = [shape((feats, atoms), F32)] * 4
        return pl.pallas_call(
            functools.partial(mix_kernel, totals is not None, final, mix_part),
            grid_spec=pltpu.PrefetchScalarGridSpec(
                num_scalar_prefetch=2,
                grid=(blocks, groups),
                in_specs=specs,
                out_specs=out_specs,
                scratch_shapes=scratch,
            ),
            out_shape=out_shape,
            compiler_params=params,
            cost_estimate=pl.CostEstimate(
                flops=8 * groups * WIDTH * blocks * half_atoms * feats,
                bytes_accessed=5 * groups * WIDTH * blocks * half_atoms, transcendentals=0,
            ),
            name="mix",
        )(index, half[None], *operands)

    made = []
    first = 0
    for groups in CHUNKS:
        pieces, kept = make_states(first, groups)
        made.append((summed(pieces), kept, groups))
        first += groups
    totals = None
    for pieces, kept, groups in made[:-1]:
        totals = mix(jnp.int32(0), pieces, groups, kept, totals, False, F32)
    pieces, kept, groups = made[-1]
    away = mix(1 - mine, pieces, groups, kept, totals, True, BF16)
    arrived = [lax.ppermute(x, "dirs", [(0, 1), (1, 0)]) for x in away]
    own = mix(mine, pieces, groups, kept, totals, True, F32)
    return tuple(
        (ours + theirs.astype(F32)).astype(BF16) for ours, theirs in zip(own, arrived)
    )


def solution(mesh):
    return jax.shard_map(
        functools.partial(per_device, mesh.shape["atoms"]),
        mesh=mesh,
        in_specs=(
            P("atoms", None),
            P("atoms", None),
            P("atoms", None),
            P("atoms", None),
            P(None, "atoms"),
            P("atoms"),
            P("atoms"),
            P(),
            P(),
            P(None, "dirs"),
            P("dirs"),
            P("dirs"),
        ),
        out_specs=(
            P(("atoms", "dirs"), None),
            P(("atoms", "dirs"), None),
            P(("atoms", "dirs"), None),
            P(("atoms", "dirs"), None),
        ),
        check_vma=False,
    )
```

time: 1030 us -> 210 us (0.20)
  other arithmetic: 526 us -> 8.78 us
  matrix products: 203 us -> 0 us
  blocking collectives: 153 us -> 0 us
  Pallas kernels: 0 us -> 111 us
  local copies, waits for them, and re-layouts: 62.8 us -> 2.88 us
  starting transfers between devices: 0.16 us -> 54.5 us
  waiting for transfers between devices: 61.5 us -> 31.8 us
  between operations: 13.9 us -> 1.21 us
    sub x11 -> x0, other arithmetic: 219 us -> none  [rotate(): leading * cosine - trailing * sine_val]
    another operation x22 -> x0, other arithmetic: 215 us -> none
    dot_general x66 -> x0, matrix products: 203 us -> none  [the longest x11 42.8 us: query_step(): jnp.einsum('nb,gab->gna', grad_live, state_group, preferred_element_type=...]
    psum x2 -> x0, blocking collectives: 153 us -> none  [the longest x1 79 us: sum_states(): return lax.psum(states, 'atoms').astype(jnp.bfloat16)]
    pallas_call x0 -> x10, Pallas kernels: none -> 111 us  [the longest x5 60.2 us: mix(): pl.pallas_call(functools.partial(mix_kernel, totals is not None, final, m...]
    add x23 -> x0, other arithmetic: 63.2 us -> none  [the longest x11 37 us: query_step(): query_total + jnp.sum(rotate(dir_scale[:, None, None] * back_proj, cosine...]
    reduce_scatter x4 -> x0, waiting for transfers between devices: 60.8 us -> none  [the longest x1 17.5 us: per_device(): lax.psum_scatter(key_terms.astype(jnp.bfloat16), 'dirs', scatter_dimensio...]
    ppermute x0 -> x52, starting transfers between devices: none -> 54.5 us  [the longest x48 50.4 us: moved(): lax.ppermute(x, 'atoms', [(i, target(i)) for i in range(atom_devices)])]
  transfers between devices with their start and end apart: 4 -> 52, of which waited for: 4 -> 15; matrix products, arithmetic and copies ran while one was open for 0% -> 3% of each run, Pallas kernels for 0% -> 41%
where the time goes in v2:
time: 210 us
  Pallas kernels  111 us (53%)
  starting transfers between devices  54.5 us (26%)
  waiting for transfers between devices  31.8 us (15%)
  other arithmetic  8.78 us (4%)
  local copies, waits for them, and re-layouts  2.88 us (1%)
    pallas_call x5, Pallas kernels, mix(): pl.pallas_call(functools.partial(mix_kernel, totals is not None, final, m...  60.2 us
    ppermute x48, starting transfers between devices, moved(): lax.ppermute(x, 'atoms', [(i, target(i)) for i in range(atom_devices)])  50.4 us
    pallas_call x4, Pallas kernels, make_states(): pl.pallas_call(functools.partial(states_kernel, first, chunk, part, 1.0 /...  46.3 us
    ppermute x48, waiting for transfers between devices, moved(): lax.ppermute(x, 'atoms', [(i, target(i)) for i in range(atom_devices)])  24.1 us
    ppermute x4, waiting for transfers between devices, per_device(): arrived = [lax.ppermute(x, 'dirs', [(0, 1), (1, 0)]) for x in away]  7.76 us
    convert_element_type x4, other arithmetic, per_device(): (ours + theirs.astype(F32)).astype(BF16)  7.19 us
  transfers between devices with their start and end apart: 52, of which 15 were waited for; matrix products, arithmetic and copies ran while one was open for 3% of the time, Pallas kernels for 41%

profile of v2, /device:TPU:0, one launch (start us, length us, event | category | flops | bytes accessed | tf_op | source)
XLA Modules:
  0.0 209.7 jit_solution(783830029631985631)
XLA Ops:
  0.6 4.1 %prepare.1 = (f32[128,2048]{1,0:T(8,128)}, f32[128,2048]{1,0:T(8,128)}, bf16[128,2048]{1,0:T(8,128)(2,1)}, bf16[128,2048]{1,0:T(8,128)(2,1)}, f32[128,2048]{1,0:T(8,128)}) custom-call(s32[1]{0:T(128)} %bitcast.index_ref, s32[1,2048]{1,0:T(1,128)} %bitcast.50, s32[1,2048]{1,0:T(1,128)} %bitcast.51, f32[5,128]{1,0:T(8,128)} %gain_ref.1, ...), custom_call_target="tpu_custom_call" | custom-call | tf_op jit(solution)/shard_map/prepare/pallas_call | solution.py:202
  4.7 12.1 %states.7 = (bf16[4,192,128]{2,1,0:T(8,128)(2,1)}, bf16[4,192,128]{2,1,0:T(8,128)(2,1)}, bf16[4,192,128]{2,1,0:T(8,128)(2,1)}, bf16[4,192,128]{2,1,0:T(8,128)(2,...) custom-call(s32[1]{0:T(128)} %bitcast.index_ref, ...), custom_call_target="tpu_custom_call" | custom-call | flops 3221225472 | bytes 18874368 | tf_op jit(solution)/shard_map/states/pallas_call | solution.py:220
  17.4 12.3 %states.6 = (bf16[4,192,128]{2,1,0:T(8,128)(2,1)}, bf16[4,192,128]{2,1,0:T(8,128)(2,1)}, bf16[4,192,128]{2,1,0:T(8,128)(2,1)}, bf16[4,192,128]{2,1,0:T(8,128)(2,...) custom-call(s32[1]{0:T(128)} %bitcast.index_ref, ...), custom_call_target="tpu_custom_call" | custom-call | flops 3221225472 | bytes 18874368 | tf_op jit(solution)/shard_map/states/pallas_call | solution.py:220
  30.1 9.6 %states.4 = (bf16[4,128,128]{2,1,0:T(8,128)(2,1)}, bf16[4,128,128]{2,1,0:T(8,128)(2,1)}, bf16[4,128,128]{2,1,0:T(8,128)(2,1)}, bf16[4,128,128]{2,1,0:T(8,128)(2,...) custom-call(s32[1]{0:T(128)} %bitcast.index_ref, ...), custom_call_target="tpu_custom_call" | custom-call | flops 2147483648 | bytes 12582912 | tf_op jit(solution)/shard_map/states/pallas_call | solution.py:220
  39.9 12.3 %states.5 = (bf16[4,192,128]{2,1,0:T(8,128)(2,1)}, bf16[4,192,128]{2,1,0:T(8,128)(2,1)}, bf16[4,192,128]{2,1,0:T(8,128)(2,1)}, bf16[4,192,128]{2,1,0:T(8,128)(2,...) custom-call(s32[1]{0:T(128)} %bitcast.index_ref, ...), custom_call_target="tpu_custom_call" | custom-call | flops 3221225472 | bytes 18874368 | tf_op jit(solution)/shard_map/states/pallas_call | solution.py:220
  52.9 2.8 %collective-permute-start.2 = (bf16[4,128,128]{2,1,0:T(8,128)(2,1)S(1)}, bf16[4,128,128]{2,1,0:T(8,128)(2,1)S(1)}, u32[]{:S(2)}, u32[]{:S(2)}) collective-permute-start(bf16[4,128,128]{2,1,0:T(8,128)(2,1)S(1)} %add_convert_fusion.11), channel_id=1, source_target_pairs={{0,4},{2,6},{4,0},{6,2},{8,12},{10,14},{12,8},{14,10},{16,20},{18,... | collective-permute-start | bytes 393224 | tf_op jit(solution)/shard_map/ppermute | solution.py:248
  55.8 3.9 %collective-permute-done.2 = bf16[4,128,128]{2,1,0:T(8,128)(2,1)S(1)} collective-permute-done((bf16[4,128,128]{2,1,0:T(8,128)(2,1)S(1)}, bf16[4,128,128]{2,1,0:T(8,128)(2,1)S(1)}, u32[]{:S(2)}, u32[]{:S(2)}) %collective-permute-start.2) | collective-permute-done | bytes 131104 | tf_op jit(solution)/shard_map/ppermute | solution.py:248
  61.6 2.6 %collective-permute-start.4 = (bf16[128,128]{1,0:T(8,128)(2,1)S(1)}, bf16[128,128]{1,0:T(8,128)(2,1)S(1)}, u32[]{:S(2)}, u32[]{:S(2)}) collective-permute-start(bf16[128,128]{1,0:T(8,128)(2,1)S(1)} %get-tuple-element.129), channel_id=1, source_target_pairs={{0,16},{2,18},{4,20},{6,22},{8,24},{10,26},{12,28},{14,30},{16,0},... | collective-permute-start | bytes 98312 | tf_op jit(solution)/shard_map/ppermute | solution.py:248
  68.1 3.4 %collective-permute-start.6 = (bf16[128,128]{1,0:T(8,128)(2,1)S(1)}, bf16[128,128]{1,0:T(8,128)(2,1)S(1)}, u32[]{:S(2)}, u32[]{:S(2)}) collective-permute-start(bf16[128,128]{1,0:T(8,128)(2,1)S(1)} %fusion.11), channel_id=1, source_target_pairs={{0,24},{2,26},{4,28},{6,30},{8,0},{10,2},{12,4},{14,6},{16,8},{18,... | collective-permute-start | bytes 98312 | tf_op jit(solution)/shard_map/ppermute | solution.py:248
  73.2 3.1 %collective-permute-done.7 = bf16[128,128]{1,0:T(8,128)(2,1)S(1)} collective-permute-done((bf16[128,128]{1,0:T(8,128)(2,1)S(1)}, bf16[128,128]{1,0:T(8,128)(2,1)S(1)}, u32[]{:S(2)}, u32[]{:S(2)}) %collective-permute-start.7) | collective-permute-done | bytes 32800 | tf_op jit(solution)/shard_map/ppermute | solution.py:248
  81.1 4.0 %collective-permute-done.26 = bf16[4,192,128]{2,1,0:T(8,128)(2,1)S(1)} collective-permute-done((bf16[4,192,128]{2,1,0:T(8,128)(2,1)S(1)}, bf16[4,192,128]{2,1,0:T(8,128)(2,1)S(1)}, u32[]{:S(2)}, u32[]{:S(2)}) %collective-permute-start.26) | collective-permute-done | bytes 196640 | tf_op jit(solution)/shard_map/ppermute | solution.py:248
  90.5 2.8 %collective-permute-start.29 = (bf16[192,128]{1,0:T(8,128)(2,1)S(1)}, bf16[192,128]{1,0:T(8,128)(2,1)S(1)}, u32[]{:S(2)}, u32[]{:S(2)}) collective-permute-start(bf16[192,128]{1,0:T(8,128)(2,1)S(1)} %get-tuple-element.122), channel_id=1, source_target_pairs={{0,24},{2,26},{4,28},{6,30},{8,0},{10,2},{12,4},{14,6},{16,8},{18,... | collective-permute-start | bytes 147464 | tf_op jit(solution)/shard_map/ppermute | solution.py:248
  97.4 3.4 %collective-permute-start.44 = (bf16[192,128]{1,0:T(8,128)(2,1)S(1)}, bf16[192,128]{1,0:T(8,128)(2,1)S(1)}, u32[]{:S(2)}, u32[]{:S(2)}) collective-permute-start(bf16[192,128]{1,0:T(8,128)(2,1)S(1)} %fusion.2), channel_id=1, source_target_pairs={{0,8},{2,10},{4,12},{6,14},{8,16},{10,18},{12,20},{14,22},{16,24},... | collective-permute-start | bytes 147464 | tf_op jit(solution)/shard_map/ppermute | solution.py:248
  103.0 3.8 %collective-permute-start.17 = (bf16[192,128]{1,0:T(8,128)(2,1)S(1)}, bf16[192,128]{1,0:T(8,128)(2,1)S(1)}, u32[]{:S(2)}, u32[]{:S(2)}) collective-permute-start(bf16[192,128]{1,0:T(8,128)(2,1)S(1)} %get-tuple-element.125), channel_id=1, source_target_pairs={{0,24},{2,26},{4,28},{6,30},{8,0},{10,2},{12,4},{14,6},{16,8},{18,... | collective-permute-start | bytes 147464 | tf_op jit(solution)/shard_map/ppermute | solution.py:248
  111.7 2.6 %collective-permute-start.18 = (bf16[192,128]{1,0:T(8,128)(2,1)S(1)}, bf16[192,128]{1,0:T(8,128)(2,1)S(1)}, u32[]{:S(2)}, u32[]{:S(2)}) collective-permute-start(bf16[192,128]{1,0:T(8,128)(2,1)S(1)} %fusion.8), channel_id=1, source_target_pairs={{0,24},{2,26},{4,28},{6,30},{8,0},{10,2},{12,4},{14,6},{16,8},{18,... | collective-permute-start | bytes 147464 | tf_op jit(solution)/shard_map/ppermute | solution.py:248
  115.8 2.5 %collective-permute-start.19 = (bf16[192,128]{1,0:T(8,128)(2,1)S(1)}, bf16[192,128]{1,0:T(8,128)(2,1)S(1)}, u32[]{:S(2)}, u32[]{:S(2)}) collective-permute-start(bf16[192,128]{1,0:T(8,128)(2,1)S(1)} %fusion.8), channel_id=1, source_target_pairs={{0,16},{2,18},{4,20},{6,22},{8,24},{10,26},{12,28},{14,30},{16,0},... | collective-permute-start | bytes 147464 | tf_op jit(solution)/shard_map/ppermute | solution.py:248
  119.1 2.8 %collective-permute-done.19 = bf16[192,128]{1,0:T(8,128)(2,1)S(1)} collective-permute-done((bf16[192,128]{1,0:T(8,128)(2,1)S(1)}, bf16[192,128]{1,0:T(8,128)(2,1)S(1)}, u32[]{:S(2)}, u32[]{:S(2)}) %collective-permute-start.19) | collective-permute-done | bytes 49184 | tf_op jit(solution)/shard_map/ppermute | solution.py:248
  127.6 13.7 %mix.5 = (f32[128,2048]{1,0:T(8,128)}, f32[128,2048]{1,0:T(8,128)}, f32[128,2048]{1,0:T(8,128)}, f32[128,2048]{1,0:T(8,128)}) custom-call(s32[1]{0:T(128)} %bitcast.index_ref, s32[1]{0:T(128)} %constant.10.clone.1.half_ref, bf16[768,128]{1,0:T(8,128)(2,1)} %copy-done.1, bf16[768,128]{1,0:T(8,128)(2,1)} %copy-done.8, bf16[768,128]{1,0:T(8,128)(2,1)} %copy-done.9, ...), custom_call_target="tpu_custom_call" | custom-call | flops 3221225472 | bytes 15728640 | tf_op jit(solution)/shard_map/mix/pallas_call | solution.py:311
  142.6 15.4 %mix.6 = (f32[128,2048]{1,0:T(8,128)}, f32[128,2048]{1,0:T(8,128)}, f32[128,2048]{1,0:T(8,128)}, f32[128,2048]{1,0:T(8,128)}) custom-call(s32[1]{0:T(128)} %bitcast.index_ref, s32[1]{0:T(128)} %constant.10.clone.1.half_ref, bf16[768,128]{1,0:T(8,128)(2,1)} %copy-done.2, bf16[768,128]{1,0:T(8,128)(2,1)} %copy-done.7, bf16[768,128]{1,0:T(8,128)(2,1)} %copy-done.12, ...), custom_call_target="tpu_custom_call" | custom-call | flops 3221225472 | bytes 15728640 | tf_op jit(solution)/shard_map/mix/pallas_call | solution.py:311
  158.8 15.5 %mix.7 = (f32[128,2048]{1,0:T(8,128)}, f32[128,2048]{1,0:T(8,128)}, f32[128,2048]{1,0:T(8,128)}, f32[128,2048]{1,0:T(8,128)}) custom-call(s32[1]{0:T(128)} %bitcast.index_ref, s32[1]{0:T(128)} %constant.10.clone.1.half_ref, bf16[768,128]{1,0:T(8,128)(2,1)} %copy-done.3, bf16[768,128]{1,0:T(8,128)(2,1)} %copy-done.10, bf16[768,128]{1,0:T(8,128)(2,1)} %copy-done.13, ...), custom_call_target="tpu_custom_call" | custom-call | flops 3221225472 | bytes 15728640 | tf_op jit(solution)/shard_map/mix/pallas_call | solution.py:311
  174.9 7.6 %mix.9 = (bf16[1024,128]{1,0:T(8,128)(2,1)}, bf16[1024,128]{1,0:T(8,128)(2,1)}, bf16[1024,128]{1,0:T(8,128)(2,1)}, bf16[1024,128]{1,0:T(8,128)(2,1)}) custom-call(s32[1]{0:T(128)} %bitcast.index_ref, s32[1]{0:T(128)} %bitcast.21.half_ref, bf16[512,128]{1,0:T(8,128)(2,1)} %copy-done, bf16[512,128]{1,0:T(8,128)(2,1)} %copy-done.4, bf16[512,128]{1,0:T(8,128)(2,1)} %copy-done.5, ...), custom_call_target="tpu_custom_call" | custom-call | flops 1073741824 | bytes 5242880 | tf_op jit(solution)/shard_map/mix/pallas_call | solution.py:311
  186.6 8.2 %mix.8 = (f32[1024,128]{1,0:T(8,128)}, f32[1024,128]{1,0:T(8,128)}, f32[1024,128]{1,0:T(8,128)}, f32[1024,128]{1,0:T(8,128)}) custom-call(s32[1]{0:T(128)} %bitcast.index_ref, s32[1]{0:T(128)} %bitcast.1.half_ref, bf16[512,128]{1,0:T(8,128)(2,1)} %copy-done, bf16[512,128]{1,0:T(8,128)(2,1)} %copy-done.4, bf16[512,128]{1,0:T(8,128)(2,1)} %copy-done.5, ...), custom_call_target="tpu_custom_call" | custom-call | flops 1073741824 | bytes 5242880 | tf_op jit(solution)/shard_map/mix/pallas_call | solution.py:311
  199.3 3.8 %collective-permute-done.49 = bf16[1024,128]{1,0:T(8,128)(2,1)S(1)} collective-permute-done((bf16[1024,128]{1,0:T(8,128)(2,1)}, bf16[1024,128]{1,0:T(8,128)(2,1)S(1)}, u32[]{:S(2)}, u32[]{:S(2)}) %collective-permute-start.49) | collective-permute-done | bytes 262176 | tf_op jit(solution)/shard_map/ppermute | solution.py:340
  205.0 3.0 %collective-permute-done.48 = bf16[1024,128]{1,0:T(8,128)(2,1)S(1)} collective-permute-done((bf16[1024,128]{1,0:T(8,128)(2,1)}, bf16[1024,128]{1,0:T(8,128)(2,1)S(1)}, u32[]{:S(2)}, u32[]{:S(2)}) %collective-permute-start.48) | collective-permute-done | bytes 262176 | tf_op jit(solution)/shard_map/ppermute | solution.py:340
  (164 shorter events, 53.5 us)
Async XLA Ops:
  16.8 36.1 %collective-permute-start.37 = (bf16[4,192,128]{2,1,0:T(8,128)(2,1)}, bf16[4,192,128]{2,1,0:T(8,128)(2,1)S(1)}, u32[]{:S(2)}, u32[]{:S(2)}) collective-permute-start(bf16[4,192,128]{2,1,0:T(8,128)(2,1)} %get-tuple-element.93), channel_id=1, source_target_pairs={{0,2},{2,0},{4,6},{6,4},{8,10},{10,8},{12,14},{14,12},{16,18},{18,... | collective-permute-start | bytes 589832 | tf_op jit(solution)/shard_map/ppermute | solution.py:248
  17.3 61.5 %collective-permute-start.36 = (bf16[4,192,128]{2,1,0:T(8,128)(2,1)}, bf16[4,192,128]{2,1,0:T(8,128)(2,1)S(1)}, u32[]{:S(2)}, u32[]{:S(2)}) collective-permute-start(bf16[4,192,128]{2,1,0:T(8,128)(2,1)} %get-tuple-element.91), channel_id=1, source_target_pairs={{0,2},{2,0},{4,6},{6,4},{8,10},{10,8},{12,14},{14,12},{16,18},{18,... | collective-permute-start | bytes 589832 | tf_op jit(solution)/shard_map/ppermute | solution.py:248
  29.6 34.6 %collective-permute-start.25 = (bf16[4,192,128]{2,1,0:T(8,128)(2,1)}, bf16[4,192,128]{2,1,0:T(8,128)(2,1)S(1)}, u32[]{:S(2)}, u32[]{:S(2)}) collective-permute-start(bf16[4,192,128]{2,1,0:T(8,128)(2,1)} %get-tuple-element.85), channel_id=1, source_target_pairs={{0,2},{2,0},{4,6},{6,4},{8,10},{10,8},{12,14},{14,12},{16,18},{18,... | collective-permute-start | bytes 589832 | tf_op jit(solution)/shard_map/ppermute | solution.py:248
  39.8 12.8 %collective-permute-start.1 = (bf16[4,128,128]{2,1,0:T(8,128)(2,1)}, bf16[4,128,128]{2,1,0:T(8,128)(2,1)S(1)}, u32[]{:S(2)}, u32[]{:S(2)}) collective-permute-start(bf16[4,128,128]{2,1,0:T(8,128)(2,1)} %get-tuple-element.66), channel_id=1, source_target_pairs={{0,2},{2,0},{4,6},{6,4},{8,10},{10,8},{12,14},{14,12},{16,18},{18,... | collective-permute-start | bytes 393224 | tf_op jit(solution)/shard_map/ppermute | solution.py:248
  52.3 19.2 %collective-permute-start.13 = (bf16[4,192,128]{2,1,0:T(8,128)(2,1)}, bf16[4,192,128]{2,1,0:T(8,128)(2,1)S(1)}, u32[]{:S(2)}, u32[]{:S(2)}) collective-permute-start(bf16[4,192,128]{2,1,0:T(8,128)(2,1)} %get-tuple-element.77), channel_id=1, source_target_pairs={{0,2},{2,0},{4,6},{6,4},{8,10},{10,8},{12,14},{14,12},{16,18},{18,... | collective-permute-start | bytes 589832 | tf_op jit(solution)/shard_map/ppermute | solution.py:248
  65.8 13.5 %collective-permute-start.38 = (bf16[4,192,128]{2,1,0:T(8,128)(2,1)S(1)}, bf16[4,192,128]{2,1,0:T(8,128)(2,1)S(1)}, u32[]{:S(2)}, u32[]{:S(2)}) collective-permute-start(bf16[4,192,128]{2,1,0:T(8,128)(2,1)S(1)} %add_convert_fusion.5), channel_id=1, source_target_pairs={{0,4},{2,6},{4,0},{6,2},{8,12},{10,14},{12,8},{14,10},{16,20},{18,... | collective-permute-start | bytes 589832 | tf_op jit(solution)/shard_map/ppermute | solution.py:248
  76.3 10.0 %collective-permute-start.12 = (bf16[4,192,128]{2,1,0:T(8,128)(2,1)}, bf16[4,192,128]{2,1,0:T(8,128)(2,1)S(1)}, u32[]{:S(2)}, u32[]{:S(2)}) collective-permute-start(bf16[4,192,128]{2,1,0:T(8,128)(2,1)} %get-tuple-element.75), channel_id=1, source_target_pairs={{0,2},{2,0},{4,6},{6,4},{8,10},{10,8},{12,14},{14,12},{16,18},{18,... | collective-permute-start | bytes 589832 | tf_op jit(solution)/shard_map/ppermute | solution.py:248
  78.8 10.5 %collective-permute-start.14 = (bf16[4,192,128]{2,1,0:T(8,128)(2,1)S(1)}, bf16[4,192,128]{2,1,0:T(8,128)(2,1)S(1)}, u32[]{:S(2)}, u32[]{:S(2)}) collective-permute-start(bf16[4,192,128]{2,1,0:T(8,128)(2,1)S(1)} %add_convert_fusion.9), channel_id=1, source_target_pairs={{0,4},{2,6},{4,0},{6,2},{8,12},{10,14},{12,8},{14,10},{16,20},{18,... | collective-permute-start | bytes 589832 | tf_op jit(solution)/shard_map/ppermute | solution.py:248
  79.3 36.4 %collective-permute-start.9 = (bf16[512,128]{1,0:T(8,128)(2,1)S(1)}, bf16[512,128]{1,0:T(8,128)(2,1)S(1)}, u32[]{:S(2)}, u32[]{:S(2)}) collective-permute-start(bf16[512,128]{1,0:T(8,128)(2,1)S(1)} %pad_maximum_fusion.3.refs_0_), channel_id=1, source_target_pairs={{0,4},{2,6},{4,0},{6,2},{8,12},{10,14},{12,8},{14,10},{16,20},{18,... | collective-permute-start | bytes 393224 | tf_op jit(solution)/shard_map/ppermute | solution.py:248
  93.4 13.5 %collective-permute-start.15 = (bf16[192,128]{1,0:T(8,128)(2,1)S(1)}, bf16[192,128]{1,0:T(8,128)(2,1)S(1)}, u32[]{:S(2)}, u32[]{:S(2)}) collective-permute-start(bf16[192,128]{1,0:T(8,128)(2,1)S(1)} %get-tuple-element.124), channel_id=1, source_target_pairs={{0,8},{2,10},{4,12},{6,14},{8,16},{10,18},{12,20},{14,22},{16,24},... | collective-permute-start | bytes 147464 | tf_op jit(solution)/shard_map/ppermute | solution.py:248
  114.3 10.0 %collective-permute-start.46 = (bf16[768,128]{1,0:T(8,128)(2,1)S(1)}, bf16[768,128]{1,0:T(8,128)(2,1)S(1)}, u32[]{:S(2)}, u32[]{:S(2)}) collective-permute-start(bf16[768,128]{1,0:T(8,128)(2,1)S(1)} %pad_maximum_fusion.2.refs_0_), channel_id=1, source_target_pairs={{0,2},{2,0},{4,6},{6,4},{8,10},{10,8},{12,14},{14,12},{16,18},{18,... | collective-permute-start | bytes 589832 | tf_op jit(solution)/shard_map/ppermute | solution.py:248
  114.3 10.5 %collective-permute-start.33 = (bf16[768,128]{1,0:T(8,128)(2,1)S(1)}, bf16[768,128]{1,0:T(8,128)(2,1)S(1)}, u32[]{:S(2)}, u32[]{:S(2)}) collective-permute-start(bf16[768,128]{1,0:T(8,128)(2,1)S(1)} %pad_maximum_fusion.1.refs_0_), channel_id=1, source_target_pairs={{0,4},{2,6},{4,0},{6,2},{8,12},{10,14},{12,8},{14,10},{16,20},{18,... | collective-permute-start | bytes 589832 | tf_op jit(solution)/shard_map/ppermute | solution.py:248
  115.8 11.1 %collective-permute-start.47 = (bf16[768,128]{1,0:T(8,128)(2,1)S(1)}, bf16[768,128]{1,0:T(8,128)(2,1)S(1)}, u32[]{:S(2)}, u32[]{:S(2)}) collective-permute-start(bf16[768,128]{1,0:T(8,128)(2,1)S(1)} %collective-permute-done.45.refs_1_), channel_id=1, source_target_pairs={{0,2},{2,0},{4,6},{6,4},{8,10},{10,8},{12,14},{14,12},{16,18},{18,... | collective-permute-start | bytes 589832 | tf_op jit(solution)/shard_map/ppermute | solution.py:248
  121.9 52.3 %collective-permute-start.10 = (bf16[512,128]{1,0:T(8,128)(2,1)S(1)}, bf16[512,128]{1,0:T(8,128)(2,1)S(1)}, u32[]{:S(2)}, u32[]{:S(2)}) collective-permute-start(bf16[512,128]{1,0:T(8,128)(2,1)S(1)} %pad_maximum_fusion.3.refs_0_), channel_id=1, source_target_pairs={{0,2},{2,0},{4,6},{6,4},{8,10},{10,8},{12,14},{14,12},{16,18},{18,... | collective-permute-start | bytes 393224 | tf_op jit(solution)/shard_map/ppermute | solution.py:248
  124.2 50.1 %collective-permute-start.11 = (bf16[512,128]{1,0:T(8,128)(2,1)S(1)}, bf16[512,128]{1,0:T(8,128)(2,1)S(1)}, u32[]{:S(2)}, u32[]{:S(2)}) collective-permute-start(bf16[512,128]{1,0:T(8,128)(2,1)S(1)} %collective-permute-done.9.refs_1_), channel_id=1, source_target_pairs={{0,2},{2,0},{4,6},{6,4},{8,10},{10,8},{12,14},{14,12},{16,18},{18,... | collective-permute-start | bytes 393224 | tf_op jit(solution)/shard_map/ppermute | solution.py:248
  124.2 17.1 %collective-permute-start.34 = (bf16[768,128]{1,0:T(8,128)(2,1)S(1)}, bf16[768,128]{1,0:T(8,128)(2,1)S(1)}, u32[]{:S(2)}, u32[]{:S(2)}) collective-permute-start(bf16[768,128]{1,0:T(8,128)(2,1)S(1)} %pad_maximum_fusion.1.refs_0_), channel_id=1, source_target_pairs={{0,2},{2,0},{4,6},{6,4},{8,10},{10,8},{12,14},{14,12},{16,18},{18,... | collective-permute-start | bytes 589832 | tf_op jit(solution)/shard_map/ppermute | solution.py:248
  124.8 16.6 %collective-permute-start.21 = (bf16[768,128]{1,0:T(8,128)(2,1)S(1)}, bf16[768,128]{1,0:T(8,128)(2,1)S(1)}, u32[]{:S(2)}, u32[]{:S(2)}) collective-permute-start(bf16[768,128]{1,0:T(8,128)(2,1)S(1)} %pad_maximum_fusion.refs_0_), channel_id=1, source_target_pairs={{0,4},{2,6},{4,0},{6,2},{8,12},{10,14},{12,8},{14,10},{16,20},{18,... | collective-permute-start | bytes 589832 | tf_op jit(solution)/shard_map/ppermute | solution.py:248
  126.9 15.0 %collective-permute-start.35 = (bf16[768,128]{1,0:T(8,128)(2,1)S(1)}, bf16[768,128]{1,0:T(8,128)(2,1)S(1)}, u32[]{:S(2)}, u32[]{:S(2)}) collective-permute-start(bf16[768,128]{1,0:T(8,128)(2,1)S(1)} %collective-permute-done.33.refs_1_), channel_id=1, source_target_pairs={{0,2},{2,0},{4,6},{6,4},{8,10},{10,8},{12,14},{14,12},{16,18},{18,... | collective-permute-start | bytes 589832 | tf_op jit(solution)/shard_map/ppermute | solution.py:248
  141.3 16.7 %collective-permute-start.22 = (bf16[768,128]{1,0:T(8,128)(2,1)S(1)}, bf16[768,128]{1,0:T(8,128)(2,1)S(1)}, u32[]{:S(2)}, u32[]{:S(2)}) collective-permute-start(bf16[768,128]{1,0:T(8,128)(2,1)S(1)} %pad_maximum_fusion.refs_0_), channel_id=1, source_target_pairs={{0,2},{2,0},{4,6},{6,4},{8,10},{10,8},{12,14},{14,12},{16,18},{18,... | collective-permute-start | bytes 589832 | tf_op jit(solution)/shard_map/ppermute | solution.py:248
  141.4 16.6 %collective-permute-start.23 = (bf16[768,128]{1,0:T(8,128)(2,1)S(1)}, bf16[768,128]{1,0:T(8,128)(2,1)S(1)}, u32[]{:S(2)}, u32[]{:S(2)}) collective-permute-start(bf16[768,128]{1,0:T(8,128)(2,1)S(1)} %collective-permute-done.21.refs_1_), channel_id=1, source_target_pairs={{0,2},{2,0},{4,6},{6,4},{8,10},{10,8},{12,14},{14,12},{16,18},{18,... | collective-permute-start | bytes 589832 | tf_op jit(solution)/shard_map/ppermute | solution.py:248
  182.5 12.3 %collective-permute-start.51 = (bf16[1024,128]{1,0:T(8,128)(2,1)}, bf16[1024,128]{1,0:T(8,128)(2,1)S(1)}, u32[]{:S(2)}, u32[]{:S(2)}) collective-permute-start(bf16[1024,128]{1,0:T(8,128)(2,1)} %get-tuple-element.117), channel_id=1, source_target_pairs={{0,1},{1,0},{2,3},{3,2},{4,5},{5,4},{6,7},{7,6},{8,9},{9,8},{10,11... | collective-permute-start | bytes 786440 | tf_op jit(solution)/shard_map/ppermute | solution.py:340
  184.1 13.5 %collective-permute-start.50 = (bf16[1024,128]{1,0:T(8,128)(2,1)}, bf16[1024,128]{1,0:T(8,128)(2,1)S(1)}, u32[]{:S(2)}, u32[]{:S(2)}) collective-permute-start(bf16[1024,128]{1,0:T(8,128)(2,1)} %get-tuple-element.115), channel_id=1, source_target_pairs={{0,1},{1,0},{2,3},{3,2},{4,5},{5,4},{6,7},{7,6},{8,9},{9,8},{10,11... | collective-permute-start | bytes 786440 | tf_op jit(solution)/shard_map/ppermute | solution.py:340
  184.6 18.6 %collective-permute-start.49 = (bf16[1024,128]{1,0:T(8,128)(2,1)}, bf16[1024,128]{1,0:T(8,128)(2,1)S(1)}, u32[]{:S(2)}, u32[]{:S(2)}) collective-permute-start(bf16[1024,128]{1,0:T(8,128)(2,1)} %get-tuple-element.113), channel_id=1, source_target_pairs={{0,1},{1,0},{2,3},{3,2},{4,5},{5,4},{6,7},{7,6},{8,9},{9,8},{10,11... | collective-permute-start | bytes 786440 | tf_op jit(solution)/shard_map/ppermute | solution.py:340
  186.1 21.8 %collective-permute-start.48 = (bf16[1024,128]{1,0:T(8,128)(2,1)}, bf16[1024,128]{1,0:T(8,128)(2,1)S(1)}, u32[]{:S(2)}, u32[]{:S(2)}) collective-permute-start(bf16[1024,128]{1,0:T(8,128)(2,1)} %get-tuple-element.111), channel_id=1, source_target_pairs={{0,1},{1,0},{2,3},{3,2},{4,5},{5,4},{6,7},{7,6},{8,9},{9,8},{10,11... | collective-permute-start | bytes 786440 | tf_op jit(solution)/shard_map/ppermute | solution.py:340
  (53 other events, 613.7 us)

commit v3 on v2

v3 whole, which is shorter than its diff:
```python
import functools
import math

import jax
import jax.numpy as jnp
from jax import lax
from jax.experimental import pallas as pl
from jax.experimental.pallas import tpu as pltpu
from jax.sharding import PartitionSpec as P

BF16 = jnp.bfloat16
F32 = jnp.float32
GROUP = 4
QUADS = 4
LANES = 128
QUARTER = LANES // QUADS
WIDTH = GROUP * LANES
VMEM_LIMIT = 30 * 2**20
CHUNKS = (4, 4, 3)

SIN_COEF = (4.4428679, -7.30744342, 3.59478808, -0.78437403)
COS_COEF = (1.41420408, -6.97764206, 5.71523839, -1.72834866)


def cos_sin_turns(turns):
    part = turns - jnp.round(turns)
    square = part * part
    sine = SIN_COEF[2] + square * SIN_COEF[3]
    sine = SIN_COEF[1] + square * sine
    sine = part * (SIN_COEF[0] + square * sine)
    cosine = COS_COEF[2] + square * COS_COEF[3]
    cosine = COS_COEF[1] + square * cosine
    cosine = COS_COEF[0] + square * cosine
    return 1.0 - sine * sine, sine * cosine


def column(row):
    size = row.shape[1]
    at_row = lax.broadcasted_iota(jnp.int32, (size, size), 0)
    at_lane = lax.broadcasted_iota(jnp.int32, (size, size), 1)
    return jnp.sum(jnp.where(at_row == at_lane, row, 0.0), axis=1, keepdims=True)


def place_of(index):
    return index & 1, (index >> 1) & 1, (index >> 2) & 3


def prepare_kernel(
    index_ref, domain_ref, species_ref, gain_ref, q_ref, k_ref, v_ref, g_ref,
    qt_ref, kt_ref, vt_ref, gt_ref, gain_out,
):
    alive = (domain_ref[...] == index_ref[0]).astype(F32)
    species = species_ref[...]
    gain = jnp.zeros(gain_out.shape, F32)
    for s in range(gain_ref.shape[0]):
        gain = jnp.where(species == s, column(gain_ref[s : s + 1, :]), gain)
    gain_out[...] = gain
    kt_ref[...] = k_ref[...].astype(F32).T * gain * alive
    qt_ref[...] = (q_ref[...].astype(F32).T * alive).astype(BF16)
    vt_ref[...] = (v_ref[...].astype(F32).T * alive).astype(BF16)
    gt_ref[...] = (g_ref[...].astype(F32).T * alive).astype(BF16)


def states_kernel(
    first, part, scale, index_ref, dirs_ref, weight_ref, mask_ref, freq_ref, pos_ref,
    qt_ref, kt_ref, v_ref, g_ref, *refs,
):
    kept_ref, sent_ref, cos_ref, sin_ref, kr, qr, slots = refs[-7:]
    group = first + pl.program_id(0)
    atoms = pos_ref.shape[1]
    core, pair, quad = place_of(index_ref[0])
    freq = column(freq_ref[...]) * (1.0 / (2.0 * math.pi))
    for start in range(0, atoms, part):
        cols = slice(start, start + part)
        for i in range(GROUP):
            u = group * GROUP + i
            proj = (
                dirs_ref[0, u] * pos_ref[0:1, cols]
                + dirs_ref[1, u] * pos_ref[1:2, cols]
                + dirs_ref[2, u] * pos_ref[2:3, cols]
            )
            cosine, sine = cos_sin_turns(freq * proj)
            cos_ref[i * QUARTER : (i + 1) * QUARTER, cols] = cosine.astype(BF16)
            sin_ref[i * QUARTER : (i + 1) * QUARTER, cols] = sine.astype(BF16)
            for src, dst in ((kt_ref, kr), (qt_ref, qr)):
                for m in range(2):
                    lead = src[QUARTER * m : QUARTER * (m + 1), cols].astype(F32)
                    trail = src[QUARTER * (m + 2) : QUARTER * (m + 3), cols].astype(F32)
                    row = i * LANES + QUARTER * m
                    dst[row : row + QUARTER, cols] = (lead * cosine - trail * sine).astype(BF16)
                    row = row + 2 * QUARTER
                    dst[row : row + QUARTER, cols] = (lead * sine + trail * cosine).astype(BF16)

    for kind, rot, other in ((0, kr, v_ref), (1, qr, g_ref)):
        total = jnp.dot(rot[...], other[...], preferred_element_type=F32)
        for i in range(GROUP):
            u = group * GROUP + i
            coef = weight_ref[u] * mask_ref[u].astype(F32) * scale
            rows = slice(i % 2 * QUARTER, (i % 2 + 1) * QUARTER)
            for m in range(QUADS):
                row = i * LANES + m * QUARTER
                slots[kind ^ core, (i // 2) ^ pair, (m - quad) & 3, rows, :] = (
                    total[row : row + QUARTER, :] * coef
                ).astype(BF16)
    kept_ref[...] = slots[0]
    sent_ref[...] = slots[1]


def rotated(x, cosine, sine):
    pieces = []
    for i in range(GROUP):
        c = cosine[i * QUARTER : (i + 1) * QUARTER]
        s = sine[i * QUARTER : (i + 1) * QUARTER]
        quarters = [x[m * QUARTER : (m + 1) * QUARTER] for m in range(QUADS)]
        pieces += [quarters[m] * c - quarters[m + 2] * s for m in range(2)]
        pieces += [quarters[m] * s + quarters[m + 2] * c for m in range(2)]
    return jnp.concatenate(pieces, axis=0)


def mix_kernel(
    has_totals, final, part, index_ref, half_ref, *refs,
):
    del half_ref
    refs = list(refs)
    sources, refs = refs[:4], refs[4:]
    vt_ref, gt_ref, kt_ref, qt_ref, cos_ref, sin_ref = refs[:6]
    refs = refs[6:]
    if final:
        gain_ref, refs = refs[0], refs[1:]
    if has_totals:
        before, refs = refs[:4], refs[4:]
    out_count = 1 if final else 4
    outs, refs = refs[:out_count], refs[out_count:]
    slots, states, states_t = refs[:3]
    totals = refs[3:7]
    group = pl.program_id(1)
    groups = pl.num_programs(1)
    core, pair, quad = place_of(index_ref[0])

    @pl.when((group == 0) & (pl.program_id(0) == 0))
    def _():
        for at, source in enumerate(sources):
            slots[at // 2, at % 2] = source[...].reshape(slots.shape[2:])
        for g in range(slots.shape[3] // (2 * QUARTER)):
            for kind in range(2):
                for i in range(GROUP):
                    start = g * 2 * QUARTER + i % 2 * QUARTER
                    for m in range(QUADS):
                        row = i * LANES + m * QUARTER
                        states[kind, g, row : row + QUARTER, :] = slots[
                            kind ^ core, (i // 2) ^ pair, (m - quad) & 3,
                            start : start + QUARTER, :,
                        ]
                    whole = states[kind, g, i * LANES : (i + 1) * LANES, :]
                    states_t[kind, g, :, i * LANES : (i + 1) * LANES] = (
                        whole.astype(F32).T.astype(BF16)
                    )

    @pl.when(group == 0)
    def _():
        for at, total in enumerate(totals):
            total[...] = before[at][...].astype(F32) if has_totals else jnp.zeros_like(total)

    for start in range(0, vt_ref.shape[1], part):
        cols = slice(start, start + part)
        cosine = cos_ref[:, cols]
        sine = sin_ref[:, cols]
        for kind, x_ref, direct in ((0, qt_ref, totals[0]), (1, kt_ref, totals[3])):
            turned = rotated(x_ref[:, cols].astype(BF16), cosine, sine)
            direct[:, cols] += jnp.dot(states_t[kind, group], turned, preferred_element_type=F32)
        cosine = cosine.astype(F32)
        sine = sine.astype(F32)
        for kind, fixed, turned in ((0, gt_ref, totals[1]), (1, vt_ref, totals[2])):
            back = jnp.dot(states[kind, group], fixed[:, cols], preferred_element_type=F32)
            for m in range(2):
                lead_rows = slice(QUARTER * m, QUARTER * (m + 1))
                trail_rows = slice(QUARTER * (m + 2), QUARTER * (m + 3))
                lead_total = turned[lead_rows, cols]
                trail_total = turned[trail_rows, cols]
                for i in range(GROUP):
                    c = cosine[i * QUARTER : (i + 1) * QUARTER]
                    s = sine[i * QUARTER : (i + 1) * QUARTER]
                    row = i * LANES + QUARTER * m
                    lead = back[row : row + QUARTER, :]
                    trail = back[row + 2 * QUARTER : row + 3 * QUARTER, :]
                    lead_total = lead_total + (lead * c + trail * s)
                    trail_total = trail_total + (trail * c - lead * s)
                turned[lead_rows, cols] = lead_total
                turned[trail_rows, cols] = trail_total

    @pl.when(group == groups - 1)
    def _():
        for at, total in enumerate(totals):
            if final:
                whole = total[...] * gain_ref[...] if at == 2 else total[...]
                outs[0][:, at * LANES : (at + 1) * LANES] = whole.T.astype(outs[0].dtype)
            else:
                outs[at][...] = total[...].astype(outs[at].dtype)


def added(*terms):
    return sum(term.astype(F32) for term in terms).astype(BF16)


def per_device(
    atom_devices, queries, keys, values, cotangent, positions, species, domain, species_gain,
    frequency, directions, dir_weight, dir_mask,
):
    atoms, feats = queries.shape
    index = lax.axis_index("atoms")[None].astype(jnp.int32)
    mine = lax.axis_index("dirs").astype(jnp.int32)
    vmem = pl.BlockSpec(memory_space=pltpu.VMEM)
    smem = pl.BlockSpec(memory_space=pltpu.SMEM)
    params = pltpu.CompilerParams(vmem_limit_bytes=VMEM_LIMIT)
    shape = jax.ShapeDtypeStruct

    qt, kt, vt, gt, gain = pl.pallas_call(
        prepare_kernel,
        in_specs=[smem] + [vmem] * 7,
        out_specs=[vmem] * 5,
        out_shape=[
            shape((feats, atoms), BF16), shape((feats, atoms), F32), shape((feats, atoms), BF16),
            shape((feats, atoms), BF16), shape((feats, atoms), F32),
        ],
        compiler_params=params,
        name="prepare",
    )(index, domain[None, :], species[None, :], species_gain, queries, keys, values, cotangent)

    part = min(256, atoms)

    def make_states(first, groups, after):
        sent = (2, QUADS, groups * 2 * QUARTER, feats)
        sent_spec = pl.BlockSpec((2, QUADS, 2 * QUARTER, feats), lambda g: (0, 0, g, 0))
        phase_spec = pl.BlockSpec((GROUP * QUARTER, atoms), lambda g: (g, 0))
        return pl.pallas_call(
            functools.partial(states_kernel, first, part, 1.0 / math.sqrt(feats * atoms)),
            grid=(groups,),
            in_specs=[smem] * 4 + [vmem] * 6 + [pl.BlockSpec(memory_space=pl.ANY)] * len(after),
            out_specs=[sent_spec] * 2 + [phase_spec] * 2,
            out_shape=[shape(sent, BF16)] * 2
            + [shape((groups * GROUP * QUARTER, atoms), BF16)] * 2,
            scratch_shapes=[
                pltpu.VMEM((WIDTH, atoms), BF16),
                pltpu.VMEM((WIDTH, atoms), BF16),
                pltpu.VMEM((2, 2, QUADS, 2 * QUARTER, feats), BF16),
            ],
            compiler_params=params,
            cost_estimate=pl.CostEstimate(
                flops=8 * groups * WIDTH * atoms * feats,
                bytes_accessed=2 * groups * WIDTH * atoms, transcendentals=0,
            ),
            name="states",
        )(
            index, directions, dir_weight, dir_mask, frequency[None, :], positions, qt, kt,
            values, cotangent, *after,
        )

    def moved(x, target):
        return lax.ppermute(x, "atoms", [(i, target(i)) for i in range(atom_devices)])

    def by_core(x):
        return moved(x, lambda i: i ^ 1)

    def by_pair(x):
        return moved(x, lambda i: i ^ 2)

    def by_quad(x, step):
        return moved(x, lambda i: (i & ~12) | ((((i >> 2) + step) & 3) << 2))

    def crossing(kept, sent):
        arrived = by_core(sent)
        return arrived, added(kept[1], arrived[1])

    def summed(kept, arrived, crossing_out):
        half = added(kept[0], arrived[0], by_pair(crossing_out))
        quarter = added(half[0], *(by_quad(half[step], step) for step in range(1, QUADS)))
        whole = quarter
        for step in range(16, atom_devices, 16):
            whole = added(whole, moved(quarter, lambda i: (i + step) % atom_devices))
        gathered = [whole] + [by_quad(whole, QUADS - step) for step in range(1, QUADS)]
        half = jnp.concatenate(gathered, axis=0)
        other = by_pair(half)
        return half, other, by_core(half), by_core(other)

    half_atoms = atoms // 2

    def mix(half, pieces, groups, phases, totals, final, dtype):
        blocks = 1 if final else 2
        mix_part = min(256, half_atoms)
        rows_all = pl.BlockSpec((feats, half_atoms), lambda n, g, index, half: (0, half[0] + n))
        phase_spec = pl.BlockSpec(
            (GROUP * QUARTER, half_atoms), lambda n, g, index, half: (g, half[0] + n)
        )
        operands = [*pieces, vt, gt, kt, qt, *phases]
        specs = [vmem] * 4 + [rows_all] * 4 + [phase_spec] * 2
        if final:
            operands.append(gain)
            specs.append(rows_all)
        if totals is not None:
            operands += totals
            specs += [rows_all] * 4
        scratch = [
            pltpu.VMEM((2, 2, QUADS, groups * 2 * QUARTER, feats), BF16),
            pltpu.VMEM((2, groups, WIDTH, feats), BF16),
            pltpu.VMEM((2, groups, feats, WIDTH), BF16),
        ] + [pltpu.VMEM((feats, half_atoms), F32)] * 4
        if final:
            out_specs = pl.BlockSpec(
                (half_atoms, 4 * feats), lambda n, g, index, half: (0, 0)
            )
            out_shape = shape((half_atoms, 4 * feats), dtype)
        else:
            out_specs = [rows_all] * 4
            out_shape = [shape((feats, atoms), dtype)] * 4
        return pl.pallas_call(
            functools.partial(mix_kernel, totals is not None, final, mix_part),
            grid_spec=pltpu.PrefetchScalarGridSpec(
                num_scalar_prefetch=2,
                grid=(blocks, groups),
                in_specs=specs,
                out_specs=out_specs,
                scratch_shapes=scratch,
            ),
            out_shape=out_shape,
            compiler_params=params,
            cost_estimate=pl.CostEstimate(
                flops=8 * groups * WIDTH * blocks * half_atoms * feats,
                bytes_accessed=2 * groups * WIDTH * blocks * half_atoms, transcendentals=0,
            ),
            name="mix",
        )(index, half[None], *operands)

    made = []
    first = 0
    for groups in CHUNKS:
        after = [made[-2][2]] if len(made) > 1 else []
        kept, sent, *phases = make_states(first, groups, after)
        made.append((kept, *crossing(kept, sent), phases, groups))
        first += groups
    totals = None
    for kept, arrived, crossing_out, phases, groups in made[:-1]:
        pieces = summed(kept, arrived, crossing_out)
        totals = mix(jnp.int32(0), pieces, groups, phases, totals, False, BF16)
    kept, arrived, crossing_out, phases, groups = made[-1]
    pieces = summed(kept, arrived, crossing_out)
    away = mix(1 - mine, pieces, groups, phases, totals, True, BF16)
    theirs = lax.ppermute(away, "dirs", [(0, 1), (1, 0)])
    ours = mix(mine, pieces, groups, phases, totals, True, F32)
    total = (ours + theirs.astype(F32)).astype(BF16)
    return tuple(total[:, at * feats : (at + 1) * feats] for at in range(4))


def solution(mesh):
    return jax.shard_map(
        functools.partial(per_device, mesh.shape["atoms"]),
        mesh=mesh,
        in_specs=(
            P("atoms", None),
            P("atoms", None),
            P("atoms", None),
            P("atoms", None),
            P(None, "atoms"),
            P("atoms"),
            P("atoms"),
            P(),
            P(),
            P(None, "dirs"),
            P("dirs"),
            P("dirs"),
        ),
        out_specs=(
            P(("atoms", "dirs"), None),
            P(("atoms", "dirs"), None),
            P(("atoms", "dirs"), None),
            P(("atoms", "dirs"), None),
        ),
        check_vma=False,
    )
```

time: 210 us -> 170 us (0.81)
  Pallas kernels: 111 us -> 72.6 us
  local copies, waits for them, and re-layouts: 2.88 us -> 20.2 us
  starting transfers between devices: 54.5 us -> 37.2 us
  other arithmetic: 8.78 us -> 2.49 us
  waiting for transfers between devices: 31.8 us -> 35.5 us
    pallas_call x5 -> x4, Pallas kernels: 60.2 us -> 41.1 us  [mix(): pl.pallas_call(functools.partial(mix_kernel, totals is not None, final, m...]
    unnamed x50 -> x60, local copies, waits for them, and re-layouts: 2.83 us -> 19.1 us
    pallas_call x4 -> x3, Pallas kernels: 46.3 us -> 30.5 us  [make_states(): pl.pallas_call(functools.partial(states_kernel, first, part, 1.0 / math.s...]
    ppermute x48 -> x33, starting transfers between devices: 50.4 us -> 35.6 us  [moved(): lax.ppermute(x, 'atoms', [(i, target(i)) for i in range(atom_devices)])]
    ppermute x4 -> x1, waiting for transfers between devices: 7.76 us -> 18.3 us  [per_device(): theirs = lax.ppermute(away, 'dirs', [(0, 1), (1, 0)])]
    ppermute x48 -> x33, waiting for transfers between devices: 24.1 us -> 17.1 us  [moved(): lax.ppermute(x, 'atoms', [(i, target(i)) for i in range(atom_devices)])]
    convert_element_type x4 -> x1, other arithmetic: 7.19 us -> 0.43 us  [per_device(): total = (ours + theirs.astype(F32)).astype(BF16)]
    pallas_call x1, Pallas kernels: 4.06 us -> 0.95 us  [per_device(): pl.pallas_call(prepare_kernel, in_specs=[smem] + [vmem] * 7, out_specs=[v...]
  transfers between devices with their start and end apart: 52 -> 34, of which waited for: 15 -> 12; matrix products, arithmetic and copies ran while one was open for 3% -> 1% of each run, Pallas kernels for 41% -> 33%
where the time goes in v3:
time: 170 us; the launch traced here: 169 us
  Pallas kernels  72.6 us (43%)
  starting transfers between devices  37.2 us (22%)
  waiting for transfers between devices  35.5 us (21%)
  local copies, waits for them, and re-layouts  20.2 us (12%)
  other arithmetic  2.49 us (1%)
    pallas_call x4, Pallas kernels, mix(): pl.pallas_call(functools.partial(mix_kernel, totals is not None, final, m...  41.1 us
    ppermute x33, starting transfers between devices, moved(): lax.ppermute(x, 'atoms', [(i, target(i)) for i in range(atom_devices)])  35.6 us
    pallas_call x3, Pallas kernels, make_states(): pl.pallas_call(functools.partial(states_kernel, first, part, 1.0 / math.s...  30.5 us
    unnamed x60, local copies, waits for them, and re-layouts  19.1 us
    ppermute x1, waiting for transfers between devices, per_device(): theirs = lax.ppermute(away, 'dirs', [(0, 1), (1, 0)])  18.3 us
    ppermute x33, waiting for transfers between devices, moved(): lax.ppermute(x, 'atoms', [(i, target(i)) for i in range(atom_devices)])  17.1 us
  transfers between devices with their start and end apart: 34, of which 12 were waited for; matrix products, arithmetic and copies ran while one was open for 1% of the time, Pallas kernels for 33%

profile of v3, /device:TPU:0, one launch (start us, length us, event | category | flops | bytes accessed | tf_op | source)
XLA Modules:
  0.0 168.9 jit_solution(17609608566222798347)
XLA Ops:
  10.5 11.1 %states.3 = (bf16[2,4,256,128]{3,2,1,0:T(8,128)(2,1)S(1)}, bf16[2,4,256,128]{3,2,1,0:T(8,128)(2,1)S(1)}, bf16[512,2048]{1,0:T(8,128)(2,1)S(1)}, bf16[512,2048]{1,0:T(8,128)(2,1)S(1)}) custom-call(s32[1]{0:T(128)} %bitcast.index_ref, f32[3,44]{1,0:T(4,128)S(1)} %copy-done.18, f32[44]{0:T(128)S(1)} %copy-done.19, s32[44]{0:T(128)S(1)} %copy-done.20, ...), custom_call_target="tpu_custom_call" | custom-call | flops 4294967296 | bytes 8388608 | tf_op jit(solution)/shard_map/states/pallas_call | solution.py:235
  24.8 11.0 %states.5 = (bf16[2,4,256,128]{3,2,1,0:T(8,128)(2,1)S(1)}, bf16[2,4,256,128]{3,2,1,0:T(8,128)(2,1)S(1)}, bf16[512,2048]{1,0:T(8,128)(2,1)S(1)}, bf16[512,2048]{1,0:T(8,128)(2,1)S(1)}) custom-call(s32[1]{0:T(128)} %bitcast.index_ref, f32[3,44]{1,0:T(4,128)S(1)} %copy-done.18, f32[44]{0:T(128)S(1)} %copy-done.19, s32[44]{0:T(128)S(1)} %copy-done.20, ...), custom_call_target="tpu_custom_call" | custom-call | flops 4294967296 | bytes 8388608 | tf_op jit(solution)/shard_map/states/pallas_call | solution.py:235
  36.0 3.0 %collective-permute-start.23 = (bf16[4,256,128]{2,1,0:T(8,128)(2,1)S(1)}, bf16[4,256,128]{2,1,0:T(8,128)(2,1)S(1)}, u32[]{:S(2)}, u32[]{:S(2)}) collective-permute-start(bf16[4,256,128]{2,1,0:T(8,128)(2,1)S(1)} %fusion.3.refs_0_), channel_id=1, source_target_pairs={{0,4},{2,6},{4,0},{6,2},{8,12},{10,14},{12,8},{14,10},{16,20},{18,... | collective-permute-start | bytes 786440 | tf_op jit(solution)/shard_map/ppermute | solution.py:259
  40.6 8.4 %states.4 = (bf16[2,4,192,128]{3,2,1,0:T(8,128)(2,1)S(1)}, bf16[2,4,192,128]{3,2,1,0:T(8,128)(2,1)S(1)}, bf16[384,2048]{1,0:T(8,128)(2,1)S(1)}, bf16[384,2048]{1,0:T(8,128)(2,1)S(1)}) custom-call(s32[1]{0:T(128)} %bitcast.index_ref, f32[3,44]{1,0:T(4,128)S(1)} %copy-done.18, f32[44]{0:T(128)S(1)} %copy-done.19, s32[44]{0:T(128)S(1)} %copy-done.20, ...), custom_call_target="tpu_custom_call" | custom-call | flops 3221225472 | bytes 6291456 | tf_op jit(solution)/shard_map/states/pallas_call | solution.py:235
  49.3 1.6 collective-permute-start.24
  51.0 2.6 %collective-permute-start.25 = (bf16[256,128]{1,0:T(8,128)(2,1)S(1)}, bf16[256,128]{1,0:T(8,128)(2,1)S(1)}, u32[]{:S(2)}, u32[]{:S(2)}) collective-permute-start(bf16[256,128]{1,0:T(8,128)(2,1)S(1)} %get-tuple-element.60), channel_id=1, source_target_pairs={{0,16},{2,18},{4,20},{6,22},{8,24},{10,26},{12,28},{14,30},{16,0},... | collective-permute-start | bytes 196616 | tf_op jit(solution)/shard_map/ppermute | solution.py:259
  56.8 1.8 %collective-permute-done.25 = bf16[256,128]{1,0:T(8,128)(2,1)S(1)} collective-permute-done((bf16[256,128]{1,0:T(8,128)(2,1)S(1)}, bf16[256,128]{1,0:T(8,128)(2,1)S(1)}, u32[]{:S(2)}, u32[]{:S(2)}) %collective-permute-start.25) | collective-permute-done | bytes 65568 | tf_op jit(solution)/shard_map/ppermute | solution.py:259
  58.6 3.5 %collective-permute-start.16 = (bf16[256,128]{1,0:T(8,128)(2,1)S(1)}, bf16[256,128]{1,0:T(8,128)(2,1)S(1)}, u32[]{:S(2)}, u32[]{:S(2)}) collective-permute-start(bf16[256,128]{1,0:T(8,128)(2,1)S(1)} %get-tuple-element.62), channel_id=1, source_target_pairs={{0,24},{2,26},{4,28},{6,30},{8,0},{10,2},{12,4},{14,6},{16,8},{18,... | collective-permute-start | bytes 196616 | tf_op jit(solution)/shard_map/ppermute | solution.py:259
  62.2 2.7 %collective-permute-start.28 = (bf16[256,128]{1,0:T(8,128)(2,1)S(1)}, bf16[256,128]{1,0:T(8,128)(2,1)S(1)}, u32[]{:S(2)}, u32[]{:S(2)}) collective-permute-start(bf16[256,128]{1,0:T(8,128)(2,1)S(1)} %fusion.8), channel_id=1, source_target_pairs={{0,16},{2,18},{4,20},{6,22},{8,24},{10,26},{12,28},{14,30},{16,0},... | collective-permute-start | bytes 196616 | tf_op jit(solution)/shard_map/ppermute | solution.py:259
  65.8 3.8 %collective-permute-start.17 = (bf16[256,128]{1,0:T(8,128)(2,1)S(1)}, bf16[256,128]{1,0:T(8,128)(2,1)S(1)}, u32[]{:S(2)}, u32[]{:S(2)}) collective-permute-start(bf16[256,128]{1,0:T(8,128)(2,1)S(1)} %fusion.11), channel_id=1, source_target_pairs={{0,24},{2,26},{4,28},{6,30},{8,0},{10,2},{12,4},{14,6},{16,8},{18,... | collective-permute-start | bytes 196616 | tf_op jit(solution)/shard_map/ppermute | solution.py:259
  69.6 1.8 %collective-permute-done.2 = bf16[4,192,128]{2,1,0:T(8,128)(2,1)S(1)} collective-permute-done((bf16[4,192,128]{2,1,0:T(8,128)(2,1)S(1)}, bf16[4,192,128]{2,1,0:T(8,128)(2,1)S(1)}, u32[]{:S(2)}, u32[]{:S(2)}) %collective-permute-start.2) | collective-permute-done | bytes 196640 | tf_op jit(solution)/shard_map/ppermute | solution.py:259
  71.3 1.6 collective-permute-start.18
  73.0 2.5 %collective-permute-start.3 = (bf16[192,128]{1,0:T(8,128)(2,1)S(1)}, bf16[192,128]{1,0:T(8,128)(2,1)S(1)}, u32[]{:S(2)}, u32[]{:S(2)}) collective-permute-start(bf16[192,128]{1,0:T(8,128)(2,1)S(1)} %get-tuple-element.64), channel_id=1, source_target_pairs={{0,8},{2,10},{4,12},{6,14},{8,16},{10,18},{12,20},{14,22},{16,24},... | collective-permute-start | bytes 147464 | tf_op jit(solution)/shard_map/ppermute | solution.py:259
  75.5 2.4 %collective-permute-start.5 = (bf16[192,128]{1,0:T(8,128)(2,1)S(1)}, bf16[192,128]{1,0:T(8,128)(2,1)S(1)}, u32[]{:S(2)}, u32[]{:S(2)}) collective-permute-start(bf16[192,128]{1,0:T(8,128)(2,1)S(1)} %get-tuple-element.65), channel_id=1, source_target_pairs={{0,24},{2,26},{4,28},{6,30},{8,0},{10,2},{12,4},{14,6},{16,8},{18,... | collective-permute-start | bytes 147464 | tf_op jit(solution)/shard_map/ppermute | solution.py:259
  81.9 2.0 %collective-permute-start.6 = (bf16[192,128]{1,0:T(8,128)(2,1)S(1)}, bf16[192,128]{1,0:T(8,128)(2,1)S(1)}, u32[]{:S(2)}, u32[]{:S(2)}) collective-permute-start(bf16[192,128]{1,0:T(8,128)(2,1)S(1)} %fusion.14), channel_id=1, source_target_pairs={{0,24},{2,26},{4,28},{6,30},{8,0},{10,2},{12,4},{14,6},{16,8},{18,... | collective-permute-start | bytes 147464 | tf_op jit(solution)/shard_map/ppermute | solution.py:259
  85.9 2.1 %collective-permute-done.30.refs_1_ = bf16[1024,128]{1,0:T(8,128)(2,1)} collective-permute-done((bf16[1024,128]{1,0:T(8,128)(2,1)}, bf16[1024,128]{1,0:T(8,128)(2,1)}, u32[]{:S(2)}, u32[]{:S(2)}) %collective-permute-start.30) | collective-permute-done | bytes 262176 | tf_op jit(solution)/shard_map/ppermute | solution.py:259
  91.8 4.9 %collective-permute-done.20.refs_1_ = bf16[1024,128]{1,0:T(8,128)(2,1)} collective-permute-done((bf16[1024,128]{1,0:T(8,128)(2,1)}, bf16[1024,128]{1,0:T(8,128)(2,1)}, u32[]{:S(2)}, u32[]{:S(2)}) %collective-permute-start.20) | collective-permute-done | bytes 262176 | tf_op jit(solution)/shard_map/ppermute | solution.py:259
  103.1 1.6 copy-done.27
  104.7 1.6 copy-done.29
  106.3 14.7 %mix.4 = (bf16[128,2048]{1,0:T(8,128)(2,1)S(1)}, bf16[128,2048]{1,0:T(8,128)(2,1)S(1)}, bf16[128,2048]{1,0:T(8,128)(2,1)S(1)}, bf16[128,2048]{1,0:T(8,128)(2,1)S(1)}) custom-call(s32[1]{0:T(128)} %bitcast.index_ref, s32[1]{0:T(128)} %constant.10.clone.1.half_ref, bf16[1024,128]{1,0:T(8,128)(2,1)} %pad_maximum_fusion.1.refs_0_, ...), custom_call_target="tpu_custom_call" | custom-call | flops 4294967296 | bytes 8388608 | tf_op jit(solution)/shard_map/mix/pallas_call | solution.py:315
  121.1 15.1 %mix.5 = (bf16[128,2048]{1,0:T(8,128)(2,1)S(1)}, bf16[128,2048]{1,0:T(8,128)(2,1)S(1)}, bf16[128,2048]{1,0:T(8,128)(2,1)S(1)}, bf16[128,2048]{1,0:T(8,128)(2,1)S(1)}) custom-call(s32[1]{0:T(128)} %bitcast.index_ref, s32[1]{0:T(128)} %constant.10.clone.1.half_ref, bf16[1024,128]{1,0:T(8,128)(2,1)} %pad_maximum_fusion.refs_0_, ...), custom_call_target="tpu_custom_call" | custom-call | flops 4294967296 | bytes 8388608 | tf_op jit(solution)/shard_map/mix/pallas_call | solution.py:315
  136.2 5.6 %mix.7 = bf16[1024,512]{1,0:T(8,128)(2,1)S(1)} custom-call(s32[1]{0:T(128)} %bitcast.index_ref, s32[1]{0:T(128)} %bitcast.23.half_ref, bf16[768,128]{1,0:T(8,128)(2,1)S(1)} %pad_maximum_fusion.2.refs_0_, bf16[768,128]{1,0:T(8,128)(2,1)S(1)} %collective-permute-done.9.refs_1_, bf16[768,128]{1,0:T(8,128)(2,1)S(1)} %collective-permute-done.10.refs_2_, ...), custom_call_target="tpu_custom_call" | custom-call | flops 1610612736 | bytes 3145728 | tf_op jit(solution)/shard_map/mix/pallas_call | solution.py:315
  143.3 5.8 %mix.6 = f32[1024,512]{1,0:T(8,128)S(1)} custom-call(s32[1]{0:T(128)} %bitcast.index_ref, s32[1]{0:T(128)} %bitcast.1.half_ref, bf16[768,128]{1,0:T(8,128)(2,1)S(1)} %pad_maximum_fusion.2.refs_0_, bf16[768,128]{1,0:T(8,128)(2,1)S(1)} %collective-permute-done.9.refs_1_, bf16[768,128]{1,0:T(8,128)(2,1)S(1)} %collective-permute-done.10.refs_2_, ...), custom_call_target="tpu_custom_call" | custom-call | flops 1610612736 | bytes 3145728 | tf_op jit(solution)/shard_map/mix/pallas_call | solution.py:315
  149.1 18.3 %collective-permute-done.33 = bf16[1024,512]{1,0:T(8,128)(2,1)S(1)} collective-permute-done((bf16[1024,512]{1,0:T(8,128)(2,1)S(1)}, bf16[1024,512]{1,0:T(8,128)(2,1)S(1)}, u32[]{:S(2)}, u32[]{:S(2)}) %collective-permute-start.33) | collective-permute-done | bytes 1048608 | tf_op jit(solution)/shard_map/ppermute | solution.py:347
  (129 shorter events, 38.4 us)
Async XLA Ops:
  24.3 11.6 %collective-permute-start = (bf16[2,4,256,128]{3,2,1,0:T(8,128)(2,1)S(1)}, bf16[2,4,256,128]{3,2,1,0:T(8,128)(2,1)S(1)}, u32[]{:S(2)}, u32[]{:S(2)}) collective-permute-start(bf16[2,4,256,128]{3,2,1,0:T(8,128)(2,1)S(1)} %get-tuple-element.32), channel_id=1, source_target_pairs={{0,2},{2,0},{4,6},{6,4},{8,10},{10,8},{12,14},{14,12},{16,18},{18,... | collective-permute-start | bytes 1572872 | tf_op jit(solution)/shard_map/ppermute | solution.py:259
  36.0 13.2 %collective-permute-start.23 = (bf16[4,256,128]{2,1,0:T(8,128)(2,1)S(1)}, bf16[4,256,128]{2,1,0:T(8,128)(2,1)S(1)}, u32[]{:S(2)}, u32[]{:S(2)}) collective-permute-start(bf16[4,256,128]{2,1,0:T(8,128)(2,1)S(1)} %fusion.3.refs_0_), channel_id=1, source_target_pairs={{0,4},{2,6},{4,0},{6,2},{8,12},{10,14},{12,8},{14,10},{16,20},{18,... | collective-permute-start | bytes 786440 | tf_op jit(solution)/shard_map/ppermute | solution.py:259
  39.1 15.8 %collective-permute-start.13 = (bf16[4,256,128]{2,1,0:T(8,128)(2,1)S(1)}, bf16[4,256,128]{2,1,0:T(8,128)(2,1)S(1)}, u32[]{:S(2)}, u32[]{:S(2)}) collective-permute-start(bf16[4,256,128]{2,1,0:T(8,128)(2,1)S(1)} %fusion.4), channel_id=1, source_target_pairs={{0,4},{2,6},{4,0},{6,2},{8,12},{10,14},{12,8},{14,10},{16,20},{18,... | collective-permute-start | bytes 786440 | tf_op jit(solution)/shard_map/ppermute | solution.py:259
  49.0 13.1 %collective-permute-start.1 = (bf16[2,4,192,128]{3,2,1,0:T(8,128)(2,1)S(1)}, bf16[2,4,192,128]{3,2,1,0:T(8,128)(2,1)S(1)}, u32[]{:S(2)}, u32[]{:S(2)}) collective-permute-start(bf16[2,4,192,128]{3,2,1,0:T(8,128)(2,1)S(1)} %get-tuple-element.34), channel_id=1, source_target_pairs={{0,2},{2,0},{4,6},{6,4},{8,10},{10,8},{12,14},{14,12},{16,18},{18,... | collective-permute-start | bytes 1179656 | tf_op jit(solution)/shard_map/ppermute | solution.py:259
  51.0 7.6 %collective-permute-start.25 = (bf16[256,128]{1,0:T(8,128)(2,1)S(1)}, bf16[256,128]{1,0:T(8,128)(2,1)S(1)}, u32[]{:S(2)}, u32[]{:S(2)}) collective-permute-start(bf16[256,128]{1,0:T(8,128)(2,1)S(1)} %get-tuple-element.60), channel_id=1, source_target_pairs={{0,16},{2,18},{4,20},{6,22},{8,24},{10,26},{12,28},{14,30},{16,0},... | collective-permute-start | bytes 196616 | tf_op jit(solution)/shard_map/ppermute | solution.py:259
  53.5 8.5 %collective-permute-start.26 = (bf16[256,128]{1,0:T(8,128)(2,1)S(1)}, bf16[256,128]{1,0:T(8,128)(2,1)S(1)}, u32[]{:S(2)}, u32[]{:S(2)}) collective-permute-start(bf16[256,128]{1,0:T(8,128)(2,1)S(1)} %get-tuple-element.59), channel_id=1, source_target_pairs={{0,24},{2,26},{4,28},{6,30},{8,0},{10,2},{12,4},{14,6},{16,8},{18,... | collective-permute-start | bytes 196616 | tf_op jit(solution)/shard_map/ppermute | solution.py:259
  55.0 9.9 %collective-permute-start.14 = (bf16[256,128]{1,0:T(8,128)(2,1)S(1)}, bf16[256,128]{1,0:T(8,128)(2,1)S(1)}, u32[]{:S(2)}, u32[]{:S(2)}) collective-permute-start(bf16[256,128]{1,0:T(8,128)(2,1)S(1)} %get-tuple-element.61), channel_id=1, source_target_pairs={{0,8},{2,10},{4,12},{6,14},{8,16},{10,18},{12,20},{14,22},{16,24},... | collective-permute-start | bytes 196616 | tf_op jit(solution)/shard_map/ppermute | solution.py:259
  55.8 9.2 %collective-permute-start.15 = (bf16[256,128]{1,0:T(8,128)(2,1)S(1)}, bf16[256,128]{1,0:T(8,128)(2,1)S(1)}, u32[]{:S(2)}, u32[]{:S(2)}) collective-permute-start(bf16[256,128]{1,0:T(8,128)(2,1)S(1)} %get-tuple-element.63), channel_id=1, source_target_pairs={{0,16},{2,18},{4,20},{6,22},{8,24},{10,26},{12,28},{14,30},{16,0},... | collective-permute-start | bytes 196616 | tf_op jit(solution)/shard_map/ppermute | solution.py:259
  58.6 7.1 %collective-permute-start.16 = (bf16[256,128]{1,0:T(8,128)(2,1)S(1)}, bf16[256,128]{1,0:T(8,128)(2,1)S(1)}, u32[]{:S(2)}, u32[]{:S(2)}) collective-permute-start(bf16[256,128]{1,0:T(8,128)(2,1)S(1)} %get-tuple-element.62), channel_id=1, source_target_pairs={{0,24},{2,26},{4,28},{6,30},{8,0},{10,2},{12,4},{14,6},{16,8},{18,... | collective-permute-start | bytes 196616 | tf_op jit(solution)/shard_map/ppermute | solution.py:259
  62.1 10.9 %collective-permute-start.27 = (bf16[256,128]{1,0:T(8,128)(2,1)S(1)}, bf16[256,128]{1,0:T(8,128)(2,1)S(1)}, u32[]{:S(2)}, u32[]{:S(2)}) collective-permute-start(bf16[256,128]{1,0:T(8,128)(2,1)S(1)} %fusion.8), channel_id=1, source_target_pairs={{0,24},{2,26},{4,28},{6,30},{8,0},{10,2},{12,4},{14,6},{16,8},{18,... | collective-permute-start | bytes 196616 | tf_op jit(solution)/shard_map/ppermute | solution.py:259
  62.2 13.3 %collective-permute-start.28 = (bf16[256,128]{1,0:T(8,128)(2,1)S(1)}, bf16[256,128]{1,0:T(8,128)(2,1)S(1)}, u32[]{:S(2)}, u32[]{:S(2)}) collective-permute-start(bf16[256,128]{1,0:T(8,128)(2,1)S(1)} %fusion.8), channel_id=1, source_target_pairs={{0,16},{2,18},{4,20},{6,22},{8,24},{10,26},{12,28},{14,30},{16,0},... | collective-permute-start | bytes 196616 | tf_op jit(solution)/shard_map/ppermute | solution.py:259
  65.0 10.6 %collective-permute-start.29 = (bf16[256,128]{1,0:T(8,128)(2,1)S(1)}, bf16[256,128]{1,0:T(8,128)(2,1)S(1)}, u32[]{:S(2)}, u32[]{:S(2)}) collective-permute-start(bf16[256,128]{1,0:T(8,128)(2,1)S(1)} %fusion.8), channel_id=1, source_target_pairs={{0,8},{2,10},{4,12},{6,14},{8,16},{10,18},{12,20},{14,22},{16,24},... | collective-permute-start | bytes 196616 | tf_op jit(solution)/shard_map/ppermute | solution.py:259
  65.8 16.2 %collective-permute-start.17 = (bf16[256,128]{1,0:T(8,128)(2,1)S(1)}, bf16[256,128]{1,0:T(8,128)(2,1)S(1)}, u32[]{:S(2)}, u32[]{:S(2)}) collective-permute-start(bf16[256,128]{1,0:T(8,128)(2,1)S(1)} %fusion.11), channel_id=1, source_target_pairs={{0,24},{2,26},{4,28},{6,30},{8,0},{10,2},{12,4},{14,6},{16,8},{18,... | collective-permute-start | bytes 196616 | tf_op jit(solution)/shard_map/ppermute | solution.py:259
  71.3 12.6 %collective-permute-start.18 = (bf16[256,128]{1,0:T(8,128)(2,1)S(1)}, bf16[256,128]{1,0:T(8,128)(2,1)S(1)}, u32[]{:S(2)}, u32[]{:S(2)}) collective-permute-start(bf16[256,128]{1,0:T(8,128)(2,1)S(1)} %fusion.11), channel_id=1, source_target_pairs={{0,16},{2,18},{4,20},{6,22},{8,24},{10,26},{12,28},{14,30},{16,0},... | collective-permute-start | bytes 196616 | tf_op jit(solution)/shard_map/ppermute | solution.py:259
  81.2 6.7 %collective-permute-start.30 = (bf16[1024,128]{1,0:T(8,128)(2,1)}, bf16[1024,128]{1,0:T(8,128)(2,1)}, u32[]{:S(2)}, u32[]{:S(2)}) collective-permute-start(bf16[1024,128]{1,0:T(8,128)(2,1)} %pad_maximum_fusion.1.refs_0_), channel_id=1, source_target_pairs={{0,4},{2,6},{4,0},{6,2},{8,12},{10,14},{12,8},{14,10},{16,20},{18,... | collective-permute-start | bytes 786440 | tf_op jit(solution)/shard_map/ppermute | solution.py:259
  81.9 14.9 %collective-permute-start.31 = (bf16[1024,128]{1,0:T(8,128)(2,1)}, bf16[1024,128]{1,0:T(8,128)(2,1)}, u32[]{:S(2)}, u32[]{:S(2)}) collective-permute-start(bf16[1024,128]{1,0:T(8,128)(2,1)} %pad_maximum_fusion.1.refs_0_), channel_id=1, source_target_pairs={{0,2},{2,0},{4,6},{6,4},{8,10},{10,8},{12,14},{14,12},{16,18},{18,... | collective-permute-start | bytes 786440 | tf_op jit(solution)/shard_map/ppermute | solution.py:259
  87.9 8.8 %collective-permute-start.20 = (bf16[1024,128]{1,0:T(8,128)(2,1)}, bf16[1024,128]{1,0:T(8,128)(2,1)}, u32[]{:S(2)}, u32[]{:S(2)}) collective-permute-start(bf16[1024,128]{1,0:T(8,128)(2,1)} %pad_maximum_fusion.refs_0_), channel_id=1, source_target_pairs={{0,4},{2,6},{4,0},{6,2},{8,12},{10,14},{12,8},{14,10},{16,20},{18,... | collective-permute-start | bytes 786440 | tf_op jit(solution)/shard_map/ppermute | solution.py:259
  88.6 10.2 %collective-permute-start.32 = (bf16[1024,128]{1,0:T(8,128)(2,1)}, bf16[1024,128]{1,0:T(8,128)(2,1)}, u32[]{:S(2)}, u32[]{:S(2)}) collective-permute-start(bf16[1024,128]{1,0:T(8,128)(2,1)} %collective-permute-done.30.refs_1_), channel_id=1, source_target_pairs={{0,2},{2,0},{4,6},{6,4},{8,10},{10,8},{12,14},{14,12},{16,18},{18,... | collective-permute-start | bytes 786440 | tf_op jit(solution)/shard_map/ppermute | solution.py:259
  91.0 7.7 %collective-permute-start.9 = (bf16[768,128]{1,0:T(8,128)(2,1)S(1)}, bf16[768,128]{1,0:T(8,128)(2,1)S(1)}, u32[]{:S(2)}, u32[]{:S(2)}) collective-permute-start(bf16[768,128]{1,0:T(8,128)(2,1)S(1)} %pad_maximum_fusion.2.refs_0_), channel_id=1, source_target_pairs={{0,4},{2,6},{4,0},{6,2},{8,12},{10,14},{12,8},{14,10},{16,20},{18,... | collective-permute-start | bytes 589832 | tf_op jit(solution)/shard_map/ppermute | solution.py:259
  91.8 29.2 %collective-permute-start.21 = (bf16[1024,128]{1,0:T(8,128)(2,1)}, bf16[1024,128]{1,0:T(8,128)(2,1)S(1)}, u32[]{:S(2)}, u32[]{:S(2)}) collective-permute-start(bf16[1024,128]{1,0:T(8,128)(2,1)} %pad_maximum_fusion.refs_0_), channel_id=1, source_target_pairs={{0,2},{2,0},{4,6},{6,4},{8,10},{10,8},{12,14},{14,12},{16,18},{18,... | collective-permute-start | bytes 786440 | tf_op jit(solution)/shard_map/ppermute | solution.py:259
  96.7 24.3 %collective-permute-start.22 = (bf16[1024,128]{1,0:T(8,128)(2,1)}, bf16[1024,128]{1,0:T(8,128)(2,1)S(1)}, u32[]{:S(2)}, u32[]{:S(2)}) collective-permute-start(bf16[1024,128]{1,0:T(8,128)(2,1)} %collective-permute-done.20.refs_1_), channel_id=1, source_target_pairs={{0,2},{2,0},{4,6},{6,4},{8,10},{10,8},{12,14},{14,12},{16,18},{18,... | collective-permute-start | bytes 786440 | tf_op jit(solution)/shard_map/ppermute | solution.py:259
  96.7 39.4 %collective-permute-start.10 = (bf16[768,128]{1,0:T(8,128)(2,1)S(1)}, bf16[768,128]{1,0:T(8,128)(2,1)S(1)}, u32[]{:S(2)}, u32[]{:S(2)}) collective-permute-start(bf16[768,128]{1,0:T(8,128)(2,1)S(1)} %pad_maximum_fusion.2.refs_0_), channel_id=1, source_target_pairs={{0,2},{2,0},{4,6},{6,4},{8,10},{10,8},{12,14},{14,12},{16,18},{18,... | collective-permute-start | bytes 589832 | tf_op jit(solution)/shard_map/ppermute | solution.py:259
  98.7 37.4 %collective-permute-start.11 = (bf16[768,128]{1,0:T(8,128)(2,1)S(1)}, bf16[768,128]{1,0:T(8,128)(2,1)S(1)}, u32[]{:S(2)}, u32[]{:S(2)}) collective-permute-start(bf16[768,128]{1,0:T(8,128)(2,1)S(1)} %collective-permute-done.9.refs_1_), channel_id=1, source_target_pairs={{0,2},{2,0},{4,6},{6,4},{8,10},{10,8},{12,14},{14,12},{16,18},{18,... | collective-permute-start | bytes 589832 | tf_op jit(solution)/shard_map/ppermute | solution.py:259
  141.7 25.7 %collective-permute-start.33 = (bf16[1024,512]{1,0:T(8,128)(2,1)S(1)}, bf16[1024,512]{1,0:T(8,128)(2,1)S(1)}, u32[]{:S(2)}, u32[]{:S(2)}) collective-permute-start(bf16[1024,512]{1,0:T(8,128)(2,1)S(1)} %mix.7), channel_id=1, source_target_pairs={{0,1},{1,0},{2,3},{3,2},{4,5},{5,4},{6,7},{7,6},{8,9},{9,8},{10,11... | collective-permute-start | bytes 3145736 | tf_op jit(solution)/shard_map/ppermute | solution.py:347
  (40 other events, 251.8 us)

commit v4 on v3

--- a/solution.py
+++ b/solution.py
@@ -15,7 +15,7 @@
 LANES = 128
 QUARTER = LANES // QUADS
 WIDTH = GROUP * LANES
-VMEM_LIMIT = 30 * 2**20
+VMEM_LIMIT = 56 * 2**20
 CHUNKS = (4, 4, 3)
 
 SIN_COEF = (4.4428679, -7.30744342, 3.59478808, -0.78437403)
@@ -62,10 +62,13 @@
 
 
 def states_kernel(
-    first, part, scale, index_ref, dirs_ref, weight_ref, mask_ref, freq_ref, pos_ref,
+    first, part, scale, slotted, index_ref, dirs_ref, weight_ref, mask_ref, freq_ref, pos_ref,
     qt_ref, kt_ref, v_ref, g_ref, *refs,
 ):
-    kept_ref, sent_ref, cos_ref, sin_ref, kr, qr, slots = refs[-7:]
+    if slotted:
+        kept_ref, sent_ref, cos_ref, sin_ref, kr, qr, slots = refs[-7:]
+    else:
+        both_ref, cos_ref, sin_ref, kr, qr = refs[-5:]
     group = first + pl.program_id(0)
     atoms = pos_ref.shape[1]
     core, pair, quad = place_of(index_ref[0])
@@ -99,11 +102,14 @@
             rows = slice(i % 2 * QUARTER, (i % 2 + 1) * QUARTER)
             for m in range(QUADS):
                 row = i * LANES + m * QUARTER
-                slots[kind ^ core, (i // 2) ^ pair, (m - quad) & 3, rows, :] = (
-                    total[row : row + QUARTER, :] * coef
-                ).astype(BF16)
-    kept_ref[...] = slots[0]
-    sent_ref[...] = slots[1]
+                scaled = (total[row : row + QUARTER, :] * coef).astype(BF16)
+                if slotted:
+                    slots[kind ^ core, (i // 2) ^ pair, (m - quad) & 3, rows, :] = scaled
+                else:
+                    both_ref[kind, row : row + QUARTER, :] = scaled
+    if slotted:
+        kept_ref[...] = slots[0]
+        sent_ref[...] = slots[1]
 
 
 def rotated(x, cosine, sine):
@@ -118,11 +124,12 @@
 
 
 def mix_kernel(
-    has_totals, final, part, index_ref, half_ref, *refs,
+    slotted, has_totals, final, part, index_ref, half_ref, *refs,
 ):
     del half_ref
     refs = list(refs)
-    sources, refs = refs[:4], refs[4:]
+    source_count = 4 if slotted else 1
+    sources, refs = refs[:source_count], refs[source_count:]
     vt_ref, gt_ref, kt_ref, qt_ref, cos_ref, sin_ref = refs[:6]
     refs = refs[6:]
     if final:
@@ -131,21 +138,25 @@
         before, refs = refs[:4], refs[4:]
     out_count = 1 if final else 4
     outs, refs = refs[:out_count], refs[out_count:]
-    slots, states, states_t = refs[:3]
-    totals = refs[3:7]
-    group = pl.program_id(1)
-    groups = pl.num_programs(1)
+    states, states_t = refs[:2]
+    totals = refs[2:6]
+    slots = refs[6] if slotted else None
+    group = pl.program_id(0)
+    groups = pl.num_programs(0)
     core, pair, quad = place_of(index_ref[0])
 
-    @pl.when((group == 0) & (pl.program_id(0) == 0))
+    @pl.when(group == 0)
     def _():
         for at, source in enumerate(sources):
-            slots[at // 2, at % 2] = source[...].reshape(slots.shape[2:])
-        for g in range(slots.shape[3] // (2 * QUARTER)):
+            if slotted:
+                slots[at // 2, at % 2] = source[...].reshape(slots.shape[2:])
+            else:
+                states[...] = source[...].reshape(states.shape)
+        for g in range(states.shape[1]):
             for kind in range(2):
                 for i in range(GROUP):
                     start = g * 2 * QUARTER + i % 2 * QUARTER
-                    for m in range(QUADS):
+                    for m in range(QUADS if slotted else 0):
                         row = i * LANES + m * QUARTER
                         states[kind, g, row : row + QUARTER, :] = slots[
                             kind ^ core, (i // 2) ^ pair, (m - quad) & 3,
@@ -228,22 +239,29 @@
 
     part = min(256, atoms)
 
-    def make_states(first, groups, after):
-        sent = (2, QUADS, groups * 2 * QUARTER, feats)
-        sent_spec = pl.BlockSpec((2, QUADS, 2 * QUARTER, feats), lambda g: (0, 0, g, 0))
+    def make_states(first, groups, slotted, after=()):
         phase_spec = pl.BlockSpec((GROUP * QUARTER, atoms), lambda g: (g, 0))
+        if slotted:
+            sent = [shape((2, QUADS, groups * 2 * QUARTER, feats), BF16)] * 2
+            sent_spec = [pl.BlockSpec((2, QUADS, 2 * QUARTER, feats), lambda g: (0, 0, g, 0))] * 2
+            slots = [pltpu.VMEM((2, 2, QUADS, 2 * QUARTER, feats), BF16)]
+        else:
+            sent = [shape((2, groups * WIDTH, feats), BF16)]
+            sent_spec = [pl.BlockSpec((2, WIDTH, feats), lambda g: (0, g, 0))]
+            slots = []
         return pl.pallas_call(
-            functools.partial(states_kernel, first, part, 1.0 / math.sqrt(feats * atoms)),
+            functools.partial(
+                states_kernel, first, part, 1.0 / math.sqrt(feats * atoms), slotted
+            ),
             grid=(groups,),
             in_specs=[smem] * 4 + [vmem] * 6 + [pl.BlockSpec(memory_space=pl.ANY)] * len(after),
-            out_specs=[sent_spec] * 2 + [phase_spec] * 2,
-            out_shape=[shape(sent, BF16)] * 2
-            + [shape((groups * GROUP * QUARTER, atoms), BF16)] * 2,
+            out_specs=sent_spec + [phase_spec] * 2,
+            out_shape=sent + [shape((groups * GROUP * QUARTER, atoms), BF16)] * 2,
             scratch_shapes=[
                 pltpu.VMEM((WIDTH, atoms), BF16),
                 pltpu.VMEM((WIDTH, atoms), BF16),
-                pltpu.VMEM((2, 2, QUADS, 2 * QUARTER, feats), BF16),
-            ],
+            ]
+            + slots,
             compiler_params=params,
             cost_estimate=pl.CostEstimate(
                 flops=8 * groups * WIDTH * atoms * feats,
@@ -285,38 +303,39 @@
     half_atoms = atoms // 2
 
     def mix(half, pieces, groups, phases, totals, final, dtype):
-        blocks = 1 if final else 2
-        mix_part = min(256, half_atoms)
-        rows_all = pl.BlockSpec((feats, half_atoms), lambda n, g, index, half: (0, half[0] + n))
+        slotted = len(pieces) == 4
+        rows_half = pl.BlockSpec((feats, half_atoms), lambda g, index, half: (0, half[0]))
         phase_spec = pl.BlockSpec(
-            (GROUP * QUARTER, half_atoms), lambda n, g, index, half: (g, half[0] + n)
+            (GROUP * QUARTER, half_atoms), lambda g, index, half: (g, half[0])
         )
+        totals_spec = pl.BlockSpec((feats, half_atoms), lambda g, index, half: (0, 0))
         operands = [*pieces, vt, gt, kt, qt, *phases]
-        specs = [vmem] * 4 + [rows_all] * 4 + [phase_spec] * 2
+        specs = [vmem] * len(pieces) + [rows_half] * 4 + [phase_spec] * 2
         if final:
             operands.append(gain)
-            specs.append(rows_all)
+            specs.append(rows_half)
         if totals is not None:
             operands += totals
-            specs += [rows_all] * 4
+            specs += [totals_spec] * 4
         scratch = [
-            pltpu.VMEM((2, 2, QUADS, groups * 2 * QUARTER, feats), BF16),
             pltpu.VMEM((2, groups, WIDTH, feats), BF16),
             pltpu.VMEM((2, groups, feats, WIDTH), BF16),
         ] + [pltpu.VMEM((feats, half_atoms), F32)] * 4
+        if slotted:
+            scratch.append(pltpu.VMEM((2, 2, QUADS, groups * 2 * QUARTER, feats), BF16))
         if final:
-            out_specs = pl.BlockSpec(
-                (half_atoms, 4 * feats), lambda n, g, index, half: (0, 0)
-            )
+            out_specs = pl.BlockSpec((half_atoms, 4 * feats), lambda g, index, half: (0, 0))
             out_shape = shape((half_atoms, 4 * feats), dtype)
         else:
-            out_specs = [rows_all] * 4
-            out_shape = [shape((feats, atoms), dtype)] * 4
+            out_specs = [totals_spec] * 4
+            out_shape = [shape((feats, half_atoms), dtype)] * 4
         return pl.pallas_call(
-            functools.partial(mix_kernel, totals is not None, final, mix_part),
+            functools.partial(
+                mix_kernel, slotted, totals is not None, final, min(256, half_atoms)
+            ),
             grid_spec=pltpu.PrefetchScalarGridSpec(
                 num_scalar_prefetch=2,
-                grid=(blocks, groups),
+                grid=(groups,),
                 in_specs=specs,
                 out_specs=out_specs,
                 scratch_shapes=scratch,
@@ -324,29 +343,48 @@
             out_shape=out_shape,
             compiler_params=params,
             cost_estimate=pl.CostEstimate(
-                flops=8 * groups * WIDTH * blocks * half_atoms * feats,
-                bytes_accessed=2 * groups * WIDTH * blocks * half_atoms, transcendentals=0,
+                flops=8 * groups * WIDTH * half_atoms * feats,
+                bytes_accessed=2 * groups * WIDTH * half_atoms, transcendentals=0,
             ),
             name="mix",
         )(index, half[None], *operands)
 
-    made = []
-    first = 0
-    for groups in CHUNKS:
-        after = [made[-2][2]] if len(made) > 1 else []
-        kept, sent, *phases = make_states(first, groups, after)
-        made.append((kept, *crossing(kept, sent), phases, groups))
-        first += groups
-    totals = None
-    for kept, arrived, crossing_out, phases, groups in made[:-1]:
-        pieces = summed(kept, arrived, crossing_out)
-        totals = mix(jnp.int32(0), pieces, groups, phases, totals, False, BF16)
-    kept, arrived, crossing_out, phases, groups = made[-1]
-    pieces = summed(kept, arrived, crossing_out)
-    away = mix(1 - mine, pieces, groups, phases, totals, True, BF16)
-    theirs = lax.ppermute(away, "dirs", [(0, 1), (1, 0)])
-    ours = mix(mine, pieces, groups, phases, totals, True, F32)
-    total = (ours + theirs.astype(F32)).astype(BF16)
+    def after(x, *others):
+        return pl.pallas_call(
+            lambda x_ref, *refs: refs[-1].__setitem__(..., x_ref[...]),
+            in_specs=[vmem] + [pl.BlockSpec(memory_space=pl.ANY)] * len(others),
+            out_specs=vmem,
+            out_shape=shape(x.shape, x.dtype),
+            name="after",
+        )(x, *others)
+
+    bounds = [sum(CHUNKS[:at]) for at in range(len(CHUNKS))]
+    both, *phases = make_states(bounds[0], CHUNKS[0], False)
+    made = [phases]
+    shard = lax.psum_scatter(
+        both.reshape(-1, feats), "atoms", scatter_dimension=0, tiled=True
+    )
+    kept, sent, *phases = make_states(bounds[1], CHUNKS[1], True, [both])
+    made.append(phases)
+    crossed = [(kept, *crossing(kept, sent))]
+    kept, sent, *phases = make_states(bounds[2], CHUNKS[2], True, [crossed[0][2]])
+    made.append(phases)
+    crossed.append((kept, *crossing(kept, sent)))
+    shard = after(shard, sent)
+    pieces = [[lax.all_gather(shard, "atoms", axis=0, tiled=True)]]
+    pieces += [summed(*each) for each in crossed]
+
+    def mix_all(half, dtype):
+        totals = None
+        for at, groups in enumerate(CHUNKS):
+            final = at == len(CHUNKS) - 1
+            totals = mix(
+                half, pieces[at], groups, made[at], totals, final, dtype if final else BF16
+            )
+        return totals
+
+    theirs = lax.ppermute(mix_all(1 - mine, BF16), "dirs", [(0, 1), (1, 0)])
+    total = (mix_all(mine, F32) + theirs.astype(F32)).astype(BF16)
     return tuple(total[:, at * feats : (at + 1) * feats] for at in range(4))
 
 

time: 170 us -> 196 us (1.15)
  Pallas kernels: 72.6 us -> 96.2 us
  waiting for transfers between devices: 35.5 us -> 53.8 us
  local copies, waits for them, and re-layouts: 20.2 us -> 2.62 us
  between operations: 1.05 us -> 14.3 us
  starting transfers between devices: 37.2 us -> 24.3 us
    reduce_scatter x0 -> x1, waiting for transfers between devices: none -> 30.7 us  [per_device(): lax.psum_scatter(both.reshape(-1, feats), 'atoms', scatter_dimension=0, t...]
    ppermute x1, waiting for transfers between devices: 18.3 us -> 0.01 us  [per_device(): theirs = lax.ppermute(mix_all(1 - mine, BF16), 'dirs', [(0, 1), (1, 0)])]
    unnamed x60 -> x22, local copies, waits for them, and re-layouts: 19.1 us -> 1.54 us
    pallas_call x4 -> x7, Pallas kernels: 41.1 us -> 55.4 us  [the longest x6 53.9 us: mix(): pl.pallas_call(functools.partial(mix_kernel, slotted, totals is not None,...]
    ppermute x33 -> x22, starting transfers between devices: 35.6 us -> 22.7 us  [moved(): lax.ppermute(x, 'atoms', [(i, target(i)) for i in range(atom_devices)])]
    pallas_call x3, Pallas kernels: 30.5 us -> 36.8 us  [make_states(): pl.pallas_call(functools.partial(states_kernel, first, part, 1.0 / math.s...]
    all_gather x0 -> x1, waiting for transfers between devices: none -> 4.96 us  [per_device(): pieces = [[lax.all_gather(shard, 'atoms', axis=0, tiled=True)]]]
    pallas_call x1, Pallas kernels: 0.95 us -> 4.02 us  [per_device(): pl.pallas_call(prepare_kernel, in_specs=[smem] + [vmem] * 7, out_specs=[v...]
  transfers between devices with their start and end apart: 34 -> 25, of which waited for: 12 -> 11; matrix products, arithmetic and copies ran while one was open for 1% -> 1% of each run, Pallas kernels for 33% -> 36%
where the time goes in v4:
time: 196 us; the launch traced here: 195 us
  Pallas kernels  96.2 us (49%)
  waiting for transfers between devices  53.8 us (27%)
  starting transfers between devices  24.3 us (12%)
  between operations  14.3 us (7%)
  other arithmetic  4.23 us (2%)
  local copies, waits for them, and re-layouts  2.62 us (1%)
    pallas_call x6, Pallas kernels, mix(): pl.pallas_call(functools.partial(mix_kernel, slotted, totals is not None,...  53.9 us
    pallas_call x3, Pallas kernels, make_states(): pl.pallas_call(functools.partial(states_kernel, first, part, 1.0 / math.s...  36.8 us
    reduce_scatter x1, waiting for transfers between devices, per_device(): lax.psum_scatter(both.reshape(-1, feats), 'atoms', scatter_dimension=0, t...  30.7 us
    ppermute x22, starting transfers between devices, moved(): lax.ppermute(x, 'atoms', [(i, target(i)) for i in range(atom_devices)])  22.7 us
    ppermute x22, waiting for transfers between devices, moved(): lax.ppermute(x, 'atoms', [(i, target(i)) for i in range(atom_devices)])  18.2 us
    all_gather x1, waiting for transfers between devices, per_device(): pieces = [[lax.all_gather(shard, 'atoms', axis=0, tiled=True)]]  4.96 us
    pallas_call x1, Pallas kernels, per_device(): pl.pallas_call(prepare_kernel, in_specs=[smem] + [vmem] * 7, out_specs=[v...  4.02 us
  transfers between devices with their start and end apart: 25, of which 11 were waited for; matrix products, arithmetic and copies ran while one was open for 1% of the time, Pallas kernels for 36%

profile of v4, /device:TPU:0, one launch (start us, length us, event | category | flops | bytes accessed | tf_op | source)
XLA Modules:
  0.0 195.5 jit_solution(12656720571556948619)
XLA Ops:
  7.2 4.0 %prepare.1 = (bf16[128,2048]{1,0:T(8,128)(2,1)}, f32[128,2048]{1,0:T(8,128)}, bf16[128,2048]{1,0:T(8,128)(2,1)}, bf16[128,2048]{1,0:T(8,128)(2,1)}, f32[128,2048]{1,0:T(8,128)}) custom-call(s32[1]{0:T(128)} %bitcast.index_ref, s32[1,2048]{1,0:T(1,128)} %bitcast.42, s32[1,2048]{1,0:T(1,128)} %bitcast.43, f32[5,128]{1,0:T(8,128)} %gain_ref.1, ...), custom_call_target="tpu_custom_call" | custom-call | tf_op jit(solution)/shard_map/prepare/pallas_call | solution.py:228
  11.2 13.0 %states.3 = (bf16[2,2048,128]{2,1,0:T(8,128)(2,1)}, bf16[512,2048]{1,0:T(8,128)(2,1)}, bf16[512,2048]{1,0:T(8,128)(2,1)}) custom-call(s32[1]{0:T(128)} %bitcast.index_ref, f32[3,44]{1,0:T(4,128)} %dirs_ref.5, f32[44]{0:T(128)} %weight_ref.5, s32[44]{0:T(128)} %mask_ref.5, f32[1,32]{1,0:T(1,128)} %bitcast.44, f32[3,2048]{1,0:T(4,128)} %pos_ref.5, ...), custom_call_target="tpu_custom_call" | custom-call | flops 4294967296 | bytes 8388608 | tf_op jit(solution)/shard_map/states/pallas_call | solution.py:252
  24.3 13.1 %states.4 = (bf16[2,4,256,128]{3,2,1,0:T(8,128)(2,1)}, bf16[2,4,256,128]{3,2,1,0:T(8,128)(2,1)}, bf16[512,2048]{1,0:T(8,128)(2,1)}, bf16[512,2048]{1,0:T(8,128)(2,1)}) custom-call(s32[1]{0:T(128)} %bitcast.index_ref, f32[3,44]{1,0:T(4,128)} %dirs_ref.5, f32[44]{0:T(128)} %weight_ref.5, s32[44]{0:T(128)} %mask_ref.5, f32[1,32]{1,0:T(1,128)} %bitcast.45, ...), custom_call_target="tpu_custom_call" | custom-call | flops 4294967296 | bytes 8388608 | tf_op jit(solution)/shard_map/states/pallas_call | solution.py:252
  37.9 1.7 collective-permute-done
  40.7 2.9 %collective-permute-start.12 = (bf16[4,256,128]{2,1,0:T(8,128)(2,1)S(1)}, bf16[4,256,128]{2,1,0:T(8,128)(2,1)S(1)}, u32[]{:S(2)}, u32[]{:S(2)}) collective-permute-start(bf16[4,256,128]{2,1,0:T(8,128)(2,1)S(1)} %fusion.2.refs_0_), channel_id=1, source_target_pairs={{0,4},{2,6},{4,0},{6,2},{8,12},{10,14},{12,8},{14,10},{16,20},{18,... | collective-permute-start | bytes 786440 | tf_op jit(solution)/shard_map/ppermute | solution.py:277
  43.7 10.6 %states.5 = (bf16[2,4,192,128]{3,2,1,0:T(8,128)(2,1)}, bf16[2,4,192,128]{3,2,1,0:T(8,128)(2,1)}, bf16[384,2048]{1,0:T(8,128)(2,1)}, bf16[384,2048]{1,0:T(8,128)(2,1)}) custom-call(s32[1]{0:T(128)} %bitcast.index_ref, f32[3,44]{1,0:T(4,128)} %dirs_ref.5, f32[44]{0:T(128)} %weight_ref.5, s32[44]{0:T(128)} %mask_ref.5, f32[1,32]{1,0:T(1,128)} %bitcast.46, ...), custom_call_target="tpu_custom_call" | custom-call | flops 3221225472 | bytes 6291456 | tf_op jit(solution)/shard_map/states/pallas_call | solution.py:252
  54.4 30.7 %reduce-scatter.2.cloned.1.call-done.x_ref = bf16[256,128]{1,0:T(8,128)(2,1)} async-done(((bf16[4096,128]{1,0:T(8,128)(2,1)}), bf16[256,128]{1,0:T(8,128)(2,1)}) %reduce-scatter.2.cloned.1.call-update) | async-done | bytes 65552 | tf_op jit(solution)/shard_map/reduce_scatter | solution.py:364
  89.1 1.6 collective-permute-start.13
  90.7 2.3 %collective-permute-start.15 = (bf16[256,128]{1,0:T(8,128)(2,1)S(1)}, bf16[256,128]{1,0:T(8,128)(2,1)S(1)}, u32[]{:S(2)}, u32[]{:S(2)}) collective-permute-start(bf16[256,128]{1,0:T(8,128)(2,1)S(1)} %get-tuple-element.73), channel_id=1, source_target_pairs={{0,24},{2,26},{4,28},{6,30},{8,0},{10,2},{12,4},{14,6},{16,8},{18,... | collective-permute-start | bytes 196616 | tf_op jit(solution)/shard_map/ppermute | solution.py:277
  95.0 2.4 %collective-permute-start.5 = (bf16[192,128]{1,0:T(8,128)(2,1)S(1)}, bf16[192,128]{1,0:T(8,128)(2,1)S(1)}, u32[]{:S(2)}, u32[]{:S(2)}) collective-permute-start(bf16[192,128]{1,0:T(8,128)(2,1)S(1)} %get-tuple-element.76), channel_id=1, source_target_pairs={{0,24},{2,26},{4,28},{6,30},{8,0},{10,2},{12,4},{14,6},{16,8},{18,... | collective-permute-start | bytes 147464 | tf_op jit(solution)/shard_map/ppermute | solution.py:277
  98.1 5.2 %collective-permute-done.14 = bf16[256,128]{1,0:T(8,128)(2,1)S(1)} collective-permute-done((bf16[256,128]{1,0:T(8,128)(2,1)S(1)}, bf16[256,128]{1,0:T(8,128)(2,1)S(1)}, u32[]{:S(2)}, u32[]{:S(2)}) %collective-permute-start.14) | collective-permute-done | bytes 65568 | tf_op jit(solution)/shard_map/ppermute | solution.py:277
  103.6 3.7 %collective-permute-start.16 = (bf16[256,128]{1,0:T(8,128)(2,1)S(1)}, bf16[256,128]{1,0:T(8,128)(2,1)S(1)}, u32[]{:S(2)}, u32[]{:S(2)}) collective-permute-start(bf16[256,128]{1,0:T(8,128)(2,1)S(1)} %fusion.6), channel_id=1, source_target_pairs={{0,24},{2,26},{4,28},{6,30},{8,0},{10,2},{12,4},{14,6},{16,8},{18,... | collective-permute-start | bytes 196616 | tf_op jit(solution)/shard_map/ppermute | solution.py:277
  108.0 1.5 collective-permute-start.7
  109.8 2.5 %collective-permute-start.6 = (bf16[192,128]{1,0:T(8,128)(2,1)S(1)}, bf16[192,128]{1,0:T(8,128)(2,1)S(1)}, u32[]{:S(2)}, u32[]{:S(2)}) collective-permute-start(bf16[192,128]{1,0:T(8,128)(2,1)S(1)} %fusion.9), channel_id=1, source_target_pairs={{0,24},{2,26},{4,28},{6,30},{8,0},{10,2},{12,4},{14,6},{16,8},{18,... | collective-permute-start | bytes 147464 | tf_op jit(solution)/shard_map/ppermute | solution.py:277
  114.6 6.9 %collective-permute-done.19.refs_1_ = bf16[1024,128]{1,0:T(8,128)(2,1)S(1)} collective-permute-done((bf16[1024,128]{1,0:T(8,128)(2,1)S(1)}, bf16[1024,128]{1,0:T(8,128)(2,1)S(1)}, u32[]{:S(2)}, u32[]{:S(2)}) %collective-permute-start.19) | collective-permute-done | bytes 262176 | tf_op jit(solution)/shard_map/ppermute | solution.py:277
  122.0 1.6 collective-permute-done.9.refs_1_
  123.6 5.0 %all-gather.2.cloned.1.call-done.refs_0_ = bf16[4096,128]{1,0:T(8,128)(2,1)} async-done(((bf16[256,128]{1,0:T(8,128)(2,1)}), bf16[4096,128]{1,0:T(8,128)(2,1)}) %all-gather.2.cloned.1.call-update) | async-done | bytes 1048592 | tf_op jit(solution)/shard_map/all_gather | solution.py:374
  128.6 8.9 %mix.9 = (bf16[128,1024]{1,0:T(8,128)(2,1)}, bf16[128,1024]{1,0:T(8,128)(2,1)}, bf16[128,1024]{1,0:T(8,128)(2,1)}, bf16[128,1024]{1,0:T(8,128)(2,1)}) custom-call(s32[1]{0:T(128)} %bitcast.index_ref, s32[1]{0:T(128)} %bitcast.18.half_ref, bf16[4096,128]{1,0:T(8,128)(2,1)} %all-gather.2.cloned.1.call-done.refs_0_, ...), custom_call_target="tpu_custom_call" | custom-call | flops 2147483648 | bytes 4194304 | tf_op jit(solution)/shard_map/mix/pallas_call | solution.py:332
  138.3 9.4 %mix.10 = (bf16[128,1024]{1,0:T(8,128)(2,1)}, bf16[128,1024]{1,0:T(8,128)(2,1)}, bf16[128,1024]{1,0:T(8,128)(2,1)}, bf16[128,1024]{1,0:T(8,128)(2,1)}) custom-call(s32[1]{0:T(128)} %bitcast.index_ref, s32[1]{0:T(128)} %bitcast.18.half_ref, bf16[1024,128]{1,0:T(8,128)(2,1)} %copy-done, bf16[1024,128]{1,0:T(8,128)(2,1)} %copy-done.2, ...), custom_call_target="tpu_custom_call" | custom-call | flops 2147483648 | bytes 4194304 | tf_op jit(solution)/shard_map/mix/pallas_call | solution.py:332
  148.5 8.1 %mix.11 = bf16[1024,512]{1,0:T(8,128)(2,1)} custom-call(s32[1]{0:T(128)} %bitcast.index_ref, s32[1]{0:T(128)} %bitcast.18.half_ref, bf16[768,128]{1,0:T(8,128)(2,1)} %copy-done.1, bf16[768,128]{1,0:T(8,128)(2,1)} %copy-done.5, bf16[768,128]{1,0:T(8,128)(2,1)} %copy-done.6, bf16[768,128]{1,0:T(8,128)(2,1)} %copy-done.7, ...), custom_call_target="tpu_custom_call" | custom-call | flops 1610612736 | bytes 3145728 | tf_op jit(solution)/shard_map/mix/pallas_call | solution.py:332
  158.2 8.9 %mix.6 = (bf16[128,1024]{1,0:T(8,128)(2,1)}, bf16[128,1024]{1,0:T(8,128)(2,1)}, bf16[128,1024]{1,0:T(8,128)(2,1)}, bf16[128,1024]{1,0:T(8,128)(2,1)}) custom-call(s32[1]{0:T(128)} %bitcast.index_ref, s32[1]{0:T(128)} %bitcast.1.half_ref, bf16[4096,128]{1,0:T(8,128)(2,1)} %all-gather.2.cloned.1.call-done.refs_0_, ...), custom_call_target="tpu_custom_call" | custom-call | flops 2147483648 | bytes 4194304 | tf_op jit(solution)/shard_map/mix/pallas_call | solution.py:332
  167.1 9.4 %mix.7 = (bf16[128,1024]{1,0:T(8,128)(2,1)}, bf16[128,1024]{1,0:T(8,128)(2,1)}, bf16[128,1024]{1,0:T(8,128)(2,1)}, bf16[128,1024]{1,0:T(8,128)(2,1)}) custom-call(s32[1]{0:T(128)} %bitcast.index_ref, s32[1]{0:T(128)} %bitcast.1.half_ref, bf16[1024,128]{1,0:T(8,128)(2,1)} %copy-done, bf16[1024,128]{1,0:T(8,128)(2,1)} %copy-done.2, ...), custom_call_target="tpu_custom_call" | custom-call | flops 2147483648 | bytes 4194304 | tf_op jit(solution)/shard_map/mix/pallas_call | solution.py:332
  176.6 9.0 %mix.8 = f32[1024,512]{1,0:T(8,128)} custom-call(s32[1]{0:T(128)} %bitcast.index_ref, s32[1]{0:T(128)} %bitcast.1.half_ref, bf16[768,128]{1,0:T(8,128)(2,1)} %copy-done.1, bf16[768,128]{1,0:T(8,128)(2,1)} %copy-done.5, bf16[768,128]{1,0:T(8,128)(2,1)} %copy-done.6, bf16[768,128]{1,0:T(8,128)(2,1)} %copy-done.7, ...), custom_call_target="tpu_custom_call" | custom-call | flops 1610612736 | bytes 3145728 | tf_op jit(solution)/shard_map/mix/pallas_call | solution.py:332
  185.6 1.9 add_convert_fusion
  (73 shorter events, 16.5 us)
Async XLA Ops:
  7.2 77.9 %reduce-scatter.2.cloned.1.call-start = ((), (), s32[]{:S(2)}) async-start(), calls=%async_computation.1 | async-start | bytes 1114112 | tf_op jit(solution)/shard_map/reduce_scatter | solution.py:364
  24.3 104.3 %all-gather.2.cloned.1.call-start = ((), (), s32[]{:S(2)}) async-start(), calls=%async_computation.2 | async-start | bytes 1114112 | tf_op jit(solution)/shard_map/all_gather | solution.py:374
  40.7 45.8 %collective-permute-start.12 = (bf16[4,256,128]{2,1,0:T(8,128)(2,1)S(1)}, bf16[4,256,128]{2,1,0:T(8,128)(2,1)S(1)}, u32[]{:S(2)}, u32[]{:S(2)}) collective-permute-start(bf16[4,256,128]{2,1,0:T(8,128)(2,1)S(1)} %fusion.2.refs_0_), channel_id=1, source_target_pairs={{0,4},{2,6},{4,0},{6,2},{8,12},{10,14},{12,8},{14,10},{16,20},{18,... | collective-permute-start | bytes 786440 | tf_op jit(solution)/shard_map/ppermute | solution.py:277
  54.3 32.4 %collective-permute-start.1 = (bf16[2,4,192,128]{3,2,1,0:T(8,128)(2,1)}, bf16[2,4,192,128]{3,2,1,0:T(8,128)(2,1)S(1)}, u32[]{:S(2)}, u32[]{:S(2)}) collective-permute-start(bf16[2,4,192,128]{3,2,1,0:T(8,128)(2,1)} %get-tuple-element.42.refs_0_), channel_id=1, source_target_pairs={{0,2},{2,0},{4,6},{6,4},{8,10},{10,8},{12,14},{14,12},{16,18},{18,... | collective-permute-start | bytes 1179656 | tf_op jit(solution)/shard_map/ppermute | solution.py:277
  87.7 5.7 %collective-permute-start.2 = (bf16[4,192,128]{2,1,0:T(8,128)(2,1)S(1)}, bf16[4,192,128]{2,1,0:T(8,128)(2,1)S(1)}, u32[]{:S(2)}, u32[]{:S(2)}) collective-permute-start(bf16[4,192,128]{2,1,0:T(8,128)(2,1)S(1)} %fusion.3), channel_id=1, source_target_pairs={{0,4},{2,6},{4,0},{6,2},{8,12},{10,14},{12,8},{14,10},{16,20},{18,... | collective-permute-start | bytes 589832 | tf_op jit(solution)/shard_map/ppermute | solution.py:277
  89.1 8.3 %collective-permute-start.13 = (bf16[256,128]{1,0:T(8,128)(2,1)S(1)}, bf16[256,128]{1,0:T(8,128)(2,1)S(1)}, u32[]{:S(2)}, u32[]{:S(2)}) collective-permute-start(bf16[256,128]{1,0:T(8,128)(2,1)S(1)} %get-tuple-element.72), channel_id=1, source_target_pairs={{0,8},{2,10},{4,12},{6,14},{8,16},{10,18},{12,20},{14,22},{16,24},... | collective-permute-start | bytes 196616 | tf_op jit(solution)/shard_map/ppermute | solution.py:277
  90.7 7.5 %collective-permute-start.15 = (bf16[256,128]{1,0:T(8,128)(2,1)S(1)}, bf16[256,128]{1,0:T(8,128)(2,1)S(1)}, u32[]{:S(2)}, u32[]{:S(2)}) collective-permute-start(bf16[256,128]{1,0:T(8,128)(2,1)S(1)} %get-tuple-element.73), channel_id=1, source_target_pairs={{0,24},{2,26},{4,28},{6,30},{8,0},{10,2},{12,4},{14,6},{16,8},{18,... | collective-permute-start | bytes 196616 | tf_op jit(solution)/shard_map/ppermute | solution.py:277
  93.0 10.4 %collective-permute-start.14 = (bf16[256,128]{1,0:T(8,128)(2,1)S(1)}, bf16[256,128]{1,0:T(8,128)(2,1)S(1)}, u32[]{:S(2)}, u32[]{:S(2)}) collective-permute-start(bf16[256,128]{1,0:T(8,128)(2,1)S(1)} %get-tuple-element.74), channel_id=1, source_target_pairs={{0,16},{2,18},{4,20},{6,22},{8,24},{10,26},{12,28},{14,30},{16,0},... | collective-permute-start | bytes 196616 | tf_op jit(solution)/shard_map/ppermute | solution.py:277
  93.5 10.1 %collective-permute-start.3 = (bf16[192,128]{1,0:T(8,128)(2,1)S(1)}, bf16[192,128]{1,0:T(8,128)(2,1)S(1)}, u32[]{:S(2)}, u32[]{:S(2)}) collective-permute-start(bf16[192,128]{1,0:T(8,128)(2,1)S(1)} %get-tuple-element.75), channel_id=1, source_target_pairs={{0,8},{2,10},{4,12},{6,14},{8,16},{10,18},{12,20},{14,22},{16,24},... | collective-permute-start | bytes 147464 | tf_op jit(solution)/shard_map/ppermute | solution.py:277
  95.0 12.3 %collective-permute-start.5 = (bf16[192,128]{1,0:T(8,128)(2,1)S(1)}, bf16[192,128]{1,0:T(8,128)(2,1)S(1)}, u32[]{:S(2)}, u32[]{:S(2)}) collective-permute-start(bf16[192,128]{1,0:T(8,128)(2,1)S(1)} %get-tuple-element.76), channel_id=1, source_target_pairs={{0,24},{2,26},{4,28},{6,30},{8,0},{10,2},{12,4},{14,6},{16,8},{18,... | collective-permute-start | bytes 147464 | tf_op jit(solution)/shard_map/ppermute | solution.py:277
  97.4 9.9 %collective-permute-start.4 = (bf16[192,128]{1,0:T(8,128)(2,1)S(1)}, bf16[192,128]{1,0:T(8,128)(2,1)S(1)}, u32[]{:S(2)}, u32[]{:S(2)}) collective-permute-start(bf16[192,128]{1,0:T(8,128)(2,1)S(1)} %get-tuple-element.77), channel_id=1, source_target_pairs={{0,16},{2,18},{4,20},{6,22},{8,24},{10,26},{12,28},{14,30},{16,0},... | collective-permute-start | bytes 147464 | tf_op jit(solution)/shard_map/ppermute | solution.py:277
  103.4 6.4 %collective-permute-start.18 = (bf16[256,128]{1,0:T(8,128)(2,1)S(1)}, bf16[256,128]{1,0:T(8,128)(2,1)S(1)}, u32[]{:S(2)}, u32[]{:S(2)}) collective-permute-start(bf16[256,128]{1,0:T(8,128)(2,1)S(1)} %fusion.6), channel_id=1, source_target_pairs={{0,8},{2,10},{4,12},{6,14},{8,16},{10,18},{12,20},{14,22},{16,24},... | collective-permute-start | bytes 196616 | tf_op jit(solution)/shard_map/ppermute | solution.py:277
  103.5 8.9 %collective-permute-start.17 = (bf16[256,128]{1,0:T(8,128)(2,1)S(1)}, bf16[256,128]{1,0:T(8,128)(2,1)S(1)}, u32[]{:S(2)}, u32[]{:S(2)}) collective-permute-start(bf16[256,128]{1,0:T(8,128)(2,1)S(1)} %fusion.6), channel_id=1, source_target_pairs={{0,16},{2,18},{4,20},{6,22},{8,24},{10,26},{12,28},{14,30},{16,0},... | collective-permute-start | bytes 196616 | tf_op jit(solution)/shard_map/ppermute | solution.py:277
  103.6 8.8 %collective-permute-start.16 = (bf16[256,128]{1,0:T(8,128)(2,1)S(1)}, bf16[256,128]{1,0:T(8,128)(2,1)S(1)}, u32[]{:S(2)}, u32[]{:S(2)}) collective-permute-start(bf16[256,128]{1,0:T(8,128)(2,1)S(1)} %fusion.6), channel_id=1, source_target_pairs={{0,24},{2,26},{4,28},{6,30},{8,0},{10,2},{12,4},{14,6},{16,8},{18,... | collective-permute-start | bytes 196616 | tf_op jit(solution)/shard_map/ppermute | solution.py:277
  107.3 6.0 %collective-permute-start.8 = (bf16[192,128]{1,0:T(8,128)(2,1)S(1)}, bf16[192,128]{1,0:T(8,128)(2,1)S(1)}, u32[]{:S(2)}, u32[]{:S(2)}) collective-permute-start(bf16[192,128]{1,0:T(8,128)(2,1)S(1)} %fusion.9), channel_id=1, source_target_pairs={{0,8},{2,10},{4,12},{6,14},{8,16},{10,18},{12,20},{14,22},{16,24},... | collective-permute-start | bytes 147464 | tf_op jit(solution)/shard_map/ppermute | solution.py:277
  108.0 5.5 %collective-permute-start.7 = (bf16[192,128]{1,0:T(8,128)(2,1)S(1)}, bf16[192,128]{1,0:T(8,128)(2,1)S(1)}, u32[]{:S(2)}, u32[]{:S(2)}) collective-permute-start(bf16[192,128]{1,0:T(8,128)(2,1)S(1)} %fusion.9), channel_id=1, source_target_pairs={{0,16},{2,18},{4,20},{6,22},{8,24},{10,26},{12,28},{14,30},{16,0},... | collective-permute-start | bytes 147464 | tf_op jit(solution)/shard_map/ppermute | solution.py:277
  109.8 4.7 %collective-permute-start.6 = (bf16[192,128]{1,0:T(8,128)(2,1)S(1)}, bf16[192,128]{1,0:T(8,128)(2,1)S(1)}, u32[]{:S(2)}, u32[]{:S(2)}) collective-permute-start(bf16[192,128]{1,0:T(8,128)(2,1)S(1)} %fusion.9), channel_id=1, source_target_pairs={{0,24},{2,26},{4,28},{6,30},{8,0},{10,2},{12,4},{14,6},{16,8},{18,... | collective-permute-start | bytes 147464 | tf_op jit(solution)/shard_map/ppermute | solution.py:277
  112.4 9.1 %collective-permute-start.19 = (bf16[1024,128]{1,0:T(8,128)(2,1)S(1)}, bf16[1024,128]{1,0:T(8,128)(2,1)S(1)}, u32[]{:S(2)}, u32[]{:S(2)}) collective-permute-start(bf16[1024,128]{1,0:T(8,128)(2,1)S(1)} %pad_maximum_fusion.refs_0_), channel_id=1, source_target_pairs={{0,4},{2,6},{4,0},{6,2},{8,12},{10,14},{12,8},{14,10},{16,20},{18,... | collective-permute-start | bytes 786440 | tf_op jit(solution)/shard_map/ppermute | solution.py:277
  114.5 9.1 %collective-permute-start.9 = (bf16[768,128]{1,0:T(8,128)(2,1)S(1)}, bf16[768,128]{1,0:T(8,128)(2,1)S(1)}, u32[]{:S(2)}, u32[]{:S(2)}) collective-permute-start(bf16[768,128]{1,0:T(8,128)(2,1)S(1)} %pad_maximum_fusion.1.refs_0_), channel_id=1, source_target_pairs={{0,4},{2,6},{4,0},{6,2},{8,12},{10,14},{12,8},{14,10},{16,20},{18,... | collective-permute-start | bytes 589832 | tf_op jit(solution)/shard_map/ppermute | solution.py:277
  114.6 22.9 %collective-permute-start.20 = (bf16[1024,128]{1,0:T(8,128)(2,1)S(1)}, bf16[1024,128]{1,0:T(8,128)(2,1)S(1)}, u32[]{:S(2)}, u32[]{:S(2)}) collective-permute-start(bf16[1024,128]{1,0:T(8,128)(2,1)S(1)} %pad_maximum_fusion.refs_0_), channel_id=1, source_target_pairs={{0,2},{2,0},{4,6},{6,4},{8,10},{10,8},{12,14},{14,12},{16,18},{18,... | collective-permute-start | bytes 786440 | tf_op jit(solution)/shard_map/ppermute | solution.py:277
  121.5 16.0 %collective-permute-start.21 = (bf16[1024,128]{1,0:T(8,128)(2,1)S(1)}, bf16[1024,128]{1,0:T(8,128)(2,1)S(1)}, u32[]{:S(2)}, u32[]{:S(2)}) collective-permute-start(bf16[1024,128]{1,0:T(8,128)(2,1)S(1)} %collective-permute-done.19.refs_1_), channel_id=1, source_target_pairs={{0,2},{2,0},{4,6},{6,4},{8,10},{10,8},{12,14},{14,12},{16,18},{18,... | collective-permute-start | bytes 786440 | tf_op jit(solution)/shard_map/ppermute | solution.py:277
  121.5 26.3 %collective-permute-start.10 = (bf16[768,128]{1,0:T(8,128)(2,1)S(1)}, bf16[768,128]{1,0:T(8,128)(2,1)S(1)}, u32[]{:S(2)}, u32[]{:S(2)}) collective-permute-start(bf16[768,128]{1,0:T(8,128)(2,1)S(1)} %pad_maximum_fusion.1.refs_0_), channel_id=1, source_target_pairs={{0,2},{2,0},{4,6},{6,4},{8,10},{10,8},{12,14},{14,12},{16,18},{18,... | collective-permute-start | bytes 589832 | tf_op jit(solution)/shard_map/ppermute | solution.py:277
  123.6 24.2 %collective-permute-start.11 = (bf16[768,128]{1,0:T(8,128)(2,1)S(1)}, bf16[768,128]{1,0:T(8,128)(2,1)S(1)}, u32[]{:S(2)}, u32[]{:S(2)}) collective-permute-start(bf16[768,128]{1,0:T(8,128)(2,1)S(1)} %collective-permute-done.9.refs_1_), channel_id=1, source_target_pairs={{0,2},{2,0},{4,6},{6,4},{8,10},{10,8},{12,14},{14,12},{16,18},{18,... | collective-permute-start | bytes 589832 | tf_op jit(solution)/shard_map/ppermute | solution.py:277
  156.7 28.9 %collective-permute-start.22 = (bf16[1024,512]{1,0:T(8,128)(2,1)}, bf16[1024,512]{1,0:T(8,128)(2,1)S(1)}, u32[]{:S(2)}, u32[]{:S(2)}) collective-permute-start(bf16[1024,512]{1,0:T(8,128)(2,1)} %mix.11), channel_id=1, source_target_pairs={{0,1},{1,0},{2,3},{3,2},{4,5},{5,4},{6,7},{7,6},{8,9},{9,8},{10,11... | collective-permute-start | bytes 3145736 | tf_op jit(solution)/shard_map/ppermute | solution.py:386
  (12 other events, 171.0 us)
Sparse Core Ops, SparseCore 0:
  24.4 60.5 reduce-scatter.1
  88.0 40.5 all-gather.1

commit v5 on v3

--- a/solution.py
+++ b/solution.py
@@ -16,7 +16,9 @@
 QUARTER = LANES // QUADS
 WIDTH = GROUP * LANES
 VMEM_LIMIT = 30 * 2**20
-CHUNKS = (4, 4, 3)
+EARLY = 6
+PIECES = (1, 2, 2)
+MIX_PIECES = (3, 3)
 
 SIN_COEF = (4.4428679, -7.30744342, 3.59478808, -0.78437403)
 COS_COEF = (1.41420408, -6.97764206, 5.71523839, -1.72834866)
@@ -46,18 +48,37 @@
 
 
 def prepare_kernel(
-    index_ref, domain_ref, species_ref, gain_ref, q_ref, k_ref, v_ref, g_ref,
-    qt_ref, kt_ref, vt_ref, gt_ref, gain_out,
+    index_ref, domain_in, species_in, gain_in, q_in, k_in, v_in, g_in,
+    qt_ref, kt_ref, kt_half, vt_ref, gt_ref, gain_out, v_ref, g_ref,
+    domain_ref, species_ref, gain_ref, q_ref, k_ref, sems,
 ):
+    copies = [
+        pltpu.make_async_copy(source, target, sems.at[at])
+        for at, (source, target) in enumerate(
+            (
+                (domain_in, domain_ref), (species_in, species_ref), (gain_in, gain_ref),
+                (k_in, k_ref), (q_in, q_ref), (v_in, v_ref), (g_in, g_ref),
+            )
+        )
+    ]
+    for copy in copies:
+        copy.start()
+    for copy in copies[:4]:
+        copy.wait()
     alive = (domain_ref[...] == index_ref[0]).astype(F32)
     species = species_ref[...]
     gain = jnp.zeros(gain_out.shape, F32)
     for s in range(gain_ref.shape[0]):
         gain = jnp.where(species == s, column(gain_ref[s : s + 1, :]), gain)
     gain_out[...] = gain
-    kt_ref[...] = k_ref[...].astype(F32).T * gain * alive
+    gained = k_ref[...].astype(F32).T * gain * alive
+    kt_ref[...] = gained
+    kt_half[...] = gained.astype(BF16)
+    copies[4].wait()
     qt_ref[...] = (q_ref[...].astype(F32).T * alive).astype(BF16)
+    copies[5].wait()
     vt_ref[...] = (v_ref[...].astype(F32).T * alive).astype(BF16)
+    copies[6].wait()
     gt_ref[...] = (g_ref[...].astype(F32).T * alive).astype(BF16)
 
 
@@ -118,7 +139,7 @@
 
 
 def mix_kernel(
-    has_totals, final, part, index_ref, half_ref, *refs,
+    first, has_totals, final, part, index_ref, half_ref, *refs,
 ):
     del half_ref
     refs = list(refs)
@@ -130,21 +151,21 @@
     if has_totals:
         before, refs = refs[:4], refs[4:]
     out_count = 1 if final else 4
-    outs, refs = refs[:out_count], refs[out_count:]
-    slots, states, states_t = refs[:3]
-    totals = refs[3:7]
-    group = pl.program_id(1)
-    groups = pl.num_programs(1)
+    outs, refs = refs[-7 - out_count : -7], refs[-7:]
+    states, states_t, slots = refs[:3]
+    totals = refs[3:]
+    group = pl.program_id(0)
+    groups = pl.num_programs(0)
     core, pair, quad = place_of(index_ref[0])
 
-    @pl.when((group == 0) & (pl.program_id(0) == 0))
+    @pl.when(group == 0)
     def _():
         for at, source in enumerate(sources):
             slots[at // 2, at % 2] = source[...].reshape(slots.shape[2:])
-        for g in range(slots.shape[3] // (2 * QUARTER)):
+        for g in range(states.shape[1]):
             for kind in range(2):
                 for i in range(GROUP):
-                    start = g * 2 * QUARTER + i % 2 * QUARTER
+                    start = (first + g) * 2 * QUARTER + i % 2 * QUARTER
                     for m in range(QUADS):
                         row = i * LANES + m * QUARTER
                         states[kind, g, row : row + QUARTER, :] = slots[
@@ -166,7 +187,7 @@
         cosine = cos_ref[:, cols]
         sine = sin_ref[:, cols]
         for kind, x_ref, direct in ((0, qt_ref, totals[0]), (1, kt_ref, totals[3])):
-            turned = rotated(x_ref[:, cols].astype(BF16), cosine, sine)
+            turned = rotated(x_ref[:, cols], cosine, sine)
             direct[:, cols] += jnp.dot(states_t[kind, group], turned, preferred_element_type=F32)
         cosine = cosine.astype(F32)
         sine = sine.astype(F32)
@@ -198,8 +219,17 @@
                 outs[at][...] = total[...].astype(outs[at].dtype)
 
 
-def added(*terms):
-    return sum(term.astype(F32) for term in terms).astype(BF16)
+def add_kernel(picks, count, *refs):
+    total = sum(
+        (ref[...] if at is None else ref[at]).astype(F32) for at, ref in zip(picks, refs)
+    )
+    refs[-1][...] = total.astype(BF16)
+
+
+def join_kernel(count, *refs):
+    size = refs[0].shape[0]
+    for at in range(count):
+        refs[-1][at * size : (at + 1) * size, :] = refs[at][...]
 
 
 def per_device(
@@ -207,38 +237,57 @@
     frequency, directions, dir_weight, dir_mask,
 ):
     atoms, feats = queries.shape
+    total_groups = dir_weight.shape[0] // GROUP
+    late = total_groups - EARLY
+    half_atoms = atoms // 2
     index = lax.axis_index("atoms")[None].astype(jnp.int32)
     mine = lax.axis_index("dirs").astype(jnp.int32)
     vmem = pl.BlockSpec(memory_space=pltpu.VMEM)
     smem = pl.BlockSpec(memory_space=pltpu.SMEM)
+    hbm = pl.BlockSpec(memory_space=pltpu.HBM)
+    anywhere = pl.BlockSpec(memory_space=pl.ANY)
     params = pltpu.CompilerParams(vmem_limit_bytes=VMEM_LIMIT)
     shape = jax.ShapeDtypeStruct
 
-    qt, kt, vt, gt, gain = pl.pallas_call(
+    qt, kt, kt_half, vt, gt, gain, v_near, g_near = pl.pallas_call(
         prepare_kernel,
-        in_specs=[smem] + [vmem] * 7,
-        out_specs=[vmem] * 5,
+        in_specs=[smem] + [hbm] * 7,
+        out_specs=[vmem] * 8,
         out_shape=[
             shape((feats, atoms), BF16), shape((feats, atoms), F32), shape((feats, atoms), BF16),
-            shape((feats, atoms), BF16), shape((feats, atoms), F32),
+            shape((feats, atoms), BF16), shape((feats, atoms), BF16), shape((feats, atoms), F32),
+            shape((atoms, feats), BF16), shape((atoms, feats), BF16),
+        ],
+        scratch_shapes=[
+            pltpu.VMEM((1, atoms), jnp.int32),
+            pltpu.VMEM((1, atoms), jnp.int32),
+            pltpu.VMEM(species_gain.shape, F32),
+            pltpu.VMEM((atoms, feats), BF16),
+            pltpu.VMEM((atoms, feats), BF16),
+            pltpu.SemaphoreType.DMA((7,)),
         ],
         compiler_params=params,
         name="prepare",
     )(index, domain[None, :], species[None, :], species_gain, queries, keys, values, cotangent)
 
-    part = min(256, atoms)
-
-    def make_states(first, groups, after):
-        sent = (2, QUADS, groups * 2 * QUARTER, feats)
-        sent_spec = pl.BlockSpec((2, QUADS, 2 * QUARTER, feats), lambda g: (0, 0, g, 0))
-        phase_spec = pl.BlockSpec((GROUP * QUARTER, atoms), lambda g: (g, 0))
+    def make_states(first, groups, offset, size, after=(), into=()):
+        sent = shape((2, QUADS, size * 2 * QUARTER, feats), BF16)
+        sent_spec = pl.BlockSpec(
+            (2, QUADS, 2 * QUARTER, feats), lambda g: (0, 0, g + offset, 0)
+        )
+        phase = pltpu.HBM((size * GROUP * QUARTER, atoms), BF16)
+        phase_spec = pl.BlockSpec((GROUP * QUARTER, atoms), lambda g: (g + offset, 0))
+        operands = [
+            index, directions, dir_weight, dir_mask, frequency[None, :], positions, qt, kt,
+            v_near, g_near, *after,
+        ]
         return pl.pallas_call(
-            functools.partial(states_kernel, first, part, 1.0 / math.sqrt(feats * atoms)),
+            functools.partial(states_kernel, first, min(256, atoms), 1.0 / math.sqrt(feats * atoms)),
             grid=(groups,),
-            in_specs=[smem] * 4 + [vmem] * 6 + [pl.BlockSpec(memory_space=pl.ANY)] * len(after),
+            in_specs=[smem] * 4 + [vmem] * 6 + [anywhere] * (len(after) + len(into)),
             out_specs=[sent_spec] * 2 + [phase_spec] * 2,
-            out_shape=[shape(sent, BF16)] * 2
-            + [shape((groups * GROUP * QUARTER, atoms), BF16)] * 2,
+            out_shape=[sent] * 2 + [phase] * 2,
+            input_output_aliases={len(operands) + at: at for at in range(len(into))},
             scratch_shapes=[
                 pltpu.VMEM((WIDTH, atoms), BF16),
                 pltpu.VMEM((WIDTH, atoms), BF16),
@@ -250,10 +299,7 @@
                 bytes_accessed=2 * groups * WIDTH * atoms, transcendentals=0,
             ),
             name="states",
-        )(
-            index, directions, dir_weight, dir_mask, frequency[None, :], positions, qt, kt,
-            values, cotangent, *after,
-        )
+        )(*operands, *into)
 
     def moved(x, target):
         return lax.ppermute(x, "atoms", [(i, target(i)) for i in range(atom_devices)])
@@ -267,85 +313,120 @@
     def by_quad(x, step):
         return moved(x, lambda i: (i & ~12) | ((((i >> 2) + step) & 3) << 2))
 
-    def crossing(kept, sent):
-        arrived = by_core(sent)
-        return arrived, added(kept[1], arrived[1])
-
-    def summed(kept, arrived, crossing_out):
-        half = added(kept[0], arrived[0], by_pair(crossing_out))
-        quarter = added(half[0], *(by_quad(half[step], step) for step in range(1, QUADS)))
-        whole = quarter
+    def added(terms, after=()):
+        first, at = terms[0]
+        out = first.shape if at is None else first.shape[1:]
+        return pl.pallas_call(
+            functools.partial(add_kernel, [pick for _, pick in terms], len(terms)),
+            in_specs=[vmem] * len(terms) + [anywhere] * len(after),
+            out_specs=vmem,
+            out_shape=shape(out, BF16),
+            name="add",
+        )(*(x for x, _ in terms), *after)
+
+    def joined(parts, after=()):
+        return pl.pallas_call(
+            functools.partial(join_kernel, len(parts)),
+            in_specs=[vmem] * len(parts) + [anywhere] * len(after),
+            out_specs=vmem,
+            out_shape=shape((len(parts) * parts[0].shape[0], feats), BF16),
+            name="join",
+        )(*parts, *after)
+
+    def quarters(half):
+        return [(half, 0)] + [(by_quad(half[step], step), None) for step in range(1, QUADS)]
+
+    def whole_of(quarter):
+        terms = [(quarter, None)]
         for step in range(16, atom_devices, 16):
-            whole = added(whole, moved(quarter, lambda i: (i + step) % atom_devices))
-        gathered = [whole] + [by_quad(whole, QUADS - step) for step in range(1, QUADS)]
-        half = jnp.concatenate(gathered, axis=0)
+            terms.append((moved(quarter, lambda i: (i + step) % atom_devices), None))
+        return added(terms) if len(terms) > 1 else quarter
+
+    def spread(whole):
+        return [whole] + [by_quad(whole, QUADS - step) for step in range(1, QUADS)]
+
+    def shared(half):
         other = by_pair(half)
         return half, other, by_core(half), by_core(other)
 
-    half_atoms = atoms // 2
-
-    def mix(half, pieces, groups, phases, totals, final, dtype):
-        blocks = 1 if final else 2
-        mix_part = min(256, half_atoms)
-        rows_all = pl.BlockSpec((feats, half_atoms), lambda n, g, index, half: (0, half[0] + n))
+    def mix(half, pieces, first, groups, phases, totals, final, dtype, after=()):
+        rows_half = pl.BlockSpec((feats, half_atoms), lambda g, index, half: (0, half[0]))
         phase_spec = pl.BlockSpec(
-            (GROUP * QUARTER, half_atoms), lambda n, g, index, half: (g, half[0] + n)
+            (GROUP * QUARTER, half_atoms), lambda g, index, half: (g + first, half[0])
         )
-        operands = [*pieces, vt, gt, kt, qt, *phases]
-        specs = [vmem] * 4 + [rows_all] * 4 + [phase_spec] * 2
+        totals_spec = pl.BlockSpec((feats, half_atoms), lambda g, index, half: (0, 0))
+        operands = [*pieces, vt, gt, kt_half, qt, *phases]
+        specs = [vmem] * 4 + [rows_half] * 4 + [phase_spec] * 2
         if final:
             operands.append(gain)
-            specs.append(rows_all)
+            specs.append(rows_half)
         if totals is not None:
             operands += totals
-            specs += [rows_all] * 4
-        scratch = [
-            pltpu.VMEM((2, 2, QUADS, groups * 2 * QUARTER, feats), BF16),
-            pltpu.VMEM((2, groups, WIDTH, feats), BF16),
-            pltpu.VMEM((2, groups, feats, WIDTH), BF16),
-        ] + [pltpu.VMEM((feats, half_atoms), F32)] * 4
+            specs += [totals_spec] * 4
+        slot_rows = pieces[0].shape[0] // QUADS
         if final:
-            out_specs = pl.BlockSpec(
-                (half_atoms, 4 * feats), lambda n, g, index, half: (0, 0)
-            )
+            out_specs = pl.BlockSpec((half_atoms, 4 * feats), lambda g, index, half: (0, 0))
             out_shape = shape((half_atoms, 4 * feats), dtype)
         else:
-            out_specs = [rows_all] * 4
-            out_shape = [shape((feats, atoms), dtype)] * 4
+            out_specs = [totals_spec] * 4
+            out_shape = [shape((feats, half_atoms), BF16)] * 4
         return pl.pallas_call(
-            functools.partial(mix_kernel, totals is not None, final, mix_part),
+            functools.partial(
+                mix_kernel, first, totals is not None, final, min(256, half_atoms)
+            ),
             grid_spec=pltpu.PrefetchScalarGridSpec(
                 num_scalar_prefetch=2,
-                grid=(blocks, groups),
-                in_specs=specs,
+                grid=(groups,),
+                in_specs=specs + [anywhere] * len(after),
                 out_specs=out_specs,
-                scratch_shapes=scratch,
+                scratch_shapes=[
+                    pltpu.VMEM((2, groups, WIDTH, feats), BF16),
+                    pltpu.VMEM((2, groups, feats, WIDTH), BF16),
+                    pltpu.VMEM((2, 2, QUADS, slot_rows, feats), BF16),
+                ]
+                + [pltpu.VMEM((feats, half_atoms), F32)] * 4,
             ),
             out_shape=out_shape,
             compiler_params=params,
             cost_estimate=pl.CostEstimate(
-                flops=8 * groups * WIDTH * blocks * half_atoms * feats,
-                bytes_accessed=2 * groups * WIDTH * blocks * half_atoms, transcendentals=0,
+                flops=8 * groups * WIDTH * half_atoms * feats,
+                bytes_accessed=2 * groups * WIDTH * half_atoms, transcendentals=0,
             ),
             name="mix",
-        )(index, half[None], *operands)
-
-    made = []
-    first = 0
-    for groups in CHUNKS:
-        after = [made[-2][2]] if len(made) > 1 else []
-        kept, sent, *phases = make_states(first, groups, after)
-        made.append((kept, *crossing(kept, sent), phases, groups))
-        first += groups
-    totals = None
-    for kept, arrived, crossing_out, phases, groups in made[:-1]:
-        pieces = summed(kept, arrived, crossing_out)
-        totals = mix(jnp.int32(0), pieces, groups, phases, totals, False, BF16)
-    kept, arrived, crossing_out, phases, groups = made[-1]
-    pieces = summed(kept, arrived, crossing_out)
-    away = mix(1 - mine, pieces, groups, phases, totals, True, BF16)
-    theirs = lax.ppermute(away, "dirs", [(0, 1), (1, 0)])
-    ours = mix(mine, pieces, groups, phases, totals, True, F32)
+        )(index, half[None], *operands, *after)
+
+    kept0, sent0, *phases0 = make_states(0, EARLY, 0, EARLY)
+    arrived0 = by_core(sent0)
+    made = make_states(EARLY, PIECES[0], 0, late, [sent0])
+    cross0 = added([(kept0, 1), (arrived0, 1)], [made[0]])
+    crossed0 = by_pair(cross0)
+    made = make_states(EARLY + PIECES[0], PIECES[1], PIECES[0], late, [cross0], made)
+    half0 = added([(kept0, 0), (arrived0, 0), (crossed0, None)], [made[0]])
+    quarters0 = quarters(half0)
+    done = PIECES[0] + PIECES[1]
+    kept1, sent1, *phases1 = make_states(
+        EARLY + done, late - done, done, late, [half0], made
+    )
+    arrived1 = by_core(sent1)
+    whole0 = whole_of(added(quarters0, [sent1]))
+    spread0 = spread(whole0)
+    cross1 = added([(kept1, 1), (arrived1, 1)], [whole0])
+    crossed1 = by_pair(cross1)
+    pieces0 = shared(joined(spread0, [cross1]))
+    half1 = added([(kept1, 0), (arrived1, 0), (crossed1, None)], [pieces0[0]])
+    whole1 = whole_of(added(quarters(half1)))
+    spread1 = spread(whole1)
+    away = 1 - mine
+    totals = mix(away, pieces0, 0, MIX_PIECES[0], phases0, None, False, BF16, [whole1])
+    pieces1 = shared(joined(spread1, [totals[0]]))
+    totals = mix(
+        away, pieces0, MIX_PIECES[0], EARLY - MIX_PIECES[0], phases0, totals, False, BF16,
+        [pieces1[0]],
+    )
+    sent = mix(away, pieces1, 0, late, phases1, totals, True, BF16)
+    theirs = lax.ppermute(sent, "dirs", [(0, 1), (1, 0)])
+    totals = mix(mine, pieces0, 0, EARLY, phases0, None, False, BF16, [sent])
+    ours = mix(mine, pieces1, 0, late, phases1, totals, True, F32)
     total = (ours + theirs.astype(F32)).astype(BF16)
     return tuple(total[:, at * feats : (at + 1) * feats] for at in range(4))
 

time: 170 us -> 204 us (1.20)
  local copies, waits for them, and re-layouts: 20.2 us -> 40.3 us
  Pallas kernels: 72.6 us -> 92.4 us
  starting transfers between devices: 37.2 us -> 23.9 us
  waiting for transfers between devices: 35.5 us -> 44.5 us
  other arithmetic: 2.49 us -> 0.35 us
    ppermute x33 -> x22, waiting for transfers between devices: 17.1 us -> 40.2 us  [moved(): lax.ppermute(x, 'atoms', [(i, target(i)) for i in range(atom_devices)])]
    pallas_call x8 -> x18, Pallas kernels: 72.6 us -> 92.4 us  [the longest x5 40.6 us: mix(): pl.pallas_call(functools.partial(mix_kernel, first, totals is not None, f...]
    unnamed x60 -> x120, local copies, waits for them, and re-layouts: 19.1 us -> 37.6 us
    ppermute x1, waiting for transfers between devices: 18.3 us -> 4.29 us  [per_device(): theirs = lax.ppermute(sent, 'dirs', [(0, 1), (1, 0)])]
    ppermute x33 -> x22, starting transfers between devices: 35.6 us -> 22.3 us  [moved(): lax.ppermute(x, 'atoms', [(i, target(i)) for i in range(atom_devices)])]
  transfers between devices with their start and end apart: 34 -> 23, of which waited for: 12 -> 10; matrix products, arithmetic and copies ran while one was open for 1% -> 1% of each run, Pallas kernels for 33% -> 25%
where the time goes in v5:
time: 204 us; the launch traced here: 202 us
  Pallas kernels  92.4 us (45%)
  waiting for transfers between devices  44.5 us (22%)
  local copies, waits for them, and re-layouts  40.3 us (20%)
  starting transfers between devices  23.9 us (12%)
    pallas_call x5, Pallas kernels, mix(): pl.pallas_call(functools.partial(mix_kernel, first, totals is not None, f...  40.6 us
    ppermute x22, waiting for transfers between devices, moved(): lax.ppermute(x, 'atoms', [(i, target(i)) for i in range(atom_devices)])  40.2 us
    unnamed x120, local copies, waits for them, and re-layouts  37.6 us
    pallas_call x4, Pallas kernels, make_states(): pl.pallas_call(functools.partial(states_kernel, first, min(256, atoms), 1...  34.4 us
    ppermute x22, starting transfers between devices, moved(): lax.ppermute(x, 'atoms', [(i, target(i)) for i in range(atom_devices)])  22.3 us
    pallas_call x6, Pallas kernels, added(): pl.pallas_call(functools.partial(add_kernel, [pick for _, pick in terms],...  12.6 us
    ppermute x1, waiting for transfers between devices, per_device(): theirs = lax.ppermute(sent, 'dirs', [(0, 1), (1, 0)])  4.29 us
  transfers between devices with their start and end apart: 23, of which 10 were waited for; matrix products, arithmetic and copies ran while one was open for 1% of the time, Pallas kernels for 25%

profile of v5, /device:TPU:0, one launch (start us, length us, event | category | flops | bytes accessed | tf_op | source)
XLA Modules:
  0.0 202.4 jit_solution(4868225390884105530)
XLA Ops:
  12.7 17.0 %states.4 = (bf16[2,4,384,128]{3,2,1,0:T(8,128)(2,1)S(1)}, bf16[2,4,384,128]{3,2,1,0:T(8,128)(2,1)S(1)}, bf16[768,2048]{1,0:T(8,128)(2,1)}, bf16[768,2048]{1,0:T(8,128)(2,1)}) custom-call(s32[1]{0:T(128)} %bitcast.index_ref, f32[3,44]{1,0:T(4,128)S(1)} %copy-done.45, f32[44]{0:T(128)S(1)} %copy-done.48, s32[44]{0:T(128)S(1)} %copy-done.50, ...), custom_call_target="tpu_custom_call" | custom-call | flops 6442450944 | bytes 12582912 | tf_op jit(solution)/shard_map/states/pallas_call | solution.py:284
  30.3 4.0 %states.5 = (bf16[2,4,320,128]{3,2,1,0:T(8,128)(2,1)S(1)}, bf16[2,4,320,128]{3,2,1,0:T(8,128)(2,1)S(1)}, bf16[640,2048]{1,0:T(8,128)(2,1)}, bf16[640,2048]{1,0:T(8,128)(2,1)}) custom-call(s32[1]{0:T(128)} %bitcast.index_ref, f32[3,44]{1,0:T(4,128)S(1)} %copy-done.46, f32[44]{0:T(128)S(1)} %copy-done.49, s32[44]{0:T(128)S(1)} %copy-done.51, ...), custom_call_target="tpu_custom_call" | custom-call | flops 1073741824 | bytes 2097152 | tf_op jit(solution)/shard_map/states/pallas_call | solution.py:284
  36.0 2.3 %add.11.refs_0_ = bf16[4,384,128]{2,1,0:T(8,128)(2,1)} custom-call(bf16[2,4,384,128]{3,2,1,0:T(8,128)(2,1)} %copy-done.22, bf16[2,4,384,128]{3,2,1,0:T(8,128)(2,1)} %copy-done.54, bf16[2,4,320,128]{3,2,1,0:T(8,128)(2,1)} %copy-done.2), custom_call_target="tpu_custom_call" | custom-call | tf_op jit(solution)/shard_map/add/pallas_call | solution.py:319
  38.3 2.5 %collective-permute-start.1 = (bf16[4,384,128]{2,1,0:T(8,128)(2,1)}, bf16[4,384,128]{2,1,0:T(8,128)(2,1)}, u32[]{:S(2)}, u32[]{:S(2)}) collective-permute-start(bf16[4,384,128]{2,1,0:T(8,128)(2,1)} %add.11.refs_0_), channel_id=1, source_target_pairs={{0,4},{2,6},{4,0},{6,2},{8,12},{10,14},{12,8},{14,10},{16,20},{18,... | collective-permute-start | bytes 1179656 | tf_op jit(solution)/shard_map/ppermute | solution.py:305
  45.1 6.7 %states.6 = (bf16[2,4,320,128]{3,2,1,0:T(8,128)(2,1)S(1)}, bf16[2,4,320,128]{3,2,1,0:T(8,128)(2,1)S(1)}, bf16[640,2048]{1,0:T(8,128)(2,1)}, bf16[640,2048]{1,0:T(8,128)(2,1)}) custom-call(s32[1]{0:T(128)} %bitcast.index_ref, f32[3,44]{1,0:T(4,128)S(1)} %copy-done.46, ...), custom_call_target="tpu_custom_call", output_to_operand_aliasing={{0}: (11, {}), {1}: (12, {}), {2}: (13, {}), {3}: (14, {})} | custom-call | flops 2147483648 | bytes 4194304 | tf_op jit(solution)/shard_map/states/pallas_call | solution.py:284
  52.7 2.4 %add.12.refs_0_ = bf16[4,384,128]{2,1,0:T(8,128)(2,1)} custom-call(bf16[2,4,384,128]{3,2,1,0:T(8,128)(2,1)} %copy-done.22, bf16[2,4,384,128]{3,2,1,0:T(8,128)(2,1)} %copy-done.54, bf16[4,384,128]{2,1,0:T(8,128)(2,1)} %collective-permute-done.1.refs_2_, bf16[2,4,320,128]{3,2,1,0:T(8,128)(2,1)} %copy-done.4), custom_call_target="tpu_custom_call" | custom-call | tf_op jit(solution)/shard_map/add/pallas_call | solution.py:319
  59.4 6.7 %states.7 = (bf16[2,4,320,128]{3,2,1,0:T(8,128)(2,1)S(1)}, bf16[2,4,320,128]{3,2,1,0:T(8,128)(2,1)S(1)}, bf16[640,2048]{1,0:T(8,128)(2,1)}, bf16[640,2048]{1,0:T(8,128)(2,1)}) custom-call(s32[1]{0:T(128)} %bitcast.index_ref, f32[3,44]{1,0:T(4,128)S(1)} %copy-done.46, ...), custom_call_target="tpu_custom_call", output_to_operand_aliasing={{0}: (11, {}), {1}: (12, {}), {2}: (13, {}), {3}: (14, {})} | custom-call | flops 2147483648 | bytes 4194304 | tf_op jit(solution)/shard_map/states/pallas_call | solution.py:284
  68.1 2.6 %collective-permute-start.4 = (bf16[384,128]{1,0:T(8,128)(2,1)S(1)}, bf16[384,128]{1,0:T(8,128)(2,1)}, u32[]{:S(2)}, u32[]{:S(2)}) collective-permute-start(bf16[384,128]{1,0:T(8,128)(2,1)S(1)} %get-tuple-element.81), channel_id=1, source_target_pairs={{0,16},{2,18},{4,20},{6,22},{8,24},{10,26},{12,28},{14,30},{16,0},... | collective-permute-start | bytes 294920 | tf_op jit(solution)/shard_map/ppermute | solution.py:305
  74.1 3.8 %collective-permute-done.4.refs_2_ = bf16[384,128]{1,0:T(8,128)(2,1)} collective-permute-done((bf16[384,128]{1,0:T(8,128)(2,1)S(1)}, bf16[384,128]{1,0:T(8,128)(2,1)}, u32[]{:S(2)}, u32[]{:S(2)}) %collective-permute-start.4) | collective-permute-done | bytes 98336 | tf_op jit(solution)/shard_map/ppermute | solution.py:305
  79.6 3.7 %collective-permute-start.7 = (bf16[384,128]{1,0:T(8,128)(2,1)}, bf16[384,128]{1,0:T(8,128)(2,1)S(1)}, u32[]{:S(2)}, u32[]{:S(2)}) collective-permute-start(bf16[384,128]{1,0:T(8,128)(2,1)} %add.13.refs_2_.refs_0_), channel_id=1, source_target_pairs={{0,24},{2,26},{4,28},{6,30},{8,0},{10,2},{12,4},{14,6},{16,8},{18,... | collective-permute-start | bytes 294920 | tf_op jit(solution)/shard_map/ppermute | solution.py:305
  86.9 6.1 %collective-permute-done.8.refs_2_ = bf16[384,128]{1,0:T(8,128)(2,1)} collective-permute-done((bf16[384,128]{1,0:T(8,128)(2,1)}, bf16[384,128]{1,0:T(8,128)(2,1)}, u32[]{:S(2)}, u32[]{:S(2)}) %collective-permute-start.8) | collective-permute-done | bytes 98336 | tf_op jit(solution)/shard_map/ppermute | solution.py:305
  96.9 10.2 %collective-permute-done.16.refs_1_ = bf16[1536,128]{1,0:T(8,128)(2,1)S(1)} collective-permute-done((bf16[1536,128]{1,0:T(8,128)(2,1)}, bf16[1536,128]{1,0:T(8,128)(2,1)S(1)}, u32[]{:S(2)}, u32[]{:S(2)}) %collective-permute-start.16) | collective-permute-done | bytes 393248 | tf_op jit(solution)/shard_map/ppermute | solution.py:305
  107.1 5.4 %collective-permute-done.6.refs_2_ = bf16[4,320,128]{2,1,0:T(8,128)(2,1)} collective-permute-done((bf16[4,320,128]{2,1,0:T(8,128)(2,1)}, bf16[4,320,128]{2,1,0:T(8,128)(2,1)}, u32[]{:S(2)}, u32[]{:S(2)}) %collective-permute-start.6) | collective-permute-done | bytes 327712 | tf_op jit(solution)/shard_map/ppermute | solution.py:305
  112.5 2.2 %add.15.refs_0_ = bf16[4,320,128]{2,1,0:T(8,128)(2,1)} custom-call(bf16[2,4,320,128]{3,2,1,0:T(8,128)(2,1)} %copy-done.6, bf16[2,4,320,128]{3,2,1,0:T(8,128)(2,1)} %collective-permute-done.2.refs_1_, bf16[4,320,128]{2,1,0:T(8,128)(2,1)} %collective-permute-done.6.refs_2_, bf16[1536,128]{1,0:T(8,128)(2,1)} %join.2.refs_3_.refs_0_), custom_call_target="tpu_custom_call" | custom-call | tf_op jit(solution)/shard_map/add/pallas_call | solution.py:319
  116.9 3.3 %collective-permute-start.12 = (bf16[320,128]{1,0:T(8,128)(2,1)}, bf16[320,128]{1,0:T(8,128)(2,1)S(1)}, u32[]{:S(2)}, u32[]{:S(2)}) collective-permute-start(bf16[320,128]{1,0:T(8,128)(2,1)} %get-tuple-element.83), channel_id=1, source_target_pairs={{0,24},{2,26},{4,28},{6,30},{8,0},{10,2},{12,4},{14,6},{16,8},{18,... | collective-permute-start | bytes 245768 | tf_op jit(solution)/shard_map/ppermute | solution.py:305
  120.2 2.8 %collective-permute-done.10.refs_1_ = bf16[320,128]{1,0:T(8,128)(2,1)S(1)} collective-permute-done((bf16[320,128]{1,0:T(8,128)(2,1)}, bf16[320,128]{1,0:T(8,128)(2,1)S(1)}, u32[]{:S(2)}, u32[]{:S(2)}) %collective-permute-start.10) | collective-permute-done | bytes 81952 | tf_op jit(solution)/shard_map/ppermute | solution.py:305
  127.7 2.2 %collective-permute-start.13 = (bf16[320,128]{1,0:T(8,128)(2,1)}, bf16[320,128]{1,0:T(8,128)(2,1)}, u32[]{:S(2)}, u32[]{:S(2)}) collective-permute-start(bf16[320,128]{1,0:T(8,128)(2,1)} %add.16.refs_10_.refs_0_), channel_id=1, source_target_pairs={{0,24},{2,26},{4,28},{6,30},{8,0},{10,2},{12,4},{14,6},{16,8},{18,... | collective-permute-start | bytes 245768 | tf_op jit(solution)/shard_map/ppermute | solution.py:305
  135.1 6.0 %mix.5 = (bf16[128,1024]{1,0:T(8,128)(2,1)S(1)}, bf16[128,1024]{1,0:T(8,128)(2,1)S(1)}, bf16[128,1024]{1,0:T(8,128)(2,1)S(1)}, bf16[128,1024]{1,0:T(8,128)(2,1)S(1)}) custom-call(s32[1]{0:T(128)} %bitcast.index_ref, s32[1]{0:T(128)} %bitcast.11.half_ref, bf16[1536,128]{1,0:T(8,128)(2,1)S(1)} %copy-done.12, ...), custom_call_target="tpu_custom_call" | custom-call | flops 1610612736 | bytes 3145728 | tf_op jit(solution)/shard_map/mix/pallas_call | solution.py:373
  145.6 7.3 %collective-permute-done.19.refs_1_ = bf16[1280,128]{1,0:T(8,128)(2,1)S(1)} collective-permute-done((bf16[1280,128]{1,0:T(8,128)(2,1)}, bf16[1280,128]{1,0:T(8,128)(2,1)S(1)}, u32[]{:S(2)}, u32[]{:S(2)}) %collective-permute-start.19) | collective-permute-done | bytes 327712 | tf_op jit(solution)/shard_map/ppermute | solution.py:305
  160.4 6.2 %mix.6 = (bf16[128,1024]{1,0:T(8,128)(2,1)S(1)}, bf16[128,1024]{1,0:T(8,128)(2,1)S(1)}, bf16[128,1024]{1,0:T(8,128)(2,1)S(1)}, bf16[128,1024]{1,0:T(8,128)(2,1)S(1)}) custom-call(s32[1]{0:T(128)} %bitcast.index_ref, s32[1]{0:T(128)} %bitcast.11.half_ref, bf16[1536,128]{1,0:T(8,128)(2,1)S(1)} %copy-done.12, ...), custom_call_target="tpu_custom_call" | custom-call | flops 1610612736 | bytes 3145728 | tf_op jit(solution)/shard_map/mix/pallas_call | solution.py:373
  166.7 8.6 %mix.7.refs_10_ = bf16[1024,512]{1,0:T(8,128)(2,1)S(1)} custom-call(s32[1]{0:T(128)} %bitcast.index_ref, s32[1]{0:T(128)} %bitcast.11.half_ref, bf16[1280,128]{1,0:T(8,128)(2,1)S(1)} %copy-done.16, bf16[1280,128]{1,0:T(8,128)(2,1)S(1)} %collective-permute-done.19.refs_1_, bf16[1280,128]{1,0:T(8,128)(2,1)S(1)} %collective-permute-done.20.refs_2_, ...), custom_call_target="tpu_custom_call" | custom-call | flops 2684354560 | bytes 5242880 | tf_op jit(solution)/shard_map/mix/pallas_call | solution.py:373
  176.9 10.7 %mix.8 = (bf16[128,1024]{1,0:T(8,128)(2,1)S(1)}, bf16[128,1024]{1,0:T(8,128)(2,1)S(1)}, bf16[128,1024]{1,0:T(8,128)(2,1)S(1)}, bf16[128,1024]{1,0:T(8,128)(2,1)S(1)}) custom-call(s32[1]{0:T(128)} %bitcast.index_ref, s32[1]{0:T(128)} %bitcast.1.half_ref, bf16[1536,128]{1,0:T(8,128)(2,1)S(1)} %copy-done.12, ...), custom_call_target="tpu_custom_call" | custom-call | flops 3221225472 | bytes 6291456 | tf_op jit(solution)/shard_map/mix/pallas_call | solution.py:373
  187.6 9.1 %mix.9 = f32[1024,512]{1,0:T(8,128)S(1)} custom-call(s32[1]{0:T(128)} %bitcast.index_ref, s32[1]{0:T(128)} %bitcast.1.half_ref, bf16[1280,128]{1,0:T(8,128)(2,1)S(1)} %copy-done.16, bf16[1280,128]{1,0:T(8,128)(2,1)S(1)} %collective-permute-done.19.refs_1_, bf16[1280,128]{1,0:T(8,128)(2,1)S(1)} %collective-permute-done.20.refs_2_, ...), custom_call_target="tpu_custom_call" | custom-call | flops 2684354560 | bytes 5242880 | tf_op jit(solution)/shard_map/mix/pallas_call | solution.py:373
  196.7 4.3 %collective-permute-done.22 = bf16[1024,512]{1,0:T(8,128)(2,1)S(1)} collective-permute-done((bf16[1024,512]{1,0:T(8,128)(2,1)S(1)}, bf16[1024,512]{1,0:T(8,128)(2,1)S(1)}, u32[]{:S(2)}, u32[]{:S(2)}) %collective-permute-start.22) | collective-permute-done | bytes 1048608 | tf_op jit(solution)/shard_map/ppermute | solution.py:427
  (164 shorter events, 65.4 us)
Async XLA Ops:
  29.8 5.3 %collective-permute-start = (bf16[2,4,384,128]{3,2,1,0:T(8,128)(2,1)S(1)}, bf16[2,4,384,128]{3,2,1,0:T(8,128)(2,1)S(1)}, u32[]{:S(2)}, u32[]{:S(2)}) collective-permute-start(bf16[2,4,384,128]{3,2,1,0:T(8,128)(2,1)S(1)} %get-tuple-element.45.refs_0_), channel_id=1, source_target_pairs={{0,2},{2,0},{4,6},{6,4},{8,10},{10,8},{12,14},{14,12},{16,18},{18,... | collective-permute-start | bytes 2359304 | tf_op jit(solution)/shard_map/ppermute | solution.py:305
  38.3 14.3 %collective-permute-start.1 = (bf16[4,384,128]{2,1,0:T(8,128)(2,1)}, bf16[4,384,128]{2,1,0:T(8,128)(2,1)}, u32[]{:S(2)}, u32[]{:S(2)}) collective-permute-start(bf16[4,384,128]{2,1,0:T(8,128)(2,1)} %add.11.refs_0_), channel_id=1, source_target_pairs={{0,4},{2,6},{4,0},{6,2},{8,12},{10,14},{12,8},{14,10},{16,20},{18,... | collective-permute-start | bytes 1179656 | tf_op jit(solution)/shard_map/ppermute | solution.py:305
  66.1 17.8 %collective-permute-start.2 = (bf16[2,4,320,128]{3,2,1,0:T(8,128)(2,1)S(1)}, bf16[2,4,320,128]{3,2,1,0:T(8,128)(2,1)}, u32[]{:S(2)}, u32[]{:S(2)}) collective-permute-start(bf16[2,4,320,128]{3,2,1,0:T(8,128)(2,1)S(1)} %get-tuple-element.55.refs_4_), channel_id=1, source_target_pairs={{0,2},{2,0},{4,6},{6,4},{8,10},{10,8},{12,14},{14,12},{16,18},{18,... | collective-permute-start | bytes 1966088 | tf_op jit(solution)/shard_map/ppermute | solution.py:305
  66.3 7.7 %collective-permute-start.3 = (bf16[384,128]{1,0:T(8,128)(2,1)S(1)}, bf16[384,128]{1,0:T(8,128)(2,1)S(1)}, u32[]{:S(2)}, u32[]{:S(2)}) collective-permute-start(bf16[384,128]{1,0:T(8,128)(2,1)S(1)} %get-tuple-element.82), channel_id=1, source_target_pairs={{0,8},{2,10},{4,12},{6,14},{8,16},{10,18},{12,20},{14,22},{16,24},... | collective-permute-start | bytes 294920 | tf_op jit(solution)/shard_map/ppermute | solution.py:305
  68.1 9.7 %collective-permute-start.4 = (bf16[384,128]{1,0:T(8,128)(2,1)S(1)}, bf16[384,128]{1,0:T(8,128)(2,1)}, u32[]{:S(2)}, u32[]{:S(2)}) collective-permute-start(bf16[384,128]{1,0:T(8,128)(2,1)S(1)} %get-tuple-element.81), channel_id=1, source_target_pairs={{0,16},{2,18},{4,20},{6,22},{8,24},{10,26},{12,28},{14,30},{16,0},... | collective-permute-start | bytes 294920 | tf_op jit(solution)/shard_map/ppermute | solution.py:305
  70.7 7.1 %collective-permute-start.5 = (bf16[384,128]{1,0:T(8,128)(2,1)S(1)}, bf16[384,128]{1,0:T(8,128)(2,1)}, u32[]{:S(2)}, u32[]{:S(2)}) collective-permute-start(bf16[384,128]{1,0:T(8,128)(2,1)S(1)} %get-tuple-element.80), channel_id=1, source_target_pairs={{0,24},{2,26},{4,28},{6,30},{8,0},{10,2},{12,4},{14,6},{16,8},{18,... | collective-permute-start | bytes 294920 | tf_op jit(solution)/shard_map/ppermute | solution.py:305
  79.6 7.2 %collective-permute-start.7 = (bf16[384,128]{1,0:T(8,128)(2,1)}, bf16[384,128]{1,0:T(8,128)(2,1)S(1)}, u32[]{:S(2)}, u32[]{:S(2)}) collective-permute-start(bf16[384,128]{1,0:T(8,128)(2,1)} %add.13.refs_2_.refs_0_), channel_id=1, source_target_pairs={{0,24},{2,26},{4,28},{6,30},{8,0},{10,2},{12,4},{14,6},{16,8},{18,... | collective-permute-start | bytes 294920 | tf_op jit(solution)/shard_map/ppermute | solution.py:305
  83.3 9.7 %collective-permute-start.8 = (bf16[384,128]{1,0:T(8,128)(2,1)}, bf16[384,128]{1,0:T(8,128)(2,1)}, u32[]{:S(2)}, u32[]{:S(2)}) collective-permute-start(bf16[384,128]{1,0:T(8,128)(2,1)} %add.13.refs_2_.refs_0_), channel_id=1, source_target_pairs={{0,16},{2,18},{4,20},{6,22},{8,24},{10,26},{12,28},{14,30},{16,0},... | collective-permute-start | bytes 294920 | tf_op jit(solution)/shard_map/ppermute | solution.py:305
  83.7 9.3 %collective-permute-start.9 = (bf16[384,128]{1,0:T(8,128)(2,1)}, bf16[384,128]{1,0:T(8,128)(2,1)}, u32[]{:S(2)}, u32[]{:S(2)}) collective-permute-start(bf16[384,128]{1,0:T(8,128)(2,1)} %add.13.refs_2_.refs_0_), channel_id=1, source_target_pairs={{0,8},{2,10},{4,12},{6,14},{8,16},{10,18},{12,20},{14,22},{16,24},... | collective-permute-start | bytes 294920 | tf_op jit(solution)/shard_map/ppermute | solution.py:305
  94.8 35.6 %copy-start.12 = (bf16[1536,128]{1,0:T(8,128)(2,1)S(1)}, bf16[1536,128]{1,0:T(8,128)(2,1)}, u32[]{:S(2)}) copy-start(bf16[1536,128]{1,0:T(8,128)(2,1)} %join.2.refs_3_.refs_0_) | copy-start | bytes 1179652
  94.8 12.3 %collective-permute-start.16 = (bf16[1536,128]{1,0:T(8,128)(2,1)}, bf16[1536,128]{1,0:T(8,128)(2,1)S(1)}, u32[]{:S(2)}, u32[]{:S(2)}) collective-permute-start(bf16[1536,128]{1,0:T(8,128)(2,1)} %join.2.refs_3_.refs_0_), channel_id=1, source_target_pairs={{0,4},{2,6},{4,0},{6,2},{8,12},{10,14},{12,8},{14,10},{16,20},{18,... | collective-permute-start | bytes 1179656 | tf_op jit(solution)/shard_map/ppermute | solution.py:305
  95.4 17.1 %collective-permute-start.6 = (bf16[4,320,128]{2,1,0:T(8,128)(2,1)}, bf16[4,320,128]{2,1,0:T(8,128)(2,1)}, u32[]{:S(2)}, u32[]{:S(2)}) collective-permute-start(bf16[4,320,128]{2,1,0:T(8,128)(2,1)} %add.14.refs_4_), channel_id=1, source_target_pairs={{0,4},{2,6},{4,0},{6,2},{8,12},{10,14},{12,8},{14,10},{16,20},{18,... | collective-permute-start | bytes 983048 | tf_op jit(solution)/shard_map/ppermute | solution.py:305
  96.8 33.6 %collective-permute-start.17 = (bf16[1536,128]{1,0:T(8,128)(2,1)}, bf16[1536,128]{1,0:T(8,128)(2,1)S(1)}, u32[]{:S(2)}, u32[]{:S(2)}) collective-permute-start(bf16[1536,128]{1,0:T(8,128)(2,1)} %join.2.refs_3_.refs_0_), channel_id=1, source_target_pairs={{0,2},{2,0},{4,6},{6,4},{8,10},{10,8},{12,14},{14,12},{16,18},{18,... | collective-permute-start | bytes 1179656 | tf_op jit(solution)/shard_map/ppermute | solution.py:305
  107.1 23.4 %collective-permute-start.18 = (bf16[1536,128]{1,0:T(8,128)(2,1)S(1)}, bf16[1536,128]{1,0:T(8,128)(2,1)}, u32[]{:S(2)}, u32[]{:S(2)}) collective-permute-start(bf16[1536,128]{1,0:T(8,128)(2,1)S(1)} %collective-permute-done.16.refs_1_), channel_id=1, source_target_pairs={{0,2},{2,0},{4,6},{6,4},{8,10},{10,8},{12,14},{14,12},{16,18},{18,... | collective-permute-start | bytes 1179656 | tf_op jit(solution)/shard_map/ppermute | solution.py:305
  116.4 6.7 %collective-permute-start.10 = (bf16[320,128]{1,0:T(8,128)(2,1)}, bf16[320,128]{1,0:T(8,128)(2,1)S(1)}, u32[]{:S(2)}, u32[]{:S(2)}) collective-permute-start(bf16[320,128]{1,0:T(8,128)(2,1)} %get-tuple-element.85), channel_id=1, source_target_pairs={{0,8},{2,10},{4,12},{6,14},{8,16},{10,18},{12,20},{14,22},{16,24},... | collective-permute-start | bytes 245768 | tf_op jit(solution)/shard_map/ppermute | solution.py:305
  116.4 8.3 %collective-permute-start.11 = (bf16[320,128]{1,0:T(8,128)(2,1)}, bf16[320,128]{1,0:T(8,128)(2,1)S(1)}, u32[]{:S(2)}, u32[]{:S(2)}) collective-permute-start(bf16[320,128]{1,0:T(8,128)(2,1)} %get-tuple-element.84), channel_id=1, source_target_pairs={{0,16},{2,18},{4,20},{6,22},{8,24},{10,26},{12,28},{14,30},{16,0},... | collective-permute-start | bytes 245768 | tf_op jit(solution)/shard_map/ppermute | solution.py:305
  116.9 7.7 %collective-permute-start.12 = (bf16[320,128]{1,0:T(8,128)(2,1)}, bf16[320,128]{1,0:T(8,128)(2,1)S(1)}, u32[]{:S(2)}, u32[]{:S(2)}) collective-permute-start(bf16[320,128]{1,0:T(8,128)(2,1)} %get-tuple-element.83), channel_id=1, source_target_pairs={{0,24},{2,26},{4,28},{6,30},{8,0},{10,2},{12,4},{14,6},{16,8},{18,... | collective-permute-start | bytes 245768 | tf_op jit(solution)/shard_map/ppermute | solution.py:305
  127.7 15.6 %collective-permute-start.13 = (bf16[320,128]{1,0:T(8,128)(2,1)}, bf16[320,128]{1,0:T(8,128)(2,1)}, u32[]{:S(2)}, u32[]{:S(2)}) collective-permute-start(bf16[320,128]{1,0:T(8,128)(2,1)} %add.16.refs_10_.refs_0_), channel_id=1, source_target_pairs={{0,24},{2,26},{4,28},{6,30},{8,0},{10,2},{12,4},{14,6},{16,8},{18,... | collective-permute-start | bytes 245768 | tf_op jit(solution)/shard_map/ppermute | solution.py:305
  129.9 13.4 %collective-permute-start.14 = (bf16[320,128]{1,0:T(8,128)(2,1)}, bf16[320,128]{1,0:T(8,128)(2,1)}, u32[]{:S(2)}, u32[]{:S(2)}) collective-permute-start(bf16[320,128]{1,0:T(8,128)(2,1)} %add.16.refs_10_.refs_0_), channel_id=1, source_target_pairs={{0,16},{2,18},{4,20},{6,22},{8,24},{10,26},{12,28},{14,30},{16,0},... | collective-permute-start | bytes 245768 | tf_op jit(solution)/shard_map/ppermute | solution.py:305
  130.0 13.3 %collective-permute-start.15 = (bf16[320,128]{1,0:T(8,128)(2,1)}, bf16[320,128]{1,0:T(8,128)(2,1)}, u32[]{:S(2)}, u32[]{:S(2)}) collective-permute-start(bf16[320,128]{1,0:T(8,128)(2,1)} %add.16.refs_10_.refs_0_), channel_id=1, source_target_pairs={{0,8},{2,10},{4,12},{6,14},{8,16},{10,18},{12,20},{14,22},{16,24},... | collective-permute-start | bytes 245768 | tf_op jit(solution)/shard_map/ppermute | solution.py:305
  145.0 7.8 %collective-permute-start.19 = (bf16[1280,128]{1,0:T(8,128)(2,1)}, bf16[1280,128]{1,0:T(8,128)(2,1)S(1)}, u32[]{:S(2)}, u32[]{:S(2)}) collective-permute-start(bf16[1280,128]{1,0:T(8,128)(2,1)} %join.3.refs_14_.refs_0_), channel_id=1, source_target_pairs={{0,4},{2,6},{4,0},{6,2},{8,12},{10,14},{12,8},{14,10},{16,20},{18,... | collective-permute-start | bytes 983048 | tf_op jit(solution)/shard_map/ppermute | solution.py:305
  145.6 21.1 %collective-permute-start.20 = (bf16[1280,128]{1,0:T(8,128)(2,1)}, bf16[1280,128]{1,0:T(8,128)(2,1)S(1)}, u32[]{:S(2)}, u32[]{:S(2)}) collective-permute-start(bf16[1280,128]{1,0:T(8,128)(2,1)} %join.3.refs_14_.refs_0_), channel_id=1, source_target_pairs={{0,2},{2,0},{4,6},{6,4},{8,10},{10,8},{12,14},{14,12},{16,18},{18,... | collective-permute-start | bytes 983048 | tf_op jit(solution)/shard_map/ppermute | solution.py:305
  152.8 13.8 %collective-permute-start.21 = (bf16[1280,128]{1,0:T(8,128)(2,1)S(1)}, bf16[1280,128]{1,0:T(8,128)(2,1)S(1)}, u32[]{:S(2)}, u32[]{:S(2)}) collective-permute-start(bf16[1280,128]{1,0:T(8,128)(2,1)S(1)} %collective-permute-done.19.refs_1_), channel_id=1, source_target_pairs={{0,2},{2,0},{4,6},{6,4},{8,10},{10,8},{12,14},{14,12},{16,18},{18,... | collective-permute-start | bytes 983048 | tf_op jit(solution)/shard_map/ppermute | solution.py:305
  175.3 25.6 %collective-permute-start.22 = (bf16[1024,512]{1,0:T(8,128)(2,1)S(1)}, bf16[1024,512]{1,0:T(8,128)(2,1)S(1)}, u32[]{:S(2)}, u32[]{:S(2)}) collective-permute-start(bf16[1024,512]{1,0:T(8,128)(2,1)S(1)} %mix.7.refs_10_), channel_id=1, source_target_pairs={{0,1},{1,0},{2,3},{3,2},{4,5},{5,4},{6,7},{7,6},{8,9},{9,8},{10,11... | collective-permute-start | bytes 3145736 | tf_op jit(solution)/shard_map/ppermute | solution.py:427
  (59 other events, 276.1 us)

commit v6 on v3

v6 whole, which is shorter than its diff:
```python
import functools
import math

import jax
import jax.numpy as jnp
from jax import lax
from jax.experimental import pallas as pl
from jax.experimental.pallas import tpu as pltpu
from jax.sharding import PartitionSpec as P

BF16 = jnp.bfloat16
F32 = jnp.float32
GROUP = 4
QUADS = 4
LANES = 128
QUARTER = LANES // QUADS
WIDTH = GROUP * LANES
VMEM_LIMIT = 56 * 2**20
CHUNKS = (4, 4, 3)

SIN_COEF = (4.4428679, -7.30744342, 3.59478808, -0.78437403)
COS_COEF = (1.41420408, -6.97764206, 5.71523839, -1.72834866)


def cos_sin_turns(turns):
    part = turns - jnp.round(turns)
    square = part * part
    sine = SIN_COEF[2] + square * SIN_COEF[3]
    sine = SIN_COEF[1] + square * sine
    sine = part * (SIN_COEF[0] + square * sine)
    cosine = COS_COEF[2] + square * COS_COEF[3]
    cosine = COS_COEF[1] + square * cosine
    cosine = COS_COEF[0] + square * cosine
    return 1.0 - sine * sine, sine * cosine


def column(row):
    size = row.shape[1]
    at_row = lax.broadcasted_iota(jnp.int32, (size, size), 0)
    at_lane = lax.broadcasted_iota(jnp.int32, (size, size), 1)
    return jnp.sum(jnp.where(at_row == at_lane, row, 0.0), axis=1, keepdims=True)


def place_of(index):
    return index & 1, (index >> 1) & 1, (index >> 2) & 3


def slot_of(block, quad):
    away = block ^ quad
    return ((away & 1) << 1) | (away >> 1)


def prepare_kernel(
    index_ref, domain_ref, species_ref, gain_ref, q_ref, k_ref, v_ref, g_ref,
    qt_ref, kt_ref, vt_ref, gt_ref, gain_out,
):
    alive = (domain_ref[...] == index_ref[0]).astype(F32)
    species = species_ref[...]
    gain = jnp.zeros(gain_out.shape, F32)
    for s in range(gain_ref.shape[0]):
        gain = jnp.where(species == s, column(gain_ref[s : s + 1, :]), gain)
    gain_out[...] = gain
    kt_ref[...] = (k_ref[...].astype(F32).T * gain * alive).astype(BF16)
    qt_ref[...] = (q_ref[...].astype(F32).T * alive).astype(BF16)
    vt_ref[...] = (v_ref[...].astype(F32).T * alive).astype(BF16)
    gt_ref[...] = (g_ref[...].astype(F32).T * alive).astype(BF16)


def states_kernel(
    first, chunk, part, scale, index_ref, dirs_ref, weight_ref, mask_ref, freq_ref, pos_ref,
    qt_ref, kt_ref, v_ref, g_ref, *refs,
):
    kept_ref, sent_ref, cos_ref, sin_ref, k_even, q_even, k_odd, q_odd, totals, slots = refs[-10:]
    step = pl.program_id(0)
    steps = pl.num_programs(0)
    atoms = pos_ref.shape[1]
    core, pair, quad = place_of(index_ref[0])
    freq = column(freq_ref[...]) * (1.0 / (2.0 * math.pi))

    def rotate(which, bufs, start):
        for at in range(start, start + chunk, part):
            cols = slice(at, at + part)
            for j in range(2):
                i = 2 * which + j
                u = (first + step) * GROUP + i
                proj = (
                    dirs_ref[0, u] * pos_ref[0:1, cols]
                    + dirs_ref[1, u] * pos_ref[1:2, cols]
                    + dirs_ref[2, u] * pos_ref[2:3, cols]
                )
                cosine, sine = cos_sin_turns(freq * proj)
                cos_ref[i * QUARTER : (i + 1) * QUARTER, cols] = cosine.astype(BF16)
                sin_ref[i * QUARTER : (i + 1) * QUARTER, cols] = sine.astype(BF16)
                for src, dst in zip((kt_ref, qt_ref), bufs):
                    for m in range(2):
                        lead = src[QUARTER * m : QUARTER * (m + 1), cols].astype(F32)
                        trail = src[QUARTER * (m + 2) : QUARTER * (m + 3), cols].astype(F32)
                        row = j * LANES + QUARTER * m
                        dst[row : row + QUARTER, cols] = (lead * cosine - trail * sine).astype(BF16)
                        row = row + 2 * QUARTER
                        dst[row : row + QUARTER, cols] = (lead * sine + trail * cosine).astype(BF16)

    def multiply(bufs, start):
        cols = slice(start, start + chunk)
        for kind, (rot, other) in enumerate(zip(bufs, (v_ref, g_ref))):
            term = jnp.dot(rot[:, cols], other[cols, :], preferred_element_type=F32)
            totals[kind] = term if start == 0 else totals[kind] + term

    def write(which, at_step):
        for j in range(2):
            u = (first + at_step) * GROUP + 2 * which + j
            coef = weight_ref[u] * mask_ref[u].astype(F32) * scale
            rows = pl.ds(pl.multiple_of(at_step * 2 * QUARTER + j * QUARTER, QUARTER), QUARTER)
            for kind in range(2):
                for m in range(QUADS):
                    row = j * LANES + m * QUARTER
                    slots[kind ^ core, which ^ pair, slot_of(m, quad), rows, :] = (
                        totals[kind, row : row + QUARTER, :] * coef
                    ).astype(BF16)

    even, odd = (k_even, q_even), (k_odd, q_odd)
    for which, now, before in ((0, even, odd), (1, odd, even)):
        for start in range(0, atoms, chunk):
            multiply(before, start)
            rotate(which, now, start)
        write(1 - which, step if which == 1 else jnp.maximum(step - 1, 0))

    @pl.when(step == steps - 1)
    def _():
        for start in range(0, atoms, chunk):
            multiply(odd, start)
        write(1, step)
        kept_ref[...] = slots[0]
        sent_ref[...] = slots[1]


def rotated(x, cosine, sine):
    pieces = []
    for i in range(GROUP):
        c = cosine[i * QUARTER : (i + 1) * QUARTER]
        s = sine[i * QUARTER : (i + 1) * QUARTER]
        quarters = [x[m * QUARTER : (m + 1) * QUARTER] for m in range(QUADS)]
        pieces += [quarters[m] * c - quarters[m + 2] * s for m in range(2)]
        pieces += [quarters[m] * s + quarters[m + 2] * c for m in range(2)]
    return jnp.concatenate(pieces, axis=0)


def mix_kernel(chunks, part, index_ref, half_ref, *refs):
    del half_ref
    sources, refs = refs[: 4 * len(chunks)], refs[4 * len(chunks) :]
    vt_ref, gt_ref, kt_ref, qt_ref, cos_ref, sin_ref, gain_ref, out_ref = refs[:8]
    slots, states, states_t, *totals = refs[8:]
    group = pl.program_id(0)
    core, pair, quad = place_of(index_ref[0])

    @pl.when(group == 0)
    def _():
        done = 0
        for at, groups in enumerate(chunks):
            rows = groups * 2 * QUARTER
            for place, source in enumerate(sources[4 * at : 4 * at + 4]):
                for slot in range(QUADS):
                    slots[place // 2, place % 2, slot, done : done + rows, :] = source[
                        slot * rows : (slot + 1) * rows, :
                    ]
            done += rows
        for total in totals:
            total[...] = jnp.zeros_like(total)

    for kind in range(2):
        for i in range(GROUP):
            rows = pl.ds(
                pl.multiple_of(group * 2 * QUARTER + i % 2 * QUARTER, QUARTER), QUARTER
            )
            whole = jnp.concatenate(
                [
                    slots[kind ^ core, (i // 2) ^ pair, slot_of(m, quad), rows, :]
                    for m in range(QUADS)
                ],
                axis=0,
            )
            states[kind, i * LANES : (i + 1) * LANES, :] = whole
            states_t[kind, :, i * LANES : (i + 1) * LANES] = whole.astype(F32).T.astype(BF16)

    starts = list(range(0, vt_ref.shape[1], part))

    def backs(start):
        cols = slice(start, start + part)
        return [
            jnp.dot(states[kind], fixed[:, cols], preferred_element_type=F32)
            for kind, fixed in ((0, gt_ref), (1, vt_ref))
        ]

    def turn(start):
        cols = slice(start, start + part)
        return [
            rotated(x_ref[:, cols], cos_ref[:, cols], sin_ref[:, cols]) for x_ref in (qt_ref, kt_ref)
        ]

    back, turned = backs(starts[0]), turn(starts[0])
    for at, start in enumerate(starts):
        cols = slice(start, start + part)
        for kind, direct in ((0, totals[0]), (1, totals[3])):
            direct[:, cols] += jnp.dot(
                states_t[kind], turned[kind], preferred_element_type=F32
            )
        if start != starts[-1]:
            next_back = backs(starts[at + 1])
        cosine = cos_ref[:, cols].astype(F32)
        sine = sin_ref[:, cols].astype(F32)
        for kind, total in ((0, totals[1]), (1, totals[2])):
            for m in range(2):
                lead_rows = slice(QUARTER * m, QUARTER * (m + 1))
                trail_rows = slice(QUARTER * (m + 2), QUARTER * (m + 3))
                lead_total = total[lead_rows, cols]
                trail_total = total[trail_rows, cols]
                for i in range(GROUP):
                    c = cosine[i * QUARTER : (i + 1) * QUARTER]
                    s = sine[i * QUARTER : (i + 1) * QUARTER]
                    row = i * LANES + QUARTER * m
                    lead = back[kind][row : row + QUARTER, :]
                    trail = back[kind][row + 2 * QUARTER : row + 3 * QUARTER, :]
                    lead_total = lead_total + (lead * c + trail * s)
                    trail_total = trail_total + (trail * c - lead * s)
                total[lead_rows, cols] = lead_total
                total[trail_rows, cols] = trail_total
        if start != starts[-1]:
            back, turned = next_back, turn(starts[at + 1])

    @pl.when(group == pl.num_programs(0) - 1)
    def _():
        for at, total in enumerate(totals):
            whole = total[...] * gain_ref[...] if at == 2 else total[...]
            out_ref[:, at * LANES : (at + 1) * LANES] = whole.T.astype(out_ref.dtype)


def added(*terms):
    return sum(term.astype(F32) for term in terms).astype(BF16)


def per_device(
    atom_devices, queries, keys, values, cotangent, positions, species, domain, species_gain,
    frequency, directions, dir_weight, dir_mask,
):
    atoms, feats = queries.shape
    total_groups = dir_weight.shape[0] // GROUP
    half_atoms = atoms // 2
    index = lax.axis_index("atoms")[None].astype(jnp.int32)
    mine = lax.axis_index("dirs").astype(jnp.int32)
    vmem = pl.BlockSpec(memory_space=pltpu.VMEM)
    smem = pl.BlockSpec(memory_space=pltpu.SMEM)
    anywhere = pl.BlockSpec(memory_space=pl.ANY)
    params = pltpu.CompilerParams(vmem_limit_bytes=VMEM_LIMIT)
    shape = jax.ShapeDtypeStruct

    qt, kt, vt, gt, gain = pl.pallas_call(
        prepare_kernel,
        in_specs=[smem] + [vmem] * 7,
        out_specs=[vmem] * 5,
        out_shape=[shape((feats, atoms), BF16)] * 4 + [shape((feats, atoms), F32)],
        compiler_params=params,
        name="prepare",
    )(index, domain[None, :], species[None, :], species_gain, queries, keys, values, cotangent)

    def make_states(first, groups, after, phases):
        sent = shape((2, QUADS, groups * 2 * QUARTER, feats), BF16)
        phase = shape((total_groups * GROUP * QUARTER, atoms), BF16)
        phase_spec = pl.BlockSpec((GROUP * QUARTER, atoms), lambda g: (g + first, 0))
        operands = [
            index, directions, dir_weight, dir_mask, frequency[None, :], positions, qt, kt,
            values, cotangent, *after,
        ]
        kept, sent, *phases = pl.pallas_call(
            functools.partial(
                states_kernel, first, min(512, atoms), min(256, atoms),
                1.0 / math.sqrt(feats * atoms),
            ),
            grid=(groups,),
            in_specs=[smem] * 4 + [vmem] * 6 + [anywhere] * (len(after) + len(phases)),
            out_specs=[vmem] * 2 + [phase_spec] * 2,
            out_shape=[sent] * 2 + [phase] * 2,
            input_output_aliases={len(operands) + at: 2 + at for at in range(len(phases))},
            scratch_shapes=[pltpu.VMEM((2 * LANES, atoms), BF16)] * 4
            + [
                pltpu.VMEM((2, 2 * LANES, feats), F32),
                pltpu.VMEM((2, *sent.shape), BF16),
            ],
            compiler_params=params,
            cost_estimate=pl.CostEstimate(
                flops=8 * groups * WIDTH * atoms * feats,
                bytes_accessed=2 * groups * WIDTH * atoms, transcendentals=0,
            ),
            name="states",
        )(*operands, *phases)
        return kept, sent, phases

    def moved(x, target):
        return lax.ppermute(x, "atoms", [(i, target(i)) for i in range(atom_devices)])

    def by_bit(x, bit):
        return moved(x, lambda i: i ^ bit)

    def crossing(kept, sent):
        arrived = by_bit(sent, 1)
        return arrived, added(kept[1], arrived[1])

    def summed(kept, arrived, crossing_out):
        half = added(kept[0], arrived[0], by_bit(crossing_out, 2))
        near = added(half[:2], by_bit(half[2:], 4))
        quarter = added(near[0], by_bit(near[1], 8))
        whole = quarter
        for step in range(16, atom_devices, 16):
            whole = added(whole, moved(quarter, lambda i: (i + step) % atom_devices))
        near = jnp.concatenate([whole, by_bit(whole, 8)], axis=0)
        half = jnp.concatenate([near, by_bit(near, 4)], axis=0)
        other = by_bit(half, 2)
        return half, other, by_bit(half, 1), by_bit(other, 1)

    def mix(half, pieces, phases, dtype, after=()):
        rows_half = pl.BlockSpec((feats, half_atoms), lambda g, index, half: (0, half[0]))
        phase_spec = pl.BlockSpec(
            (GROUP * QUARTER, half_atoms), lambda g, index, half: (g, half[0])
        )
        return pl.pallas_call(
            lambda *refs: mix_kernel(
                CHUNKS, min(256, half_atoms), *refs[: 2 + len(pieces) + 7],
                *refs[2 + len(pieces) + 7 + len(after) :],
            ),
            grid_spec=pltpu.PrefetchScalarGridSpec(
                num_scalar_prefetch=2,
                grid=(total_groups,),
                in_specs=[vmem] * len(pieces) + [rows_half] * 4 + [phase_spec] * 2 + [rows_half]
                + [anywhere] * len(after),
                out_specs=pl.BlockSpec((half_atoms, 4 * feats), lambda g, index, half: (0, 0)),
                scratch_shapes=[
                    pltpu.VMEM((2, 2, QUADS, total_groups * 2 * QUARTER, feats), BF16),
                    pltpu.VMEM((2, WIDTH, feats), BF16),
                    pltpu.VMEM((2, feats, WIDTH), BF16),
                ]
                + [pltpu.VMEM((feats, half_atoms), F32)] * 4,
            ),
            out_shape=shape((half_atoms, 4 * feats), dtype),
            compiler_params=params,
            cost_estimate=pl.CostEstimate(
                flops=8 * total_groups * WIDTH * half_atoms * feats,
                bytes_accessed=2 * total_groups * WIDTH * half_atoms, transcendentals=0,
            ),
            name="mix",
        )(index, half[None], *pieces, vt, gt, kt, qt, *phases, gain, *after)

    made = []
    first = 0
    phases = []
    for groups in CHUNKS:
        after = [made[-2][2]] if len(made) > 1 else []
        kept, sent, phases = make_states(first, groups, after, phases)
        made.append((kept, *crossing(kept, sent)))
        first += groups
    pieces = [piece for each in made for piece in summed(*each)]
    sent = mix(1 - mine, pieces, phases, BF16)
    theirs = lax.ppermute(sent, "dirs", [(0, 1), (1, 0)])
    ours = mix(mine, pieces, phases, F32, [sent])
    total = (ours + theirs.astype(F32)).astype(BF16)
    return tuple(total[:, at * feats : (at + 1) * feats] for at in range(4))


def solution(mesh):
    return jax.shard_map(
        functools.partial(per_device, mesh.shape["atoms"]),
        mesh=mesh,
        in_specs=(
            P("atoms", None),
            P("atoms", None),
            P("atoms", None),
            P("atoms", None),
            P(None, "atoms"),
            P("atoms"),
            P("atoms"),
            P(),
            P(),
            P(None, "dirs"),
            P("dirs"),
            P("dirs"),
        ),
        out_specs=(
            P(("atoms", "dirs"), None),
            P(("atoms", "dirs"), None),
            P(("atoms", "dirs"), None),
            P(("atoms", "dirs"), None),
        ),
        check_vma=False,
    )
```

time: 170 us -> 164 us (0.965)
  Pallas kernels: 72.6 us -> 99.5 us
  local copies, waits for them, and re-layouts: 20.2 us -> 1.75 us
  starting transfers between devices: 37.2 us -> 28.6 us
  waiting for transfers between devices: 35.5 us -> 27.3 us
  other arithmetic: 2.49 us -> 5.47 us
    pallas_call x7 -> x5, Pallas kernels: 71.6 us -> 95.8 us  [the longest x3 51.7 us: make_states(): pl.pallas_call(functools.partial(states_kernel, first, min(512, atoms), m...]
    unnamed x60 -> x30, local copies, waits for them, and re-layouts: 19.1 us -> 0.65 us
    ppermute x1, waiting for transfers between devices: 18.3 us -> 1.53 us  [per_device(): theirs = lax.ppermute(sent, 'dirs', [(0, 1), (1, 0)])]
    ppermute x33 -> x27, waiting for transfers between devices: 17.1 us -> 25.8 us  [moved(): lax.ppermute(x, 'atoms', [(i, target(i)) for i in range(atom_devices)])]
    ppermute x33 -> x27, starting transfers between devices: 35.6 us -> 27 us  [moved(): lax.ppermute(x, 'atoms', [(i, target(i)) for i in range(atom_devices)])]
    convert_element_type x9 -> x12, other arithmetic: 0.6 us -> 3.46 us  [added(): return sum((term.astype(F32) for term in terms)).astype(BF16)]
    pallas_call x1, Pallas kernels: 0.95 us -> 3.78 us  [per_device(): pl.pallas_call(prepare_kernel, in_specs=[smem] + [vmem] * 7, out_specs=[v...]
  transfers between devices with their start and end apart: 34 -> 28, of which waited for: 12 -> 11; matrix products, arithmetic and copies ran while one was open for 1% -> 2% of each run, Pallas kernels for 33% -> 34%
where the time goes in v6:
time: 164 us
  Pallas kernels  99.5 us (61%)
  starting transfers between devices  28.6 us (17%)
  waiting for transfers between devices  27.3 us (17%)
  other arithmetic  5.47 us (3%)
  local copies, waits for them, and re-layouts  1.75 us (1%)
    pallas_call x3, Pallas kernels, make_states(): pl.pallas_call(functools.partial(states_kernel, first, min(512, atoms), m...  51.7 us
    pallas_call x2, Pallas kernels, mix(): pl.pallas_call(lambda *refs: mix_kernel(CHUNKS, min(256, half_atoms), *re...  44 us
    ppermute x27, starting transfers between devices, moved(): lax.ppermute(x, 'atoms', [(i, target(i)) for i in range(atom_devices)])  27 us
    ppermute x27, waiting for transfers between devices, moved(): lax.ppermute(x, 'atoms', [(i, target(i)) for i in range(atom_devices)])  25.8 us
    pallas_call x1, Pallas kernels, per_device(): pl.pallas_call(prepare_kernel, in_specs=[smem] + [vmem] * 7, out_specs=[v...  3.78 us
    convert_element_type x12, other arithmetic, added(): return sum((term.astype(F32) for term in terms)).astype(BF16)  3.46 us
  transfers between devices with their start and end apart: 28, of which 11 were waited for; matrix products, arithmetic and copies ran while one was open for 2% of the time, Pallas kernels for 34%

profile of v6, /device:TPU:0, one launch (start us, length us, event | category | flops | bytes accessed | tf_op | source)
XLA Modules:
  0.0 163.6 jit_solution(12766866976399400344)
XLA Ops:
  0.6 3.8 %prepare.1 = (bf16[128,2048]{1,0:T(8,128)(2,1)}, bf16[128,2048]{1,0:T(8,128)(2,1)}, bf16[128,2048]{1,0:T(8,128)(2,1)}, bf16[128,2048]{1,0:T(8,128)(2,1)}, f32[128,2048]{1,0:T(8,128)}) custom-call(s32[1]{0:T(128)} %bitcast.index_ref.refs_0_, s32[1,2048]{1,0:T(1,128)} %bitcast.45, s32[1,2048]{1,0:T(1,128)} %bitcast.46, f32[5,128]{1,0:T(8,128)} %gain_ref.1, ...), custom_call_target="tpu_custom_call" | custom-call | tf_op jit(solution)/shard_map/prepare/pallas_call | solution.py:256
  4.4 18.4 %states.3 = (bf16[2,4,256,128]{3,2,1,0:T(8,128)(2,1)}, bf16[2,4,256,128]{3,2,1,0:T(8,128)(2,1)}, bf16[1408,2048]{1,0:T(8,128)(2,1)}, bf16[1408,2048]{1,0:T(8,128)(2,1)}) custom-call(s32[1]{0:T(128)} %bitcast.index_ref.refs_0_, f32[3,44]{1,0:T(4,128)} %dirs_ref.5, f32[44]{0:T(128)} %weight_ref.5, s32[44]{0:T(128)} %mask_ref.5, f32[1,32]{1,0:T(1,128)} %bitcast.47, ...), custom_call_target="tpu_custom_call" | custom-call | flops 4294967296 | bytes 8388608 | tf_op jit(solution)/shard_map/states/pallas_call | solution.py:273
  23.3 18.5 %states.4 = (bf16[2,4,256,128]{3,2,1,0:T(8,128)(2,1)}, bf16[2,4,256,128]{3,2,1,0:T(8,128)(2,1)}, bf16[1408,2048]{1,0:T(8,128)(2,1)}, bf16[1408,2048]{1,0:T(8,128)(2,1)}) custom-call(s32[1]{0:T(128)} %bitcast.index_ref.refs_0_, f32[3,44]{1,0:T(4,128)} %dirs_ref.5, f32[44]{0:T(128)} %weight_ref.5, ...), custom_call_target="tpu_custom_call", output_to_operand_aliasing={{2}: (10, {}), {3}: (11, {})} | custom-call | flops 4294967296 | bytes 8388608 | tf_op jit(solution)/shard_map/states/pallas_call | solution.py:273
  41.9 3.0 %collective-permute-start.1 = (bf16[4,256,128]{2,1,0:T(8,128)(2,1)S(1)}, bf16[4,256,128]{2,1,0:T(8,128)(2,1)S(1)}, u32[]{:S(2)}, u32[]{:S(2)}) collective-permute-start(bf16[4,256,128]{2,1,0:T(8,128)(2,1)S(1)} %fusion.3.refs_0_), channel_id=1, source_target_pairs={{0,4},{2,6},{4,0},{6,2},{8,12},{10,14},{12,8},{14,10},{16,20},{18,... | collective-permute-start | bytes 786440 | tf_op jit(solution)/shard_map/ppermute | solution.py:298
  46.0 1.7 %collective-permute-start.10 = (bf16[4,256,128]{2,1,0:T(8,128)(2,1)S(1)}, bf16[4,256,128]{2,1,0:T(8,128)(2,1)S(1)}, u32[]{:S(2)}, u32[]{:S(2)}) collective-permute-start(bf16[4,256,128]{2,1,0:T(8,128)(2,1)S(1)} %fusion.4), channel_id=1, source_target_pairs={{0,4},{2,6},{4,0},{6,2},{8,12},{10,14},{12,8},{14,10},{16,20},{18,... | collective-permute-start | bytes 786440 | tf_op jit(solution)/shard_map/ppermute | solution.py:298
  47.6 14.8 %states.5 = (bf16[2,4,192,128]{3,2,1,0:T(8,128)(2,1)}, bf16[2,4,192,128]{3,2,1,0:T(8,128)(2,1)}, bf16[1408,2048]{1,0:T(8,128)(2,1)}, bf16[1408,2048]{1,0:T(8,128)(2,1)}) custom-call(s32[1]{0:T(128)} %bitcast.index_ref.refs_0_, f32[3,44]{1,0:T(4,128)} %dirs_ref.5, f32[44]{0:T(128)} %weight_ref.5, ...), custom_call_target="tpu_custom_call", output_to_operand_aliasing={{2}: (11, {}), {3}: (12, {})} | custom-call | flops 3221225472 | bytes 6291456 | tf_op jit(solution)/shard_map/states/pallas_call | solution.py:273
  62.7 1.6 %collective-permute-start.2 = (bf16[2,256,128]{2,1,0:T(8,128)(2,1)S(1)}, bf16[2,256,128]{2,1,0:T(8,128)(2,1)S(1)}, u32[]{:S(2)}, u32[]{:S(2)}) collective-permute-start(bf16[2,256,128]{2,1,0:T(8,128)(2,1)S(1)} %slice.115), channel_id=1, source_target_pairs={{0,8},{2,10},{4,12},{6,14},{8,0},{10,2},{12,4},{14,6},{16,24},{18,... | collective-permute-start | bytes 393224 | tf_op jit(solution)/shard_map/ppermute | solution.py:298
  65.0 4.1 %collective-permute-done.2 = bf16[2,256,128]{2,1,0:T(8,128)(2,1)S(1)} collective-permute-done((bf16[2,256,128]{2,1,0:T(8,128)(2,1)S(1)}, bf16[2,256,128]{2,1,0:T(8,128)(2,1)S(1)}, u32[]{:S(2)}, u32[]{:S(2)}) %collective-permute-start.2) | collective-permute-done | bytes 131104 | tf_op jit(solution)/shard_map/ppermute | solution.py:298
  69.1 2.7 %collective-permute-start.3 = (bf16[256,128]{1,0:T(8,128)(2,1)S(1)}, bf16[256,128]{1,0:T(8,128)(2,1)S(1)}, u32[]{:S(2)}, u32[]{:S(2)}) collective-permute-start(bf16[256,128]{1,0:T(8,128)(2,1)S(1)} %slice_bitcast_fusion.2), channel_id=1, source_target_pairs={{0,16},{2,18},{4,20},{6,22},{8,24},{10,26},{12,28},{14,30},{16,0},... | collective-permute-start | bytes 196616 | tf_op jit(solution)/shard_map/ppermute | solution.py:298
  71.8 2.7 %collective-permute-start.12 = (bf16[256,128]{1,0:T(8,128)(2,1)S(1)}, bf16[256,128]{1,0:T(8,128)(2,1)S(1)}, u32[]{:S(2)}, u32[]{:S(2)}) collective-permute-start(bf16[256,128]{1,0:T(8,128)(2,1)S(1)} %slice_bitcast_fusion), channel_id=1, source_target_pairs={{0,16},{2,18},{4,20},{6,22},{8,24},{10,26},{12,28},{14,30},{16,0},... | collective-permute-start | bytes 196616 | tf_op jit(solution)/shard_map/ppermute | solution.py:298
  78.2 2.0 %collective-permute-start.13 = (bf16[256,128]{1,0:T(8,128)(2,1)S(1)}, bf16[256,128]{1,0:T(8,128)(2,1)S(1)}, u32[]{:S(2)}, u32[]{:S(2)}) collective-permute-start(bf16[256,128]{1,0:T(8,128)(2,1)S(1)} %fusion.6), channel_id=1, source_target_pairs={{0,16},{2,18},{4,20},{6,22},{8,24},{10,26},{12,28},{14,30},{16,0},... | collective-permute-start | bytes 196616 | tf_op jit(solution)/shard_map/ppermute | solution.py:298
  82.4 3.2 %collective-permute-start.20 = (bf16[2,192,128]{2,1,0:T(8,128)(2,1)S(1)}, bf16[2,192,128]{2,1,0:T(8,128)(2,1)S(1)}, u32[]{:S(2)}, u32[]{:S(2)}) collective-permute-start(bf16[2,192,128]{2,1,0:T(8,128)(2,1)S(1)} %slice.127), channel_id=1, source_target_pairs={{0,8},{2,10},{4,12},{6,14},{8,0},{10,2},{12,4},{14,6},{16,24},{18,... | collective-permute-start | bytes 294920 | tf_op jit(solution)/shard_map/ppermute | solution.py:298
  85.7 2.5 %collective-permute-done.20 = bf16[2,192,128]{2,1,0:T(8,128)(2,1)S(1)} collective-permute-done((bf16[2,192,128]{2,1,0:T(8,128)(2,1)S(1)}, bf16[2,192,128]{2,1,0:T(8,128)(2,1)S(1)}, u32[]{:S(2)}, u32[]{:S(2)}) %collective-permute-start.20) | collective-permute-done | bytes 98336 | tf_op jit(solution)/shard_map/ppermute | solution.py:298
  89.2 1.8 %collective-permute-start.14 = (bf16[512,128]{1,0:T(8,128)(2,1)S(1)}, bf16[512,128]{1,0:T(8,128)(2,1)S(1)}, u32[]{:S(2)}, u32[]{:S(2)}) collective-permute-start(bf16[512,128]{1,0:T(8,128)(2,1)S(1)} %pad_maximum_fusion.4), channel_id=1, source_target_pairs={{0,8},{2,10},{4,12},{6,14},{8,0},{10,2},{12,4},{14,6},{16,24},{18,... | collective-permute-start | bytes 393224 | tf_op jit(solution)/shard_map/ppermute | solution.py:298
  91.0 2.9 %collective-permute-done.21 = bf16[192,128]{1,0:T(8,128)(2,1)S(1)} collective-permute-done((bf16[192,128]{1,0:T(8,128)(2,1)S(1)}, bf16[192,128]{1,0:T(8,128)(2,1)S(1)}, u32[]{:S(2)}, u32[]{:S(2)}) %collective-permute-start.21) | collective-permute-done | bytes 49184 | tf_op jit(solution)/shard_map/ppermute | solution.py:298
  95.2 3.7 %collective-permute-done.22 = bf16[192,128]{1,0:T(8,128)(2,1)S(1)} collective-permute-done((bf16[192,128]{1,0:T(8,128)(2,1)S(1)}, bf16[192,128]{1,0:T(8,128)(2,1)S(1)}, u32[]{:S(2)}, u32[]{:S(2)}) %collective-permute-start.22) | collective-permute-done | bytes 49184 | tf_op jit(solution)/shard_map/ppermute | solution.py:298
  99.0 1.8 %collective-permute-start.23 = (bf16[384,128]{1,0:T(8,128)(2,1)S(1)}, bf16[384,128]{1,0:T(8,128)(2,1)S(1)}, u32[]{:S(2)}, u32[]{:S(2)}) collective-permute-start(bf16[384,128]{1,0:T(8,128)(2,1)S(1)} %pad_maximum_fusion.5), channel_id=1, source_target_pairs={{0,8},{2,10},{4,12},{6,14},{8,0},{10,2},{12,4},{14,6},{16,24},{18,... | collective-permute-start | bytes 294920 | tf_op jit(solution)/shard_map/ppermute | solution.py:298
  101.1 2.5 %collective-permute-done.23 = bf16[384,128]{1,0:T(8,128)(2,1)S(1)} collective-permute-done((bf16[384,128]{1,0:T(8,128)(2,1)S(1)}, bf16[384,128]{1,0:T(8,128)(2,1)S(1)}, u32[]{:S(2)}, u32[]{:S(2)}) %collective-permute-start.23) | collective-permute-done | bytes 98336 | tf_op jit(solution)/shard_map/ppermute | solution.py:298
  104.4 4.9 %collective-permute-done.15.refs_7_ = bf16[1024,128]{1,0:T(8,128)(2,1)S(1)} collective-permute-done((bf16[1024,128]{1,0:T(8,128)(2,1)S(1)}, bf16[1024,128]{1,0:T(8,128)(2,1)S(1)}, u32[]{:S(2)}, u32[]{:S(2)}) %collective-permute-start.15) | collective-permute-done | bytes 262176 | tf_op jit(solution)/shard_map/ppermute | solution.py:298
  109.8 1.6 collective-permute-done.24.refs_11_
  113.5 21.7 %mix.2.refs_21_ = bf16[1024,512]{1,0:T(8,128)(2,1)} custom-call(s32[1]{0:T(128)} %bitcast.index_ref.refs_0_, s32[1]{0:T(128)} %bitcast.17.refs_1_, bf16[1024,128]{1,0:T(8,128)(2,1)} %copy-done.3, bf16[1024,128]{1,0:T(8,128)(2,1)} %copy-done.6, bf16[1024,128]{1,0:T(8,128)(2,1)} %copy-done.8, bf16[1024,128]{1,0:T(8,128)(2,1)} %copy-done.10, ...), custom_call_target="tpu_custom_call" | custom-call | flops 5905580032 | bytes 11534336 | tf_op jit(solution)/shard_map/mix/pallas_call | solution.py:324
  135.2 1.5 collective-permute-start.27
  136.7 22.4 %mix.3 = f32[1024,512]{1,0:T(8,128)} custom-call(s32[1]{0:T(128)} %bitcast.index_ref.refs_0_, s32[1]{0:T(128)} %bitcast.1.refs_1_, bf16[1024,128]{1,0:T(8,128)(2,1)} %copy-done.3, bf16[1024,128]{1,0:T(8,128)(2,1)} %copy-done.6, bf16[1024,128]{1,0:T(8,128)(2,1)} %copy-done.8, bf16[1024,128]{1,0:T(8,128)(2,1)} %copy-done.10, bf16[1024,128]{1,0:T(8,128)(2,1)} %copy-done.4, ...), custom_call_target="tpu_custom_call" | custom-call | flops 5905580032 | bytes 11534336 | tf_op jit(solution)/shard_map/mix/pallas_call | solution.py:324
  160.6 1.9 %add_convert_fusion = bf16[1024,512]{1,0:T(8,128)(2,1)S(1)} fusion(f32[1024,512]{1,0:T(8,128)} %mix.3, bf16[1024,512]{1,0:T(8,128)(2,1)S(1)} %collective-permute-done.27), kind=kLoop, calls=%fused_computation | loop fusion | flops 1572864 | bytes 4194304 | tf_op jit(solution)/shard_map/convert_element_type | solution.py:363
  (94 shorter events, 16.9 us)
Async XLA Ops:
  22.9 19.0 %collective-permute-start = (bf16[2,4,256,128]{3,2,1,0:T(8,128)(2,1)}, bf16[2,4,256,128]{3,2,1,0:T(8,128)(2,1)S(1)}, u32[]{:S(2)}, u32[]{:S(2)}) collective-permute-start(bf16[2,4,256,128]{3,2,1,0:T(8,128)(2,1)} %get-tuple-element.24), channel_id=1, source_target_pairs={{0,2},{2,0},{4,6},{6,4},{8,10},{10,8},{12,14},{14,12},{16,18},{18,... | collective-permute-start | bytes 1572872 | tf_op jit(solution)/shard_map/ppermute | solution.py:298
  41.9 20.6 %collective-permute-start.1 = (bf16[4,256,128]{2,1,0:T(8,128)(2,1)S(1)}, bf16[4,256,128]{2,1,0:T(8,128)(2,1)S(1)}, u32[]{:S(2)}, u32[]{:S(2)}) collective-permute-start(bf16[4,256,128]{2,1,0:T(8,128)(2,1)S(1)} %fusion.3.refs_0_), channel_id=1, source_target_pairs={{0,4},{2,6},{4,0},{6,2},{8,12},{10,14},{12,8},{14,10},{16,20},{18,... | collective-permute-start | bytes 786440 | tf_op jit(solution)/shard_map/ppermute | solution.py:298
  46.0 18.3 %collective-permute-start.10 = (bf16[4,256,128]{2,1,0:T(8,128)(2,1)S(1)}, bf16[4,256,128]{2,1,0:T(8,128)(2,1)S(1)}, u32[]{:S(2)}, u32[]{:S(2)}) collective-permute-start(bf16[4,256,128]{2,1,0:T(8,128)(2,1)S(1)} %fusion.4), channel_id=1, source_target_pairs={{0,4},{2,6},{4,0},{6,2},{8,12},{10,14},{12,8},{14,10},{16,20},{18,... | collective-permute-start | bytes 786440 | tf_op jit(solution)/shard_map/ppermute | solution.py:298
  62.5 12.1 %collective-permute-start.18 = (bf16[2,4,192,128]{3,2,1,0:T(8,128)(2,1)}, bf16[2,4,192,128]{3,2,1,0:T(8,128)(2,1)S(1)}, u32[]{:S(2)}, u32[]{:S(2)}) collective-permute-start(bf16[2,4,192,128]{3,2,1,0:T(8,128)(2,1)} %get-tuple-element.32), channel_id=1, source_target_pairs={{0,2},{2,0},{4,6},{6,4},{8,10},{10,8},{12,14},{14,12},{16,18},{18,... | collective-permute-start | bytes 1179656 | tf_op jit(solution)/shard_map/ppermute | solution.py:298
  62.7 6.4 %collective-permute-start.2 = (bf16[2,256,128]{2,1,0:T(8,128)(2,1)S(1)}, bf16[2,256,128]{2,1,0:T(8,128)(2,1)S(1)}, u32[]{:S(2)}, u32[]{:S(2)}) collective-permute-start(bf16[2,256,128]{2,1,0:T(8,128)(2,1)S(1)} %slice.115), channel_id=1, source_target_pairs={{0,8},{2,10},{4,12},{6,14},{8,0},{10,2},{12,4},{14,6},{16,24},{18,... | collective-permute-start | bytes 393224 | tf_op jit(solution)/shard_map/ppermute | solution.py:298
  64.4 7.3 %collective-permute-start.11 = (bf16[2,256,128]{2,1,0:T(8,128)(2,1)S(1)}, bf16[2,256,128]{2,1,0:T(8,128)(2,1)S(1)}, u32[]{:S(2)}, u32[]{:S(2)}) collective-permute-start(bf16[2,256,128]{2,1,0:T(8,128)(2,1)S(1)} %slice.121), channel_id=1, source_target_pairs={{0,8},{2,10},{4,12},{6,14},{8,0},{10,2},{12,4},{14,6},{16,24},{18,... | collective-permute-start | bytes 393224 | tf_op jit(solution)/shard_map/ppermute | solution.py:298
  69.1 7.1 %collective-permute-start.3 = (bf16[256,128]{1,0:T(8,128)(2,1)S(1)}, bf16[256,128]{1,0:T(8,128)(2,1)S(1)}, u32[]{:S(2)}, u32[]{:S(2)}) collective-permute-start(bf16[256,128]{1,0:T(8,128)(2,1)S(1)} %slice_bitcast_fusion.2), channel_id=1, source_target_pairs={{0,16},{2,18},{4,20},{6,22},{8,24},{10,26},{12,28},{14,30},{16,0},... | collective-permute-start | bytes 196616 | tf_op jit(solution)/shard_map/ppermute | solution.py:298
  71.8 6.4 %collective-permute-start.12 = (bf16[256,128]{1,0:T(8,128)(2,1)S(1)}, bf16[256,128]{1,0:T(8,128)(2,1)S(1)}, u32[]{:S(2)}, u32[]{:S(2)}) collective-permute-start(bf16[256,128]{1,0:T(8,128)(2,1)S(1)} %slice_bitcast_fusion), channel_id=1, source_target_pairs={{0,16},{2,18},{4,20},{6,22},{8,24},{10,26},{12,28},{14,30},{16,0},... | collective-permute-start | bytes 196616 | tf_op jit(solution)/shard_map/ppermute | solution.py:298
  75.5 5.8 %collective-permute-start.19 = (bf16[4,192,128]{2,1,0:T(8,128)(2,1)S(1)}, bf16[4,192,128]{2,1,0:T(8,128)(2,1)S(1)}, u32[]{:S(2)}, u32[]{:S(2)}) collective-permute-start(bf16[4,192,128]{2,1,0:T(8,128)(2,1)S(1)} %fusion.5), channel_id=1, source_target_pairs={{0,4},{2,6},{4,0},{6,2},{8,12},{10,14},{12,8},{14,10},{16,20},{18,... | collective-permute-start | bytes 589832 | tf_op jit(solution)/shard_map/ppermute | solution.py:298
  76.2 9.4 %collective-permute-start.4 = (bf16[256,128]{1,0:T(8,128)(2,1)S(1)}, bf16[256,128]{1,0:T(8,128)(2,1)S(1)}, u32[]{:S(2)}, u32[]{:S(2)}) collective-permute-start(bf16[256,128]{1,0:T(8,128)(2,1)S(1)} %fusion.7), channel_id=1, source_target_pairs={{0,16},{2,18},{4,20},{6,22},{8,24},{10,26},{12,28},{14,30},{16,0},... | collective-permute-start | bytes 196616 | tf_op jit(solution)/shard_map/ppermute | solution.py:298
  78.2 10.9 %collective-permute-start.13 = (bf16[256,128]{1,0:T(8,128)(2,1)S(1)}, bf16[256,128]{1,0:T(8,128)(2,1)S(1)}, u32[]{:S(2)}, u32[]{:S(2)}) collective-permute-start(bf16[256,128]{1,0:T(8,128)(2,1)S(1)} %fusion.6), channel_id=1, source_target_pairs={{0,16},{2,18},{4,20},{6,22},{8,24},{10,26},{12,28},{14,30},{16,0},... | collective-permute-start | bytes 196616 | tf_op jit(solution)/shard_map/ppermute | solution.py:298
  82.4 5.8 %collective-permute-start.20 = (bf16[2,192,128]{2,1,0:T(8,128)(2,1)S(1)}, bf16[2,192,128]{2,1,0:T(8,128)(2,1)S(1)}, u32[]{:S(2)}, u32[]{:S(2)}) collective-permute-start(bf16[2,192,128]{2,1,0:T(8,128)(2,1)S(1)} %slice.127), channel_id=1, source_target_pairs={{0,8},{2,10},{4,12},{6,14},{8,0},{10,2},{12,4},{14,6},{16,24},{18,... | collective-permute-start | bytes 294920 | tf_op jit(solution)/shard_map/ppermute | solution.py:298
  85.6 9.5 %collective-permute-start.5 = (bf16[512,128]{1,0:T(8,128)(2,1)S(1)}, bf16[512,128]{1,0:T(8,128)(2,1)S(1)}, u32[]{:S(2)}, u32[]{:S(2)}) collective-permute-start(bf16[512,128]{1,0:T(8,128)(2,1)S(1)} %pad_maximum_fusion.3), channel_id=1, source_target_pairs={{0,8},{2,10},{4,12},{6,14},{8,0},{10,2},{12,4},{14,6},{16,24},{18,... | collective-permute-start | bytes 393224 | tf_op jit(solution)/shard_map/ppermute | solution.py:298
  88.2 5.7 %collective-permute-start.21 = (bf16[192,128]{1,0:T(8,128)(2,1)S(1)}, bf16[192,128]{1,0:T(8,128)(2,1)S(1)}, u32[]{:S(2)}, u32[]{:S(2)}) collective-permute-start(bf16[192,128]{1,0:T(8,128)(2,1)S(1)} %slice_bitcast_fusion.4), channel_id=1, source_target_pairs={{0,16},{2,18},{4,20},{6,22},{8,24},{10,26},{12,28},{14,30},{16,0},... | collective-permute-start | bytes 147464 | tf_op jit(solution)/shard_map/ppermute | solution.py:298
  89.2 11.6 %collective-permute-start.14 = (bf16[512,128]{1,0:T(8,128)(2,1)S(1)}, bf16[512,128]{1,0:T(8,128)(2,1)S(1)}, u32[]{:S(2)}, u32[]{:S(2)}) collective-permute-start(bf16[512,128]{1,0:T(8,128)(2,1)S(1)} %pad_maximum_fusion.4), channel_id=1, source_target_pairs={{0,8},{2,10},{4,12},{6,14},{8,0},{10,2},{12,4},{14,6},{16,24},{18,... | collective-permute-start | bytes 393224 | tf_op jit(solution)/shard_map/ppermute | solution.py:298
  93.9 5.1 %collective-permute-start.22 = (bf16[192,128]{1,0:T(8,128)(2,1)S(1)}, bf16[192,128]{1,0:T(8,128)(2,1)S(1)}, u32[]{:S(2)}, u32[]{:S(2)}) collective-permute-start(bf16[192,128]{1,0:T(8,128)(2,1)S(1)} %fusion.8), channel_id=1, source_target_pairs={{0,16},{2,18},{4,20},{6,22},{8,24},{10,26},{12,28},{14,30},{16,0},... | collective-permute-start | bytes 147464 | tf_op jit(solution)/shard_map/ppermute | solution.py:298
  95.2 8.7 %collective-permute-start.6 = (bf16[1024,128]{1,0:T(8,128)(2,1)S(1)}, bf16[1024,128]{1,0:T(8,128)(2,1)S(1)}, u32[]{:S(2)}, u32[]{:S(2)}) collective-permute-start(bf16[1024,128]{1,0:T(8,128)(2,1)S(1)} %pad_maximum_fusion.refs_2_), channel_id=1, source_target_pairs={{0,4},{2,6},{4,0},{6,2},{8,12},{10,14},{12,8},{14,10},{16,20},{18,... | collective-permute-start | bytes 786440 | tf_op jit(solution)/shard_map/ppermute | solution.py:298
  99.0 4.7 %collective-permute-start.23 = (bf16[384,128]{1,0:T(8,128)(2,1)S(1)}, bf16[384,128]{1,0:T(8,128)(2,1)S(1)}, u32[]{:S(2)}, u32[]{:S(2)}) collective-permute-start(bf16[384,128]{1,0:T(8,128)(2,1)S(1)} %pad_maximum_fusion.5), channel_id=1, source_target_pairs={{0,8},{2,10},{4,12},{6,14},{8,0},{10,2},{12,4},{14,6},{16,24},{18,... | collective-permute-start | bytes 294920 | tf_op jit(solution)/shard_map/ppermute | solution.py:298
  100.8 8.5 %collective-permute-start.15 = (bf16[1024,128]{1,0:T(8,128)(2,1)S(1)}, bf16[1024,128]{1,0:T(8,128)(2,1)S(1)}, u32[]{:S(2)}, u32[]{:S(2)}) collective-permute-start(bf16[1024,128]{1,0:T(8,128)(2,1)S(1)} %pad_maximum_fusion.1.refs_6_), channel_id=1, source_target_pairs={{0,4},{2,6},{4,0},{6,2},{8,12},{10,14},{12,8},{14,10},{16,20},{18,... | collective-permute-start | bytes 786440 | tf_op jit(solution)/shard_map/ppermute | solution.py:298
  101.1 8.2 %collective-permute-start.7 = (bf16[1024,128]{1,0:T(8,128)(2,1)S(1)}, bf16[1024,128]{1,0:T(8,128)(2,1)S(1)}, u32[]{:S(2)}, u32[]{:S(2)}) collective-permute-start(bf16[1024,128]{1,0:T(8,128)(2,1)S(1)} %pad_maximum_fusion.refs_2_), channel_id=1, source_target_pairs={{0,2},{2,0},{4,6},{6,4},{8,10},{10,8},{12,14},{14,12},{16,18},{18,... | collective-permute-start | bytes 786440 | tf_op jit(solution)/shard_map/ppermute | solution.py:298
  103.7 7.7 %collective-permute-start.24 = (bf16[768,128]{1,0:T(8,128)(2,1)S(1)}, bf16[768,128]{1,0:T(8,128)(2,1)S(1)}, u32[]{:S(2)}, u32[]{:S(2)}) collective-permute-start(bf16[768,128]{1,0:T(8,128)(2,1)S(1)} %pad_maximum_fusion.2.refs_10_), channel_id=1, source_target_pairs={{0,4},{2,6},{4,0},{6,2},{8,12},{10,14},{12,8},{14,10},{16,20},{18,... | collective-permute-start | bytes 589832 | tf_op jit(solution)/shard_map/ppermute | solution.py:298
  103.8 7.5 %collective-permute-start.16 = (bf16[1024,128]{1,0:T(8,128)(2,1)S(1)}, bf16[1024,128]{1,0:T(8,128)(2,1)S(1)}, u32[]{:S(2)}, u32[]{:S(2)}) collective-permute-start(bf16[1024,128]{1,0:T(8,128)(2,1)S(1)} %pad_maximum_fusion.1.refs_6_), channel_id=1, source_target_pairs={{0,2},{2,0},{4,6},{6,4},{8,10},{10,8},{12,14},{14,12},{16,18},{18,... | collective-permute-start | bytes 786440 | tf_op jit(solution)/shard_map/ppermute | solution.py:298
  103.9 7.6 %collective-permute-start.8 = (bf16[1024,128]{1,0:T(8,128)(2,1)S(1)}, bf16[1024,128]{1,0:T(8,128)(2,1)S(1)}, u32[]{:S(2)}, u32[]{:S(2)}) collective-permute-start(bf16[1024,128]{1,0:T(8,128)(2,1)S(1)} %collective-permute-done.6.refs_3_), channel_id=1, source_target_pairs={{0,2},{2,0},{4,6},{6,4},{8,10},{10,8},{12,14},{14,12},{16,18},{18,... | collective-permute-start | bytes 786440 | tf_op jit(solution)/shard_map/ppermute | solution.py:298
  135.2 25.4 %collective-permute-start.27 = (bf16[1024,512]{1,0:T(8,128)(2,1)}, bf16[1024,512]{1,0:T(8,128)(2,1)S(1)}, u32[]{:S(2)}, u32[]{:S(2)}) collective-permute-start(bf16[1024,512]{1,0:T(8,128)(2,1)} %mix.2.refs_21_), channel_id=1, source_target_pairs={{0,1},{1,0},{2,3},{3,2},{4,5},{5,4},{6,7},{7,6},{8,9},{9,8},{10,11... | collective-permute-start | bytes 3145736 | tf_op jit(solution)/shard_map/ppermute | solution.py:361
  (19 other events, 112.9 us)

commit v7 on v6

--- a/solution.py
+++ b/solution.py
@@ -67,71 +67,46 @@
 
 
 def states_kernel(
-    first, chunk, part, scale, index_ref, dirs_ref, weight_ref, mask_ref, freq_ref, pos_ref,
+    first, part, scale, index_ref, dirs_ref, weight_ref, mask_ref, freq_ref, pos_ref,
     qt_ref, kt_ref, v_ref, g_ref, *refs,
 ):
-    kept_ref, sent_ref, cos_ref, sin_ref, k_even, q_even, k_odd, q_odd, totals, slots = refs[-10:]
-    step = pl.program_id(0)
-    steps = pl.num_programs(0)
-    atoms = pos_ref.shape[1]
+    kept_ref, sent_ref, cos_ref, sin_ref, kr, qr, slots = refs[-7:]
+    group = first + pl.program_id(0)
     core, pair, quad = place_of(index_ref[0])
     freq = column(freq_ref[...]) * (1.0 / (2.0 * math.pi))
-
-    def rotate(which, bufs, start):
-        for at in range(start, start + chunk, part):
-            cols = slice(at, at + part)
-            for j in range(2):
-                i = 2 * which + j
-                u = (first + step) * GROUP + i
-                proj = (
-                    dirs_ref[0, u] * pos_ref[0:1, cols]
-                    + dirs_ref[1, u] * pos_ref[1:2, cols]
-                    + dirs_ref[2, u] * pos_ref[2:3, cols]
-                )
-                cosine, sine = cos_sin_turns(freq * proj)
-                cos_ref[i * QUARTER : (i + 1) * QUARTER, cols] = cosine.astype(BF16)
-                sin_ref[i * QUARTER : (i + 1) * QUARTER, cols] = sine.astype(BF16)
-                for src, dst in zip((kt_ref, qt_ref), bufs):
-                    for m in range(2):
-                        lead = src[QUARTER * m : QUARTER * (m + 1), cols].astype(F32)
-                        trail = src[QUARTER * (m + 2) : QUARTER * (m + 3), cols].astype(F32)
-                        row = j * LANES + QUARTER * m
-                        dst[row : row + QUARTER, cols] = (lead * cosine - trail * sine).astype(BF16)
-                        row = row + 2 * QUARTER
-                        dst[row : row + QUARTER, cols] = (lead * sine + trail * cosine).astype(BF16)
-
-    def multiply(bufs, start):
-        cols = slice(start, start + chunk)
-        for kind, (rot, other) in enumerate(zip(bufs, (v_ref, g_ref))):
-            term = jnp.dot(rot[:, cols], other[cols, :], preferred_element_type=F32)
-            totals[kind] = term if start == 0 else totals[kind] + term
-
-    def write(which, at_step):
-        for j in range(2):
-            u = (first + at_step) * GROUP + 2 * which + j
+    for start in range(0, pos_ref.shape[1], part):
+        cols = slice(start, start + part)
+        cosines, sines = [], []
+        for i in range(GROUP):
+            u = group * GROUP + i
+            proj = (
+                dirs_ref[0, u] * pos_ref[0:1, cols]
+                + dirs_ref[1, u] * pos_ref[1:2, cols]
+                + dirs_ref[2, u] * pos_ref[2:3, cols]
+            )
+            cosine, sine = cos_sin_turns(freq * proj)
+            cosines.append(cosine.astype(BF16))
+            sines.append(sine.astype(BF16))
+        cosine = jnp.concatenate(cosines, axis=0)
+        sine = jnp.concatenate(sines, axis=0)
+        cos_ref[:, cols] = cosine
+        sin_ref[:, cols] = sine
+        kr[:, cols] = rotated(kt_ref[:, cols], cosine, sine)
+        qr[:, cols] = rotated(qt_ref[:, cols], cosine, sine)
+
+    for kind, rot, other in ((0, kr, v_ref), (1, qr, g_ref)):
+        total = jnp.dot(rot[...], other[...], preferred_element_type=F32)
+        for i in range(GROUP):
+            u = group * GROUP + i
             coef = weight_ref[u] * mask_ref[u].astype(F32) * scale
-            rows = pl.ds(pl.multiple_of(at_step * 2 * QUARTER + j * QUARTER, QUARTER), QUARTER)
-            for kind in range(2):
-                for m in range(QUADS):
-                    row = j * LANES + m * QUARTER
-                    slots[kind ^ core, which ^ pair, slot_of(m, quad), rows, :] = (
-                        totals[kind, row : row + QUARTER, :] * coef
-                    ).astype(BF16)
-
-    even, odd = (k_even, q_even), (k_odd, q_odd)
-    for which, now, before in ((0, even, odd), (1, odd, even)):
-        for start in range(0, atoms, chunk):
-            multiply(before, start)
-            rotate(which, now, start)
-        write(1 - which, step if which == 1 else jnp.maximum(step - 1, 0))
-
-    @pl.when(step == steps - 1)
-    def _():
-        for start in range(0, atoms, chunk):
-            multiply(odd, start)
-        write(1, step)
-        kept_ref[...] = slots[0]
-        sent_ref[...] = slots[1]
+            rows = slice(i % 2 * QUARTER, (i % 2 + 1) * QUARTER)
+            for m in range(QUADS):
+                row = i * LANES + m * QUARTER
+                slots[kind ^ core, (i // 2) ^ pair, slot_of(m, quad), rows, :] = (
+                    total[row : row + QUARTER, :] * coef
+                ).astype(BF16)
+    kept_ref[...] = slots[0]
+    sent_ref[...] = slots[1]
 
 
 def rotated(x, cosine, sine):
@@ -264,6 +239,7 @@
 
     def make_states(first, groups, after, phases):
         sent = shape((2, QUADS, groups * 2 * QUARTER, feats), BF16)
+        sent_spec = pl.BlockSpec((2, QUADS, 2 * QUARTER, feats), lambda g: (0, 0, g, 0))
         phase = shape((total_groups * GROUP * QUARTER, atoms), BF16)
         phase_spec = pl.BlockSpec((GROUP * QUARTER, atoms), lambda g: (g + first, 0))
         operands = [
@@ -271,20 +247,14 @@
             values, cotangent, *after,
         ]
         kept, sent, *phases = pl.pallas_call(
-            functools.partial(
-                states_kernel, first, min(512, atoms), min(256, atoms),
-                1.0 / math.sqrt(feats * atoms),
-            ),
+            functools.partial(states_kernel, first, min(256, atoms), 1.0 / math.sqrt(feats * atoms)),
             grid=(groups,),
             in_specs=[smem] * 4 + [vmem] * 6 + [anywhere] * (len(after) + len(phases)),
-            out_specs=[vmem] * 2 + [phase_spec] * 2,
+            out_specs=[sent_spec] * 2 + [phase_spec] * 2,
             out_shape=[sent] * 2 + [phase] * 2,
             input_output_aliases={len(operands) + at: 2 + at for at in range(len(phases))},
-            scratch_shapes=[pltpu.VMEM((2 * LANES, atoms), BF16)] * 4
-            + [
-                pltpu.VMEM((2, 2 * LANES, feats), F32),
-                pltpu.VMEM((2, *sent.shape), BF16),
-            ],
+            scratch_shapes=[pltpu.VMEM((WIDTH, atoms), BF16)] * 2
+            + [pltpu.VMEM((2, 2, QUADS, 2 * QUARTER, feats), BF16)],
             compiler_params=params,
             cost_estimate=pl.CostEstimate(
                 flops=8 * groups * WIDTH * atoms * feats,
@@ -307,11 +277,11 @@
     def summed(kept, arrived, crossing_out):
         half = added(kept[0], arrived[0], by_bit(crossing_out, 2))
         near = added(half[:2], by_bit(half[2:], 4))
-        quarter = added(near[0], by_bit(near[1], 8))
-        whole = quarter
+        near = added(near, by_bit(near, 8)[::-1])
+        total = near
         for step in range(16, atom_devices, 16):
-            whole = added(whole, moved(quarter, lambda i: (i + step) % atom_devices))
-        near = jnp.concatenate([whole, by_bit(whole, 8)], axis=0)
+            total = added(total, moved(near, lambda i: (i + step) % atom_devices))
+        near = total.reshape(-1, feats)
         half = jnp.concatenate([near, by_bit(near, 4)], axis=0)
         other = by_bit(half, 2)
         return half, other, by_bit(half, 1), by_bit(other, 1)
@@ -360,8 +330,8 @@
     sent = mix(1 - mine, pieces, phases, BF16)
     theirs = lax.ppermute(sent, "dirs", [(0, 1), (1, 0)])
     ours = mix(mine, pieces, phases, F32, [sent])
-    total = (ours + theirs.astype(F32)).astype(BF16)
-    return tuple(total[:, at * feats : (at + 1) * feats] for at in range(4))
+    lanes = [slice(at * feats, (at + 1) * feats) for at in range(4)]
+    return tuple((ours[:, at] + theirs[:, at].astype(F32)).astype(BF16) for at in lanes)
 
 
 def solution(mesh):

time: 164 us -> 137 us (0.84)
  Pallas kernels: 99.5 us -> 76.2 us
  starting transfers between devices: 28.6 us -> 22.7 us
  waiting for transfers between devices: 27.3 us -> 29.6 us
    pallas_call x3, Pallas kernels: 51.7 us -> 28.3 us  [make_states(): pl.pallas_call(functools.partial(states_kernel, first, min(256, atoms), 1...]
    ppermute x27 -> x24, starting transfers between devices: 27 us -> 21.1 us  [moved(): lax.ppermute(x, 'atoms', [(i, target(i)) for i in range(atom_devices)])]
    ppermute x27 -> x24, waiting for transfers between devices: 25.8 us -> 28 us  [moved(): lax.ppermute(x, 'atoms', [(i, target(i)) for i in range(atom_devices)])]
  transfers between devices with their start and end apart: 28 -> 25, of which waited for: 11 -> 9; matrix products, arithmetic and copies ran while one was open for 2% -> 3% of each run, Pallas kernels for 34% -> 30%
where the time goes in v7:
time: 137 us; the launch traced here: 136 us
  Pallas kernels  76.2 us (56%)
  waiting for transfers between devices  29.6 us (22%)
  starting transfers between devices  22.7 us (17%)
  other arithmetic  6.18 us (5%)
    pallas_call x2, Pallas kernels, mix(): pl.pallas_call(lambda *refs: mix_kernel(CHUNKS, min(256, half_atoms), *re...  44.1 us
    pallas_call x3, Pallas kernels, make_states(): pl.pallas_call(functools.partial(states_kernel, first, min(256, atoms), 1...  28.3 us
    ppermute x24, waiting for transfers between devices, moved(): lax.ppermute(x, 'atoms', [(i, target(i)) for i in range(atom_devices)])  28 us
    ppermute x24, starting transfers between devices, moved(): lax.ppermute(x, 'atoms', [(i, target(i)) for i in range(atom_devices)])  21.1 us
    pallas_call x1, Pallas kernels, per_device(): pl.pallas_call(prepare_kernel, in_specs=[smem] + [vmem] * 7, out_specs=[v...  3.78 us
    convert_element_type x12, other arithmetic, added(): return sum((term.astype(F32) for term in terms)).astype(BF16)  3.51 us
  transfers between devices with their start and end apart: 25, of which 9 were waited for; matrix products, arithmetic and copies ran while one was open for 3% of the time, Pallas kernels for 30%

profile of v7, /device:TPU:0, one launch (start us, length us, event | category | flops | bytes accessed | tf_op | source)
XLA Modules:
  0.0 136.2 jit_solution(846261808133228675)
XLA Ops:
  0.6 3.8 %prepare.1 = (bf16[128,2048]{1,0:T(8,128)(2,1)}, bf16[128,2048]{1,0:T(8,128)(2,1)}, bf16[128,2048]{1,0:T(8,128)(2,1)}, bf16[128,2048]{1,0:T(8,128)(2,1)}, f32[128,2048]{1,0:T(8,128)}) custom-call(s32[1]{0:T(128)} %bitcast.index_ref.refs_0_, s32[1,2048]{1,0:T(1,128)} %bitcast.33, s32[1,2048]{1,0:T(1,128)} %bitcast.34, f32[5,128]{1,0:T(8,128)} %gain_ref.1, ...), custom_call_target="tpu_custom_call" | custom-call | tf_op jit(solution)/shard_map/prepare/pallas_call | solution.py:231
  4.4 10.0 %states.3 = (bf16[2,4,256,128]{3,2,1,0:T(8,128)(2,1)}, bf16[2,4,256,128]{3,2,1,0:T(8,128)(2,1)}, bf16[1408,2048]{1,0:T(8,128)(2,1)}, bf16[1408,2048]{1,0:T(8,128)(2,1)}) custom-call(s32[1]{0:T(128)} %bitcast.index_ref.refs_0_, f32[3,44]{1,0:T(4,128)} %dirs_ref.5, f32[44]{0:T(128)} %weight_ref.5, s32[44]{0:T(128)} %mask_ref.5, f32[1,32]{1,0:T(1,128)} %bitcast.35, ...), custom_call_target="tpu_custom_call" | custom-call | flops 4294967296 | bytes 8388608 | tf_op jit(solution)/shard_map/states/pallas_call | solution.py:249
  14.9 10.0 %states.4 = (bf16[2,4,256,128]{3,2,1,0:T(8,128)(2,1)}, bf16[2,4,256,128]{3,2,1,0:T(8,128)(2,1)}, bf16[1408,2048]{1,0:T(8,128)(2,1)}, bf16[1408,2048]{1,0:T(8,128)(2,1)}) custom-call(s32[1]{0:T(128)} %bitcast.index_ref.refs_0_, f32[3,44]{1,0:T(4,128)} %dirs_ref.5, f32[44]{0:T(128)} %weight_ref.5, ...), custom_call_target="tpu_custom_call", output_to_operand_aliasing={{2}: (10, {}), {3}: (11, {})} | custom-call | flops 4294967296 | bytes 8388608 | tf_op jit(solution)/shard_map/states/pallas_call | solution.py:249
  25.1 3.0 %collective-permute-start.1 = (bf16[4,256,128]{2,1,0:T(8,128)(2,1)S(1)}, bf16[4,256,128]{2,1,0:T(8,128)(2,1)S(1)}, u32[]{:S(2)}, u32[]{:S(2)}) collective-permute-start(bf16[4,256,128]{2,1,0:T(8,128)(2,1)S(1)} %fusion.7.refs_0_), channel_id=1, source_target_pairs={{0,4},{2,6},{4,0},{6,2},{8,12},{10,14},{12,8},{14,10},{16,20},{18,... | collective-permute-start | bytes 786440 | tf_op jit(solution)/shard_map/ppermute | solution.py:268
  29.1 1.7 %collective-permute-start.9 = (bf16[4,256,128]{2,1,0:T(8,128)(2,1)S(1)}, bf16[4,256,128]{2,1,0:T(8,128)(2,1)S(1)}, u32[]{:S(2)}, u32[]{:S(2)}) collective-permute-start(bf16[4,256,128]{2,1,0:T(8,128)(2,1)S(1)} %fusion.8), channel_id=1, source_target_pairs={{0,4},{2,6},{4,0},{6,2},{8,12},{10,14},{12,8},{14,10},{16,20},{18,... | collective-permute-start | bytes 786440 | tf_op jit(solution)/shard_map/ppermute | solution.py:268
  30.8 8.2 %states.5 = (bf16[2,4,192,128]{3,2,1,0:T(8,128)(2,1)}, bf16[2,4,192,128]{3,2,1,0:T(8,128)(2,1)}, bf16[1408,2048]{1,0:T(8,128)(2,1)}, bf16[1408,2048]{1,0:T(8,128)(2,1)}) custom-call(s32[1]{0:T(128)} %bitcast.index_ref.refs_0_, f32[3,44]{1,0:T(4,128)} %dirs_ref.5, f32[44]{0:T(128)} %weight_ref.5, ...), custom_call_target="tpu_custom_call", output_to_operand_aliasing={{2}: (11, {}), {3}: (12, {})} | custom-call | flops 3221225472 | bytes 6291456 | tf_op jit(solution)/shard_map/states/pallas_call | solution.py:249
  39.2 1.7 %collective-permute-start.2 = (bf16[2,256,128]{2,1,0:T(8,128)(2,1)S(1)}, bf16[2,256,128]{2,1,0:T(8,128)(2,1)S(1)}, u32[]{:S(2)}, u32[]{:S(2)}) collective-permute-start(bf16[2,256,128]{2,1,0:T(8,128)(2,1)S(1)} %slice.107), channel_id=1, source_target_pairs={{0,8},{2,10},{4,12},{6,14},{8,0},{10,2},{12,4},{14,6},{16,24},{18,... | collective-permute-start | bytes 393224 | tf_op jit(solution)/shard_map/ppermute | solution.py:268
  42.2 3.4 %collective-permute-done.2 = bf16[2,256,128]{2,1,0:T(8,128)(2,1)S(1)} collective-permute-done((bf16[2,256,128]{2,1,0:T(8,128)(2,1)S(1)}, bf16[2,256,128]{2,1,0:T(8,128)(2,1)S(1)}, u32[]{:S(2)}, u32[]{:S(2)}) %collective-permute-start.2) | collective-permute-done | bytes 131104 | tf_op jit(solution)/shard_map/ppermute | solution.py:268
  45.6 2.7 %collective-permute-start.3 = (bf16[2,256,128]{2,1,0:T(8,128)(2,1)S(1)}, bf16[2,256,128]{2,1,0:T(8,128)(2,1)S(1)}, u32[]{:S(2)}, u32[]{:S(2)}) collective-permute-start(bf16[2,256,128]{2,1,0:T(8,128)(2,1)S(1)} %add_convert_fusion.6), channel_id=1, source_target_pairs={{0,16},{2,18},{4,20},{6,22},{8,24},{10,26},{12,28},{14,30},{16,0},... | collective-permute-start | bytes 393224 | tf_op jit(solution)/shard_map/ppermute | solution.py:268
  48.4 2.8 %collective-permute-start.11 = (bf16[2,256,128]{2,1,0:T(8,128)(2,1)S(1)}, bf16[2,256,128]{2,1,0:T(8,128)(2,1)S(1)}, u32[]{:S(2)}, u32[]{:S(2)}) collective-permute-start(bf16[2,256,128]{2,1,0:T(8,128)(2,1)S(1)} %add_convert_fusion.4), channel_id=1, source_target_pairs={{0,16},{2,18},{4,20},{6,22},{8,24},{10,26},{12,28},{14,30},{16,0},... | collective-permute-start | bytes 393224 | tf_op jit(solution)/shard_map/ppermute | solution.py:268
  52.7 5.3 %collective-permute-done.3 = bf16[2,256,128]{2,1,0:T(8,128)(2,1)S(1)} collective-permute-done((bf16[2,256,128]{2,1,0:T(8,128)(2,1)S(1)}, bf16[2,256,128]{2,1,0:T(8,128)(2,1)S(1)}, u32[]{:S(2)}, u32[]{:S(2)}) %collective-permute-start.3) | collective-permute-done | bytes 131104 | tf_op jit(solution)/shard_map/ppermute | solution.py:268
  59.2 2.1 %collective-permute-start.18 = (bf16[2,192,128]{2,1,0:T(8,128)(2,1)S(1)}, bf16[2,192,128]{2,1,0:T(8,128)(2,1)S(1)}, u32[]{:S(2)}, u32[]{:S(2)}) collective-permute-start(bf16[2,192,128]{2,1,0:T(8,128)(2,1)S(1)} %slice.115), channel_id=1, source_target_pairs={{0,8},{2,10},{4,12},{6,14},{8,0},{10,2},{12,4},{14,6},{16,24},{18,... | collective-permute-start | bytes 294920 | tf_op jit(solution)/shard_map/ppermute | solution.py:268
  61.4 4.6 %collective-permute-done.18 = bf16[2,192,128]{2,1,0:T(8,128)(2,1)S(1)} collective-permute-done((bf16[2,192,128]{2,1,0:T(8,128)(2,1)S(1)}, bf16[2,192,128]{2,1,0:T(8,128)(2,1)S(1)}, u32[]{:S(2)}, u32[]{:S(2)}) %collective-permute-start.18) | collective-permute-done | bytes 98336 | tf_op jit(solution)/shard_map/ppermute | solution.py:268
  66.0 1.9 %collective-permute-start.19 = (bf16[2,192,128]{2,1,0:T(8,128)(2,1)S(1)}, bf16[2,192,128]{2,1,0:T(8,128)(2,1)S(1)}, u32[]{:S(2)}, u32[]{:S(2)}) collective-permute-start(bf16[2,192,128]{2,1,0:T(8,128)(2,1)S(1)} %add_convert_fusion.8), channel_id=1, source_target_pairs={{0,16},{2,18},{4,20},{6,22},{8,24},{10,26},{12,28},{14,30},{16,0},... | collective-permute-start | bytes 294920 | tf_op jit(solution)/shard_map/ppermute | solution.py:268
  68.6 4.1 %collective-permute-done.19 = bf16[2,192,128]{2,1,0:T(8,128)(2,1)S(1)} collective-permute-done((bf16[2,192,128]{2,1,0:T(8,128)(2,1)S(1)}, bf16[2,192,128]{2,1,0:T(8,128)(2,1)S(1)}, u32[]{:S(2)}, u32[]{:S(2)}) %collective-permute-start.19) | collective-permute-done | bytes 98336 | tf_op jit(solution)/shard_map/ppermute | solution.py:268
  73.5 3.9 %collective-permute-done.20 = bf16[384,128]{1,0:T(8,128)(2,1)S(1)} collective-permute-done((bf16[384,128]{1,0:T(8,128)(2,1)S(1)}, bf16[384,128]{1,0:T(8,128)(2,1)S(1)}, u32[]{:S(2)}, u32[]{:S(2)}) %collective-permute-start.20) | collective-permute-done | bytes 98336 | tf_op jit(solution)/shard_map/ppermute | solution.py:268
  78.4 3.7 %collective-permute-done.13.refs_7_ = bf16[1024,128]{1,0:T(8,128)(2,1)S(1)} collective-permute-done((bf16[1024,128]{1,0:T(8,128)(2,1)S(1)}, bf16[1024,128]{1,0:T(8,128)(2,1)S(1)}, u32[]{:S(2)}, u32[]{:S(2)}) %collective-permute-start.13) | collective-permute-done | bytes 262176 | tf_op jit(solution)/shard_map/ppermute | solution.py:268
  82.7 1.6 %collective-permute-done.21.refs_11_ = bf16[768,128]{1,0:T(8,128)(2,1)S(1)} collective-permute-done((bf16[768,128]{1,0:T(8,128)(2,1)S(1)}, bf16[768,128]{1,0:T(8,128)(2,1)S(1)}, u32[]{:S(2)}, u32[]{:S(2)}) %collective-permute-start.21) | collective-permute-done | bytes 196640 | tf_op jit(solution)/shard_map/ppermute | solution.py:268
  84.4 1.4 collective-permute-done.23.refs_13_
  86.4 21.7 %mix.2.refs_21_ = bf16[1024,512]{1,0:T(8,128)(2,1)} custom-call(s32[1]{0:T(128)} %bitcast.index_ref.refs_0_, s32[1]{0:T(128)} %bitcast.14.refs_1_, bf16[1024,128]{1,0:T(8,128)(2,1)} %copy-done.3, bf16[1024,128]{1,0:T(8,128)(2,1)} %copy-done.6, bf16[1024,128]{1,0:T(8,128)(2,1)} %copy-done.8, bf16[1024,128]{1,0:T(8,128)(2,1)} %copy-done.10, ...), custom_call_target="tpu_custom_call" | custom-call | flops 5905580032 | bytes 11534336 | tf_op jit(solution)/shard_map/mix/pallas_call | solution.py:294
  108.1 1.5 %collective-permute-start.24 = (bf16[1024,512]{1,0:T(8,128)(2,1)}, bf16[1024,512]{1,0:T(8,128)(2,1)S(1)}, u32[]{:S(2)}, u32[]{:S(2)}) collective-permute-start(bf16[1024,512]{1,0:T(8,128)(2,1)} %mix.2.refs_21_), channel_id=1, source_target_pairs={{0,1},{1,0},{2,3},{3,2},{4,5},{5,4},{6,7},{7,6},{8,9},{9,8},{10,11... | collective-permute-start | bytes 3145736 | tf_op jit(solution)/shard_map/ppermute | solution.py:331
  109.6 22.4 %mix.3 = f32[1024,512]{1,0:T(8,128)} custom-call(s32[1]{0:T(128)} %bitcast.index_ref.refs_0_, s32[1]{0:T(128)} %bitcast.1.refs_1_, bf16[1024,128]{1,0:T(8,128)(2,1)} %copy-done.3, bf16[1024,128]{1,0:T(8,128)(2,1)} %copy-done.6, bf16[1024,128]{1,0:T(8,128)(2,1)} %copy-done.8, bf16[1024,128]{1,0:T(8,128)(2,1)} %copy-done.10, bf16[1024,128]{1,0:T(8,128)(2,1)} %copy-done.4, ...), custom_call_target="tpu_custom_call" | custom-call | flops 5905580032 | bytes 11534336 | tf_op jit(solution)/shard_map/mix/pallas_call | solution.py:294
  132.1 1.5 %collective-permute-done.24 = bf16[1024,512]{1,0:T(8,128)(2,1)S(1)} collective-permute-done((bf16[1024,512]{1,0:T(8,128)(2,1)}, bf16[1024,512]{1,0:T(8,128)(2,1)S(1)}, u32[]{:S(2)}, u32[]{:S(2)}) %collective-permute-start.24) | collective-permute-done | bytes 1048608 | tf_op jit(solution)/shard_map/ppermute | solution.py:331
  133.6 2.6 %fusion = (bf16[1024,128]{1,0:T(8,128)(2,1)}, bf16[1024,128]{1,0:T(8,128)(2,1)}, bf16[1024,128]{1,0:T(8,128)(2,1)}, bf16[1024,128]{1,0:T(8,128)(2,1)}) fusion(f32[1024,512]{1,0:T(8,128)} %mix.3, bf16[1024,512]{1,0:T(8,128)(2,1)S(1)} %collective-permute-done.24), kind=kLoop, calls=%fused_computation.1 | loop fusion | flops 1572864 | bytes 4194304 | tf_op jit(solution)/shard_map/convert_element_type | solution.py:334
  (81 shorter events, 9.6 us)
Async XLA Ops:
  14.4 10.6 %collective-permute-start = (bf16[2,4,256,128]{3,2,1,0:T(8,128)(2,1)}, bf16[2,4,256,128]{3,2,1,0:T(8,128)(2,1)S(1)}, u32[]{:S(2)}, u32[]{:S(2)}) collective-permute-start(bf16[2,4,256,128]{3,2,1,0:T(8,128)(2,1)} %get-tuple-element.24), channel_id=1, source_target_pairs={{0,2},{2,0},{4,6},{6,4},{8,10},{10,8},{12,14},{14,12},{16,18},{18,... | collective-permute-start | bytes 1572872 | tf_op jit(solution)/shard_map/ppermute | solution.py:268
  24.9 3.2 %collective-permute-start.8 = (bf16[2,4,256,128]{3,2,1,0:T(8,128)(2,1)}, bf16[2,4,256,128]{3,2,1,0:T(8,128)(2,1)S(1)}, u32[]{:S(2)}, u32[]{:S(2)}) collective-permute-start(bf16[2,4,256,128]{3,2,1,0:T(8,128)(2,1)} %get-tuple-element.28), channel_id=1, source_target_pairs={{0,2},{2,0},{4,6},{6,4},{8,10},{10,8},{12,14},{14,12},{16,18},{18,... | collective-permute-start | bytes 1572872 | tf_op jit(solution)/shard_map/ppermute | solution.py:268
  25.1 14.0 %collective-permute-start.1 = (bf16[4,256,128]{2,1,0:T(8,128)(2,1)S(1)}, bf16[4,256,128]{2,1,0:T(8,128)(2,1)S(1)}, u32[]{:S(2)}, u32[]{:S(2)}) collective-permute-start(bf16[4,256,128]{2,1,0:T(8,128)(2,1)S(1)} %fusion.7.refs_0_), channel_id=1, source_target_pairs={{0,4},{2,6},{4,0},{6,2},{8,12},{10,14},{12,8},{14,10},{16,20},{18,... | collective-permute-start | bytes 786440 | tf_op jit(solution)/shard_map/ppermute | solution.py:268
  29.1 11.8 %collective-permute-start.9 = (bf16[4,256,128]{2,1,0:T(8,128)(2,1)S(1)}, bf16[4,256,128]{2,1,0:T(8,128)(2,1)S(1)}, u32[]{:S(2)}, u32[]{:S(2)}) collective-permute-start(bf16[4,256,128]{2,1,0:T(8,128)(2,1)S(1)} %fusion.8), channel_id=1, source_target_pairs={{0,4},{2,6},{4,0},{6,2},{8,12},{10,14},{12,8},{14,10},{16,20},{18,... | collective-permute-start | bytes 786440 | tf_op jit(solution)/shard_map/ppermute | solution.py:268
  39.0 12.1 %collective-permute-start.16 = (bf16[2,4,192,128]{3,2,1,0:T(8,128)(2,1)}, bf16[2,4,192,128]{3,2,1,0:T(8,128)(2,1)S(1)}, u32[]{:S(2)}, u32[]{:S(2)}) collective-permute-start(bf16[2,4,192,128]{3,2,1,0:T(8,128)(2,1)} %get-tuple-element.32), channel_id=1, source_target_pairs={{0,2},{2,0},{4,6},{6,4},{8,10},{10,8},{12,14},{14,12},{16,18},{18,... | collective-permute-start | bytes 1179656 | tf_op jit(solution)/shard_map/ppermute | solution.py:268
  39.2 6.4 %collective-permute-start.2 = (bf16[2,256,128]{2,1,0:T(8,128)(2,1)S(1)}, bf16[2,256,128]{2,1,0:T(8,128)(2,1)S(1)}, u32[]{:S(2)}, u32[]{:S(2)}) collective-permute-start(bf16[2,256,128]{2,1,0:T(8,128)(2,1)S(1)} %slice.107), channel_id=1, source_target_pairs={{0,8},{2,10},{4,12},{6,14},{8,0},{10,2},{12,4},{14,6},{16,24},{18,... | collective-permute-start | bytes 393224 | tf_op jit(solution)/shard_map/ppermute | solution.py:268
  41.0 7.3 %collective-permute-start.10 = (bf16[2,256,128]{2,1,0:T(8,128)(2,1)S(1)}, bf16[2,256,128]{2,1,0:T(8,128)(2,1)S(1)}, u32[]{:S(2)}, u32[]{:S(2)}) collective-permute-start(bf16[2,256,128]{2,1,0:T(8,128)(2,1)S(1)} %slice.111), channel_id=1, source_target_pairs={{0,8},{2,10},{4,12},{6,14},{8,0},{10,2},{12,4},{14,6},{16,24},{18,... | collective-permute-start | bytes 393224 | tf_op jit(solution)/shard_map/ppermute | solution.py:268
  45.6 12.4 %collective-permute-start.3 = (bf16[2,256,128]{2,1,0:T(8,128)(2,1)S(1)}, bf16[2,256,128]{2,1,0:T(8,128)(2,1)S(1)}, u32[]{:S(2)}, u32[]{:S(2)}) collective-permute-start(bf16[2,256,128]{2,1,0:T(8,128)(2,1)S(1)} %add_convert_fusion.6), channel_id=1, source_target_pairs={{0,16},{2,18},{4,20},{6,22},{8,24},{10,26},{12,28},{14,30},{16,0},... | collective-permute-start | bytes 393224 | tf_op jit(solution)/shard_map/ppermute | solution.py:268
  48.4 12.9 %collective-permute-start.11 = (bf16[2,256,128]{2,1,0:T(8,128)(2,1)S(1)}, bf16[2,256,128]{2,1,0:T(8,128)(2,1)S(1)}, u32[]{:S(2)}, u32[]{:S(2)}) collective-permute-start(bf16[2,256,128]{2,1,0:T(8,128)(2,1)S(1)} %add_convert_fusion.4), channel_id=1, source_target_pairs={{0,16},{2,18},{4,20},{6,22},{8,24},{10,26},{12,28},{14,30},{16,0},... | collective-permute-start | bytes 393224 | tf_op jit(solution)/shard_map/ppermute | solution.py:268
  52.1 6.0 %collective-permute-start.17 = (bf16[4,192,128]{2,1,0:T(8,128)(2,1)S(1)}, bf16[4,192,128]{2,1,0:T(8,128)(2,1)S(1)}, u32[]{:S(2)}, u32[]{:S(2)}) collective-permute-start(bf16[4,192,128]{2,1,0:T(8,128)(2,1)S(1)} %fusion.9), channel_id=1, source_target_pairs={{0,4},{2,6},{4,0},{6,2},{8,12},{10,14},{12,8},{14,10},{16,20},{18,... | collective-permute-start | bytes 589832 | tf_op jit(solution)/shard_map/ppermute | solution.py:268
  58.1 9.9 %collective-permute-start.4 = (bf16[512,128]{1,0:T(8,128)(2,1)S(1)}, bf16[512,128]{1,0:T(8,128)(2,1)S(1)}, u32[]{:S(2)}, u32[]{:S(2)}) collective-permute-start(bf16[512,128]{1,0:T(8,128)(2,1)S(1)} %bitcast.27), channel_id=1, source_target_pairs={{0,8},{2,10},{4,12},{6,14},{8,0},{10,2},{12,4},{14,6},{16,24},{18,... | collective-permute-start | bytes 393224 | tf_op jit(solution)/shard_map/ppermute | solution.py:268
  59.2 6.8 %collective-permute-start.18 = (bf16[2,192,128]{2,1,0:T(8,128)(2,1)S(1)}, bf16[2,192,128]{2,1,0:T(8,128)(2,1)S(1)}, u32[]{:S(2)}, u32[]{:S(2)}) collective-permute-start(bf16[2,192,128]{2,1,0:T(8,128)(2,1)S(1)} %slice.115), channel_id=1, source_target_pairs={{0,8},{2,10},{4,12},{6,14},{8,0},{10,2},{12,4},{14,6},{16,24},{18,... | collective-permute-start | bytes 294920 | tf_op jit(solution)/shard_map/ppermute | solution.py:268
  61.3 11.6 %collective-permute-start.12 = (bf16[512,128]{1,0:T(8,128)(2,1)S(1)}, bf16[512,128]{1,0:T(8,128)(2,1)S(1)}, u32[]{:S(2)}, u32[]{:S(2)}) collective-permute-start(bf16[512,128]{1,0:T(8,128)(2,1)S(1)} %bitcast.29), channel_id=1, source_target_pairs={{0,8},{2,10},{4,12},{6,14},{8,0},{10,2},{12,4},{14,6},{16,24},{18,... | collective-permute-start | bytes 393224 | tf_op jit(solution)/shard_map/ppermute | solution.py:268
  66.0 6.6 %collective-permute-start.19 = (bf16[2,192,128]{2,1,0:T(8,128)(2,1)S(1)}, bf16[2,192,128]{2,1,0:T(8,128)(2,1)S(1)}, u32[]{:S(2)}, u32[]{:S(2)}) collective-permute-start(bf16[2,192,128]{2,1,0:T(8,128)(2,1)S(1)} %add_convert_fusion.8), channel_id=1, source_target_pairs={{0,16},{2,18},{4,20},{6,22},{8,24},{10,26},{12,28},{14,30},{16,0},... | collective-permute-start | bytes 294920 | tf_op jit(solution)/shard_map/ppermute | solution.py:268
  68.0 9.9 %collective-permute-start.5 = (bf16[1024,128]{1,0:T(8,128)(2,1)S(1)}, bf16[1024,128]{1,0:T(8,128)(2,1)S(1)}, u32[]{:S(2)}, u32[]{:S(2)}) collective-permute-start(bf16[1024,128]{1,0:T(8,128)(2,1)S(1)} %pad_maximum_fusion.refs_2_), channel_id=1, source_target_pairs={{0,4},{2,6},{4,0},{6,2},{8,12},{10,14},{12,8},{14,10},{16,20},{18,... | collective-permute-start | bytes 786440 | tf_op jit(solution)/shard_map/ppermute | solution.py:268
  72.7 4.7 %collective-permute-start.20 = (bf16[384,128]{1,0:T(8,128)(2,1)S(1)}, bf16[384,128]{1,0:T(8,128)(2,1)S(1)}, u32[]{:S(2)}, u32[]{:S(2)}) collective-permute-start(bf16[384,128]{1,0:T(8,128)(2,1)S(1)} %bitcast.31), channel_id=1, source_target_pairs={{0,8},{2,10},{4,12},{6,14},{8,0},{10,2},{12,4},{14,6},{16,24},{18,... | collective-permute-start | bytes 294920 | tf_op jit(solution)/shard_map/ppermute | solution.py:268
  72.9 9.3 %collective-permute-start.13 = (bf16[1024,128]{1,0:T(8,128)(2,1)S(1)}, bf16[1024,128]{1,0:T(8,128)(2,1)S(1)}, u32[]{:S(2)}, u32[]{:S(2)}) collective-permute-start(bf16[1024,128]{1,0:T(8,128)(2,1)S(1)} %pad_maximum_fusion.1.refs_6_), channel_id=1, source_target_pairs={{0,4},{2,6},{4,0},{6,2},{8,12},{10,14},{12,8},{14,10},{16,20},{18,... | collective-permute-start | bytes 786440 | tf_op jit(solution)/shard_map/ppermute | solution.py:268
  73.5 8.7 %collective-permute-start.6 = (bf16[1024,128]{1,0:T(8,128)(2,1)S(1)}, bf16[1024,128]{1,0:T(8,128)(2,1)S(1)}, u32[]{:S(2)}, u32[]{:S(2)}) collective-permute-start(bf16[1024,128]{1,0:T(8,128)(2,1)S(1)} %pad_maximum_fusion.refs_2_), channel_id=1, source_target_pairs={{0,2},{2,0},{4,6},{6,4},{8,10},{10,8},{12,14},{14,12},{16,18},{18,... | collective-permute-start | bytes 786440 | tf_op jit(solution)/shard_map/ppermute | solution.py:268
  77.4 6.9 %collective-permute-start.21 = (bf16[768,128]{1,0:T(8,128)(2,1)S(1)}, bf16[768,128]{1,0:T(8,128)(2,1)S(1)}, u32[]{:S(2)}, u32[]{:S(2)}) collective-permute-start(bf16[768,128]{1,0:T(8,128)(2,1)S(1)} %pad_maximum_fusion.2.refs_10_), channel_id=1, source_target_pairs={{0,4},{2,6},{4,0},{6,2},{8,12},{10,14},{12,8},{14,10},{16,20},{18,... | collective-permute-start | bytes 589832 | tf_op jit(solution)/shard_map/ppermute | solution.py:268
  77.9 6.4 %collective-permute-start.14 = (bf16[1024,128]{1,0:T(8,128)(2,1)S(1)}, bf16[1024,128]{1,0:T(8,128)(2,1)S(1)}, u32[]{:S(2)}, u32[]{:S(2)}) collective-permute-start(bf16[1024,128]{1,0:T(8,128)(2,1)S(1)} %pad_maximum_fusion.1.refs_6_), channel_id=1, source_target_pairs={{0,2},{2,0},{4,6},{6,4},{8,10},{10,8},{12,14},{14,12},{16,18},{18,... | collective-permute-start | bytes 786440 | tf_op jit(solution)/shard_map/ppermute | solution.py:268
  77.9 6.4 %collective-permute-start.7 = (bf16[1024,128]{1,0:T(8,128)(2,1)S(1)}, bf16[1024,128]{1,0:T(8,128)(2,1)S(1)}, u32[]{:S(2)}, u32[]{:S(2)}) collective-permute-start(bf16[1024,128]{1,0:T(8,128)(2,1)S(1)} %collective-permute-done.5.refs_3_), channel_id=1, source_target_pairs={{0,2},{2,0},{4,6},{6,4},{8,10},{10,8},{12,14},{14,12},{16,18},{18,... | collective-permute-start | bytes 786440 | tf_op jit(solution)/shard_map/ppermute | solution.py:268
  82.2 2.2 %collective-permute-start.15 = (bf16[1024,128]{1,0:T(8,128)(2,1)S(1)}, bf16[1024,128]{1,0:T(8,128)(2,1)S(1)}, u32[]{:S(2)}, u32[]{:S(2)}) collective-permute-start(bf16[1024,128]{1,0:T(8,128)(2,1)S(1)} %collective-permute-done.13.refs_7_), channel_id=1, source_target_pairs={{0,2},{2,0},{4,6},{6,4},{8,10},{10,8},{12,14},{14,12},{16,18},{18,... | collective-permute-start | bytes 786440 | tf_op jit(solution)/shard_map/ppermute | solution.py:268
  82.2 2.1 %collective-permute-start.22 = (bf16[768,128]{1,0:T(8,128)(2,1)S(1)}, bf16[768,128]{1,0:T(8,128)(2,1)S(1)}, u32[]{:S(2)}, u32[]{:S(2)}) collective-permute-start(bf16[768,128]{1,0:T(8,128)(2,1)S(1)} %pad_maximum_fusion.2.refs_10_), channel_id=1, source_target_pairs={{0,2},{2,0},{4,6},{6,4},{8,10},{10,8},{12,14},{14,12},{16,18},{18,... | collective-permute-start | bytes 589832 | tf_op jit(solution)/shard_map/ppermute | solution.py:268
  108.1 25.5 %collective-permute-start.24 = (bf16[1024,512]{1,0:T(8,128)(2,1)}, bf16[1024,512]{1,0:T(8,128)(2,1)S(1)}, u32[]{:S(2)}, u32[]{:S(2)}) collective-permute-start(bf16[1024,512]{1,0:T(8,128)(2,1)} %mix.2.refs_21_), channel_id=1, source_target_pairs={{0,1},{1,0},{2,3},{3,2},{4,5},{5,4},{6,7},{7,6},{8,9},{9,8},{10,11... | collective-permute-start | bytes 3145736 | tf_op jit(solution)/shard_map/ppermute | solution.py:331
  (16 other events, 89.3 us)

commit v8 on v7

--- a/solution.py
+++ b/solution.py
@@ -16,7 +16,7 @@
 QUARTER = LANES // QUADS
 WIDTH = GROUP * LANES
 VMEM_LIMIT = 56 * 2**20
-CHUNKS = (4, 4, 3)
+CHUNKS = (5, 4, 2)
 
 SIN_COEF = (4.4428679, -7.30744342, 3.59478808, -0.78437403)
 COS_COEF = (1.41420408, -6.97764206, 5.71523839, -1.72834866)
@@ -181,24 +181,23 @@
             )
         if start != starts[-1]:
             next_back = backs(starts[at + 1])
-        cosine = cos_ref[:, cols].astype(F32)
-        sine = sin_ref[:, cols].astype(F32)
+        cosine = cos_ref[:, cols]
+        sine = sin_ref[:, cols]
         for kind, total in ((0, totals[1]), (1, totals[2])):
+            lower = back[kind].astype(BF16)
             for m in range(2):
-                lead_rows = slice(QUARTER * m, QUARTER * (m + 1))
-                trail_rows = slice(QUARTER * (m + 2), QUARTER * (m + 3))
-                lead_total = total[lead_rows, cols]
-                trail_total = total[trail_rows, cols]
+                leads, trails = [], []
                 for i in range(GROUP):
                     c = cosine[i * QUARTER : (i + 1) * QUARTER]
                     s = sine[i * QUARTER : (i + 1) * QUARTER]
                     row = i * LANES + QUARTER * m
-                    lead = back[kind][row : row + QUARTER, :]
-                    trail = back[kind][row + 2 * QUARTER : row + 3 * QUARTER, :]
-                    lead_total = lead_total + (lead * c + trail * s)
-                    trail_total = trail_total + (trail * c - lead * s)
-                total[lead_rows, cols] = lead_total
-                total[trail_rows, cols] = trail_total
+                    lead = lower[row : row + QUARTER, :]
+                    trail = lower[row + 2 * QUARTER : row + 3 * QUARTER, :]
+                    leads.append(lead * c + trail * s)
+                    trails.append(trail * c - lead * s)
+                for block, terms in ((m, leads), (m + 2, trails)):
+                    rows = slice(QUARTER * block, QUARTER * (block + 1))
+                    total[rows, cols] += ((terms[0] + terms[1]) + (terms[2] + terms[3])).astype(F32)
         if start != starts[-1]:
             back, turned = next_back, turn(starts[at + 1])
 

time: 137 us -> 145 us (1.058)
  waiting for transfers between devices: 29.6 us -> 39.6 us
  Pallas kernels: 76.2 us -> 70.2 us
  starting transfers between devices: 22.7 us -> 25 us
  other arithmetic: 6.18 us -> 7.82 us
    ppermute x24, waiting for transfers between devices: 28 us -> 35.1 us  [moved(): lax.ppermute(x, 'atoms', [(i, target(i)) for i in range(atom_devices)])]
    pallas_call x2, Pallas kernels: 44.1 us -> 38.1 us  [mix(): pl.pallas_call(lambda *refs: mix_kernel(CHUNKS, min(256, half_atoms), *re...]
    ppermute x1, waiting for transfers between devices: 1.55 us -> 4.55 us  [per_device(): theirs = lax.ppermute(sent, 'dirs', [(0, 1), (1, 0)])]
    ppermute x24, starting transfers between devices: 21.1 us -> 23.5 us  [moved(): lax.ppermute(x, 'atoms', [(i, target(i)) for i in range(atom_devices)])]
    convert_element_type x12, other arithmetic: 3.51 us -> 5.15 us  [added(): return sum((term.astype(F32) for term in terms)).astype(BF16)]
  transfers between devices with their start and end apart: 25 -> 25, of which waited for: 9 -> 14; matrix products, arithmetic and copies ran while one was open for 3% -> 3% of each run, Pallas kernels for 30% -> 18%
where the time goes in v8:
time: 145 us; the launch traced here: 144 us
  Pallas kernels  70.2 us (48%)
  waiting for transfers between devices  39.6 us (27%)
  starting transfers between devices  25 us (17%)
  other arithmetic  7.82 us (5%)
    pallas_call x2, Pallas kernels, mix(): pl.pallas_call(lambda *refs: mix_kernel(CHUNKS, min(256, half_atoms), *re...  38.1 us
    ppermute x24, waiting for transfers between devices, moved(): lax.ppermute(x, 'atoms', [(i, target(i)) for i in range(atom_devices)])  35.1 us
    pallas_call x3, Pallas kernels, make_states(): pl.pallas_call(functools.partial(states_kernel, first, min(256, atoms), 1...  28.3 us
    ppermute x24, starting transfers between devices, moved(): lax.ppermute(x, 'atoms', [(i, target(i)) for i in range(atom_devices)])  23.5 us
    convert_element_type x12, other arithmetic, added(): return sum((term.astype(F32) for term in terms)).astype(BF16)  5.15 us
    ppermute x1, waiting for transfers between devices, per_device(): theirs = lax.ppermute(sent, 'dirs', [(0, 1), (1, 0)])  4.55 us
    pallas_call x1, Pallas kernels, per_device(): pl.pallas_call(prepare_kernel, in_specs=[smem] + [vmem] * 7, out_specs=[v...  3.78 us
  transfers between devices with their start and end apart: 25, of which 14 were waited for; matrix products, arithmetic and copies ran while one was open for 3% of the time, Pallas kernels for 18%

profile of v8, /device:TPU:0, one launch (start us, length us, event | category | flops | bytes accessed | tf_op | source)
XLA Modules:
  0.0 144.5 jit_solution(2309296372083003031)
XLA Ops:
  0.6 3.8 %prepare.1 = (bf16[128,2048]{1,0:T(8,128)(2,1)}, bf16[128,2048]{1,0:T(8,128)(2,1)}, bf16[128,2048]{1,0:T(8,128)(2,1)}, bf16[128,2048]{1,0:T(8,128)(2,1)}, f32[128,2048]{1,0:T(8,128)}) custom-call(s32[1]{0:T(128)} %bitcast.index_ref.refs_0_, s32[1,2048]{1,0:T(1,128)} %bitcast.33, s32[1,2048]{1,0:T(1,128)} %bitcast.34, f32[5,128]{1,0:T(8,128)} %gain_ref.1, ...), custom_call_target="tpu_custom_call" | custom-call | tf_op jit(solution)/shard_map/prepare/pallas_call | solution.py:230
  4.4 11.9 %states.3 = (bf16[2,4,320,128]{3,2,1,0:T(8,128)(2,1)}, bf16[2,4,320,128]{3,2,1,0:T(8,128)(2,1)}, bf16[1408,2048]{1,0:T(8,128)(2,1)}, bf16[1408,2048]{1,0:T(8,128)(2,1)}) custom-call(s32[1]{0:T(128)} %bitcast.index_ref.refs_0_, f32[3,44]{1,0:T(4,128)} %dirs_ref.5, f32[44]{0:T(128)} %weight_ref.5, s32[44]{0:T(128)} %mask_ref.5, f32[1,32]{1,0:T(1,128)} %bitcast.35, ...), custom_call_target="tpu_custom_call" | custom-call | flops 5368709120 | bytes 10485760 | tf_op jit(solution)/shard_map/states/pallas_call | solution.py:248
  16.3 10.1 %states.4 = (bf16[2,4,256,128]{3,2,1,0:T(8,128)(2,1)}, bf16[2,4,256,128]{3,2,1,0:T(8,128)(2,1)}, bf16[1408,2048]{1,0:T(8,128)(2,1)}, bf16[1408,2048]{1,0:T(8,128)(2,1)}) custom-call(s32[1]{0:T(128)} %bitcast.index_ref.refs_0_, f32[3,44]{1,0:T(4,128)} %dirs_ref.5, f32[44]{0:T(128)} %weight_ref.5, ...), custom_call_target="tpu_custom_call", output_to_operand_aliasing={{2}: (10, {}), {3}: (11, {})} | custom-call | flops 4294967296 | bytes 8388608 | tf_op jit(solution)/shard_map/states/pallas_call | solution.py:248
  26.9 1.7 %collective-permute-done.8 = bf16[2,4,256,128]{3,2,1,0:T(8,128)(2,1)S(1)} collective-permute-done((bf16[2,4,256,128]{3,2,1,0:T(8,128)(2,1)}, bf16[2,4,256,128]{3,2,1,0:T(8,128)(2,1)S(1)}, u32[]{:S(2)}, u32[]{:S(2)}) %collective-permute-start.8) | collective-permute-done | bytes 524320 | tf_op jit(solution)/shard_map/ppermute | solution.py:267
  29.6 2.9 %collective-permute-start.9 = (bf16[4,256,128]{2,1,0:T(8,128)(2,1)S(1)}, bf16[4,256,128]{2,1,0:T(8,128)(2,1)S(1)}, u32[]{:S(2)}, u32[]{:S(2)}) collective-permute-start(bf16[4,256,128]{2,1,0:T(8,128)(2,1)S(1)} %fusion.7), channel_id=1, source_target_pairs={{0,4},{2,6},{4,0},{6,2},{8,12},{10,14},{12,8},{14,10},{16,20},{18,... | collective-permute-start | bytes 786440 | tf_op jit(solution)/shard_map/ppermute | solution.py:267
  33.4 5.8 %collective-permute-done.9 = bf16[4,256,128]{2,1,0:T(8,128)(2,1)S(1)} collective-permute-done((bf16[4,256,128]{2,1,0:T(8,128)(2,1)S(1)}, bf16[4,256,128]{2,1,0:T(8,128)(2,1)S(1)}, u32[]{:S(2)}, u32[]{:S(2)}) %collective-permute-start.9) | collective-permute-done | bytes 262176 | tf_op jit(solution)/shard_map/ppermute | solution.py:267
  40.3 1.9 %collective-permute-start.10 = (bf16[2,256,128]{2,1,0:T(8,128)(2,1)S(1)}, bf16[2,256,128]{2,1,0:T(8,128)(2,1)S(1)}, u32[]{:S(2)}, u32[]{:S(2)}) collective-permute-start(bf16[2,256,128]{2,1,0:T(8,128)(2,1)S(1)} %slice.111), channel_id=1, source_target_pairs={{0,8},{2,10},{4,12},{6,14},{8,0},{10,2},{12,4},{14,6},{16,24},{18,... | collective-permute-start | bytes 393224 | tf_op jit(solution)/shard_map/ppermute | solution.py:267
  42.2 6.3 %states.5 = (bf16[2,4,128,128]{3,2,1,0:T(8,128)(2,1)}, bf16[2,4,128,128]{3,2,1,0:T(8,128)(2,1)}, bf16[1408,2048]{1,0:T(8,128)(2,1)}, bf16[1408,2048]{1,0:T(8,128)(2,1)}) custom-call(s32[1]{0:T(128)} %bitcast.index_ref.refs_0_, f32[3,44]{1,0:T(4,128)} %dirs_ref.5, f32[44]{0:T(128)} %weight_ref.5, ...), custom_call_target="tpu_custom_call", output_to_operand_aliasing={{2}: (11, {}), {3}: (12, {})} | custom-call | flops 2147483648 | bytes 4194304 | tf_op jit(solution)/shard_map/states/pallas_call | solution.py:248
  50.1 2.7 %collective-permute-start.11 = (bf16[2,256,128]{2,1,0:T(8,128)(2,1)S(1)}, bf16[2,256,128]{2,1,0:T(8,128)(2,1)S(1)}, u32[]{:S(2)}, u32[]{:S(2)}) collective-permute-start(bf16[2,256,128]{2,1,0:T(8,128)(2,1)S(1)} %add_convert_fusion.6), channel_id=1, source_target_pairs={{0,16},{2,18},{4,20},{6,22},{8,24},{10,26},{12,28},{14,30},{16,0},... | collective-permute-start | bytes 393224 | tf_op jit(solution)/shard_map/ppermute | solution.py:267
  54.3 4.8 %collective-permute-done.1 = bf16[4,320,128]{2,1,0:T(8,128)(2,1)S(1)} collective-permute-done((bf16[4,320,128]{2,1,0:T(8,128)(2,1)S(1)}, bf16[4,320,128]{2,1,0:T(8,128)(2,1)S(1)}, u32[]{:S(2)}, u32[]{:S(2)}) %collective-permute-start.1) | collective-permute-done | bytes 327712 | tf_op jit(solution)/shard_map/ppermute | solution.py:267
  59.5 1.9 %collective-permute-start.12 = (bf16[512,128]{1,0:T(8,128)(2,1)S(1)}, bf16[512,128]{1,0:T(8,128)(2,1)S(1)}, u32[]{:S(2)}, u32[]{:S(2)}) collective-permute-start(bf16[512,128]{1,0:T(8,128)(2,1)S(1)} %bitcast.29), channel_id=1, source_target_pairs={{0,8},{2,10},{4,12},{6,14},{8,0},{10,2},{12,4},{14,6},{16,24},{18,... | collective-permute-start | bytes 393224 | tf_op jit(solution)/shard_map/ppermute | solution.py:267
  61.4 4.6 %collective-permute-done.2 = bf16[2,320,128]{2,1,0:T(8,128)(2,1)S(1)} collective-permute-done((bf16[2,320,128]{2,1,0:T(8,128)(2,1)S(1)}, bf16[2,320,128]{2,1,0:T(8,128)(2,1)S(1)}, u32[]{:S(2)}, u32[]{:S(2)}) %collective-permute-start.2) | collective-permute-done | bytes 163872 | tf_op jit(solution)/shard_map/ppermute | solution.py:267
  66.1 3.1 %collective-permute-start.3 = (bf16[2,320,128]{2,1,0:T(8,128)(2,1)S(1)}, bf16[2,320,128]{2,1,0:T(8,128)(2,1)S(1)}, u32[]{:S(2)}, u32[]{:S(2)}) collective-permute-start(bf16[2,320,128]{2,1,0:T(8,128)(2,1)S(1)} %add_convert_fusion.3), channel_id=1, source_target_pairs={{0,16},{2,18},{4,20},{6,22},{8,24},{10,26},{12,28},{14,30},{16,0},... | collective-permute-start | bytes 491528 | tf_op jit(solution)/shard_map/ppermute | solution.py:267
  70.2 4.3 %collective-permute-done.3 = bf16[2,320,128]{2,1,0:T(8,128)(2,1)S(1)} collective-permute-done((bf16[2,320,128]{2,1,0:T(8,128)(2,1)S(1)}, bf16[2,320,128]{2,1,0:T(8,128)(2,1)S(1)}, u32[]{:S(2)}, u32[]{:S(2)}) %collective-permute-start.3) | collective-permute-done | bytes 163872 | tf_op jit(solution)/shard_map/ppermute | solution.py:267
  74.8 1.6 %collective-permute-done.18 = bf16[2,128,128]{2,1,0:T(8,128)(2,1)S(1)} collective-permute-done((bf16[2,128,128]{2,1,0:T(8,128)(2,1)S(1)}, bf16[2,128,128]{2,1,0:T(8,128)(2,1)S(1)}, u32[]{:S(2)}, u32[]{:S(2)}) %collective-permute-start.18) | collective-permute-done | bytes 65568 | tf_op jit(solution)/shard_map/ppermute | solution.py:267
  77.6 2.3 %collective-permute-done.4 = bf16[640,128]{1,0:T(8,128)(2,1)S(1)} collective-permute-done((bf16[640,128]{1,0:T(8,128)(2,1)S(1)}, bf16[640,128]{1,0:T(8,128)(2,1)S(1)}, u32[]{:S(2)}, u32[]{:S(2)}) %collective-permute-start.4) | collective-permute-done | bytes 163872 | tf_op jit(solution)/shard_map/ppermute | solution.py:267
  80.0 1.9 %collective-permute-start.5 = (bf16[1280,128]{1,0:T(8,128)(2,1)S(1)}, bf16[1280,128]{1,0:T(8,128)(2,1)S(1)}, u32[]{:S(2)}, u32[]{:S(2)}) collective-permute-start(bf16[1280,128]{1,0:T(8,128)(2,1)S(1)} %pad_maximum_fusion.refs_2_), channel_id=1, source_target_pairs={{0,4},{2,6},{4,0},{6,2},{8,12},{10,14},{12,8},{14,10},{16,20},{18,... | collective-permute-start | bytes 983048 | tf_op jit(solution)/shard_map/ppermute | solution.py:267
  84.3 2.3 %collective-permute-done.20 = bf16[256,128]{1,0:T(8,128)(2,1)S(1)} collective-permute-done((bf16[256,128]{1,0:T(8,128)(2,1)S(1)}, bf16[256,128]{1,0:T(8,128)(2,1)S(1)}, u32[]{:S(2)}, u32[]{:S(2)}) %collective-permute-start.20) | collective-permute-done | bytes 65568 | tf_op jit(solution)/shard_map/ppermute | solution.py:267
  88.1 2.3 %collective-permute-done.5.refs_3_ = bf16[1280,128]{1,0:T(8,128)(2,1)S(1)} collective-permute-done((bf16[1280,128]{1,0:T(8,128)(2,1)S(1)}, bf16[1280,128]{1,0:T(8,128)(2,1)S(1)}, u32[]{:S(2)}, u32[]{:S(2)}) %collective-permute-start.5) | collective-permute-done | bytes 327712 | tf_op jit(solution)/shard_map/ppermute | solution.py:267
  90.9 3.7 %collective-permute-done.21.refs_11_ = bf16[512,128]{1,0:T(8,128)(2,1)S(1)} collective-permute-done((bf16[512,128]{1,0:T(8,128)(2,1)S(1)}, bf16[512,128]{1,0:T(8,128)(2,1)S(1)}, u32[]{:S(2)}, u32[]{:S(2)}) %collective-permute-start.21) | collective-permute-done | bytes 131104 | tf_op jit(solution)/shard_map/ppermute | solution.py:267
  97.7 18.7 %mix.2.refs_21_ = bf16[1024,512]{1,0:T(8,128)(2,1)} custom-call(s32[1]{0:T(128)} %bitcast.index_ref.refs_0_, s32[1]{0:T(128)} %bitcast.14.refs_1_, bf16[1280,128]{1,0:T(8,128)(2,1)} %copy-done.2, bf16[1280,128]{1,0:T(8,128)(2,1)} %copy-done.6, bf16[1280,128]{1,0:T(8,128)(2,1)} %copy-done.7, bf16[1280,128]{1,0:T(8,128)(2,1)} %copy-done.8, ...), custom_call_target="tpu_custom_call" | custom-call | flops 5905580032 | bytes 11534336 | tf_op jit(solution)/shard_map/mix/pallas_call | solution.py:293
  118.0 19.4 %mix.3 = f32[1024,512]{1,0:T(8,128)} custom-call(s32[1]{0:T(128)} %bitcast.index_ref.refs_0_, s32[1]{0:T(128)} %bitcast.1.refs_1_, bf16[1280,128]{1,0:T(8,128)(2,1)} %copy-done.2, bf16[1280,128]{1,0:T(8,128)(2,1)} %copy-done.6, bf16[1280,128]{1,0:T(8,128)(2,1)} %copy-done.7, bf16[1280,128]{1,0:T(8,128)(2,1)} %copy-done.8, bf16[1024,128]{1,0:T(8,128)(2,1)} %copy-done.3, ...), custom_call_target="tpu_custom_call" | custom-call | flops 5905580032 | bytes 11534336 | tf_op jit(solution)/shard_map/mix/pallas_call | solution.py:293
  137.3 4.5 %collective-permute-done.24 = bf16[1024,512]{1,0:T(8,128)(2,1)S(1)} collective-permute-done((bf16[1024,512]{1,0:T(8,128)(2,1)}, bf16[1024,512]{1,0:T(8,128)(2,1)S(1)}, u32[]{:S(2)}, u32[]{:S(2)}) %collective-permute-start.24) | collective-permute-done | bytes 1048608 | tf_op jit(solution)/shard_map/ppermute | solution.py:330
  141.9 2.6 %fusion.1 = (bf16[1024,128]{1,0:T(8,128)(2,1)}, bf16[1024,128]{1,0:T(8,128)(2,1)}, bf16[1024,128]{1,0:T(8,128)(2,1)}, bf16[1024,128]{1,0:T(8,128)(2,1)}) fusion(f32[1024,512]{1,0:T(8,128)} %mix.3, bf16[1024,512]{1,0:T(8,128)(2,1)S(1)} %collective-permute-done.24), kind=kLoop, calls=%fused_computation.4 | loop fusion | flops 1572864 | bytes 4194304 | tf_op jit(solution)/shard_map/convert_element_type | solution.py:333
  (81 shorter events, 18.5 us)
Async XLA Ops:
  26.4 2.2 %collective-permute-start.8 = (bf16[2,4,256,128]{3,2,1,0:T(8,128)(2,1)}, bf16[2,4,256,128]{3,2,1,0:T(8,128)(2,1)S(1)}, u32[]{:S(2)}, u32[]{:S(2)}) collective-permute-start(bf16[2,4,256,128]{3,2,1,0:T(8,128)(2,1)} %get-tuple-element.28), channel_id=1, source_target_pairs={{0,2},{2,0},{4,6},{6,4},{8,10},{10,8},{12,14},{14,12},{16,18},{18,... | collective-permute-start | bytes 1572872 | tf_op jit(solution)/shard_map/ppermute | solution.py:267
  26.9 5.7 %collective-permute-start = (bf16[2,4,320,128]{3,2,1,0:T(8,128)(2,1)S(1)}, bf16[2,4,320,128]{3,2,1,0:T(8,128)(2,1)S(1)}, u32[]{:S(2)}, u32[]{:S(2)}) collective-permute-start(bf16[2,4,320,128]{3,2,1,0:T(8,128)(2,1)S(1)} %copy-done.5), channel_id=1, source_target_pairs={{0,2},{2,0},{4,6},{6,4},{8,10},{10,8},{12,14},{14,12},{16,18},{18,... | collective-permute-start | bytes 1966088 | tf_op jit(solution)/shard_map/ppermute | solution.py:267
  29.6 9.5 %collective-permute-start.9 = (bf16[4,256,128]{2,1,0:T(8,128)(2,1)S(1)}, bf16[4,256,128]{2,1,0:T(8,128)(2,1)S(1)}, u32[]{:S(2)}, u32[]{:S(2)}) collective-permute-start(bf16[4,256,128]{2,1,0:T(8,128)(2,1)S(1)} %fusion.7), channel_id=1, source_target_pairs={{0,4},{2,6},{4,0},{6,2},{8,12},{10,14},{12,8},{14,10},{16,20},{18,... | collective-permute-start | bytes 786440 | tf_op jit(solution)/shard_map/ppermute | solution.py:267
  40.3 9.8 %collective-permute-start.10 = (bf16[2,256,128]{2,1,0:T(8,128)(2,1)S(1)}, bf16[2,256,128]{2,1,0:T(8,128)(2,1)S(1)}, u32[]{:S(2)}, u32[]{:S(2)}) collective-permute-start(bf16[2,256,128]{2,1,0:T(8,128)(2,1)S(1)} %slice.111), channel_id=1, source_target_pairs={{0,8},{2,10},{4,12},{6,14},{8,0},{10,2},{12,4},{14,6},{16,24},{18,... | collective-permute-start | bytes 393224 | tf_op jit(solution)/shard_map/ppermute | solution.py:267
  48.5 4.3 %collective-permute-start.16 = (bf16[2,4,128,128]{3,2,1,0:T(8,128)(2,1)}, bf16[2,4,128,128]{3,2,1,0:T(8,128)(2,1)S(1)}, u32[]{:S(2)}, u32[]{:S(2)}) collective-permute-start(bf16[2,4,128,128]{3,2,1,0:T(8,128)(2,1)} %get-tuple-element.32), channel_id=1, source_target_pairs={{0,2},{2,0},{4,6},{6,4},{8,10},{10,8},{12,14},{14,12},{16,18},{18,... | collective-permute-start | bytes 786440 | tf_op jit(solution)/shard_map/ppermute | solution.py:267
  48.5 10.6 %collective-permute-start.1 = (bf16[4,320,128]{2,1,0:T(8,128)(2,1)S(1)}, bf16[4,320,128]{2,1,0:T(8,128)(2,1)S(1)}, u32[]{:S(2)}, u32[]{:S(2)}) collective-permute-start(bf16[4,320,128]{2,1,0:T(8,128)(2,1)S(1)} %copy-done), channel_id=1, source_target_pairs={{0,4},{2,6},{4,0},{6,2},{8,12},{10,14},{12,8},{14,10},{16,20},{18,... | collective-permute-start | bytes 983048 | tf_op jit(solution)/shard_map/ppermute | solution.py:267
  50.1 9.4 %collective-permute-start.11 = (bf16[2,256,128]{2,1,0:T(8,128)(2,1)S(1)}, bf16[2,256,128]{2,1,0:T(8,128)(2,1)S(1)}, u32[]{:S(2)}, u32[]{:S(2)}) collective-permute-start(bf16[2,256,128]{2,1,0:T(8,128)(2,1)S(1)} %add_convert_fusion.6), channel_id=1, source_target_pairs={{0,16},{2,18},{4,20},{6,22},{8,24},{10,26},{12,28},{14,30},{16,0},... | collective-permute-start | bytes 393224 | tf_op jit(solution)/shard_map/ppermute | solution.py:267
  53.7 15.4 %collective-permute-start.17 = (bf16[4,128,128]{2,1,0:T(8,128)(2,1)S(1)}, bf16[4,128,128]{2,1,0:T(8,128)(2,1)S(1)}, u32[]{:S(2)}, u32[]{:S(2)}) collective-permute-start(bf16[4,128,128]{2,1,0:T(8,128)(2,1)S(1)} %fusion.9), channel_id=1, source_target_pairs={{0,4},{2,6},{4,0},{6,2},{8,12},{10,14},{12,8},{14,10},{16,20},{18,... | collective-permute-start | bytes 393224 | tf_op jit(solution)/shard_map/ppermute | solution.py:267
  59.2 6.8 %collective-permute-start.2 = (bf16[2,320,128]{2,1,0:T(8,128)(2,1)S(1)}, bf16[2,320,128]{2,1,0:T(8,128)(2,1)S(1)}, u32[]{:S(2)}, u32[]{:S(2)}) collective-permute-start(bf16[2,320,128]{2,1,0:T(8,128)(2,1)S(1)} %slice.107), channel_id=1, source_target_pairs={{0,8},{2,10},{4,12},{6,14},{8,0},{10,2},{12,4},{14,6},{16,24},{18,... | collective-permute-start | bytes 491528 | tf_op jit(solution)/shard_map/ppermute | solution.py:267
  59.5 23.1 %collective-permute-start.12 = (bf16[512,128]{1,0:T(8,128)(2,1)S(1)}, bf16[512,128]{1,0:T(8,128)(2,1)S(1)}, u32[]{:S(2)}, u32[]{:S(2)}) collective-permute-start(bf16[512,128]{1,0:T(8,128)(2,1)S(1)} %bitcast.29), channel_id=1, source_target_pairs={{0,8},{2,10},{4,12},{6,14},{8,0},{10,2},{12,4},{14,6},{16,24},{18,... | collective-permute-start | bytes 393224 | tf_op jit(solution)/shard_map/ppermute | solution.py:267
  66.1 8.5 %collective-permute-start.3 = (bf16[2,320,128]{2,1,0:T(8,128)(2,1)S(1)}, bf16[2,320,128]{2,1,0:T(8,128)(2,1)S(1)}, u32[]{:S(2)}, u32[]{:S(2)}) collective-permute-start(bf16[2,320,128]{2,1,0:T(8,128)(2,1)S(1)} %add_convert_fusion.3), channel_id=1, source_target_pairs={{0,16},{2,18},{4,20},{6,22},{8,24},{10,26},{12,28},{14,30},{16,0},... | collective-permute-start | bytes 491528 | tf_op jit(solution)/shard_map/ppermute | solution.py:267
  70.1 6.3 %collective-permute-start.18 = (bf16[2,128,128]{2,1,0:T(8,128)(2,1)S(1)}, bf16[2,128,128]{2,1,0:T(8,128)(2,1)S(1)}, u32[]{:S(2)}, u32[]{:S(2)}) collective-permute-start(bf16[2,128,128]{2,1,0:T(8,128)(2,1)S(1)} %slice.115), channel_id=1, source_target_pairs={{0,8},{2,10},{4,12},{6,14},{8,0},{10,2},{12,4},{14,6},{16,24},{18,... | collective-permute-start | bytes 196616 | tf_op jit(solution)/shard_map/ppermute | solution.py:267
  74.6 5.4 %collective-permute-start.4 = (bf16[640,128]{1,0:T(8,128)(2,1)S(1)}, bf16[640,128]{1,0:T(8,128)(2,1)S(1)}, u32[]{:S(2)}, u32[]{:S(2)}) collective-permute-start(bf16[640,128]{1,0:T(8,128)(2,1)S(1)} %bitcast.27), channel_id=1, source_target_pairs={{0,8},{2,10},{4,12},{6,14},{8,0},{10,2},{12,4},{14,6},{16,24},{18,... | collective-permute-start | bytes 491528 | tf_op jit(solution)/shard_map/ppermute | solution.py:267
  76.4 5.8 %collective-permute-start.19 = (bf16[2,128,128]{2,1,0:T(8,128)(2,1)S(1)}, bf16[2,128,128]{2,1,0:T(8,128)(2,1)S(1)}, u32[]{:S(2)}, u32[]{:S(2)}) collective-permute-start(bf16[2,128,128]{2,1,0:T(8,128)(2,1)S(1)} %add_convert_fusion.8), channel_id=1, source_target_pairs={{0,16},{2,18},{4,20},{6,22},{8,24},{10,26},{12,28},{14,30},{16,0},... | collective-permute-start | bytes 196616 | tf_op jit(solution)/shard_map/ppermute | solution.py:267
  80.0 10.4 %collective-permute-start.5 = (bf16[1280,128]{1,0:T(8,128)(2,1)S(1)}, bf16[1280,128]{1,0:T(8,128)(2,1)S(1)}, u32[]{:S(2)}, u32[]{:S(2)}) collective-permute-start(bf16[1280,128]{1,0:T(8,128)(2,1)S(1)} %pad_maximum_fusion.refs_2_), channel_id=1, source_target_pairs={{0,4},{2,6},{4,0},{6,2},{8,12},{10,14},{12,8},{14,10},{16,20},{18,... | collective-permute-start | bytes 983048 | tf_op jit(solution)/shard_map/ppermute | solution.py:267
  82.2 4.3 %collective-permute-start.20 = (bf16[256,128]{1,0:T(8,128)(2,1)S(1)}, bf16[256,128]{1,0:T(8,128)(2,1)S(1)}, u32[]{:S(2)}, u32[]{:S(2)}) collective-permute-start(bf16[256,128]{1,0:T(8,128)(2,1)S(1)} %bitcast.31), channel_id=1, source_target_pairs={{0,8},{2,10},{4,12},{6,14},{8,0},{10,2},{12,4},{14,6},{16,24},{18,... | collective-permute-start | bytes 196616 | tf_op jit(solution)/shard_map/ppermute | solution.py:267
  82.7 11.9 %collective-permute-start.13 = (bf16[1024,128]{1,0:T(8,128)(2,1)S(1)}, bf16[1024,128]{1,0:T(8,128)(2,1)S(1)}, u32[]{:S(2)}, u32[]{:S(2)}) collective-permute-start(bf16[1024,128]{1,0:T(8,128)(2,1)S(1)} %pad_maximum_fusion.1.refs_6_), channel_id=1, source_target_pairs={{0,4},{2,6},{4,0},{6,2},{8,12},{10,14},{12,8},{14,10},{16,20},{18,... | collective-permute-start | bytes 786440 | tf_op jit(solution)/shard_map/ppermute | solution.py:267
  86.6 8.1 %collective-permute-start.21 = (bf16[512,128]{1,0:T(8,128)(2,1)S(1)}, bf16[512,128]{1,0:T(8,128)(2,1)S(1)}, u32[]{:S(2)}, u32[]{:S(2)}) collective-permute-start(bf16[512,128]{1,0:T(8,128)(2,1)S(1)} %pad_maximum_fusion.2.refs_10_), channel_id=1, source_target_pairs={{0,4},{2,6},{4,0},{6,2},{8,12},{10,14},{12,8},{14,10},{16,20},{18,... | collective-permute-start | bytes 393224 | tf_op jit(solution)/shard_map/ppermute | solution.py:267
  88.1 8.6 %collective-permute-start.6 = (bf16[1280,128]{1,0:T(8,128)(2,1)S(1)}, bf16[1280,128]{1,0:T(8,128)(2,1)S(1)}, u32[]{:S(2)}, u32[]{:S(2)}) collective-permute-start(bf16[1280,128]{1,0:T(8,128)(2,1)S(1)} %pad_maximum_fusion.refs_2_), channel_id=1, source_target_pairs={{0,2},{2,0},{4,6},{6,4},{8,10},{10,8},{12,14},{14,12},{16,18},{18,... | collective-permute-start | bytes 983048 | tf_op jit(solution)/shard_map/ppermute | solution.py:267
  90.4 6.3 %collective-permute-start.7 = (bf16[1280,128]{1,0:T(8,128)(2,1)S(1)}, bf16[1280,128]{1,0:T(8,128)(2,1)S(1)}, u32[]{:S(2)}, u32[]{:S(2)}) collective-permute-start(bf16[1280,128]{1,0:T(8,128)(2,1)S(1)} %collective-permute-done.5.refs_3_), channel_id=1, source_target_pairs={{0,2},{2,0},{4,6},{6,4},{8,10},{10,8},{12,14},{14,12},{16,18},{18,... | collective-permute-start | bytes 983048 | tf_op jit(solution)/shard_map/ppermute | solution.py:267
  90.4 4.7 %collective-permute-start.22 = (bf16[512,128]{1,0:T(8,128)(2,1)S(1)}, bf16[512,128]{1,0:T(8,128)(2,1)S(1)}, u32[]{:S(2)}, u32[]{:S(2)}) collective-permute-start(bf16[512,128]{1,0:T(8,128)(2,1)S(1)} %pad_maximum_fusion.2.refs_10_), channel_id=1, source_target_pairs={{0,2},{2,0},{4,6},{6,4},{8,10},{10,8},{12,14},{14,12},{16,18},{18,... | collective-permute-start | bytes 393224 | tf_op jit(solution)/shard_map/ppermute | solution.py:267
  94.7 2.1 %collective-permute-start.15 = (bf16[1024,128]{1,0:T(8,128)(2,1)S(1)}, bf16[1024,128]{1,0:T(8,128)(2,1)S(1)}, u32[]{:S(2)}, u32[]{:S(2)}) collective-permute-start(bf16[1024,128]{1,0:T(8,128)(2,1)S(1)} %collective-permute-done.13.refs_7_), channel_id=1, source_target_pairs={{0,2},{2,0},{4,6},{6,4},{8,10},{10,8},{12,14},{14,12},{16,18},{18,... | collective-permute-start | bytes 786440 | tf_op jit(solution)/shard_map/ppermute | solution.py:267
  95.2 1.6 %collective-permute-start.23 = (bf16[512,128]{1,0:T(8,128)(2,1)S(1)}, bf16[512,128]{1,0:T(8,128)(2,1)S(1)}, u32[]{:S(2)}, u32[]{:S(2)}) collective-permute-start(bf16[512,128]{1,0:T(8,128)(2,1)S(1)} %collective-permute-done.21.refs_11_), channel_id=1, source_target_pairs={{0,2},{2,0},{4,6},{6,4},{8,10},{10,8},{12,14},{14,12},{16,18},{18,... | collective-permute-start | bytes 393224 | tf_op jit(solution)/shard_map/ppermute | solution.py:267
  116.4 25.4 %collective-permute-start.24 = (bf16[1024,512]{1,0:T(8,128)(2,1)}, bf16[1024,512]{1,0:T(8,128)(2,1)S(1)}, u32[]{:S(2)}, u32[]{:S(2)}) collective-permute-start(bf16[1024,512]{1,0:T(8,128)(2,1)} %mix.2.refs_21_), channel_id=1, source_target_pairs={{0,1},{1,0},{2,3},{3,2},{4,5},{5,4},{6,7},{7,6},{8,9},{9,8},{10,11... | collective-permute-start | bytes 3145736 | tf_op jit(solution)/shard_map/ppermute | solution.py:330
  (16 other events, 92.2 us)

commit v9 on v8

--- a/solution.py
+++ b/solution.py
@@ -16,7 +16,7 @@
 QUARTER = LANES // QUADS
 WIDTH = GROUP * LANES
 VMEM_LIMIT = 56 * 2**20
-CHUNKS = (5, 4, 2)
+CHUNKS = (4, 4, 3)
 
 SIN_COEF = (4.4428679, -7.30744342, 3.59478808, -0.78437403)
 COS_COEF = (1.41420408, -6.97764206, 5.71523839, -1.72834866)
@@ -68,10 +68,20 @@
 
 def states_kernel(
     first, part, scale, index_ref, dirs_ref, weight_ref, mask_ref, freq_ref, pos_ref,
-    qt_ref, kt_ref, v_ref, g_ref, *refs,
+    qt_ref, kt_ref, v_in, g_in, *refs,
 ):
-    kept_ref, sent_ref, cos_ref, sin_ref, kr, qr, slots = refs[-7:]
+    kept_ref, sent_ref, cos_ref, sin_ref, kr, qr, slots, v_ref, g_ref, sems = refs[-10:]
     group = first + pl.program_id(0)
+    copies = [
+        pltpu.make_async_copy(v_in, v_ref, sems.at[0]),
+        pltpu.make_async_copy(g_in, g_ref, sems.at[1]),
+    ]
+
+    @pl.when(pl.program_id(0) == 0)
+    def _():
+        for copy in copies:
+            copy.start()
+
     core, pair, quad = place_of(index_ref[0])
     freq = column(freq_ref[...]) * (1.0 / (2.0 * math.pi))
     for start in range(0, pos_ref.shape[1], part):
@@ -94,6 +104,11 @@
         kr[:, cols] = rotated(kt_ref[:, cols], cosine, sine)
         qr[:, cols] = rotated(qt_ref[:, cols], cosine, sine)
 
+    @pl.when(pl.program_id(0) == 0)
+    def _():
+        for copy in copies:
+            copy.wait()
+
     for kind, rot, other in ((0, kr, v_ref), (1, qr, g_ref)):
         total = jnp.dot(rot[...], other[...], preferred_element_type=F32)
         for i in range(GROUP):
@@ -120,16 +135,21 @@
     return jnp.concatenate(pieces, axis=0)
 
 
-def mix_kernel(chunks, part, index_ref, half_ref, *refs):
-    del half_ref
+def mix_kernel(chunks, part, direct_too, back_too, index_ref, half_ref, *refs):
     sources, refs = refs[: 4 * len(chunks)], refs[4 * len(chunks) :]
-    vt_ref, gt_ref, kt_ref, qt_ref, cos_ref, sin_ref, gain_ref, out_ref = refs[:8]
-    slots, states, states_t, *totals = refs[8:]
+    vt_ref, gt_ref, kt_ref, qt_ref, cos_ref, sin_ref, gain_in, out_ref = refs[:8]
+    slots, states, states_t, *totals, gain_ref, sem = refs[8:]
     group = pl.program_id(0)
+    atoms = gain_ref.shape[1]
+    gain_copy = back_too and pltpu.make_async_copy(
+        gain_in.at[:, pl.ds(pl.multiple_of(half_ref[0] * atoms, atoms), atoms)], gain_ref, sem
+    )
     core, pair, quad = place_of(index_ref[0])
 
     @pl.when(group == 0)
     def _():
+        if back_too:
+            gain_copy.start()
         done = 0
         for at, groups in enumerate(chunks):
             rows = groups * 2 * QUARTER
@@ -161,21 +181,21 @@
 
     def backs(start):
         cols = slice(start, start + part)
-        return [
+        return back_too and [
             jnp.dot(states[kind], fixed[:, cols], preferred_element_type=F32)
             for kind, fixed in ((0, gt_ref), (1, vt_ref))
         ]
 
     def turn(start):
         cols = slice(start, start + part)
-        return [
+        return direct_too and [
             rotated(x_ref[:, cols], cos_ref[:, cols], sin_ref[:, cols]) for x_ref in (qt_ref, kt_ref)
         ]
 
     back, turned = backs(starts[0]), turn(starts[0])
     for at, start in enumerate(starts):
         cols = slice(start, start + part)
-        for kind, direct in ((0, totals[0]), (1, totals[3])):
+        for kind, direct in ((0, totals[0]), (1, totals[3])) if direct_too else ():
             direct[:, cols] += jnp.dot(
                 states_t[kind], turned[kind], preferred_element_type=F32
             )
@@ -183,7 +203,7 @@
             next_back = backs(starts[at + 1])
         cosine = cos_ref[:, cols]
         sine = sin_ref[:, cols]
-        for kind, total in ((0, totals[1]), (1, totals[2])):
+        for kind, total in ((0, totals[1]), (1, totals[2])) if back_too else ():
             lower = back[kind].astype(BF16)
             for m in range(2):
                 leads, trails = [], []
@@ -203,9 +223,14 @@
 
     @pl.when(group == pl.num_programs(0) - 1)
     def _():
+        if back_too:
+            gain_copy.wait()
+        done = 0
         for at, total in enumerate(totals):
-            whole = total[...] * gain_ref[...] if at == 2 else total[...]
-            out_ref[:, at * LANES : (at + 1) * LANES] = whole.T.astype(out_ref.dtype)
+            if back_too if at in (1, 2) else direct_too:
+                whole = total[...] * gain_ref[...] if at == 2 else total[...]
+                out_ref[:, done : done + LANES] = whole.T.astype(out_ref.dtype)
+                done += LANES
 
 
 def added(*terms):
@@ -248,12 +273,14 @@
         kept, sent, *phases = pl.pallas_call(
             functools.partial(states_kernel, first, min(256, atoms), 1.0 / math.sqrt(feats * atoms)),
             grid=(groups,),
-            in_specs=[smem] * 4 + [vmem] * 6 + [anywhere] * (len(after) + len(phases)),
+            in_specs=[smem] * 4 + [vmem] * 4 + [anywhere] * (2 + len(after) + len(phases)),
             out_specs=[sent_spec] * 2 + [phase_spec] * 2,
             out_shape=[sent] * 2 + [phase] * 2,
             input_output_aliases={len(operands) + at: 2 + at for at in range(len(phases))},
             scratch_shapes=[pltpu.VMEM((WIDTH, atoms), BF16)] * 2
-            + [pltpu.VMEM((2, 2, QUADS, 2 * QUARTER, feats), BF16)],
+            + [pltpu.VMEM((2, 2, QUADS, 2 * QUARTER, feats), BF16)]
+            + [pltpu.VMEM((atoms, feats), BF16)] * 2
+            + [pltpu.SemaphoreType.DMA((2,))],
             compiler_params=params,
             cost_estimate=pl.CostEstimate(
                 flops=8 * groups * WIDTH * atoms * feats,
@@ -285,30 +312,32 @@
         other = by_bit(half, 2)
         return half, other, by_bit(half, 1), by_bit(other, 1)
 
-    def mix(half, pieces, phases, dtype, after=()):
+    def mix(half, pieces, phases, direct_too, back_too, after=()):
+        lanes = 2 * feats * (direct_too + back_too)
         rows_half = pl.BlockSpec((feats, half_atoms), lambda g, index, half: (0, half[0]))
         phase_spec = pl.BlockSpec(
             (GROUP * QUARTER, half_atoms), lambda g, index, half: (g, half[0])
         )
         return pl.pallas_call(
             lambda *refs: mix_kernel(
-                CHUNKS, min(256, half_atoms), *refs[: 2 + len(pieces) + 7],
+                CHUNKS, min(256, half_atoms), direct_too, back_too, *refs[: 2 + len(pieces) + 7],
                 *refs[2 + len(pieces) + 7 + len(after) :],
             ),
             grid_spec=pltpu.PrefetchScalarGridSpec(
                 num_scalar_prefetch=2,
                 grid=(total_groups,),
-                in_specs=[vmem] * len(pieces) + [rows_half] * 4 + [phase_spec] * 2 + [rows_half]
+                in_specs=[vmem] * len(pieces) + [rows_half] * 4 + [phase_spec] * 2 + [anywhere]
                 + [anywhere] * len(after),
-                out_specs=pl.BlockSpec((half_atoms, 4 * feats), lambda g, index, half: (0, 0)),
+                out_specs=pl.BlockSpec((half_atoms, lanes), lambda g, index, half: (0, 0)),
                 scratch_shapes=[
                     pltpu.VMEM((2, 2, QUADS, total_groups * 2 * QUARTER, feats), BF16),
                     pltpu.VMEM((2, WIDTH, feats), BF16),
                     pltpu.VMEM((2, feats, WIDTH), BF16),
                 ]
-                + [pltpu.VMEM((feats, half_atoms), F32)] * 4,
+                + [pltpu.VMEM((feats, half_atoms), F32)] * 5
+                + [pltpu.SemaphoreType.DMA],
             ),
-            out_shape=shape((half_atoms, 4 * feats), dtype),
+            out_shape=shape((half_atoms, lanes), BF16),
             compiler_params=params,
             cost_estimate=pl.CostEstimate(
                 flops=8 * total_groups * WIDTH * half_atoms * feats,
@@ -326,11 +355,19 @@
         made.append((kept, *crossing(kept, sent)))
         first += groups
     pieces = [piece for each in made for piece in summed(*each)]
-    sent = mix(1 - mine, pieces, phases, BF16)
-    theirs = lax.ppermute(sent, "dirs", [(0, 1), (1, 0)])
-    ours = mix(mine, pieces, phases, F32, [sent])
-    lanes = [slice(at * feats, (at + 1) * feats) for at in range(4)]
-    return tuple((ours[:, at] + theirs[:, at].astype(F32)).astype(BF16) for at in lanes)
+    sent_direct = mix(1 - mine, pieces, phases, True, False)
+    sent_back = mix(1 - mine, pieces, phases, False, True, [sent_direct])
+    theirs_direct, theirs_back = (
+        lax.ppermute(x, "dirs", [(0, 1), (1, 0)]) for x in (sent_direct, sent_back)
+    )
+    ours = mix(mine, pieces, phases, True, True, [sent_back])
+    theirs = (
+        theirs_direct[:, :feats], theirs_back[:, :feats], theirs_back[:, feats:],
+        theirs_direct[:, feats:],
+    )
+    return tuple(
+        added(ours[:, at * feats : (at + 1) * feats], other) for at, other in enumerate(theirs)
+    )
 
 
 def solution(mesh):

time: 145 us -> 150 us (1.034)
  Pallas kernels: 70.2 us -> 89.3 us
  waiting for transfers between devices: 39.6 us -> 26.9 us
  other arithmetic: 7.82 us -> 5.92 us
    pallas_call x3, Pallas kernels: 28.3 us -> 40.2 us  [make_states(): pl.pallas_call(functools.partial(states_kernel, first, min(256, atoms), 1...]
    ppermute x24, waiting for transfers between devices: 35.1 us -> 26.9 us  [moved(): lax.ppermute(x, 'atoms', [(i, target(i)) for i in range(atom_devices)])]
    pallas_call x2 -> x3, Pallas kernels: 38.1 us -> 45.3 us  [mix(): pl.pallas_call(lambda *refs: mix_kernel(CHUNKS, min(256, half_atoms), dir...]
    ppermute x1 -> x2, waiting for transfers between devices: 4.55 us -> 0.01 us  [per_device(): lax.ppermute(x, 'dirs', [(0, 1), (1, 0)])]
    convert_element_type x1 -> x0, other arithmetic: 2.62 us -> none  [per_device(): (ours[:, at] + theirs[:, at].astype(F32)).astype(BF16)]
    convert_element_type x12 -> x13, other arithmetic: 5.15 us -> 5.87 us  [added(): return sum((term.astype(F32) for term in terms)).astype(BF16)]
  transfers between devices with their start and end apart: 25 -> 26, of which waited for: 14 -> 9; matrix products, arithmetic and copies ran while one was open for 3% -> 2% of each run, Pallas kernels for 18% -> 29%
where the time goes in v9:
time: 150 us; the launch traced here: 149 us
  Pallas kernels  89.3 us (60%)
  waiting for transfers between devices  26.9 us (18%)
  starting transfers between devices  24.7 us (16%)
  other arithmetic  5.92 us (4%)
    pallas_call x3, Pallas kernels, mix(): pl.pallas_call(lambda *refs: mix_kernel(CHUNKS, min(256, half_atoms), dir...  45.3 us
    pallas_call x3, Pallas kernels, make_states(): pl.pallas_call(functools.partial(states_kernel, first, min(256, atoms), 1...  40.2 us
    ppermute x24, waiting for transfers between devices, moved(): lax.ppermute(x, 'atoms', [(i, target(i)) for i in range(atom_devices)])  26.9 us
    ppermute x24, starting transfers between devices, moved(): lax.ppermute(x, 'atoms', [(i, target(i)) for i in range(atom_devices)])  22.5 us
    convert_element_type x13, other arithmetic, added(): return sum((term.astype(F32) for term in terms)).astype(BF16)  5.87 us
    pallas_call x1, Pallas kernels, per_device(): pl.pallas_call(prepare_kernel, in_specs=[smem] + [vmem] * 7, out_specs=[v...  3.83 us
  transfers between devices with their start and end apart: 26, of which 9 were waited for; matrix products, arithmetic and copies ran while one was open for 2% of the time, Pallas kernels for 29%

profile of v9, /device:TPU:0, one launch (start us, length us, event | category | flops | bytes accessed | tf_op | source)
XLA Modules:
  0.0 149.2 jit_solution(4847326680821672044)
XLA Ops:
  0.6 3.8 %prepare.1 = (bf16[128,2048]{1,0:T(8,128)(2,1)}, bf16[128,2048]{1,0:T(8,128)(2,1)}, bf16[128,2048]{1,0:T(8,128)(2,1)}, bf16[128,2048]{1,0:T(8,128)(2,1)}, f32[128,2048]{1,0:T(8,128)}) custom-call(s32[1]{0:T(128)} %bitcast.index_ref.refs_0_, s32[1,2048]{1,0:T(1,128)} %bitcast.33, s32[1,2048]{1,0:T(1,128)} %bitcast.34, f32[5,128]{1,0:T(8,128)} %gain_ref.1, ...), custom_call_target="tpu_custom_call" | custom-call | tf_op jit(solution)/shard_map/prepare/pallas_call | solution.py:255
  4.5 14.3 %states.3 = (bf16[2,4,256,128]{3,2,1,0:T(8,128)(2,1)}, bf16[2,4,256,128]{3,2,1,0:T(8,128)(2,1)}, bf16[1408,2048]{1,0:T(8,128)(2,1)}, bf16[1408,2048]{1,0:T(8,128)(2,1)}) custom-call(s32[1]{0:T(128)} %bitcast.index_ref.refs_0_, f32[3,44]{1,0:T(4,128)} %dirs_ref.5, f32[44]{0:T(128)} %weight_ref.5, s32[44]{0:T(128)} %mask_ref.5, f32[1,32]{1,0:T(1,128)} %bitcast.35, ...), custom_call_target="tpu_custom_call" | custom-call | flops 4294967296 | bytes 8388608 | tf_op jit(solution)/shard_map/states/pallas_call | solution.py:273
  18.8 14.5 %states.4 = (bf16[2,4,256,128]{3,2,1,0:T(8,128)(2,1)}, bf16[2,4,256,128]{3,2,1,0:T(8,128)(2,1)}, bf16[1408,2048]{1,0:T(8,128)(2,1)}, bf16[1408,2048]{1,0:T(8,128)(2,1)}) custom-call(s32[1]{0:T(128)} %bitcast.index_ref.refs_0_, f32[3,44]{1,0:T(4,128)} %dirs_ref.5, f32[44]{0:T(128)} %weight_ref.5, ...), custom_call_target="tpu_custom_call", output_to_operand_aliasing={{2}: (10, {}), {3}: (11, {})} | custom-call | flops 4294967296 | bytes 8388608 | tf_op jit(solution)/shard_map/states/pallas_call | solution.py:273
  33.9 1.7 %collective-permute-done.8 = bf16[2,4,256,128]{3,2,1,0:T(8,128)(2,1)S(1)} collective-permute-done((bf16[2,4,256,128]{3,2,1,0:T(8,128)(2,1)}, bf16[2,4,256,128]{3,2,1,0:T(8,128)(2,1)S(1)}, u32[]{:S(2)}, u32[]{:S(2)}) %collective-permute-start.8) | collective-permute-done | bytes 524320 | tf_op jit(solution)/shard_map/ppermute | solution.py:294
  36.6 2.9 %collective-permute-start.9 = (bf16[4,256,128]{2,1,0:T(8,128)(2,1)S(1)}, bf16[4,256,128]{2,1,0:T(8,128)(2,1)S(1)}, u32[]{:S(2)}, u32[]{:S(2)}) collective-permute-start(bf16[4,256,128]{2,1,0:T(8,128)(2,1)S(1)} %fusion.4), channel_id=1, source_target_pairs={{0,4},{2,6},{4,0},{6,2},{8,12},{10,14},{12,8},{14,10},{16,20},{18,... | collective-permute-start | bytes 786440 | tf_op jit(solution)/shard_map/ppermute | solution.py:294
  40.3 11.4 %states.5 = (bf16[2,4,192,128]{3,2,1,0:T(8,128)(2,1)}, bf16[2,4,192,128]{3,2,1,0:T(8,128)(2,1)}, bf16[1408,2048]{1,0:T(8,128)(2,1)}, bf16[1408,2048]{1,0:T(8,128)(2,1)}) custom-call(s32[1]{0:T(128)} %bitcast.index_ref.refs_0_, f32[3,44]{1,0:T(4,128)} %dirs_ref.5, f32[44]{0:T(128)} %weight_ref.5, ...), custom_call_target="tpu_custom_call", output_to_operand_aliasing={{2}: (11, {}), {3}: (12, {})} | custom-call | flops 3221225472 | bytes 6291456 | tf_op jit(solution)/shard_map/states/pallas_call | solution.py:273
  52.0 1.6 %collective-permute-start.10 = (bf16[2,256,128]{2,1,0:T(8,128)(2,1)S(1)}, bf16[2,256,128]{2,1,0:T(8,128)(2,1)S(1)}, u32[]{:S(2)}, u32[]{:S(2)}) collective-permute-start(bf16[2,256,128]{2,1,0:T(8,128)(2,1)S(1)} %slice.111), channel_id=1, source_target_pairs={{0,8},{2,10},{4,12},{6,14},{8,0},{10,2},{12,4},{14,6},{16,24},{18,... | collective-permute-start | bytes 393224 | tf_op jit(solution)/shard_map/ppermute | solution.py:294
  54.3 4.1 %collective-permute-done.10 = bf16[2,256,128]{2,1,0:T(8,128)(2,1)S(1)} collective-permute-done((bf16[2,256,128]{2,1,0:T(8,128)(2,1)S(1)}, bf16[2,256,128]{2,1,0:T(8,128)(2,1)S(1)}, u32[]{:S(2)}, u32[]{:S(2)}) %collective-permute-start.10) | collective-permute-done | bytes 131104 | tf_op jit(solution)/shard_map/ppermute | solution.py:294
  58.4 2.7 %collective-permute-start.11 = (bf16[2,256,128]{2,1,0:T(8,128)(2,1)S(1)}, bf16[2,256,128]{2,1,0:T(8,128)(2,1)S(1)}, u32[]{:S(2)}, u32[]{:S(2)}) collective-permute-start(bf16[2,256,128]{2,1,0:T(8,128)(2,1)S(1)} %add_convert_fusion.8), channel_id=1, source_target_pairs={{0,16},{2,18},{4,20},{6,22},{8,24},{10,26},{12,28},{14,30},{16,0},... | collective-permute-start | bytes 393224 | tf_op jit(solution)/shard_map/ppermute | solution.py:294
  61.1 2.8 %collective-permute-start.3 = (bf16[2,256,128]{2,1,0:T(8,128)(2,1)S(1)}, bf16[2,256,128]{2,1,0:T(8,128)(2,1)S(1)}, u32[]{:S(2)}, u32[]{:S(2)}) collective-permute-start(bf16[2,256,128]{2,1,0:T(8,128)(2,1)S(1)} %add_convert_fusion.10), channel_id=1, source_target_pairs={{0,16},{2,18},{4,20},{6,22},{8,24},{10,26},{12,28},{14,30},{16,0},... | collective-permute-start | bytes 393224 | tf_op jit(solution)/shard_map/ppermute | solution.py:294
  66.3 4.5 %collective-permute-done.11 = bf16[2,256,128]{2,1,0:T(8,128)(2,1)S(1)} collective-permute-done((bf16[2,256,128]{2,1,0:T(8,128)(2,1)S(1)}, bf16[2,256,128]{2,1,0:T(8,128)(2,1)S(1)}, u32[]{:S(2)}, u32[]{:S(2)}) %collective-permute-start.11) | collective-permute-done | bytes 131104 | tf_op jit(solution)/shard_map/ppermute | solution.py:294
  72.0 2.1 %collective-permute-start.18 = (bf16[2,192,128]{2,1,0:T(8,128)(2,1)S(1)}, bf16[2,192,128]{2,1,0:T(8,128)(2,1)S(1)}, u32[]{:S(2)}, u32[]{:S(2)}) collective-permute-start(bf16[2,192,128]{2,1,0:T(8,128)(2,1)S(1)} %slice.115), channel_id=1, source_target_pairs={{0,8},{2,10},{4,12},{6,14},{8,0},{10,2},{12,4},{14,6},{16,24},{18,... | collective-permute-start | bytes 294920 | tf_op jit(solution)/shard_map/ppermute | solution.py:294
  74.2 4.6 %collective-permute-done.18 = bf16[2,192,128]{2,1,0:T(8,128)(2,1)S(1)} collective-permute-done((bf16[2,192,128]{2,1,0:T(8,128)(2,1)S(1)}, bf16[2,192,128]{2,1,0:T(8,128)(2,1)S(1)}, u32[]{:S(2)}, u32[]{:S(2)}) %collective-permute-start.18) | collective-permute-done | bytes 98336 | tf_op jit(solution)/shard_map/ppermute | solution.py:294
  78.8 2.1 %collective-permute-start.19 = (bf16[2,192,128]{2,1,0:T(8,128)(2,1)S(1)}, bf16[2,192,128]{2,1,0:T(8,128)(2,1)S(1)}, u32[]{:S(2)}, u32[]{:S(2)}) collective-permute-start(bf16[2,192,128]{2,1,0:T(8,128)(2,1)S(1)} %add_convert_fusion.12), channel_id=1, source_target_pairs={{0,16},{2,18},{4,20},{6,22},{8,24},{10,26},{12,28},{14,30},{16,0},... | collective-permute-start | bytes 294920 | tf_op jit(solution)/shard_map/ppermute | solution.py:294
  82.4 3.2 %collective-permute-done.19 = bf16[2,192,128]{2,1,0:T(8,128)(2,1)S(1)} collective-permute-done((bf16[2,192,128]{2,1,0:T(8,128)(2,1)S(1)}, bf16[2,192,128]{2,1,0:T(8,128)(2,1)S(1)}, u32[]{:S(2)}, u32[]{:S(2)}) %collective-permute-start.19) | collective-permute-done | bytes 98336 | tf_op jit(solution)/shard_map/ppermute | solution.py:294
  85.7 1.5 collective-permute-start.5
  87.2 3.1 %collective-permute-done.20 = bf16[384,128]{1,0:T(8,128)(2,1)S(1)} collective-permute-done((bf16[384,128]{1,0:T(8,128)(2,1)S(1)}, bf16[384,128]{1,0:T(8,128)(2,1)S(1)}, u32[]{:S(2)}, u32[]{:S(2)}) %collective-permute-start.20) | collective-permute-done | bytes 98336 | tf_op jit(solution)/shard_map/ppermute | solution.py:294
  92.3 2.7 %collective-permute-done.5.refs_3_ = bf16[1024,128]{1,0:T(8,128)(2,1)S(1)} collective-permute-done((bf16[1024,128]{1,0:T(8,128)(2,1)S(1)}, bf16[1024,128]{1,0:T(8,128)(2,1)S(1)}, u32[]{:S(2)}, u32[]{:S(2)}) %collective-permute-start.5) | collective-permute-done | bytes 262176 | tf_op jit(solution)/shard_map/ppermute | solution.py:294
  95.5 1.7 %collective-permute-done.21.refs_11_ = bf16[768,128]{1,0:T(8,128)(2,1)S(1)} collective-permute-done((bf16[768,128]{1,0:T(8,128)(2,1)S(1)}, bf16[768,128]{1,0:T(8,128)(2,1)S(1)}, u32[]{:S(2)}, u32[]{:S(2)}) %collective-permute-start.21) | collective-permute-done | bytes 196640 | tf_op jit(solution)/shard_map/ppermute | solution.py:294
  99.3 13.0 %mix.3.refs_21_ = bf16[1024,256]{1,0:T(8,128)(2,1)} custom-call(s32[1]{0:T(128)} %bitcast.index_ref.refs_0_, s32[1]{0:T(128)} %bitcast.14.refs_1_, bf16[1024,128]{1,0:T(8,128)(2,1)} %copy-done.4, bf16[1024,128]{1,0:T(8,128)(2,1)} %copy-done.8, bf16[1024,128]{1,0:T(8,128)(2,1)} %copy-done.10, bf16[1024,128]{1,0:T(8,128)(2,1)} %copy-done.12, ...), custom_call_target="tpu_custom_call" | custom-call | flops 5905580032 | bytes 11534336 | tf_op jit(solution)/shard_map/mix/pallas_call | solution.py:321
  112.3 1.6 %collective-permute-start.24 = (bf16[1024,256]{1,0:T(8,128)(2,1)}, bf16[1024,256]{1,0:T(8,128)(2,1)S(1)}, u32[]{:S(2)}, u32[]{:S(2)}) collective-permute-start(bf16[1024,256]{1,0:T(8,128)(2,1)} %mix.3.refs_21_), channel_id=1, source_target_pairs={{0,1},{1,0},{2,3},{3,2},{4,5},{5,4},{6,7},{7,6},{8,9},{9,8},{10,11... | collective-permute-start | bytes 1572872 | tf_op jit(solution)/shard_map/ppermute | solution.py:361
  113.9 13.9 %mix.4.refs_21_ = bf16[1024,256]{1,0:T(8,128)(2,1)} custom-call(s32[1]{0:T(128)} %bitcast.index_ref.refs_0_, s32[1]{0:T(128)} %bitcast.14.refs_1_, bf16[1024,128]{1,0:T(8,128)(2,1)} %copy-done.4, bf16[1024,128]{1,0:T(8,128)(2,1)} %copy-done.8, bf16[1024,128]{1,0:T(8,128)(2,1)} %copy-done.10, bf16[1024,128]{1,0:T(8,128)(2,1)} %copy-done.12, ...), custom_call_target="tpu_custom_call" | custom-call | flops 5905580032 | bytes 11534336 | tf_op jit(solution)/shard_map/mix/pallas_call | solution.py:321
  128.4 18.4 %mix.5 = bf16[1024,512]{1,0:T(8,128)(2,1)} custom-call(s32[1]{0:T(128)} %bitcast.index_ref.refs_0_, s32[1]{0:T(128)} %bitcast.1.refs_1_, bf16[1024,128]{1,0:T(8,128)(2,1)} %copy-done.4, bf16[1024,128]{1,0:T(8,128)(2,1)} %copy-done.8, bf16[1024,128]{1,0:T(8,128)(2,1)} %copy-done.10, bf16[1024,128]{1,0:T(8,128)(2,1)} %copy-done.12, ...), custom_call_target="tpu_custom_call" | custom-call | flops 5905580032 | bytes 11534336 | tf_op jit(solution)/shard_map/mix/pallas_call | solution.py:321
  146.8 2.4 %add_convert_fusion = (bf16[1024,128]{1,0:T(8,128)(2,1)}, bf16[1024,128]{1,0:T(8,128)(2,1)}, bf16[1024,128]{1,0:T(8,128)(2,1)}, bf16[1024,128]{1,0:T(8,128)(2,1)}) fusion(bf16[1024,256]{1,0:T(8,128)(2,1)S(1)} %collective-permute-done.24, bf16[1024,512]{1,0:T(8,128)(2,1)} %mix.5, bf16[1024,256]{1,0:T(8,128)(2,1)S(1)} %collective-permute-done.25), kind=kLoop, calls=%fused_computation.4 | loop fusion | flops 2097152 | bytes 3145728 | tf_op jit(solution)/shard_map/convert_element_type | solution.py:237
  (86 shorter events, 13.8 us)
Async XLA Ops:
  33.3 2.3 %collective-permute-start.8 = (bf16[2,4,256,128]{3,2,1,0:T(8,128)(2,1)}, bf16[2,4,256,128]{3,2,1,0:T(8,128)(2,1)S(1)}, u32[]{:S(2)}, u32[]{:S(2)}) collective-permute-start(bf16[2,4,256,128]{3,2,1,0:T(8,128)(2,1)} %get-tuple-element.28), channel_id=1, source_target_pairs={{0,2},{2,0},{4,6},{6,4},{8,10},{10,8},{12,14},{14,12},{16,18},{18,... | collective-permute-start | bytes 1572872 | tf_op jit(solution)/shard_map/ppermute | solution.py:294
  33.8 5.7 %collective-permute-start = (bf16[2,4,256,128]{3,2,1,0:T(8,128)(2,1)S(1)}, bf16[2,4,256,128]{3,2,1,0:T(8,128)(2,1)S(1)}, u32[]{:S(2)}, u32[]{:S(2)}) collective-permute-start(bf16[2,4,256,128]{3,2,1,0:T(8,128)(2,1)S(1)} %copy-done.6), channel_id=1, source_target_pairs={{0,2},{2,0},{4,6},{6,4},{8,10},{10,8},{12,14},{14,12},{16,18},{18,... | collective-permute-start | bytes 1572872 | tf_op jit(solution)/shard_map/ppermute | solution.py:294
  36.6 15.2 %collective-permute-start.9 = (bf16[4,256,128]{2,1,0:T(8,128)(2,1)S(1)}, bf16[4,256,128]{2,1,0:T(8,128)(2,1)S(1)}, u32[]{:S(2)}, u32[]{:S(2)}) collective-permute-start(bf16[4,256,128]{2,1,0:T(8,128)(2,1)S(1)} %fusion.4), channel_id=1, source_target_pairs={{0,4},{2,6},{4,0},{6,2},{8,12},{10,14},{12,8},{14,10},{16,20},{18,... | collective-permute-start | bytes 786440 | tf_op jit(solution)/shard_map/ppermute | solution.py:294
  39.6 14.0 %collective-permute-start.1 = (bf16[4,256,128]{2,1,0:T(8,128)(2,1)S(1)}, bf16[4,256,128]{2,1,0:T(8,128)(2,1)S(1)}, u32[]{:S(2)}, u32[]{:S(2)}) collective-permute-start(bf16[4,256,128]{2,1,0:T(8,128)(2,1)S(1)} %fusion.3.refs_0_), channel_id=1, source_target_pairs={{0,4},{2,6},{4,0},{6,2},{8,12},{10,14},{12,8},{14,10},{16,20},{18,... | collective-permute-start | bytes 786440 | tf_op jit(solution)/shard_map/ppermute | solution.py:294
  51.7 12.1 %collective-permute-start.16 = (bf16[2,4,192,128]{3,2,1,0:T(8,128)(2,1)}, bf16[2,4,192,128]{3,2,1,0:T(8,128)(2,1)S(1)}, u32[]{:S(2)}, u32[]{:S(2)}) collective-permute-start(bf16[2,4,192,128]{3,2,1,0:T(8,128)(2,1)} %get-tuple-element.32), channel_id=1, source_target_pairs={{0,2},{2,0},{4,6},{6,4},{8,10},{10,8},{12,14},{14,12},{16,18},{18,... | collective-permute-start | bytes 1179656 | tf_op jit(solution)/shard_map/ppermute | solution.py:294
  52.0 6.4 %collective-permute-start.10 = (bf16[2,256,128]{2,1,0:T(8,128)(2,1)S(1)}, bf16[2,256,128]{2,1,0:T(8,128)(2,1)S(1)}, u32[]{:S(2)}, u32[]{:S(2)}) collective-permute-start(bf16[2,256,128]{2,1,0:T(8,128)(2,1)S(1)} %slice.111), channel_id=1, source_target_pairs={{0,8},{2,10},{4,12},{6,14},{8,0},{10,2},{12,4},{14,6},{16,24},{18,... | collective-permute-start | bytes 393224 | tf_op jit(solution)/shard_map/ppermute | solution.py:294
  53.7 7.3 %collective-permute-start.2 = (bf16[2,256,128]{2,1,0:T(8,128)(2,1)S(1)}, bf16[2,256,128]{2,1,0:T(8,128)(2,1)S(1)}, u32[]{:S(2)}, u32[]{:S(2)}) collective-permute-start(bf16[2,256,128]{2,1,0:T(8,128)(2,1)S(1)} %slice.107), channel_id=1, source_target_pairs={{0,8},{2,10},{4,12},{6,14},{8,0},{10,2},{12,4},{14,6},{16,24},{18,... | collective-permute-start | bytes 393224 | tf_op jit(solution)/shard_map/ppermute | solution.py:294
  58.4 12.4 %collective-permute-start.11 = (bf16[2,256,128]{2,1,0:T(8,128)(2,1)S(1)}, bf16[2,256,128]{2,1,0:T(8,128)(2,1)S(1)}, u32[]{:S(2)}, u32[]{:S(2)}) collective-permute-start(bf16[2,256,128]{2,1,0:T(8,128)(2,1)S(1)} %add_convert_fusion.8), channel_id=1, source_target_pairs={{0,16},{2,18},{4,20},{6,22},{8,24},{10,26},{12,28},{14,30},{16,0},... | collective-permute-start | bytes 393224 | tf_op jit(solution)/shard_map/ppermute | solution.py:294
  61.1 13.0 %collective-permute-start.3 = (bf16[2,256,128]{2,1,0:T(8,128)(2,1)S(1)}, bf16[2,256,128]{2,1,0:T(8,128)(2,1)S(1)}, u32[]{:S(2)}, u32[]{:S(2)}) collective-permute-start(bf16[2,256,128]{2,1,0:T(8,128)(2,1)S(1)} %add_convert_fusion.10), channel_id=1, source_target_pairs={{0,16},{2,18},{4,20},{6,22},{8,24},{10,26},{12,28},{14,30},{16,0},... | collective-permute-start | bytes 393224 | tf_op jit(solution)/shard_map/ppermute | solution.py:294
  64.8 6.1 %collective-permute-start.17 = (bf16[4,192,128]{2,1,0:T(8,128)(2,1)S(1)}, bf16[4,192,128]{2,1,0:T(8,128)(2,1)S(1)}, u32[]{:S(2)}, u32[]{:S(2)}) collective-permute-start(bf16[4,192,128]{2,1,0:T(8,128)(2,1)S(1)} %fusion.5), channel_id=1, source_target_pairs={{0,4},{2,6},{4,0},{6,2},{8,12},{10,14},{12,8},{14,10},{16,20},{18,... | collective-permute-start | bytes 589832 | tf_op jit(solution)/shard_map/ppermute | solution.py:294
  70.8 10.0 %collective-permute-start.12 = (bf16[512,128]{1,0:T(8,128)(2,1)S(1)}, bf16[512,128]{1,0:T(8,128)(2,1)S(1)}, u32[]{:S(2)}, u32[]{:S(2)}) collective-permute-start(bf16[512,128]{1,0:T(8,128)(2,1)S(1)} %bitcast.27), channel_id=1, source_target_pairs={{0,8},{2,10},{4,12},{6,14},{8,0},{10,2},{12,4},{14,6},{16,24},{18,... | collective-permute-start | bytes 393224 | tf_op jit(solution)/shard_map/ppermute | solution.py:294
  72.0 6.8 %collective-permute-start.18 = (bf16[2,192,128]{2,1,0:T(8,128)(2,1)S(1)}, bf16[2,192,128]{2,1,0:T(8,128)(2,1)S(1)}, u32[]{:S(2)}, u32[]{:S(2)}) collective-permute-start(bf16[2,192,128]{2,1,0:T(8,128)(2,1)S(1)} %slice.115), channel_id=1, source_target_pairs={{0,8},{2,10},{4,12},{6,14},{8,0},{10,2},{12,4},{14,6},{16,24},{18,... | collective-permute-start | bytes 294920 | tf_op jit(solution)/shard_map/ppermute | solution.py:294
  74.1 11.6 %collective-permute-start.4 = (bf16[512,128]{1,0:T(8,128)(2,1)S(1)}, bf16[512,128]{1,0:T(8,128)(2,1)S(1)}, u32[]{:S(2)}, u32[]{:S(2)}) collective-permute-start(bf16[512,128]{1,0:T(8,128)(2,1)S(1)} %bitcast.29), channel_id=1, source_target_pairs={{0,8},{2,10},{4,12},{6,14},{8,0},{10,2},{12,4},{14,6},{16,24},{18,... | collective-permute-start | bytes 393224 | tf_op jit(solution)/shard_map/ppermute | solution.py:294
  78.8 6.7 %collective-permute-start.19 = (bf16[2,192,128]{2,1,0:T(8,128)(2,1)S(1)}, bf16[2,192,128]{2,1,0:T(8,128)(2,1)S(1)}, u32[]{:S(2)}, u32[]{:S(2)}) collective-permute-start(bf16[2,192,128]{2,1,0:T(8,128)(2,1)S(1)} %add_convert_fusion.12), channel_id=1, source_target_pairs={{0,16},{2,18},{4,20},{6,22},{8,24},{10,26},{12,28},{14,30},{16,0},... | collective-permute-start | bytes 294920 | tf_op jit(solution)/shard_map/ppermute | solution.py:294
  80.9 10.8 %collective-permute-start.13 = (bf16[1024,128]{1,0:T(8,128)(2,1)S(1)}, bf16[1024,128]{1,0:T(8,128)(2,1)S(1)}, u32[]{:S(2)}, u32[]{:S(2)}) collective-permute-start(bf16[1024,128]{1,0:T(8,128)(2,1)S(1)} %pad_maximum_fusion.1.refs_6_), channel_id=1, source_target_pairs={{0,4},{2,6},{4,0},{6,2},{8,12},{10,14},{12,8},{14,10},{16,20},{18,... | collective-permute-start | bytes 786440 | tf_op jit(solution)/shard_map/ppermute | solution.py:294
  85.6 4.7 %collective-permute-start.20 = (bf16[384,128]{1,0:T(8,128)(2,1)S(1)}, bf16[384,128]{1,0:T(8,128)(2,1)S(1)}, u32[]{:S(2)}, u32[]{:S(2)}) collective-permute-start(bf16[384,128]{1,0:T(8,128)(2,1)S(1)} %bitcast.31), channel_id=1, source_target_pairs={{0,8},{2,10},{4,12},{6,14},{8,0},{10,2},{12,4},{14,6},{16,24},{18,... | collective-permute-start | bytes 294920 | tf_op jit(solution)/shard_map/ppermute | solution.py:294
  85.7 9.3 %collective-permute-start.5 = (bf16[1024,128]{1,0:T(8,128)(2,1)S(1)}, bf16[1024,128]{1,0:T(8,128)(2,1)S(1)}, u32[]{:S(2)}, u32[]{:S(2)}) collective-permute-start(bf16[1024,128]{1,0:T(8,128)(2,1)S(1)} %pad_maximum_fusion.refs_2_), channel_id=1, source_target_pairs={{0,4},{2,6},{4,0},{6,2},{8,12},{10,14},{12,8},{14,10},{16,20},{18,... | collective-permute-start | bytes 786440 | tf_op jit(solution)/shard_map/ppermute | solution.py:294
  87.2 7.9 %collective-permute-start.14 = (bf16[1024,128]{1,0:T(8,128)(2,1)S(1)}, bf16[1024,128]{1,0:T(8,128)(2,1)S(1)}, u32[]{:S(2)}, u32[]{:S(2)}) collective-permute-start(bf16[1024,128]{1,0:T(8,128)(2,1)S(1)} %pad_maximum_fusion.1.refs_6_), channel_id=1, source_target_pairs={{0,2},{2,0},{4,6},{6,4},{8,10},{10,8},{12,14},{14,12},{16,18},{18,... | collective-permute-start | bytes 786440 | tf_op jit(solution)/shard_map/ppermute | solution.py:294
  90.3 6.9 %collective-permute-start.21 = (bf16[768,128]{1,0:T(8,128)(2,1)S(1)}, bf16[768,128]{1,0:T(8,128)(2,1)S(1)}, u32[]{:S(2)}, u32[]{:S(2)}) collective-permute-start(bf16[768,128]{1,0:T(8,128)(2,1)S(1)} %pad_maximum_fusion.2.refs_10_), channel_id=1, source_target_pairs={{0,4},{2,6},{4,0},{6,2},{8,12},{10,14},{12,8},{14,10},{16,20},{18,... | collective-permute-start | bytes 589832 | tf_op jit(solution)/shard_map/ppermute | solution.py:294
  91.7 5.5 %collective-permute-start.6 = (bf16[1024,128]{1,0:T(8,128)(2,1)S(1)}, bf16[1024,128]{1,0:T(8,128)(2,1)S(1)}, u32[]{:S(2)}, u32[]{:S(2)}) collective-permute-start(bf16[1024,128]{1,0:T(8,128)(2,1)S(1)} %pad_maximum_fusion.refs_2_), channel_id=1, source_target_pairs={{0,2},{2,0},{4,6},{6,4},{8,10},{10,8},{12,14},{14,12},{16,18},{18,... | collective-permute-start | bytes 786440 | tf_op jit(solution)/shard_map/ppermute | solution.py:294
  91.8 5.5 %collective-permute-start.15 = (bf16[1024,128]{1,0:T(8,128)(2,1)S(1)}, bf16[1024,128]{1,0:T(8,128)(2,1)S(1)}, u32[]{:S(2)}, u32[]{:S(2)}) collective-permute-start(bf16[1024,128]{1,0:T(8,128)(2,1)S(1)} %collective-permute-done.13.refs_7_), channel_id=1, source_target_pairs={{0,2},{2,0},{4,6},{6,4},{8,10},{10,8},{12,14},{14,12},{16,18},{18,... | collective-permute-start | bytes 786440 | tf_op jit(solution)/shard_map/ppermute | solution.py:294
  95.0 2.2 %collective-permute-start.7 = (bf16[1024,128]{1,0:T(8,128)(2,1)S(1)}, bf16[1024,128]{1,0:T(8,128)(2,1)S(1)}, u32[]{:S(2)}, u32[]{:S(2)}) collective-permute-start(bf16[1024,128]{1,0:T(8,128)(2,1)S(1)} %collective-permute-done.5.refs_3_), channel_id=1, source_target_pairs={{0,2},{2,0},{4,6},{6,4},{8,10},{10,8},{12,14},{14,12},{16,18},{18,... | collective-permute-start | bytes 786440 | tf_op jit(solution)/shard_map/ppermute | solution.py:294
  112.3 34.5 %collective-permute-start.24 = (bf16[1024,256]{1,0:T(8,128)(2,1)}, bf16[1024,256]{1,0:T(8,128)(2,1)S(1)}, u32[]{:S(2)}, u32[]{:S(2)}) collective-permute-start(bf16[1024,256]{1,0:T(8,128)(2,1)} %mix.3.refs_21_), channel_id=1, source_target_pairs={{0,1},{1,0},{2,3},{3,2},{4,5},{5,4},{6,7},{7,6},{8,9},{9,8},{10,11... | collective-permute-start | bytes 1572872 | tf_op jit(solution)/shard_map/ppermute | solution.py:361
  127.8 19.1 %collective-permute-start.25 = (bf16[1024,256]{1,0:T(8,128)(2,1)}, bf16[1024,256]{1,0:T(8,128)(2,1)S(1)}, u32[]{:S(2)}, u32[]{:S(2)}) collective-permute-start(bf16[1024,256]{1,0:T(8,128)(2,1)} %mix.4.refs_21_), channel_id=1, source_target_pairs={{0,1},{1,0},{2,3},{3,2},{4,5},{5,4},{6,7},{7,6},{8,9},{9,8},{10,11... | collective-permute-start | bytes 1572872 | tf_op jit(solution)/shard_map/ppermute | solution.py:361
  (18 other events, 112.9 us)

commit v10 on v8

--- a/solution.py
+++ b/solution.py
@@ -16,7 +16,7 @@
 QUARTER = LANES // QUADS
 WIDTH = GROUP * LANES
 VMEM_LIMIT = 56 * 2**20
-CHUNKS = (5, 4, 2)
+CHUNKS = (4, 4, 3)
 
 SIN_COEF = (4.4428679, -7.30744342, 3.59478808, -0.78437403)
 COS_COEF = (1.41420408, -6.97764206, 5.71523839, -1.72834866)

time: 145 us -> 134 us (0.924)
  waiting for transfers between devices: 39.6 us -> 32.6 us
  starting transfers between devices: 25 us -> 22.7 us
  other arithmetic: 7.82 us -> 6.18 us
    ppermute x24, waiting for transfers between devices: 35.1 us -> 28 us  [moved(): lax.ppermute(x, 'atoms', [(i, target(i)) for i in range(atom_devices)])]
    ppermute x24, starting transfers between devices: 23.5 us -> 21.1 us  [moved(): lax.ppermute(x, 'atoms', [(i, target(i)) for i in range(atom_devices)])]
    convert_element_type x12, other arithmetic: 5.15 us -> 3.51 us  [added(): return sum((term.astype(F32) for term in terms)).astype(BF16)]
  transfers between devices with their start and end apart: 25 -> 25, of which waited for: 14 -> 9; matrix products, arithmetic and copies ran while one was open for 3% -> 3% of each run, Pallas kernels for 18% -> 28%
where the time goes in v10:
time: 134 us; the launch traced here: 133 us
  Pallas kernels  70.1 us (52%)
  waiting for transfers between devices  32.6 us (24%)
  starting transfers between devices  22.7 us (17%)
  other arithmetic  6.18 us (5%)
    pallas_call x2, Pallas kernels, mix(): pl.pallas_call(lambda *refs: mix_kernel(CHUNKS, min(256, half_atoms), *re...  38.1 us
    pallas_call x3, Pallas kernels, make_states(): pl.pallas_call(functools.partial(states_kernel, first, min(256, atoms), 1...  28.3 us
    ppermute x24, waiting for transfers between devices, moved(): lax.ppermute(x, 'atoms', [(i, target(i)) for i in range(atom_devices)])  28 us
    ppermute x24, starting transfers between devices, moved(): lax.ppermute(x, 'atoms', [(i, target(i)) for i in range(atom_devices)])  21.1 us
    ppermute x1, waiting for transfers between devices, per_device(): theirs = lax.ppermute(sent, 'dirs', [(0, 1), (1, 0)])  4.54 us
    pallas_call x1, Pallas kernels, per_device(): pl.pallas_call(prepare_kernel, in_specs=[smem] + [vmem] * 7, out_specs=[v...  3.78 us
    convert_element_type x12, other arithmetic, added(): return sum((term.astype(F32) for term in terms)).astype(BF16)  3.51 us
  transfers between devices with their start and end apart: 25, of which 9 were waited for; matrix products, arithmetic and copies ran while one was open for 3% of the time, Pallas kernels for 28%

profile of v10, /device:TPU:0, one launch (start us, length us, event | category | flops | bytes accessed | tf_op | source)
XLA Modules:
  0.0 133.2 jit_solution(2797406052815929612)
XLA Ops:
  0.6 3.8 %prepare.1 = (bf16[128,2048]{1,0:T(8,128)(2,1)}, bf16[128,2048]{1,0:T(8,128)(2,1)}, bf16[128,2048]{1,0:T(8,128)(2,1)}, bf16[128,2048]{1,0:T(8,128)(2,1)}, f32[128,2048]{1,0:T(8,128)}) custom-call(s32[1]{0:T(128)} %bitcast.index_ref.refs_0_, s32[1,2048]{1,0:T(1,128)} %bitcast.33, s32[1,2048]{1,0:T(1,128)} %bitcast.34, f32[5,128]{1,0:T(8,128)} %gain_ref.1, ...), custom_call_target="tpu_custom_call" | custom-call | tf_op jit(solution)/shard_map/prepare/pallas_call | solution.py:230
  4.4 10.0 %states.3 = (bf16[2,4,256,128]{3,2,1,0:T(8,128)(2,1)}, bf16[2,4,256,128]{3,2,1,0:T(8,128)(2,1)}, bf16[1408,2048]{1,0:T(8,128)(2,1)}, bf16[1408,2048]{1,0:T(8,128)(2,1)}) custom-call(s32[1]{0:T(128)} %bitcast.index_ref.refs_0_, f32[3,44]{1,0:T(4,128)} %dirs_ref.5, f32[44]{0:T(128)} %weight_ref.5, s32[44]{0:T(128)} %mask_ref.5, f32[1,32]{1,0:T(1,128)} %bitcast.35, ...), custom_call_target="tpu_custom_call" | custom-call | flops 4294967296 | bytes 8388608 | tf_op jit(solution)/shard_map/states/pallas_call | solution.py:248
  14.9 10.0 %states.4 = (bf16[2,4,256,128]{3,2,1,0:T(8,128)(2,1)}, bf16[2,4,256,128]{3,2,1,0:T(8,128)(2,1)}, bf16[1408,2048]{1,0:T(8,128)(2,1)}, bf16[1408,2048]{1,0:T(8,128)(2,1)}) custom-call(s32[1]{0:T(128)} %bitcast.index_ref.refs_0_, f32[3,44]{1,0:T(4,128)} %dirs_ref.5, f32[44]{0:T(128)} %weight_ref.5, ...), custom_call_target="tpu_custom_call", output_to_operand_aliasing={{2}: (10, {}), {3}: (11, {})} | custom-call | flops 4294967296 | bytes 8388608 | tf_op jit(solution)/shard_map/states/pallas_call | solution.py:248
  25.1 3.0 %collective-permute-start.1 = (bf16[4,256,128]{2,1,0:T(8,128)(2,1)S(1)}, bf16[4,256,128]{2,1,0:T(8,128)(2,1)S(1)}, u32[]{:S(2)}, u32[]{:S(2)}) collective-permute-start(bf16[4,256,128]{2,1,0:T(8,128)(2,1)S(1)} %fusion.7.refs_0_), channel_id=1, source_target_pairs={{0,4},{2,6},{4,0},{6,2},{8,12},{10,14},{12,8},{14,10},{16,20},{18,... | collective-permute-start | bytes 786440 | tf_op jit(solution)/shard_map/ppermute | solution.py:267
  29.1 1.7 %collective-permute-start.9 = (bf16[4,256,128]{2,1,0:T(8,128)(2,1)S(1)}, bf16[4,256,128]{2,1,0:T(8,128)(2,1)S(1)}, u32[]{:S(2)}, u32[]{:S(2)}) collective-permute-start(bf16[4,256,128]{2,1,0:T(8,128)(2,1)S(1)} %fusion.8), channel_id=1, source_target_pairs={{0,4},{2,6},{4,0},{6,2},{8,12},{10,14},{12,8},{14,10},{16,20},{18,... | collective-permute-start | bytes 786440 | tf_op jit(solution)/shard_map/ppermute | solution.py:267
  30.8 8.2 %states.5 = (bf16[2,4,192,128]{3,2,1,0:T(8,128)(2,1)}, bf16[2,4,192,128]{3,2,1,0:T(8,128)(2,1)}, bf16[1408,2048]{1,0:T(8,128)(2,1)}, bf16[1408,2048]{1,0:T(8,128)(2,1)}) custom-call(s32[1]{0:T(128)} %bitcast.index_ref.refs_0_, f32[3,44]{1,0:T(4,128)} %dirs_ref.5, f32[44]{0:T(128)} %weight_ref.5, ...), custom_call_target="tpu_custom_call", output_to_operand_aliasing={{2}: (11, {}), {3}: (12, {})} | custom-call | flops 3221225472 | bytes 6291456 | tf_op jit(solution)/shard_map/states/pallas_call | solution.py:248
  39.2 1.7 %collective-permute-start.2 = (bf16[2,256,128]{2,1,0:T(8,128)(2,1)S(1)}, bf16[2,256,128]{2,1,0:T(8,128)(2,1)S(1)}, u32[]{:S(2)}, u32[]{:S(2)}) collective-permute-start(bf16[2,256,128]{2,1,0:T(8,128)(2,1)S(1)} %slice.107), channel_id=1, source_target_pairs={{0,8},{2,10},{4,12},{6,14},{8,0},{10,2},{12,4},{14,6},{16,24},{18,... | collective-permute-start | bytes 393224 | tf_op jit(solution)/shard_map/ppermute | solution.py:267
  42.2 3.4 %collective-permute-done.2 = bf16[2,256,128]{2,1,0:T(8,128)(2,1)S(1)} collective-permute-done((bf16[2,256,128]{2,1,0:T(8,128)(2,1)S(1)}, bf16[2,256,128]{2,1,0:T(8,128)(2,1)S(1)}, u32[]{:S(2)}, u32[]{:S(2)}) %collective-permute-start.2) | collective-permute-done | bytes 131104 | tf_op jit(solution)/shard_map/ppermute | solution.py:267
  45.6 2.7 %collective-permute-start.3 = (bf16[2,256,128]{2,1,0:T(8,128)(2,1)S(1)}, bf16[2,256,128]{2,1,0:T(8,128)(2,1)S(1)}, u32[]{:S(2)}, u32[]{:S(2)}) collective-permute-start(bf16[2,256,128]{2,1,0:T(8,128)(2,1)S(1)} %add_convert_fusion.6), channel_id=1, source_target_pairs={{0,16},{2,18},{4,20},{6,22},{8,24},{10,26},{12,28},{14,30},{16,0},... | collective-permute-start | bytes 393224 | tf_op jit(solution)/shard_map/ppermute | solution.py:267
  48.4 2.8 %collective-permute-start.11 = (bf16[2,256,128]{2,1,0:T(8,128)(2,1)S(1)}, bf16[2,256,128]{2,1,0:T(8,128)(2,1)S(1)}, u32[]{:S(2)}, u32[]{:S(2)}) collective-permute-start(bf16[2,256,128]{2,1,0:T(8,128)(2,1)S(1)} %add_convert_fusion.4), channel_id=1, source_target_pairs={{0,16},{2,18},{4,20},{6,22},{8,24},{10,26},{12,28},{14,30},{16,0},... | collective-permute-start | bytes 393224 | tf_op jit(solution)/shard_map/ppermute | solution.py:267
  52.7 5.3 %collective-permute-done.3 = bf16[2,256,128]{2,1,0:T(8,128)(2,1)S(1)} collective-permute-done((bf16[2,256,128]{2,1,0:T(8,128)(2,1)S(1)}, bf16[2,256,128]{2,1,0:T(8,128)(2,1)S(1)}, u32[]{:S(2)}, u32[]{:S(2)}) %collective-permute-start.3) | collective-permute-done | bytes 131104 | tf_op jit(solution)/shard_map/ppermute | solution.py:267
  59.2 2.1 %collective-permute-start.18 = (bf16[2,192,128]{2,1,0:T(8,128)(2,1)S(1)}, bf16[2,192,128]{2,1,0:T(8,128)(2,1)S(1)}, u32[]{:S(2)}, u32[]{:S(2)}) collective-permute-start(bf16[2,192,128]{2,1,0:T(8,128)(2,1)S(1)} %slice.115), channel_id=1, source_target_pairs={{0,8},{2,10},{4,12},{6,14},{8,0},{10,2},{12,4},{14,6},{16,24},{18,... | collective-permute-start | bytes 294920 | tf_op jit(solution)/shard_map/ppermute | solution.py:267
  61.4 4.6 %collective-permute-done.18 = bf16[2,192,128]{2,1,0:T(8,128)(2,1)S(1)} collective-permute-done((bf16[2,192,128]{2,1,0:T(8,128)(2,1)S(1)}, bf16[2,192,128]{2,1,0:T(8,128)(2,1)S(1)}, u32[]{:S(2)}, u32[]{:S(2)}) %collective-permute-start.18) | collective-permute-done | bytes 98336 | tf_op jit(solution)/shard_map/ppermute | solution.py:267
  66.0 1.9 %collective-permute-start.19 = (bf16[2,192,128]{2,1,0:T(8,128)(2,1)S(1)}, bf16[2,192,128]{2,1,0:T(8,128)(2,1)S(1)}, u32[]{:S(2)}, u32[]{:S(2)}) collective-permute-start(bf16[2,192,128]{2,1,0:T(8,128)(2,1)S(1)} %add_convert_fusion.8), channel_id=1, source_target_pairs={{0,16},{2,18},{4,20},{6,22},{8,24},{10,26},{12,28},{14,30},{16,0},... | collective-permute-start | bytes 294920 | tf_op jit(solution)/shard_map/ppermute | solution.py:267
  68.6 4.1 %collective-permute-done.19 = bf16[2,192,128]{2,1,0:T(8,128)(2,1)S(1)} collective-permute-done((bf16[2,192,128]{2,1,0:T(8,128)(2,1)S(1)}, bf16[2,192,128]{2,1,0:T(8,128)(2,1)S(1)}, u32[]{:S(2)}, u32[]{:S(2)}) %collective-permute-start.19) | collective-permute-done | bytes 98336 | tf_op jit(solution)/shard_map/ppermute | solution.py:267
  73.5 3.9 %collective-permute-done.20 = bf16[384,128]{1,0:T(8,128)(2,1)S(1)} collective-permute-done((bf16[384,128]{1,0:T(8,128)(2,1)S(1)}, bf16[384,128]{1,0:T(8,128)(2,1)S(1)}, u32[]{:S(2)}, u32[]{:S(2)}) %collective-permute-start.20) | collective-permute-done | bytes 98336 | tf_op jit(solution)/shard_map/ppermute | solution.py:267
  78.4 3.7 %collective-permute-done.13.refs_7_ = bf16[1024,128]{1,0:T(8,128)(2,1)S(1)} collective-permute-done((bf16[1024,128]{1,0:T(8,128)(2,1)S(1)}, bf16[1024,128]{1,0:T(8,128)(2,1)S(1)}, u32[]{:S(2)}, u32[]{:S(2)}) %collective-permute-start.13) | collective-permute-done | bytes 262176 | tf_op jit(solution)/shard_map/ppermute | solution.py:267
  82.7 1.6 %collective-permute-done.21.refs_11_ = bf16[768,128]{1,0:T(8,128)(2,1)S(1)} collective-permute-done((bf16[768,128]{1,0:T(8,128)(2,1)S(1)}, bf16[768,128]{1,0:T(8,128)(2,1)S(1)}, u32[]{:S(2)}, u32[]{:S(2)}) %collective-permute-start.21) | collective-permute-done | bytes 196640 | tf_op jit(solution)/shard_map/ppermute | solution.py:267
  84.4 1.4 %collective-permute-done.23.refs_13_ = bf16[768,128]{1,0:T(8,128)(2,1)S(1)} collective-permute-done((bf16[768,128]{1,0:T(8,128)(2,1)S(1)}, bf16[768,128]{1,0:T(8,128)(2,1)S(1)}, u32[]{:S(2)}, u32[]{:S(2)}) %collective-permute-start.23) | collective-permute-done | bytes 196640 | tf_op jit(solution)/shard_map/ppermute | solution.py:267
  86.4 18.7 %mix.2.refs_21_ = bf16[1024,512]{1,0:T(8,128)(2,1)} custom-call(s32[1]{0:T(128)} %bitcast.index_ref.refs_0_, s32[1]{0:T(128)} %bitcast.14.refs_1_, bf16[1024,128]{1,0:T(8,128)(2,1)} %copy-done.3, bf16[1024,128]{1,0:T(8,128)(2,1)} %copy-done.6, bf16[1024,128]{1,0:T(8,128)(2,1)} %copy-done.8, bf16[1024,128]{1,0:T(8,128)(2,1)} %copy-done.10, ...), custom_call_target="tpu_custom_call" | custom-call | flops 5905580032 | bytes 11534336 | tf_op jit(solution)/shard_map/mix/pallas_call | solution.py:293
  105.1 1.5 %collective-permute-start.24 = (bf16[1024,512]{1,0:T(8,128)(2,1)}, bf16[1024,512]{1,0:T(8,128)(2,1)S(1)}, u32[]{:S(2)}, u32[]{:S(2)}) collective-permute-start(bf16[1024,512]{1,0:T(8,128)(2,1)} %mix.2.refs_21_), channel_id=1, source_target_pairs={{0,1},{1,0},{2,3},{3,2},{4,5},{5,4},{6,7},{7,6},{8,9},{9,8},{10,11... | collective-permute-start | bytes 3145736 | tf_op jit(solution)/shard_map/ppermute | solution.py:330
  106.7 19.4 %mix.3 = f32[1024,512]{1,0:T(8,128)} custom-call(s32[1]{0:T(128)} %bitcast.index_ref.refs_0_, s32[1]{0:T(128)} %bitcast.1.refs_1_, bf16[1024,128]{1,0:T(8,128)(2,1)} %copy-done.3, bf16[1024,128]{1,0:T(8,128)(2,1)} %copy-done.6, bf16[1024,128]{1,0:T(8,128)(2,1)} %copy-done.8, bf16[1024,128]{1,0:T(8,128)(2,1)} %copy-done.10, bf16[1024,128]{1,0:T(8,128)(2,1)} %copy-done.4, ...), custom_call_target="tpu_custom_call" | custom-call | flops 5905580032 | bytes 11534336 | tf_op jit(solution)/shard_map/mix/pallas_call | solution.py:293
  126.0 4.5 %collective-permute-done.24 = bf16[1024,512]{1,0:T(8,128)(2,1)S(1)} collective-permute-done((bf16[1024,512]{1,0:T(8,128)(2,1)}, bf16[1024,512]{1,0:T(8,128)(2,1)S(1)}, u32[]{:S(2)}, u32[]{:S(2)}) %collective-permute-start.24) | collective-permute-done | bytes 1048608 | tf_op jit(solution)/shard_map/ppermute | solution.py:330
  130.6 2.6 %fusion = (bf16[1024,128]{1,0:T(8,128)(2,1)}, bf16[1024,128]{1,0:T(8,128)(2,1)}, bf16[1024,128]{1,0:T(8,128)(2,1)}, bf16[1024,128]{1,0:T(8,128)(2,1)}) fusion(f32[1024,512]{1,0:T(8,128)} %mix.3, bf16[1024,512]{1,0:T(8,128)(2,1)S(1)} %collective-permute-done.24), kind=kLoop, calls=%fused_computation.1 | loop fusion | flops 1572864 | bytes 4194304 | tf_op jit(solution)/shard_map/convert_element_type | solution.py:333
  (81 shorter events, 9.6 us)
Async XLA Ops:
  14.4 10.6 %collective-permute-start = (bf16[2,4,256,128]{3,2,1,0:T(8,128)(2,1)}, bf16[2,4,256,128]{3,2,1,0:T(8,128)(2,1)S(1)}, u32[]{:S(2)}, u32[]{:S(2)}) collective-permute-start(bf16[2,4,256,128]{3,2,1,0:T(8,128)(2,1)} %get-tuple-element.24), channel_id=1, source_target_pairs={{0,2},{2,0},{4,6},{6,4},{8,10},{10,8},{12,14},{14,12},{16,18},{18,... | collective-permute-start | bytes 1572872 | tf_op jit(solution)/shard_map/ppermute | solution.py:267
  24.9 3.2 %collective-permute-start.8 = (bf16[2,4,256,128]{3,2,1,0:T(8,128)(2,1)}, bf16[2,4,256,128]{3,2,1,0:T(8,128)(2,1)S(1)}, u32[]{:S(2)}, u32[]{:S(2)}) collective-permute-start(bf16[2,4,256,128]{3,2,1,0:T(8,128)(2,1)} %get-tuple-element.28), channel_id=1, source_target_pairs={{0,2},{2,0},{4,6},{6,4},{8,10},{10,8},{12,14},{14,12},{16,18},{18,... | collective-permute-start | bytes 1572872 | tf_op jit(solution)/shard_map/ppermute | solution.py:267
  25.1 14.0 %collective-permute-start.1 = (bf16[4,256,128]{2,1,0:T(8,128)(2,1)S(1)}, bf16[4,256,128]{2,1,0:T(8,128)(2,1)S(1)}, u32[]{:S(2)}, u32[]{:S(2)}) collective-permute-start(bf16[4,256,128]{2,1,0:T(8,128)(2,1)S(1)} %fusion.7.refs_0_), channel_id=1, source_target_pairs={{0,4},{2,6},{4,0},{6,2},{8,12},{10,14},{12,8},{14,10},{16,20},{18,... | collective-permute-start | bytes 786440 | tf_op jit(solution)/shard_map/ppermute | solution.py:267
  29.1 11.8 %collective-permute-start.9 = (bf16[4,256,128]{2,1,0:T(8,128)(2,1)S(1)}, bf16[4,256,128]{2,1,0:T(8,128)(2,1)S(1)}, u32[]{:S(2)}, u32[]{:S(2)}) collective-permute-start(bf16[4,256,128]{2,1,0:T(8,128)(2,1)S(1)} %fusion.8), channel_id=1, source_target_pairs={{0,4},{2,6},{4,0},{6,2},{8,12},{10,14},{12,8},{14,10},{16,20},{18,... | collective-permute-start | bytes 786440 | tf_op jit(solution)/shard_map/ppermute | solution.py:267
  39.0 12.1 %collective-permute-start.16 = (bf16[2,4,192,128]{3,2,1,0:T(8,128)(2,1)}, bf16[2,4,192,128]{3,2,1,0:T(8,128)(2,1)S(1)}, u32[]{:S(2)}, u32[]{:S(2)}) collective-permute-start(bf16[2,4,192,128]{3,2,1,0:T(8,128)(2,1)} %get-tuple-element.32), channel_id=1, source_target_pairs={{0,2},{2,0},{4,6},{6,4},{8,10},{10,8},{12,14},{14,12},{16,18},{18,... | collective-permute-start | bytes 1179656 | tf_op jit(solution)/shard_map/ppermute | solution.py:267
  39.2 6.4 %collective-permute-start.2 = (bf16[2,256,128]{2,1,0:T(8,128)(2,1)S(1)}, bf16[2,256,128]{2,1,0:T(8,128)(2,1)S(1)}, u32[]{:S(2)}, u32[]{:S(2)}) collective-permute-start(bf16[2,256,128]{2,1,0:T(8,128)(2,1)S(1)} %slice.107), channel_id=1, source_target_pairs={{0,8},{2,10},{4,12},{6,14},{8,0},{10,2},{12,4},{14,6},{16,24},{18,... | collective-permute-start | bytes 393224 | tf_op jit(solution)/shard_map/ppermute | solution.py:267
  41.0 7.3 %collective-permute-start.10 = (bf16[2,256,128]{2,1,0:T(8,128)(2,1)S(1)}, bf16[2,256,128]{2,1,0:T(8,128)(2,1)S(1)}, u32[]{:S(2)}, u32[]{:S(2)}) collective-permute-start(bf16[2,256,128]{2,1,0:T(8,128)(2,1)S(1)} %slice.111), channel_id=1, source_target_pairs={{0,8},{2,10},{4,12},{6,14},{8,0},{10,2},{12,4},{14,6},{16,24},{18,... | collective-permute-start | bytes 393224 | tf_op jit(solution)/shard_map/ppermute | solution.py:267
  45.6 12.4 %collective-permute-start.3 = (bf16[2,256,128]{2,1,0:T(8,128)(2,1)S(1)}, bf16[2,256,128]{2,1,0:T(8,128)(2,1)S(1)}, u32[]{:S(2)}, u32[]{:S(2)}) collective-permute-start(bf16[2,256,128]{2,1,0:T(8,128)(2,1)S(1)} %add_convert_fusion.6), channel_id=1, source_target_pairs={{0,16},{2,18},{4,20},{6,22},{8,24},{10,26},{12,28},{14,30},{16,0},... | collective-permute-start | bytes 393224 | tf_op jit(solution)/shard_map/ppermute | solution.py:267
  48.4 12.9 %collective-permute-start.11 = (bf16[2,256,128]{2,1,0:T(8,128)(2,1)S(1)}, bf16[2,256,128]{2,1,0:T(8,128)(2,1)S(1)}, u32[]{:S(2)}, u32[]{:S(2)}) collective-permute-start(bf16[2,256,128]{2,1,0:T(8,128)(2,1)S(1)} %add_convert_fusion.4), channel_id=1, source_target_pairs={{0,16},{2,18},{4,20},{6,22},{8,24},{10,26},{12,28},{14,30},{16,0},... | collective-permute-start | bytes 393224 | tf_op jit(solution)/shard_map/ppermute | solution.py:267
  52.1 6.0 %collective-permute-start.17 = (bf16[4,192,128]{2,1,0:T(8,128)(2,1)S(1)}, bf16[4,192,128]{2,1,0:T(8,128)(2,1)S(1)}, u32[]{:S(2)}, u32[]{:S(2)}) collective-permute-start(bf16[4,192,128]{2,1,0:T(8,128)(2,1)S(1)} %fusion.9), channel_id=1, source_target_pairs={{0,4},{2,6},{4,0},{6,2},{8,12},{10,14},{12,8},{14,10},{16,20},{18,... | collective-permute-start | bytes 589832 | tf_op jit(solution)/shard_map/ppermute | solution.py:267
  58.1 9.9 %collective-permute-start.4 = (bf16[512,128]{1,0:T(8,128)(2,1)S(1)}, bf16[512,128]{1,0:T(8,128)(2,1)S(1)}, u32[]{:S(2)}, u32[]{:S(2)}) collective-permute-start(bf16[512,128]{1,0:T(8,128)(2,1)S(1)} %bitcast.27), channel_id=1, source_target_pairs={{0,8},{2,10},{4,12},{6,14},{8,0},{10,2},{12,4},{14,6},{16,24},{18,... | collective-permute-start | bytes 393224 | tf_op jit(solution)/shard_map/ppermute | solution.py:267
  59.2 6.8 %collective-permute-start.18 = (bf16[2,192,128]{2,1,0:T(8,128)(2,1)S(1)}, bf16[2,192,128]{2,1,0:T(8,128)(2,1)S(1)}, u32[]{:S(2)}, u32[]{:S(2)}) collective-permute-start(bf16[2,192,128]{2,1,0:T(8,128)(2,1)S(1)} %slice.115), channel_id=1, source_target_pairs={{0,8},{2,10},{4,12},{6,14},{8,0},{10,2},{12,4},{14,6},{16,24},{18,... | collective-permute-start | bytes 294920 | tf_op jit(solution)/shard_map/ppermute | solution.py:267
  61.3 11.6 %collective-permute-start.12 = (bf16[512,128]{1,0:T(8,128)(2,1)S(1)}, bf16[512,128]{1,0:T(8,128)(2,1)S(1)}, u32[]{:S(2)}, u32[]{:S(2)}) collective-permute-start(bf16[512,128]{1,0:T(8,128)(2,1)S(1)} %bitcast.29), channel_id=1, source_target_pairs={{0,8},{2,10},{4,12},{6,14},{8,0},{10,2},{12,4},{14,6},{16,24},{18,... | collective-permute-start | bytes 393224 | tf_op jit(solution)/shard_map/ppermute | solution.py:267
  66.0 6.6 %collective-permute-start.19 = (bf16[2,192,128]{2,1,0:T(8,128)(2,1)S(1)}, bf16[2,192,128]{2,1,0:T(8,128)(2,1)S(1)}, u32[]{:S(2)}, u32[]{:S(2)}) collective-permute-start(bf16[2,192,128]{2,1,0:T(8,128)(2,1)S(1)} %add_convert_fusion.8), channel_id=1, source_target_pairs={{0,16},{2,18},{4,20},{6,22},{8,24},{10,26},{12,28},{14,30},{16,0},... | collective-permute-start | bytes 294920 | tf_op jit(solution)/shard_map/ppermute | solution.py:267
  68.0 9.9 %collective-permute-start.5 = (bf16[1024,128]{1,0:T(8,128)(2,1)S(1)}, bf16[1024,128]{1,0:T(8,128)(2,1)S(1)}, u32[]{:S(2)}, u32[]{:S(2)}) collective-permute-start(bf16[1024,128]{1,0:T(8,128)(2,1)S(1)} %pad_maximum_fusion.refs_2_), channel_id=1, source_target_pairs={{0,4},{2,6},{4,0},{6,2},{8,12},{10,14},{12,8},{14,10},{16,20},{18,... | collective-permute-start | bytes 786440 | tf_op jit(solution)/shard_map/ppermute | solution.py:267
  72.7 4.7 %collective-permute-start.20 = (bf16[384,128]{1,0:T(8,128)(2,1)S(1)}, bf16[384,128]{1,0:T(8,128)(2,1)S(1)}, u32[]{:S(2)}, u32[]{:S(2)}) collective-permute-start(bf16[384,128]{1,0:T(8,128)(2,1)S(1)} %bitcast.31), channel_id=1, source_target_pairs={{0,8},{2,10},{4,12},{6,14},{8,0},{10,2},{12,4},{14,6},{16,24},{18,... | collective-permute-start | bytes 294920 | tf_op jit(solution)/shard_map/ppermute | solution.py:267
  72.9 9.3 %collective-permute-start.13 = (bf16[1024,128]{1,0:T(8,128)(2,1)S(1)}, bf16[1024,128]{1,0:T(8,128)(2,1)S(1)}, u32[]{:S(2)}, u32[]{:S(2)}) collective-permute-start(bf16[1024,128]{1,0:T(8,128)(2,1)S(1)} %pad_maximum_fusion.1.refs_6_), channel_id=1, source_target_pairs={{0,4},{2,6},{4,0},{6,2},{8,12},{10,14},{12,8},{14,10},{16,20},{18,... | collective-permute-start | bytes 786440 | tf_op jit(solution)/shard_map/ppermute | solution.py:267
  73.5 8.7 %collective-permute-start.6 = (bf16[1024,128]{1,0:T(8,128)(2,1)S(1)}, bf16[1024,128]{1,0:T(8,128)(2,1)S(1)}, u32[]{:S(2)}, u32[]{:S(2)}) collective-permute-start(bf16[1024,128]{1,0:T(8,128)(2,1)S(1)} %pad_maximum_fusion.refs_2_), channel_id=1, source_target_pairs={{0,2},{2,0},{4,6},{6,4},{8,10},{10,8},{12,14},{14,12},{16,18},{18,... | collective-permute-start | bytes 786440 | tf_op jit(solution)/shard_map/ppermute | solution.py:267
  77.4 6.9 %collective-permute-start.21 = (bf16[768,128]{1,0:T(8,128)(2,1)S(1)}, bf16[768,128]{1,0:T(8,128)(2,1)S(1)}, u32[]{:S(2)}, u32[]{:S(2)}) collective-permute-start(bf16[768,128]{1,0:T(8,128)(2,1)S(1)} %pad_maximum_fusion.2.refs_10_), channel_id=1, source_target_pairs={{0,4},{2,6},{4,0},{6,2},{8,12},{10,14},{12,8},{14,10},{16,20},{18,... | collective-permute-start | bytes 589832 | tf_op jit(solution)/shard_map/ppermute | solution.py:267
  77.9 6.4 %collective-permute-start.14 = (bf16[1024,128]{1,0:T(8,128)(2,1)S(1)}, bf16[1024,128]{1,0:T(8,128)(2,1)S(1)}, u32[]{:S(2)}, u32[]{:S(2)}) collective-permute-start(bf16[1024,128]{1,0:T(8,128)(2,1)S(1)} %pad_maximum_fusion.1.refs_6_), channel_id=1, source_target_pairs={{0,2},{2,0},{4,6},{6,4},{8,10},{10,8},{12,14},{14,12},{16,18},{18,... | collective-permute-start | bytes 786440 | tf_op jit(solution)/shard_map/ppermute | solution.py:267
  77.9 6.4 %collective-permute-start.7 = (bf16[1024,128]{1,0:T(8,128)(2,1)S(1)}, bf16[1024,128]{1,0:T(8,128)(2,1)S(1)}, u32[]{:S(2)}, u32[]{:S(2)}) collective-permute-start(bf16[1024,128]{1,0:T(8,128)(2,1)S(1)} %collective-permute-done.5.refs_3_), channel_id=1, source_target_pairs={{0,2},{2,0},{4,6},{6,4},{8,10},{10,8},{12,14},{14,12},{16,18},{18,... | collective-permute-start | bytes 786440 | tf_op jit(solution)/shard_map/ppermute | solution.py:267
  82.2 2.2 %collective-permute-start.15 = (bf16[1024,128]{1,0:T(8,128)(2,1)S(1)}, bf16[1024,128]{1,0:T(8,128)(2,1)S(1)}, u32[]{:S(2)}, u32[]{:S(2)}) collective-permute-start(bf16[1024,128]{1,0:T(8,128)(2,1)S(1)} %collective-permute-done.13.refs_7_), channel_id=1, source_target_pairs={{0,2},{2,0},{4,6},{6,4},{8,10},{10,8},{12,14},{14,12},{16,18},{18,... | collective-permute-start | bytes 786440 | tf_op jit(solution)/shard_map/ppermute | solution.py:267
  82.2 2.1 %collective-permute-start.22 = (bf16[768,128]{1,0:T(8,128)(2,1)S(1)}, bf16[768,128]{1,0:T(8,128)(2,1)S(1)}, u32[]{:S(2)}, u32[]{:S(2)}) collective-permute-start(bf16[768,128]{1,0:T(8,128)(2,1)S(1)} %pad_maximum_fusion.2.refs_10_), channel_id=1, source_target_pairs={{0,2},{2,0},{4,6},{6,4},{8,10},{10,8},{12,14},{14,12},{16,18},{18,... | collective-permute-start | bytes 589832 | tf_op jit(solution)/shard_map/ppermute | solution.py:267
  105.1 25.4 %collective-permute-start.24 = (bf16[1024,512]{1,0:T(8,128)(2,1)}, bf16[1024,512]{1,0:T(8,128)(2,1)S(1)}, u32[]{:S(2)}, u32[]{:S(2)}) collective-permute-start(bf16[1024,512]{1,0:T(8,128)(2,1)} %mix.2.refs_21_), channel_id=1, source_target_pairs={{0,1},{1,0},{2,3},{3,2},{4,5},{5,4},{6,7},{7,6},{8,9},{9,8},{10,11... | collective-permute-start | bytes 3145736 | tf_op jit(solution)/shard_map/ppermute | solution.py:330
  (16 other events, 89.3 us)

commit v11 on v10

--- a/solution.py
+++ b/solution.py
@@ -292,7 +292,7 @@
         )
         return pl.pallas_call(
             lambda *refs: mix_kernel(
-                CHUNKS, min(256, half_atoms), *refs[: 2 + len(pieces) + 7],
+                CHUNKS, min(512, half_atoms), *refs[: 2 + len(pieces) + 7],
                 *refs[2 + len(pieces) + 7 + len(after) :],
             ),
             grid_spec=pltpu.PrefetchScalarGridSpec(
@@ -328,7 +328,7 @@
     pieces = [piece for each in made for piece in summed(*each)]
     sent = mix(1 - mine, pieces, phases, BF16)
     theirs = lax.ppermute(sent, "dirs", [(0, 1), (1, 0)])
-    ours = mix(mine, pieces, phases, F32, [sent])
+    ours = mix(mine, pieces, phases, BF16, [sent])
     lanes = [slice(at * feats, (at + 1) * feats) for at in range(4)]
     return tuple((ours[:, at] + theirs[:, at].astype(F32)).astype(BF16) for at in lanes)
 

time: 134 us -> 136 us (1.015)
  waiting for transfers between devices: 32.6 us -> 28.6 us
  Pallas kernels: 70.1 us -> 73.7 us
  starting transfers between devices: 22.7 us -> 25.4 us
    pallas_call x2, Pallas kernels: 38.1 us -> 41.5 us  [mix(): pl.pallas_call(lambda *refs: mix_kernel(CHUNKS, min(512, half_atoms), *re...]
    ppermute x24, starting transfers between devices: 21.1 us -> 23.9 us  [moved(): lax.ppermute(x, 'atoms', [(i, target(i)) for i in range(atom_devices)])]
    ppermute x24, waiting for transfers between devices: 28 us -> 25.4 us  [moved(): lax.ppermute(x, 'atoms', [(i, target(i)) for i in range(atom_devices)])]
  transfers between devices with their start and end apart: 25 -> 25, of which waited for: 9 -> 11; matrix products, arithmetic and copies ran while one was open for 3% -> 3% of each run, Pallas kernels for 28% -> 21%
where the time goes in v11:
time: 136 us
  Pallas kernels  73.7 us (54%)
  waiting for transfers between devices  28.6 us (21%)
  starting transfers between devices  25.4 us (19%)
  other arithmetic  5.92 us (4%)
    pallas_call x2, Pallas kernels, mix(): pl.pallas_call(lambda *refs: mix_kernel(CHUNKS, min(512, half_atoms), *re...  41.5 us
    pallas_call x3, Pallas kernels, make_states(): pl.pallas_call(functools.partial(states_kernel, first, min(256, atoms), 1...  28.3 us
    ppermute x24, waiting for transfers between devices, moved(): lax.ppermute(x, 'atoms', [(i, target(i)) for i in range(atom_devices)])  25.4 us
    ppermute x24, starting transfers between devices, moved(): lax.ppermute(x, 'atoms', [(i, target(i)) for i in range(atom_devices)])  23.9 us
    pallas_call x1, Pallas kernels, per_device(): pl.pallas_call(prepare_kernel, in_specs=[smem] + [vmem] * 7, out_specs=[v...  3.81 us
    convert_element_type x12, other arithmetic, added(): return sum((term.astype(F32) for term in terms)).astype(BF16)  3.51 us
    ppermute x1, waiting for transfers between devices, per_device(): theirs = lax.ppermute(sent, 'dirs', [(0, 1), (1, 0)])  3.19 us
  transfers between devices with their start and end apart: 25, of which 11 were waited for; matrix products, arithmetic and copies ran while one was open for 3% of the time, Pallas kernels for 21%

profile of v11, /device:TPU:0, one launch (start us, length us, event | category | flops | bytes accessed | tf_op | source)
XLA Modules:
  0.0 135.8 jit_solution(5993198270027660964)
XLA Ops:
  0.6 3.8 %prepare.1 = (bf16[128,2048]{1,0:T(8,128)(2,1)}, bf16[128,2048]{1,0:T(8,128)(2,1)}, bf16[128,2048]{1,0:T(8,128)(2,1)}, bf16[128,2048]{1,0:T(8,128)(2,1)}, f32[128,2048]{1,0:T(8,128)}) custom-call(s32[1]{0:T(128)} %bitcast.index_ref.refs_0_, s32[1,2048]{1,0:T(1,128)} %bitcast.33, s32[1,2048]{1,0:T(1,128)} %bitcast.34, f32[5,128]{1,0:T(8,128)} %gain_ref.1, ...), custom_call_target="tpu_custom_call" | custom-call | tf_op jit(solution)/shard_map/prepare/pallas_call | solution.py:230
  4.4 10.0 %states.3 = (bf16[2,4,256,128]{3,2,1,0:T(8,128)(2,1)}, bf16[2,4,256,128]{3,2,1,0:T(8,128)(2,1)}, bf16[1408,2048]{1,0:T(8,128)(2,1)}, bf16[1408,2048]{1,0:T(8,128)(2,1)}) custom-call(s32[1]{0:T(128)} %bitcast.index_ref.refs_0_, f32[3,44]{1,0:T(4,128)} %dirs_ref.5, f32[44]{0:T(128)} %weight_ref.5, s32[44]{0:T(128)} %mask_ref.5, f32[1,32]{1,0:T(1,128)} %bitcast.35, ...), custom_call_target="tpu_custom_call" | custom-call | flops 4294967296 | bytes 8388608 | tf_op jit(solution)/shard_map/states/pallas_call | solution.py:248
  14.5 10.1 %states.4 = (bf16[2,4,256,128]{3,2,1,0:T(8,128)(2,1)}, bf16[2,4,256,128]{3,2,1,0:T(8,128)(2,1)}, bf16[1408,2048]{1,0:T(8,128)(2,1)}, bf16[1408,2048]{1,0:T(8,128)(2,1)}) custom-call(s32[1]{0:T(128)} %bitcast.index_ref.refs_0_, f32[3,44]{1,0:T(4,128)} %dirs_ref.5, f32[44]{0:T(128)} %weight_ref.5, ...), custom_call_target="tpu_custom_call", output_to_operand_aliasing={{2}: (10, {}), {3}: (11, {})} | custom-call | flops 4294967296 | bytes 8388608 | tf_op jit(solution)/shard_map/states/pallas_call | solution.py:248
  25.1 1.7 %collective-permute-done.8 = bf16[2,4,256,128]{3,2,1,0:T(8,128)(2,1)S(1)} collective-permute-done((bf16[2,4,256,128]{3,2,1,0:T(8,128)(2,1)}, bf16[2,4,256,128]{3,2,1,0:T(8,128)(2,1)S(1)}, u32[]{:S(2)}, u32[]{:S(2)}) %collective-permute-start.8) | collective-permute-done | bytes 524320 | tf_op jit(solution)/shard_map/ppermute | solution.py:267
  27.8 2.9 %collective-permute-start.9 = (bf16[4,256,128]{2,1,0:T(8,128)(2,1)S(1)}, bf16[4,256,128]{2,1,0:T(8,128)(2,1)S(1)}, u32[]{:S(2)}, u32[]{:S(2)}) collective-permute-start(bf16[4,256,128]{2,1,0:T(8,128)(2,1)S(1)} %fusion.4), channel_id=1, source_target_pairs={{0,4},{2,6},{4,0},{6,2},{8,12},{10,14},{12,8},{14,10},{16,20},{18,... | collective-permute-start | bytes 786440 | tf_op jit(solution)/shard_map/ppermute | solution.py:267
  31.5 8.2 %states.5 = (bf16[2,4,192,128]{3,2,1,0:T(8,128)(2,1)}, bf16[2,4,192,128]{3,2,1,0:T(8,128)(2,1)}, bf16[1408,2048]{1,0:T(8,128)(2,1)}, bf16[1408,2048]{1,0:T(8,128)(2,1)}) custom-call(s32[1]{0:T(128)} %bitcast.index_ref.refs_0_, f32[3,44]{1,0:T(4,128)} %dirs_ref.5, f32[44]{0:T(128)} %weight_ref.5, ...), custom_call_target="tpu_custom_call", output_to_operand_aliasing={{2}: (11, {}), {3}: (12, {})} | custom-call | flops 3221225472 | bytes 6291456 | tf_op jit(solution)/shard_map/states/pallas_call | solution.py:248
  39.9 1.6 %collective-permute-start.10 = (bf16[2,256,128]{2,1,0:T(8,128)(2,1)S(1)}, bf16[2,256,128]{2,1,0:T(8,128)(2,1)S(1)}, u32[]{:S(2)}, u32[]{:S(2)}) collective-permute-start(bf16[2,256,128]{2,1,0:T(8,128)(2,1)S(1)} %slice.111), channel_id=1, source_target_pairs={{0,8},{2,10},{4,12},{6,14},{8,0},{10,2},{12,4},{14,6},{16,24},{18,... | collective-permute-start | bytes 393224 | tf_op jit(solution)/shard_map/ppermute | solution.py:267
  43.1 1.9 %collective-permute-start.2 = (bf16[2,256,128]{2,1,0:T(8,128)(2,1)S(1)}, bf16[2,256,128]{2,1,0:T(8,128)(2,1)S(1)}, u32[]{:S(2)}, u32[]{:S(2)}) collective-permute-start(bf16[2,256,128]{2,1,0:T(8,128)(2,1)S(1)} %slice.107), channel_id=1, source_target_pairs={{0,8},{2,10},{4,12},{6,14},{8,0},{10,2},{12,4},{14,6},{16,24},{18,... | collective-permute-start | bytes 393224 | tf_op jit(solution)/shard_map/ppermute | solution.py:267
  46.3 2.7 %collective-permute-start.11 = (bf16[2,256,128]{2,1,0:T(8,128)(2,1)S(1)}, bf16[2,256,128]{2,1,0:T(8,128)(2,1)S(1)}, u32[]{:S(2)}, u32[]{:S(2)}) collective-permute-start(bf16[2,256,128]{2,1,0:T(8,128)(2,1)S(1)} %add_convert_fusion.8), channel_id=1, source_target_pairs={{0,16},{2,18},{4,20},{6,22},{8,24},{10,26},{12,28},{14,30},{16,0},... | collective-permute-start | bytes 393224 | tf_op jit(solution)/shard_map/ppermute | solution.py:267
  49.0 2.8 %collective-permute-start.3 = (bf16[2,256,128]{2,1,0:T(8,128)(2,1)S(1)}, bf16[2,256,128]{2,1,0:T(8,128)(2,1)S(1)}, u32[]{:S(2)}, u32[]{:S(2)}) collective-permute-start(bf16[2,256,128]{2,1,0:T(8,128)(2,1)S(1)} %add_convert_fusion.10), channel_id=1, source_target_pairs={{0,16},{2,18},{4,20},{6,22},{8,24},{10,26},{12,28},{14,30},{16,0},... | collective-permute-start | bytes 393224 | tf_op jit(solution)/shard_map/ppermute | solution.py:267
  52.8 1.5 %collective-permute-start.17 = (bf16[4,192,128]{2,1,0:T(8,128)(2,1)S(1)}, bf16[4,192,128]{2,1,0:T(8,128)(2,1)S(1)}, u32[]{:S(2)}, u32[]{:S(2)}) collective-permute-start(bf16[4,192,128]{2,1,0:T(8,128)(2,1)S(1)} %fusion.5), channel_id=1, source_target_pairs={{0,4},{2,6},{4,0},{6,2},{8,12},{10,14},{12,8},{14,10},{16,20},{18,... | collective-permute-start | bytes 589832 | tf_op jit(solution)/shard_map/ppermute | solution.py:267
  54.3 4.5 %collective-permute-done.11 = bf16[2,256,128]{2,1,0:T(8,128)(2,1)S(1)} collective-permute-done((bf16[2,256,128]{2,1,0:T(8,128)(2,1)S(1)}, bf16[2,256,128]{2,1,0:T(8,128)(2,1)S(1)}, u32[]{:S(2)}, u32[]{:S(2)}) %collective-permute-start.11) | collective-permute-done | bytes 131104 | tf_op jit(solution)/shard_map/ppermute | solution.py:267
  59.9 2.1 %collective-permute-start.18 = (bf16[2,192,128]{2,1,0:T(8,128)(2,1)S(1)}, bf16[2,192,128]{2,1,0:T(8,128)(2,1)S(1)}, u32[]{:S(2)}, u32[]{:S(2)}) collective-permute-start(bf16[2,192,128]{2,1,0:T(8,128)(2,1)S(1)} %slice.115), channel_id=1, source_target_pairs={{0,8},{2,10},{4,12},{6,14},{8,0},{10,2},{12,4},{14,6},{16,24},{18,... | collective-permute-start | bytes 294920 | tf_op jit(solution)/shard_map/ppermute | solution.py:267
  62.1 4.6 %collective-permute-done.18 = bf16[2,192,128]{2,1,0:T(8,128)(2,1)S(1)} collective-permute-done((bf16[2,192,128]{2,1,0:T(8,128)(2,1)S(1)}, bf16[2,192,128]{2,1,0:T(8,128)(2,1)S(1)}, u32[]{:S(2)}, u32[]{:S(2)}) %collective-permute-start.18) | collective-permute-done | bytes 98336 | tf_op jit(solution)/shard_map/ppermute | solution.py:267
  66.7 2.1 %collective-permute-start.19 = (bf16[2,192,128]{2,1,0:T(8,128)(2,1)S(1)}, bf16[2,192,128]{2,1,0:T(8,128)(2,1)S(1)}, u32[]{:S(2)}, u32[]{:S(2)}) collective-permute-start(bf16[2,192,128]{2,1,0:T(8,128)(2,1)S(1)} %add_convert_fusion.12), channel_id=1, source_target_pairs={{0,16},{2,18},{4,20},{6,22},{8,24},{10,26},{12,28},{14,30},{16,0},... | collective-permute-start | bytes 294920 | tf_op jit(solution)/shard_map/ppermute | solution.py:267
  70.3 3.1 %collective-permute-done.19 = bf16[2,192,128]{2,1,0:T(8,128)(2,1)S(1)} collective-permute-done((bf16[2,192,128]{2,1,0:T(8,128)(2,1)S(1)}, bf16[2,192,128]{2,1,0:T(8,128)(2,1)S(1)}, u32[]{:S(2)}, u32[]{:S(2)}) %collective-permute-start.19) | collective-permute-done | bytes 98336 | tf_op jit(solution)/shard_map/ppermute | solution.py:267
  75.1 3.1 %collective-permute-done.20 = bf16[384,128]{1,0:T(8,128)(2,1)S(1)} collective-permute-done((bf16[384,128]{1,0:T(8,128)(2,1)S(1)}, bf16[384,128]{1,0:T(8,128)(2,1)S(1)}, u32[]{:S(2)}, u32[]{:S(2)}) %collective-permute-start.20) | collective-permute-done | bytes 98336 | tf_op jit(solution)/shard_map/ppermute | solution.py:267
  80.2 2.7 %collective-permute-done.5.refs_3_ = bf16[1024,128]{1,0:T(8,128)(2,1)S(1)} collective-permute-done((bf16[1024,128]{1,0:T(8,128)(2,1)S(1)}, bf16[1024,128]{1,0:T(8,128)(2,1)S(1)}, u32[]{:S(2)}, u32[]{:S(2)}) %collective-permute-start.5) | collective-permute-done | bytes 262176 | tf_op jit(solution)/shard_map/ppermute | solution.py:267
  83.5 1.7 %collective-permute-done.21.refs_11_ = bf16[768,128]{1,0:T(8,128)(2,1)S(1)} collective-permute-done((bf16[768,128]{1,0:T(8,128)(2,1)S(1)}, bf16[768,128]{1,0:T(8,128)(2,1)S(1)}, u32[]{:S(2)}, u32[]{:S(2)}) %collective-permute-start.21) | collective-permute-done | bytes 196640 | tf_op jit(solution)/shard_map/ppermute | solution.py:267
  87.3 20.8 %mix.2.refs_21_ = bf16[1024,512]{1,0:T(8,128)(2,1)} custom-call(s32[1]{0:T(128)} %bitcast.index_ref.refs_0_, s32[1]{0:T(128)} %bitcast.14.refs_1_, bf16[1024,128]{1,0:T(8,128)(2,1)} %copy-done.4, bf16[1024,128]{1,0:T(8,128)(2,1)} %copy-done.8, bf16[1024,128]{1,0:T(8,128)(2,1)} %copy-done.10, bf16[1024,128]{1,0:T(8,128)(2,1)} %copy-done.12, ...), custom_call_target="tpu_custom_call" | custom-call | flops 5905580032 | bytes 11534336 | tf_op jit(solution)/shard_map/mix/pallas_call | solution.py:293
  108.0 1.5 %collective-permute-start.24 = (bf16[1024,512]{1,0:T(8,128)(2,1)}, bf16[1024,512]{1,0:T(8,128)(2,1)S(1)}, u32[]{:S(2)}, u32[]{:S(2)}) collective-permute-start(bf16[1024,512]{1,0:T(8,128)(2,1)} %mix.2.refs_21_), channel_id=1, source_target_pairs={{0,1},{1,0},{2,3},{3,2},{4,5},{5,4},{6,7},{7,6},{8,9},{9,8},{10,11... | collective-permute-start | bytes 3145736 | tf_op jit(solution)/shard_map/ppermute | solution.py:330
  109.5 20.7 %mix.3 = bf16[1024,512]{1,0:T(8,128)(2,1)} custom-call(s32[1]{0:T(128)} %bitcast.index_ref.refs_0_, s32[1]{0:T(128)} %bitcast.1.refs_1_, bf16[1024,128]{1,0:T(8,128)(2,1)} %copy-done.4, bf16[1024,128]{1,0:T(8,128)(2,1)} %copy-done.8, bf16[1024,128]{1,0:T(8,128)(2,1)} %copy-done.10, bf16[1024,128]{1,0:T(8,128)(2,1)} %copy-done.12, ...), custom_call_target="tpu_custom_call" | custom-call | flops 5905580032 | bytes 11534336 | tf_op jit(solution)/shard_map/mix/pallas_call | solution.py:293
  130.3 3.2 %collective-permute-done.24 = bf16[1024,512]{1,0:T(8,128)(2,1)S(1)} collective-permute-done((bf16[1024,512]{1,0:T(8,128)(2,1)}, bf16[1024,512]{1,0:T(8,128)(2,1)S(1)}, u32[]{:S(2)}, u32[]{:S(2)}) %collective-permute-start.24) | collective-permute-done | bytes 1048608 | tf_op jit(solution)/shard_map/ppermute | solution.py:330
  133.5 2.4 %add_convert_fusion = (bf16[1024,128]{1,0:T(8,128)(2,1)}, bf16[1024,128]{1,0:T(8,128)(2,1)}, bf16[1024,128]{1,0:T(8,128)(2,1)}, bf16[1024,128]{1,0:T(8,128)(2,1)}) fusion(bf16[1024,512]{1,0:T(8,128)(2,1)S(1)} %collective-permute-done.24, bf16[1024,512]{1,0:T(8,128)(2,1)} %mix.3), kind=kLoop, calls=%fused_computation.4 | loop fusion | flops 2097152 | bytes 3145728 | tf_op jit(solution)/shard_map/convert_element_type | solution.py:333
  (83 shorter events, 15.2 us)
Async XLA Ops:
  24.6 2.2 %collective-permute-start.8 = (bf16[2,4,256,128]{3,2,1,0:T(8,128)(2,1)}, bf16[2,4,256,128]{3,2,1,0:T(8,128)(2,1)S(1)}, u32[]{:S(2)}, u32[]{:S(2)}) collective-permute-start(bf16[2,4,256,128]{3,2,1,0:T(8,128)(2,1)} %get-tuple-element.28), channel_id=1, source_target_pairs={{0,2},{2,0},{4,6},{6,4},{8,10},{10,8},{12,14},{14,12},{16,18},{18,... | collective-permute-start | bytes 1572872 | tf_op jit(solution)/shard_map/ppermute | solution.py:267
  25.0 5.7 %collective-permute-start = (bf16[2,4,256,128]{3,2,1,0:T(8,128)(2,1)S(1)}, bf16[2,4,256,128]{3,2,1,0:T(8,128)(2,1)S(1)}, u32[]{:S(2)}, u32[]{:S(2)}) collective-permute-start(bf16[2,4,256,128]{3,2,1,0:T(8,128)(2,1)S(1)} %copy-done.6), channel_id=1, source_target_pairs={{0,2},{2,0},{4,6},{6,4},{8,10},{10,8},{12,14},{14,12},{16,18},{18,... | collective-permute-start | bytes 1572872 | tf_op jit(solution)/shard_map/ppermute | solution.py:267
  27.8 11.9 %collective-permute-start.9 = (bf16[4,256,128]{2,1,0:T(8,128)(2,1)S(1)}, bf16[4,256,128]{2,1,0:T(8,128)(2,1)S(1)}, u32[]{:S(2)}, u32[]{:S(2)}) collective-permute-start(bf16[4,256,128]{2,1,0:T(8,128)(2,1)S(1)} %fusion.4), channel_id=1, source_target_pairs={{0,4},{2,6},{4,0},{6,2},{8,12},{10,14},{12,8},{14,10},{16,20},{18,... | collective-permute-start | bytes 786440 | tf_op jit(solution)/shard_map/ppermute | solution.py:267
  30.8 12.1 %collective-permute-start.1 = (bf16[4,256,128]{2,1,0:T(8,128)(2,1)S(1)}, bf16[4,256,128]{2,1,0:T(8,128)(2,1)S(1)}, u32[]{:S(2)}, u32[]{:S(2)}) collective-permute-start(bf16[4,256,128]{2,1,0:T(8,128)(2,1)S(1)} %fusion.3.refs_0_), channel_id=1, source_target_pairs={{0,4},{2,6},{4,0},{6,2},{8,12},{10,14},{12,8},{14,10},{16,20},{18,... | collective-permute-start | bytes 786440 | tf_op jit(solution)/shard_map/ppermute | solution.py:267
  39.7 12.1 %collective-permute-start.16 = (bf16[2,4,192,128]{3,2,1,0:T(8,128)(2,1)}, bf16[2,4,192,128]{3,2,1,0:T(8,128)(2,1)S(1)}, u32[]{:S(2)}, u32[]{:S(2)}) collective-permute-start(bf16[2,4,192,128]{3,2,1,0:T(8,128)(2,1)} %get-tuple-element.32), channel_id=1, source_target_pairs={{0,2},{2,0},{4,6},{6,4},{8,10},{10,8},{12,14},{14,12},{16,18},{18,... | collective-permute-start | bytes 1179656 | tf_op jit(solution)/shard_map/ppermute | solution.py:267
  39.9 6.4 %collective-permute-start.10 = (bf16[2,256,128]{2,1,0:T(8,128)(2,1)S(1)}, bf16[2,256,128]{2,1,0:T(8,128)(2,1)S(1)}, u32[]{:S(2)}, u32[]{:S(2)}) collective-permute-start(bf16[2,256,128]{2,1,0:T(8,128)(2,1)S(1)} %slice.111), channel_id=1, source_target_pairs={{0,8},{2,10},{4,12},{6,14},{8,0},{10,2},{12,4},{14,6},{16,24},{18,... | collective-permute-start | bytes 393224 | tf_op jit(solution)/shard_map/ppermute | solution.py:267
  43.1 5.9 %collective-permute-start.2 = (bf16[2,256,128]{2,1,0:T(8,128)(2,1)S(1)}, bf16[2,256,128]{2,1,0:T(8,128)(2,1)S(1)}, u32[]{:S(2)}, u32[]{:S(2)}) collective-permute-start(bf16[2,256,128]{2,1,0:T(8,128)(2,1)S(1)} %slice.107), channel_id=1, source_target_pairs={{0,8},{2,10},{4,12},{6,14},{8,0},{10,2},{12,4},{14,6},{16,24},{18,... | collective-permute-start | bytes 393224 | tf_op jit(solution)/shard_map/ppermute | solution.py:267
  46.3 12.5 %collective-permute-start.11 = (bf16[2,256,128]{2,1,0:T(8,128)(2,1)S(1)}, bf16[2,256,128]{2,1,0:T(8,128)(2,1)S(1)}, u32[]{:S(2)}, u32[]{:S(2)}) collective-permute-start(bf16[2,256,128]{2,1,0:T(8,128)(2,1)S(1)} %add_convert_fusion.8), channel_id=1, source_target_pairs={{0,16},{2,18},{4,20},{6,22},{8,24},{10,26},{12,28},{14,30},{16,0},... | collective-permute-start | bytes 393224 | tf_op jit(solution)/shard_map/ppermute | solution.py:267
  49.0 13.0 %collective-permute-start.3 = (bf16[2,256,128]{2,1,0:T(8,128)(2,1)S(1)}, bf16[2,256,128]{2,1,0:T(8,128)(2,1)S(1)}, u32[]{:S(2)}, u32[]{:S(2)}) collective-permute-start(bf16[2,256,128]{2,1,0:T(8,128)(2,1)S(1)} %add_convert_fusion.10), channel_id=1, source_target_pairs={{0,16},{2,18},{4,20},{6,22},{8,24},{10,26},{12,28},{14,30},{16,0},... | collective-permute-start | bytes 393224 | tf_op jit(solution)/shard_map/ppermute | solution.py:267
  52.8 6.1 %collective-permute-start.17 = (bf16[4,192,128]{2,1,0:T(8,128)(2,1)S(1)}, bf16[4,192,128]{2,1,0:T(8,128)(2,1)S(1)}, u32[]{:S(2)}, u32[]{:S(2)}) collective-permute-start(bf16[4,192,128]{2,1,0:T(8,128)(2,1)S(1)} %fusion.5), channel_id=1, source_target_pairs={{0,4},{2,6},{4,0},{6,2},{8,12},{10,14},{12,8},{14,10},{16,20},{18,... | collective-permute-start | bytes 589832 | tf_op jit(solution)/shard_map/ppermute | solution.py:267
  58.8 10.1 %collective-permute-start.12 = (bf16[512,128]{1,0:T(8,128)(2,1)S(1)}, bf16[512,128]{1,0:T(8,128)(2,1)S(1)}, u32[]{:S(2)}, u32[]{:S(2)}) collective-permute-start(bf16[512,128]{1,0:T(8,128)(2,1)S(1)} %bitcast.27), channel_id=1, source_target_pairs={{0,8},{2,10},{4,12},{6,14},{8,0},{10,2},{12,4},{14,6},{16,24},{18,... | collective-permute-start | bytes 393224 | tf_op jit(solution)/shard_map/ppermute | solution.py:267
  59.9 6.8 %collective-permute-start.18 = (bf16[2,192,128]{2,1,0:T(8,128)(2,1)S(1)}, bf16[2,192,128]{2,1,0:T(8,128)(2,1)S(1)}, u32[]{:S(2)}, u32[]{:S(2)}) collective-permute-start(bf16[2,192,128]{2,1,0:T(8,128)(2,1)S(1)} %slice.115), channel_id=1, source_target_pairs={{0,8},{2,10},{4,12},{6,14},{8,0},{10,2},{12,4},{14,6},{16,24},{18,... | collective-permute-start | bytes 294920 | tf_op jit(solution)/shard_map/ppermute | solution.py:267
  62.0 11.6 %collective-permute-start.4 = (bf16[512,128]{1,0:T(8,128)(2,1)S(1)}, bf16[512,128]{1,0:T(8,128)(2,1)S(1)}, u32[]{:S(2)}, u32[]{:S(2)}) collective-permute-start(bf16[512,128]{1,0:T(8,128)(2,1)S(1)} %bitcast.29), channel_id=1, source_target_pairs={{0,8},{2,10},{4,12},{6,14},{8,0},{10,2},{12,4},{14,6},{16,24},{18,... | collective-permute-start | bytes 393224 | tf_op jit(solution)/shard_map/ppermute | solution.py:267
  66.7 6.7 %collective-permute-start.19 = (bf16[2,192,128]{2,1,0:T(8,128)(2,1)S(1)}, bf16[2,192,128]{2,1,0:T(8,128)(2,1)S(1)}, u32[]{:S(2)}, u32[]{:S(2)}) collective-permute-start(bf16[2,192,128]{2,1,0:T(8,128)(2,1)S(1)} %add_convert_fusion.12), channel_id=1, source_target_pairs={{0,16},{2,18},{4,20},{6,22},{8,24},{10,26},{12,28},{14,30},{16,0},... | collective-permute-start | bytes 294920 | tf_op jit(solution)/shard_map/ppermute | solution.py:267
  68.9 10.8 %collective-permute-start.13 = (bf16[1024,128]{1,0:T(8,128)(2,1)S(1)}, bf16[1024,128]{1,0:T(8,128)(2,1)S(1)}, u32[]{:S(2)}, u32[]{:S(2)}) collective-permute-start(bf16[1024,128]{1,0:T(8,128)(2,1)S(1)} %pad_maximum_fusion.1.refs_6_), channel_id=1, source_target_pairs={{0,4},{2,6},{4,0},{6,2},{8,12},{10,14},{12,8},{14,10},{16,20},{18,... | collective-permute-start | bytes 786440 | tf_op jit(solution)/shard_map/ppermute | solution.py:267
  73.5 4.7 %collective-permute-start.20 = (bf16[384,128]{1,0:T(8,128)(2,1)S(1)}, bf16[384,128]{1,0:T(8,128)(2,1)S(1)}, u32[]{:S(2)}, u32[]{:S(2)}) collective-permute-start(bf16[384,128]{1,0:T(8,128)(2,1)S(1)} %bitcast.31), channel_id=1, source_target_pairs={{0,8},{2,10},{4,12},{6,14},{8,0},{10,2},{12,4},{14,6},{16,24},{18,... | collective-permute-start | bytes 294920 | tf_op jit(solution)/shard_map/ppermute | solution.py:267
  73.6 9.3 %collective-permute-start.5 = (bf16[1024,128]{1,0:T(8,128)(2,1)S(1)}, bf16[1024,128]{1,0:T(8,128)(2,1)S(1)}, u32[]{:S(2)}, u32[]{:S(2)}) collective-permute-start(bf16[1024,128]{1,0:T(8,128)(2,1)S(1)} %pad_maximum_fusion.refs_2_), channel_id=1, source_target_pairs={{0,4},{2,6},{4,0},{6,2},{8,12},{10,14},{12,8},{14,10},{16,20},{18,... | collective-permute-start | bytes 786440 | tf_op jit(solution)/shard_map/ppermute | solution.py:267
  75.1 7.8 %collective-permute-start.14 = (bf16[1024,128]{1,0:T(8,128)(2,1)S(1)}, bf16[1024,128]{1,0:T(8,128)(2,1)S(1)}, u32[]{:S(2)}, u32[]{:S(2)}) collective-permute-start(bf16[1024,128]{1,0:T(8,128)(2,1)S(1)} %pad_maximum_fusion.1.refs_6_), channel_id=1, source_target_pairs={{0,2},{2,0},{4,6},{6,4},{8,10},{10,8},{12,14},{14,12},{16,18},{18,... | collective-permute-start | bytes 786440 | tf_op jit(solution)/shard_map/ppermute | solution.py:267
  78.2 6.9 %collective-permute-start.21 = (bf16[768,128]{1,0:T(8,128)(2,1)S(1)}, bf16[768,128]{1,0:T(8,128)(2,1)S(1)}, u32[]{:S(2)}, u32[]{:S(2)}) collective-permute-start(bf16[768,128]{1,0:T(8,128)(2,1)S(1)} %pad_maximum_fusion.2.refs_10_), channel_id=1, source_target_pairs={{0,4},{2,6},{4,0},{6,2},{8,12},{10,14},{12,8},{14,10},{16,20},{18,... | collective-permute-start | bytes 589832 | tf_op jit(solution)/shard_map/ppermute | solution.py:267
  79.7 5.5 %collective-permute-start.6 = (bf16[1024,128]{1,0:T(8,128)(2,1)S(1)}, bf16[1024,128]{1,0:T(8,128)(2,1)S(1)}, u32[]{:S(2)}, u32[]{:S(2)}) collective-permute-start(bf16[1024,128]{1,0:T(8,128)(2,1)S(1)} %pad_maximum_fusion.refs_2_), channel_id=1, source_target_pairs={{0,2},{2,0},{4,6},{6,4},{8,10},{10,8},{12,14},{14,12},{16,18},{18,... | collective-permute-start | bytes 786440 | tf_op jit(solution)/shard_map/ppermute | solution.py:267
  79.7 5.5 %collective-permute-start.15 = (bf16[1024,128]{1,0:T(8,128)(2,1)S(1)}, bf16[1024,128]{1,0:T(8,128)(2,1)S(1)}, u32[]{:S(2)}, u32[]{:S(2)}) collective-permute-start(bf16[1024,128]{1,0:T(8,128)(2,1)S(1)} %collective-permute-done.13.refs_7_), channel_id=1, source_target_pairs={{0,2},{2,0},{4,6},{6,4},{8,10},{10,8},{12,14},{14,12},{16,18},{18,... | collective-permute-start | bytes 786440 | tf_op jit(solution)/shard_map/ppermute | solution.py:267
  82.9 2.3 %collective-permute-start.7 = (bf16[1024,128]{1,0:T(8,128)(2,1)S(1)}, bf16[1024,128]{1,0:T(8,128)(2,1)S(1)}, u32[]{:S(2)}, u32[]{:S(2)}) collective-permute-start(bf16[1024,128]{1,0:T(8,128)(2,1)S(1)} %collective-permute-done.5.refs_3_), channel_id=1, source_target_pairs={{0,2},{2,0},{4,6},{6,4},{8,10},{10,8},{12,14},{14,12},{16,18},{18,... | collective-permute-start | bytes 786440 | tf_op jit(solution)/shard_map/ppermute | solution.py:267
  83.0 2.2 %collective-permute-start.22 = (bf16[768,128]{1,0:T(8,128)(2,1)S(1)}, bf16[768,128]{1,0:T(8,128)(2,1)S(1)}, u32[]{:S(2)}, u32[]{:S(2)}) collective-permute-start(bf16[768,128]{1,0:T(8,128)(2,1)S(1)} %pad_maximum_fusion.2.refs_10_), channel_id=1, source_target_pairs={{0,2},{2,0},{4,6},{6,4},{8,10},{10,8},{12,14},{14,12},{16,18},{18,... | collective-permute-start | bytes 589832 | tf_op jit(solution)/shard_map/ppermute | solution.py:267
  108.0 25.4 %collective-permute-start.24 = (bf16[1024,512]{1,0:T(8,128)(2,1)}, bf16[1024,512]{1,0:T(8,128)(2,1)S(1)}, u32[]{:S(2)}, u32[]{:S(2)}) collective-permute-start(bf16[1024,512]{1,0:T(8,128)(2,1)} %mix.2.refs_21_), channel_id=1, source_target_pairs={{0,1},{1,0},{2,3},{3,2},{4,5},{5,4},{6,7},{7,6},{8,9},{9,8},{10,11... | collective-permute-start | bytes 3145736 | tf_op jit(solution)/shard_map/ppermute | solution.py:330
  (17 other events, 98.6 us)
